TPU v7x, 32 devices: a whole 2x2x4 slice. The times are simulated.
32 devices in a mesh: dp: 4 (over y, x), section: 2 (over core), tensor: 4 (over z).
Axes of the slice: x: 2, y: 2, z: 4, core: 2. Of those that a mesh axis runs over, the one named last changes fastest.
Arguments:
- inputs: bfloat16 [8, 1024, 1152], P('dp', 'tensor'), may hold values from -6 to 6
- time_emb: bfloat16 [8, 1152], P('dp'), may hold values from -6 to 6
- lengths: int32 [8], P('dp'), may hold values from 256 to 1024, as said below
- key_mask: int32 [8, 1024], P('dp'), may hold values from 0 to 1, as said below
- rel_index: int32 [2, 1024, 1024], replicated, may hold values from 0 to 3968, as said below
- w_qkv: bfloat16 [2, 1152, 3, 1152], P('section', None, None, 'tensor'), may hold values from -0.1875 to 0.1875
- w_time: bfloat16 [2, 1152, 2, 1152], P('section', None, None, 'tensor'), may hold values from -0.046875 to 0.046875
- w_proj: bfloat16 [2, 1152, 1152], P('section', None, 'tensor'), may hold values from -0.5 to 0.5
- w_fc1: bfloat16 [2, 1152, 4608], P('section', None, 'tensor'), may hold values from -0.1875 to 0.1875
- w_fc2: bfloat16 [2, 1152, 4608], P('section', None, 'tensor'), may hold values from -0.125 to 0.125
- rel_table: float32 [2, 16, 3969], P('section', 'tensor'), may hold values from -4 to 4
- norm_gains: float32 [2, 2, 1152], P('section'), may hold values from 0.1 to 1.9
- norm_biases: float32 [2, 2, 1152], P('section'), may hold values from -2 to 2
- cotangent: bfloat16 [8, 1024, 1152], P('dp', 'tensor'), may hold values from -6 to 6
Outputs:
- acts: bfloat16 [2, 8, 1024, 1152], P('section', 'dp', 'tensor')
- input_grads: float32 [2, 8, 1024, 1152], P('section', 'dp', 'tensor')
- grad_qkv: float32 [2, 1152, 3, 1152], P('section', 'dp', None, 'tensor')
- grad_time: float32 [2, 1152, 2, 1152], P('section', 'dp', None, 'tensor')
- grad_proj: float32 [2, 1152, 1152], P('section', 'dp', 'tensor')
- grad_fc1: float32 [2, 1152, 4608], P('section', 'dp', 'tensor')
- grad_fc2: float32 [2, 1152, 4608], P('section', 'dp', 'tensor')
- grad_rel: float32 [2, 16, 3969], P('section', 'tensor')
- grad_gains: float32 [2, 2, 1152], P('section', None, ('dp', 'tensor'))
- grad_biases: float32 [2, 2, 1152], P('section', None, ('dp', 'tensor'))
Inputs may be any that keep to these rules, and one draw needn't show every extreme that they name: `lengths`: each length is 256 or 1024; each aligned block of 2 images holds at least one image of length 1024. `key_mask`: zero at every slot at or beyond the image's length; slot 0 is always 1. `rel_index`: table 0 labels the offset between slots a and b of a 32 by 32 grid in row-major order, table 1 that of a 16 by 16 grid for slots below 256 and one label elsewhere; the labels are a permutation of the 3969 offsets.
All inputs are finite; a program needn't handle non-finite values.
Results may differ from a plain program's by a relative error of at most 0.024.
Values may be sent and summed in bfloat16 or wider, within the bound.
A program may use at most 320 MiB of HBM per device.

v0:
```python
import math

import jax
import jax.numpy as jnp
from jax import lax
from jax.sharding import PartitionSpec as P

EPSILON = 1e-05


def from_behind(shard, axis, by):
    count = lax.axis_size(axis)
    pairs = [(i, i + by) for i in range(count) if 0 <= i + by < count]
    return lax.ppermute(shard, axis, pairs)


def layer_norm(values, gain, shift):
    center = values - jnp.mean(values, axis=-1, keepdims=True)
    spread = jnp.mean(center * center, axis=-1, keepdims=True)
    return center * lax.rsqrt(spread + EPSILON) * gain + shift


def gelu_tanh(values):
    return jax.nn.gelu(values, approximate=True)


def offset_table(extent, grid_side):
    places = jnp.arange(extent)
    apart = places[:, None] - places[None, :] + grid_side - 1
    return (apart[:, :, None] == jnp.arange(2 * grid_side - 1)[None, None, :]).astype(jnp.bfloat16)


def offset_sums(score_grads, extent, table):
    heads_here = score_grads.shape[0]
    laid_out = score_grads.reshape(heads_here, extent, extent, extent, extent)
    by_rows = jnp.einsum("hiajb,ijx->hxab", laid_out, table, preferred_element_type=jnp.float32)
    return jnp.einsum(
        "hxab,aby->hxy",
        by_rows,
        table.astype(jnp.float32),
        precision=lax.Precision.HIGHEST,
        preferred_element_type=jnp.float32,
    )


def expand_offsets(offset_grid, extent, table):
    heads_here = offset_grid.shape[0]
    table_f = table.astype(jnp.float32)
    by_rows = jnp.einsum("hxy,ijx->hijy", offset_grid, table_f, precision=lax.Precision.HIGHEST)
    spread_out = jnp.einsum("hijy,aby->hiajb", by_rows, table_f, precision=lax.Precision.HIGHEST)
    return spread_out.reshape(heads_here, extent * extent, extent * extent)


def local(
    inputs,
    time_emb,
    lengths,
    key_mask,
    rel_index,
    w_qkv,
    w_time,
    w_proj,
    w_fc1,
    w_fc2,
    rel_table,
    norm_gains,
    norm_biases,
    cotangent,
):
    mb_count, tok_rows, width = inputs.shape
    seq_len = key_mask.shape[1]
    section_idx = lax.axis_index("section")
    tensor_idx = lax.axis_index("tensor")
    qkv_weight = w_qkv[0]
    time_weight = w_time[0]
    proj_weight = w_proj[0]
    up_weight = w_fc1[0]
    down_weight = w_fc2[0]
    bias_table = rel_table[0]
    gains = norm_gains[0]
    shifts = norm_biases[0]
    num_heads = bias_table.shape[0]
    buckets = bias_table.shape[1]
    local_width = qkv_weight.shape[2]
    head_dim = local_width // num_heads
    hidden_local = up_weight.shape[1]
    q_block = min(512, seq_len)
    num_blocks = seq_len // q_block
    score_scale = 1.0 / math.sqrt(head_dim)
    grid_side = math.isqrt(seq_len)
    half_side = grid_side // 2
    short_len = half_side * half_side
    offsets_across = 2 * grid_side - 1
    big_offsets = offset_table(grid_side, grid_side)
    small_offsets = offset_table(half_side, grid_side)
    offset_ids = jnp.arange(offsets_across * offsets_across)
    row_apart = offset_ids // offsets_across - (grid_side - 1)
    col_apart = offset_ids % offsets_across - (grid_side - 1)
    query_slot = jnp.maximum(row_apart, 0) * grid_side + jnp.maximum(col_apart, 0)
    key_slot = jnp.maximum(-row_apart, 0) * grid_side + jnp.maximum(-col_apart, 0)
    offset_labels = rel_index[0][query_slot, key_slot]
    offset_grid = bias_table[:, offset_labels].reshape(num_heads, offsets_across, offsets_across)
    big_bias = expand_offsets(offset_grid, grid_side, big_offsets)
    small_core = expand_offsets(offset_grid, half_side, small_offsets)
    outside_value = bias_table[:, rel_index[1][seq_len - 1, seq_len - 1]]
    small_bias = jnp.broadcast_to(outside_value[:, None, None], (num_heads, seq_len, seq_len))
    small_bias = lax.dynamic_update_slice(small_bias, small_core, (0, 0, 0))
    bias_all = jnp.stack([big_bias, small_bias])

    def block_scores(queries_h, keys_h, grid_kind, key_valid, row_start):
        bias_blk = lax.dynamic_slice(
            bias_all, (grid_kind, 0, row_start, 0), (1, num_heads, q_block, seq_len)
        )[0]
        scores = (
            jnp.einsum(
                "qhe,khe->hqk",
                queries_h[row_start : row_start + q_block],
                keys_h,
                preferred_element_type=jnp.float32,
            )
            * score_scale
            + bias_blk
        )
        return jnp.where(key_valid[None, None, :], scores, -1e30)

    def forward(layer_in, time_vec, grid_kind, key_valid):
        normed_local = layer_norm(layer_in, gains[0], shifts[0]).astype(jnp.bfloat16)
        normed = lax.all_gather(normed_local, "tensor", axis=0, tiled=True)
        qkv_all = jnp.einsum("rd,dcn->rcn", normed, qkv_weight, preferred_element_type=jnp.float32)
        time_terms = jnp.einsum(
            "d,dcn->cn", time_vec, time_weight, preferred_element_type=jnp.float32
        )
        queries = (qkv_all[:, 0] + time_terms[0]).astype(jnp.bfloat16)
        keys_all = qkv_all[:, 1].astype(jnp.bfloat16)
        values = (qkv_all[:, 2] + time_terms[1]).astype(jnp.bfloat16)
        queries_h = queries.reshape(seq_len, num_heads, head_dim)
        keys_h = keys_all.reshape(seq_len, num_heads, head_dim)
        values_h = values.reshape(seq_len, num_heads, head_dim)
        blk_outputs = []
        blk_sums = []
        for blk_idx in range(num_blocks):
            row_start = blk_idx * q_block
            scores = block_scores(queries_h, keys_h, grid_kind, key_valid, row_start)
            row_max = jnp.max(scores, axis=-1, keepdims=True)
            exp_scores = jnp.exp(scores - row_max)
            row_sum = jnp.sum(exp_scores, axis=-1, keepdims=True)
            attn_probs = (exp_scores / row_sum).astype(jnp.bfloat16)
            blk_outputs.append(
                jnp.einsum("hqk,khe->qhe", attn_probs, values_h, preferred_element_type=jnp.float32)
            )
            blk_sums.append(row_max[..., 0] + jnp.log(row_sum[..., 0]))
        attended = (
            jnp.concatenate(blk_outputs, axis=0).reshape(seq_len, local_width).astype(jnp.bfloat16)
        )
        log_sums = jnp.concatenate(blk_sums, axis=1)
        row_piece = attended
        hidden = layer_in + lax.psum_scatter(
            jnp.einsum(
                "rn,dn->rd", row_piece, proj_weight, preferred_element_type=jnp.float32
            ).astype(jnp.bfloat16),
            "tensor",
            scatter_dimension=0,
            tiled=True,
        ).astype(jnp.float32)
        normed_mlp_local = layer_norm(hidden, gains[1], shifts[1]).astype(jnp.bfloat16)
        normed_mlp = lax.all_gather(normed_mlp_local, "tensor", axis=0, tiled=True)
        pre_act = jnp.dot(normed_mlp, up_weight, preferred_element_type=jnp.float32)
        gelu_out = gelu_tanh(pre_act).astype(jnp.bfloat16)
        row_piece = gelu_out
        result = hidden + lax.psum_scatter(
            jnp.einsum(
                "rf,df->rd", row_piece, down_weight, preferred_element_type=jnp.float32
            ).astype(jnp.bfloat16),
            "tensor",
            scatter_dimension=0,
            tiled=True,
        ).astype(jnp.float32)
        kept_state = (
            layer_in,
            normed,
            queries,
            keys_all,
            values,
            log_sums,
            attended,
            hidden,
            normed_mlp,
            pre_act,
            gelu_out,
        )
        return (result, kept_state)

    def backward(grad_out, kept_state, time_vec, grid_kind, key_valid):
        (
            layer_in,
            normed,
            queries,
            keys_all,
            values,
            log_sums,
            attended,
            hidden,
            normed_mlp,
            pre_act,
            gelu_out,
        ) = kept_state
        dout_low = grad_out.astype(jnp.bfloat16)
        dout_all = lax.all_gather(dout_low, "tensor", axis=0, tiled=True)
        grad_down = jnp.einsum("rd,rf->df", dout_all, gelu_out, preferred_element_type=jnp.float32)
        grad_gelu = jnp.dot(dout_all, down_weight, preferred_element_type=jnp.float32)
        grad_pre = jax.vjp(gelu_tanh, pre_act)[1](grad_gelu)[0].astype(jnp.bfloat16)
        grad_up = jnp.einsum("rd,rf->df", normed_mlp, grad_pre, preferred_element_type=jnp.float32)
        row_piece = grad_pre
        grad_normed_mlp = lax.psum_scatter(
            jnp.einsum(
                "rf,df->rd", row_piece, up_weight, preferred_element_type=jnp.float32
            ).astype(jnp.bfloat16),
            "tensor",
            scatter_dimension=0,
            tiled=True,
        ).astype(jnp.float32)
        ln_pull_mlp = jax.vjp(layer_norm, hidden, gains[1], shifts[1])[1]
        grad_hid_ln, gain_grad_mlp, shift_grad_mlp = ln_pull_mlp(grad_normed_mlp)
        grad_hidden = grad_out + grad_hid_ln
        grad_branch = lax.all_gather(grad_hidden.astype(jnp.bfloat16), "tensor", axis=0, tiled=True)
        grad_proj = jnp.einsum(
            "rd,rn->dn", grad_branch, attended, preferred_element_type=jnp.float32
        )
        grad_attn = jnp.dot(grad_branch, proj_weight, preferred_element_type=jnp.float32).astype(
            jnp.bfloat16
        )
        grad_attn_h = grad_attn.reshape(seq_len, num_heads, head_dim)
        queries_h = queries.reshape(seq_len, num_heads, head_dim)
        keys_h = keys_all.reshape(seq_len, num_heads, head_dim)
        values_h = values.reshape(seq_len, num_heads, head_dim)
        grad_q_blocks = []
        score_blocks = []
        grad_k = jnp.zeros((seq_len, num_heads, head_dim), jnp.float32)
        grad_v = jnp.zeros((seq_len, num_heads, head_dim), jnp.float32)
        for blk_idx in range(num_blocks):
            row_start = blk_idx * q_block
            scores = block_scores(queries_h, keys_h, grid_kind, key_valid, row_start)
            attn_probs = jnp.exp(scores - log_sums[:, row_start : row_start + q_block, None])
            grad_out_h = grad_attn_h[row_start : row_start + q_block]
            grad_probs = jnp.einsum(
                "qhe,khe->hqk", grad_out_h, values_h, preferred_element_type=jnp.float32
            )
            row_inner = jnp.sum(attn_probs * grad_probs, axis=-1, keepdims=True)
            grad_scores = (attn_probs * (grad_probs - row_inner)).astype(jnp.bfloat16)
            grad_v = grad_v + jnp.einsum(
                "hqk,qhe->khe",
                attn_probs.astype(jnp.bfloat16),
                grad_out_h,
                preferred_element_type=jnp.float32,
            )
            grad_q_blocks.append(
                jnp.einsum("hqk,khe->qhe", grad_scores, keys_h, preferred_element_type=jnp.float32)
                * score_scale
            )
            grad_k = (
                grad_k
                + jnp.einsum(
                    "hqk,qhe->khe",
                    grad_scores,
                    queries_h[row_start : row_start + q_block],
                    preferred_element_type=jnp.float32,
                )
                * score_scale
            )
            score_blocks.append(grad_scores)
        all_scores = jnp.concatenate(score_blocks, axis=1)
        big_sums = offset_sums(all_scores, grid_side, big_offsets)
        small_sums = offset_sums(all_scores[:, :short_len, :short_len], half_side, small_offsets)
        tick_bias = jnp.where(grid_kind == 0, big_sums, small_sums)
        grad_q = jnp.concatenate(grad_q_blocks, axis=0)
        grad_qkv = jnp.stack(
            [
                grad_q.reshape(seq_len, local_width),
                grad_k.reshape(seq_len, local_width),
                grad_v.reshape(seq_len, local_width),
            ],
            axis=1,
        ).astype(jnp.bfloat16)
        grad_qkv_w = jnp.einsum("rd,rcn->dcn", normed, grad_qkv, preferred_element_type=jnp.float32)
        col_sums = jnp.sum(grad_qkv, axis=0, dtype=jnp.float32)
        grad_time = (
            time_vec.astype(jnp.float32)[:, None, None]
            * jnp.stack([col_sums[0], col_sums[2]])[None]
        )
        row_piece = grad_qkv
        grad_normed = lax.psum_scatter(
            jnp.einsum(
                "rcn,dcn->rd", row_piece, qkv_weight, preferred_element_type=jnp.float32
            ).astype(jnp.bfloat16),
            "tensor",
            scatter_dimension=0,
            tiled=True,
        ).astype(jnp.float32)
        ln_pull_attn = jax.vjp(layer_norm, layer_in, gains[0], shifts[0])[1]
        grad_in_ln, gain_grad_attn, shift_grad_attn = ln_pull_attn(grad_normed)
        grad_in = grad_hidden + grad_in_ln
        tick_weights = (grad_qkv_w, grad_time, grad_proj, grad_up, grad_down)
        tick_norms = (
            jnp.stack([gain_grad_attn, gain_grad_mlp]),
            jnp.stack([shift_grad_attn, shift_grad_mlp]),
        )
        return (grad_in, tick_weights, tick_norms, tick_bias)

    acc_rows = width // lax.axis_size("dp")
    weight_init = (
        jnp.zeros((acc_rows, 3, local_width), jnp.float32),
        jnp.zeros((acc_rows, 2, local_width), jnp.float32),
        jnp.zeros((acc_rows, local_width), jnp.float32),
        jnp.zeros((acc_rows, hidden_local), jnp.float32),
        jnp.zeros((acc_rows, hidden_local), jnp.float32),
    )
    norm_init = (jnp.zeros((2, width), jnp.float32), jnp.zeros((2, width), jnp.float32))
    cycle_init = (
        jnp.zeros((3, tok_rows, width), jnp.float32),
        jnp.zeros((3, seq_len, width), jnp.bfloat16),
        jnp.zeros((3, seq_len, local_width), jnp.bfloat16),
        jnp.zeros((3, seq_len, local_width), jnp.bfloat16),
        jnp.zeros((3, seq_len, local_width), jnp.bfloat16),
        jnp.zeros((3, num_heads, seq_len), jnp.float32),
        jnp.zeros((3, seq_len, local_width), jnp.bfloat16),
        jnp.zeros((3, tok_rows, width), jnp.float32),
        jnp.zeros((3, seq_len, width), jnp.bfloat16),
        jnp.zeros((3, seq_len, hidden_local), jnp.float32),
        jnp.zeros((3, seq_len, hidden_local), jnp.bfloat16),
    )
    loop_init = (
        jnp.zeros((tok_rows, width), jnp.bfloat16),
        jnp.zeros((tok_rows, width), jnp.bfloat16),
        cycle_init,
        jnp.zeros((mb_count, tok_rows, width), jnp.bfloat16),
        jnp.zeros((mb_count, tok_rows, width), jnp.float32),
        weight_init,
        norm_init,
        jnp.zeros((num_heads, offsets_across, offsets_across), jnp.float32),
    )

    def one_tick(tick_num, loop_state):
        recv_fwd, recv_bwd, cycle, acts_buf, grads_buf, weight_acc, norm_acc, bias_acc = loop_state
        fwd_mb = tick_num - section_idx
        bwd_mb = tick_num - 2 + section_idx
        fwd_ok = (fwd_mb >= 0) & (fwd_mb < mb_count)
        bwd_ok = (bwd_mb >= 0) & (bwd_mb < mb_count)
        fwd_at = jnp.clip(fwd_mb, 0, mb_count - 1)
        bwd_at = jnp.clip(bwd_mb, 0, mb_count - 1)
        first_in = inputs[fwd_at].astype(jnp.float32)
        layer_in = jnp.where(section_idx == 0, first_in, recv_fwd.astype(jnp.float32))
        kind_fwd = (lengths[fwd_at] < seq_len).astype(jnp.int32)
        result, kept_state = forward(layer_in, time_emb[fwd_at], kind_fwd, key_mask[fwd_at] > 0)
        slot_fwd = jnp.mod(fwd_mb, 3)
        cycle = tuple(
            (
                lax.dynamic_update_index_in_dim(buffer, entry, slot_fwd, 0)
                for buffer, entry in zip(cycle, kept_state)
            )
        )
        out_low = result.astype(jnp.bfloat16)
        acts_buf = lax.dynamic_update_index_in_dim(
            acts_buf, jnp.where(fwd_ok, out_low, acts_buf[fwd_at]), fwd_at, 0
        )
        slot_bwd = jnp.mod(bwd_mb, 3)
        kept_back = tuple(
            (lax.dynamic_index_in_dim(buffer, slot_bwd, 0, keepdims=False) for buffer in cycle)
        )
        row_ids = tensor_idx * tok_rows + jnp.arange(tok_rows)
        row_live = (row_ids < lengths[bwd_at]).astype(jnp.float32)
        last_grad = cotangent[bwd_at].astype(jnp.float32) * row_live[:, None]
        grad_out = jnp.where(
            section_idx == 1, last_grad, recv_bwd.astype(jnp.float32)
        ) * bwd_ok.astype(jnp.float32)
        kind_bwd = (lengths[bwd_at] < seq_len).astype(jnp.int32)
        grad_in, tick_weights, tick_norms, tick_bias = backward(
            grad_out, kept_back, time_emb[bwd_at], kind_bwd, key_mask[bwd_at] > 0
        )
        grads_buf = lax.dynamic_update_index_in_dim(
            grads_buf, jnp.where(bwd_ok, grad_in, grads_buf[bwd_at]), bwd_at, 0
        )
        reduced = (
            lax.psum_scatter(
                tick_weights[0].astype(jnp.bfloat16), "dp", scatter_dimension=0, tiled=True
            ).astype(jnp.float32),
            lax.psum_scatter(
                tick_weights[1].astype(jnp.bfloat16), "dp", scatter_dimension=0, tiled=True
            ).astype(jnp.float32),
            lax.psum_scatter(
                tick_weights[2].astype(jnp.bfloat16), "dp", scatter_dimension=0, tiled=True
            ).astype(jnp.float32),
            lax.psum_scatter(
                tick_weights[3].astype(jnp.bfloat16), "dp", scatter_dimension=0, tiled=True
            ).astype(jnp.float32),
            lax.psum_scatter(
                tick_weights[4].astype(jnp.bfloat16), "dp", scatter_dimension=0, tiled=True
            ).astype(jnp.float32),
        )
        weight_acc = tuple((acc_part + new_part for acc_part, new_part in zip(weight_acc, reduced)))
        norm_acc = (norm_acc[0] + tick_norms[0], norm_acc[1] + tick_norms[1])
        bias_acc = bias_acc + tick_bias
        recv_fwd = from_behind(out_low, "section", 1)
        recv_bwd = from_behind(grad_in.astype(jnp.bfloat16), "section", -1)
        return (recv_fwd, recv_bwd, cycle, acts_buf, grads_buf, weight_acc, norm_acc, bias_acc)

    final_state = lax.fori_loop(0, mb_count + 2, one_tick, loop_init)
    acts_buf, grads_buf, weight_acc, norm_acc, bias_acc = (
        final_state[3],
        final_state[4],
        final_state[5],
        final_state[6],
        final_state[7],
    )
    flat_bias = bias_acc.reshape(num_heads, offsets_across * offsets_across)
    rel_grad = jnp.zeros((num_heads, buckets), jnp.float32).at[:, offset_labels].add(flat_bias)
    rel_grad = lax.psum(rel_grad.astype(jnp.bfloat16), "dp").astype(jnp.float32)
    gain_grad, shift_grad = (
        lax.psum_scatter(norm_acc[0], ("dp", "tensor"), scatter_dimension=1, tiled=True),
        lax.psum_scatter(norm_acc[1], ("dp", "tensor"), scatter_dimension=1, tiled=True),
    )
    return (
        acts_buf[None],
        grads_buf[None],
        weight_acc[0][None],
        weight_acc[1][None],
        weight_acc[2][None],
        weight_acc[3][None],
        weight_acc[4][None],
        rel_grad[None],
        gain_grad[None],
        shift_grad[None],
    )


def solution(mesh):
    return jax.shard_map(
        local,
        mesh=mesh,
        in_specs=(
            P("dp", "tensor", None),
            P("dp", None),
            P("dp"),
            P("dp", None),
            P(),
            P("section", None, None, "tensor"),
            P("section", None, None, "tensor"),
            P("section", None, "tensor"),
            P("section", None, "tensor"),
            P("section", None, "tensor"),
            P("section", "tensor", None),
            P("section", None, None),
            P("section", None, None),
            P("dp", "tensor", None),
        ),
        out_specs=(
            P("section", "dp", "tensor", None),
            P("section", "dp", "tensor", None),
            P("section", "dp", None, "tensor"),
            P("section", "dp", None, "tensor"),
            P("section", "dp", "tensor"),
            P("section", "dp", "tensor"),
            P("section", "dp", "tensor"),
            P("section", "tensor", None),
            P("section", None, ("dp", "tensor")),
            P("section", None, ("dp", "tensor")),
        ),
        check_vma=False,
    )
```

profile of v0, /device:TPU:1, one launch (start us, length us, event | category | flops | bytes accessed | tf_op | source)
XLA Modules:
  0.0 3319.0 jit_solution(10935119222323101914)
XLA Ops:
  24.7 106.3 %gather_fusion = s32[3969]{0:T(1024)S(1)} fusion(s32[1024,1024]{1,0:T(8,128)} %get-tuple-element.1381, s32[3969]{0:T(1024)S(1)} %bitcast.555), kind=kCustom, calls=%fused_computation | custom fusion | bytes 63504 | tf_op jit(solution)/shard_map/gather | solution.py:101
  203.2 61.4 %copy.45 = f32[4,32,32,32,32]{4,3,2,1,0:T(8,128)} copy(f32[4,32,32,32,32]{3,4,1,0,2:T(8,128)} %convolution_bitcast_fusion.2) | data formatting | bytes 33554432 | tf_op jit(solution)/shard_map/hijy,aby->hiajb/transpose | solution.py:50
  264.6 50.8 %stack_reshape.3 = f32[1,4,1024,1024]{3,2,1,0:T(8,128)} reshape(f32[4,32,32,32,32]{4,3,2,1,0:T(8,128)} %copy.45) | data formatting | bytes 33554432 | tf_op jit(solution)/shard_map/stack;reshape | solution.py:108
  374.3 2818.4 %while.61 = (s32[]{:T(128)}, bf16[256,1152]{1,0:T(8,128)(2,1)S(1)}, bf16[256,1152]{1,0:T(8,128)(2,1)S(1)}, f32[3,256,1152]{2,1,0:T(8,128)}, bf16[3,1024,1152]{2,...) while((s32[]{:T(128)}, bf16[256,1152]{1,0:T(8,128)(2,1)S(1)}, ...), condition=%wide.region_33.34_spmd.clone.clone, body=%wide.region_0.33_spmd.clone.clone.sunk | while | flops 29700546560 | bytes 1030733120 | solution.py:406
  385.4 48.8 %all-gather.5.cloned.1.call-done = bf16[1024,1152]{1,0:T(8,128)(2,1)} async-done(((bf16[256,1152]{1,0:T(8,128)(2,1)}), bf16[1024,1152]{1,0:T(8,128)(2,1)}) %all-gather.5.cloned.1.call-update) | async-done | bytes 2359312 | tf_op jit(solution)/shard_map/while/body/eval_jaxpr/all_gather | solution.py:128
  474.0 46.6 %reduce-scatter.11.cloned.1.call-done = bf16[256,1152]{1,0:T(8,128)(2,1)} async-done(((bf16[1024,1152]{1,0:T(8,128)(2,1)}), bf16[256,1152]{1,0:T(8,128)(2,1)}) %reduce-scatter.11.cloned.1.call-update) | async-done | bytes 589840 | tf_op jit(solution)/shard_map/while/body/eval_jaxpr/reduce_scatter | solution.py:157
  527.2 48.4 %all-gather.7.cloned.1.call-done = bf16[1024,1152]{1,0:T(8,128)(2,1)} async-done(((bf16[256,1152]{1,0:T(8,128)(2,1)}), bf16[1024,1152]{1,0:T(8,128)(2,1)}) %all-gather.7.cloned.1.call-update) | async-done | bytes 2359312 | tf_op jit(solution)/shard_map/while/body/eval_jaxpr/all_gather | solution.py:166
  643.1 45.4 %reduce-scatter.15.cloned.1.call-done = bf16[256,1152]{1,0:T(8,128)(2,1)} async-done(((bf16[1024,1152]{1,0:T(8,128)(2,1)}), bf16[256,1152]{1,0:T(8,128)(2,1)}) %reduce-scatter.15.cloned.1.call-update) | async-done | bytes 589840 | tf_op jit(solution)/shard_map/while/body/eval_jaxpr/reduce_scatter | solution.py:214
  1023.4 47.9 %reduce-scatter.17.cloned.1.call-done = bf16[256,1152]{1,0:T(8,128)(2,1)} async-done(((bf16[1024,1152]{1,0:T(8,128)(2,1)}), bf16[256,1152]{1,0:T(8,128)(2,1)}) %reduce-scatter.17.cloned.1.call-update) | async-done | bytes 589840 | tf_op jit(solution)/shard_map/while/body/eval_jaxpr/reduce_scatter | solution.py:291
  1091.6 45.7 %all-gather.5.cloned.1.call-done = bf16[1024,1152]{1,0:T(8,128)(2,1)} async-done(((bf16[256,1152]{1,0:T(8,128)(2,1)}), bf16[1024,1152]{1,0:T(8,128)(2,1)}) %all-gather.5.cloned.1.call-update) | async-done | bytes 2359312 | tf_op jit(solution)/shard_map/while/body/eval_jaxpr/all_gather | solution.py:128
  1177.2 46.6 %reduce-scatter.11.cloned.1.call-done = bf16[256,1152]{1,0:T(8,128)(2,1)} async-done(((bf16[1024,1152]{1,0:T(8,128)(2,1)}), bf16[256,1152]{1,0:T(8,128)(2,1)}) %reduce-scatter.11.cloned.1.call-update) | async-done | bytes 589840 | tf_op jit(solution)/shard_map/while/body/eval_jaxpr/reduce_scatter | solution.py:157
  1230.4 48.3 %all-gather.7.cloned.1.call-done = bf16[1024,1152]{1,0:T(8,128)(2,1)} async-done(((bf16[256,1152]{1,0:T(8,128)(2,1)}), bf16[1024,1152]{1,0:T(8,128)(2,1)}) %all-gather.7.cloned.1.call-update) | async-done | bytes 2359312 | tf_op jit(solution)/shard_map/while/body/eval_jaxpr/all_gather | solution.py:166
  1346.2 45.4 %reduce-scatter.15.cloned.1.call-done = bf16[256,1152]{1,0:T(8,128)(2,1)} async-done(((bf16[1024,1152]{1,0:T(8,128)(2,1)}), bf16[256,1152]{1,0:T(8,128)(2,1)}) %reduce-scatter.15.cloned.1.call-update) | async-done | bytes 589840 | tf_op jit(solution)/shard_map/while/body/eval_jaxpr/reduce_scatter | solution.py:214
  1726.8 47.4 %reduce-scatter.17.cloned.1.call-done = bf16[256,1152]{1,0:T(8,128)(2,1)} async-done(((bf16[1024,1152]{1,0:T(8,128)(2,1)}), bf16[256,1152]{1,0:T(8,128)(2,1)}) %reduce-scatter.17.cloned.1.call-update) | async-done | bytes 589840 | tf_op jit(solution)/shard_map/while/body/eval_jaxpr/reduce_scatter | solution.py:291
  1794.6 45.7 %all-gather.5.cloned.1.call-done = bf16[1024,1152]{1,0:T(8,128)(2,1)} async-done(((bf16[256,1152]{1,0:T(8,128)(2,1)}), bf16[1024,1152]{1,0:T(8,128)(2,1)}) %all-gather.5.cloned.1.call-update) | async-done | bytes 2359312 | tf_op jit(solution)/shard_map/while/body/eval_jaxpr/all_gather | solution.py:128
  1880.1 46.6 %reduce-scatter.11.cloned.1.call-done = bf16[256,1152]{1,0:T(8,128)(2,1)} async-done(((bf16[1024,1152]{1,0:T(8,128)(2,1)}), bf16[256,1152]{1,0:T(8,128)(2,1)}) %reduce-scatter.11.cloned.1.call-update) | async-done | bytes 589840 | tf_op jit(solution)/shard_map/while/body/eval_jaxpr/reduce_scatter | solution.py:157
  1933.2 48.4 %all-gather.7.cloned.1.call-done = bf16[1024,1152]{1,0:T(8,128)(2,1)} async-done(((bf16[256,1152]{1,0:T(8,128)(2,1)}), bf16[1024,1152]{1,0:T(8,128)(2,1)}) %all-gather.7.cloned.1.call-update) | async-done | bytes 2359312 | tf_op jit(solution)/shard_map/while/body/eval_jaxpr/all_gather | solution.py:166
  2429.7 47.4 %reduce-scatter.17.cloned.1.call-done = bf16[256,1152]{1,0:T(8,128)(2,1)} async-done(((bf16[1024,1152]{1,0:T(8,128)(2,1)}), bf16[256,1152]{1,0:T(8,128)(2,1)}) %reduce-scatter.17.cloned.1.call-update) | async-done | bytes 589840 | tf_op jit(solution)/shard_map/while/body/eval_jaxpr/reduce_scatter | solution.py:291
  2497.4 45.7 %all-gather.5.cloned.1.call-done = bf16[1024,1152]{1,0:T(8,128)(2,1)} async-done(((bf16[256,1152]{1,0:T(8,128)(2,1)}), bf16[1024,1152]{1,0:T(8,128)(2,1)}) %all-gather.5.cloned.1.call-update) | async-done | bytes 2359312 | tf_op jit(solution)/shard_map/while/body/eval_jaxpr/all_gather | solution.py:128
  2582.9 46.6 %reduce-scatter.11.cloned.1.call-done = bf16[256,1152]{1,0:T(8,128)(2,1)} async-done(((bf16[1024,1152]{1,0:T(8,128)(2,1)}), bf16[256,1152]{1,0:T(8,128)(2,1)}) %reduce-scatter.11.cloned.1.call-update) | async-done | bytes 589840 | tf_op jit(solution)/shard_map/while/body/eval_jaxpr/reduce_scatter | solution.py:157
  2636.1 48.4 %all-gather.7.cloned.1.call-done = bf16[1024,1152]{1,0:T(8,128)(2,1)} async-done(((bf16[256,1152]{1,0:T(8,128)(2,1)}), bf16[1024,1152]{1,0:T(8,128)(2,1)}) %all-gather.7.cloned.1.call-update) | async-done | bytes 2359312 | tf_op jit(solution)/shard_map/while/body/eval_jaxpr/all_gather | solution.py:166
  2751.9 45.4 %reduce-scatter.15.cloned.1.call-done = bf16[256,1152]{1,0:T(8,128)(2,1)} async-done(((bf16[1024,1152]{1,0:T(8,128)(2,1)}), bf16[256,1152]{1,0:T(8,128)(2,1)}) %reduce-scatter.15.cloned.1.call-update) | async-done | bytes 589840 | tf_op jit(solution)/shard_map/while/body/eval_jaxpr/reduce_scatter | solution.py:214
  3132.2 47.5 %reduce-scatter.17.cloned.1.call-done = bf16[256,1152]{1,0:T(8,128)(2,1)} async-done(((bf16[1024,1152]{1,0:T(8,128)(2,1)}), bf16[256,1152]{1,0:T(8,128)(2,1)}) %reduce-scatter.17.cloned.1.call-update) | async-done | bytes 589840 | tf_op jit(solution)/shard_map/while/body/eval_jaxpr/reduce_scatter | solution.py:291
  3192.8 61.4 %all-reduce.3 = (f32[2,1152]{1,0:T(2,128)S(1)}, f32[2,1152]{1,0:T(2,128)S(1)}) all-reduce(f32[2,1152]{1,0:T(2,128)} %get-tuple-element.2049, f32[2,1152]{1,0:T(2,128)} %get-tuple-element.2050), channel_id=11, replica_groups=mesh['dp'=4,'section'=2,'tensor'=4] {'dp','tensor'}, use_global_device_ids=true, to_apply=%region_36.37.clone | all-reduce | flops 4608 | bytes 36864
  (1271 shorter events, 2113.3 us)
Async XLA Ops:
  716.0 165.4 %reduce-scatter.25.cloned.1.call-start = ((), (), s32[]{:S(2)}) async-start(), calls=%async_computation.20 | async-start | bytes 3317760 | tf_op jit(solution)/shard_map/while/body/eval_jaxpr/reduce_scatter | solution.py:395
  735.1 223.0 %reduce-scatter.21.cloned.1.call-start = ((), (), s32[]{:S(2)}) async-start(), calls=%async_computation.18 | async-start | bytes 1105920 | tf_op jit(solution)/shard_map/while/body/eval_jaxpr/reduce_scatter | solution.py:389
  789.1 189.2 %all-reduce.8.cloned.1.call-start = ((), (), s32[]{:S(2)}) async-start(), calls=%async_computation.17 | async-start | bytes 3538944 | tf_op jit(solution)/shard_map/while
  797.4 223.7 %reduce-scatter.19.cloned.1.call-start = ((), (), s32[]{:S(2)}) async-start(), calls=%async_computation.16 | async-start | bytes 3317760 | tf_op jit(solution)/shard_map/while/body/eval_jaxpr/reduce_scatter | solution.py:383
  808.1 263.2 %reduce-scatter.17.cloned.1.call-start = ((), (), s32[]{:S(2)}) async-start(), calls=%async_computation.15 | async-start | bytes 2949120 | tf_op jit(solution)/shard_map/while/body/eval_jaxpr/reduce_scatter | solution.py:291
  817.3 261.7 %collective-permute-start = (bf16[256,1152]{1,0:T(8,128)(2,1)}, bf16[256,1152]{1,0:T(8,128)(2,1)S(1)}, u32[]{:S(2)}, u32[]{:S(2)}) collective-permute-start(bf16[256,1152]{1,0:T(8,128)(2,1)} %get-tuple-element.1716), channel_id=1, source_target_pairs={{0,4},{1,5},{2,6},{3,7},{8,12},{9,13},{10,14},{11,15},{16,20},{17,... | collective-permute-start | bytes 1769480 | tf_op jit(solution)/shard_map/while/body/eval_jaxpr/ppermute | solution.py:14
  1419.1 165.2 %reduce-scatter.25.cloned.1.call-start = ((), (), s32[]{:S(2)}) async-start(), calls=%async_computation.20 | async-start | bytes 3317760 | tf_op jit(solution)/shard_map/while/body/eval_jaxpr/reduce_scatter | solution.py:395
  1438.1 223.4 %reduce-scatter.21.cloned.1.call-start = ((), (), s32[]{:S(2)}) async-start(), calls=%async_computation.18 | async-start | bytes 1105920 | tf_op jit(solution)/shard_map/while/body/eval_jaxpr/reduce_scatter | solution.py:389
  1492.2 189.1 %all-reduce.8.cloned.1.call-start = ((), (), s32[]{:S(2)}) async-start(), calls=%async_computation.17 | async-start | bytes 3538944 | tf_op jit(solution)/shard_map/while
  1500.5 223.7 %reduce-scatter.19.cloned.1.call-start = ((), (), s32[]{:S(2)}) async-start(), calls=%async_computation.16 | async-start | bytes 3317760 | tf_op jit(solution)/shard_map/while/body/eval_jaxpr/reduce_scatter | solution.py:383
  1511.0 263.2 %reduce-scatter.17.cloned.1.call-start = ((), (), s32[]{:S(2)}) async-start(), calls=%async_computation.15 | async-start | bytes 2949120 | tf_op jit(solution)/shard_map/while/body/eval_jaxpr/reduce_scatter | solution.py:291
  1520.3 261.6 %collective-permute-start = (bf16[256,1152]{1,0:T(8,128)(2,1)}, bf16[256,1152]{1,0:T(8,128)(2,1)S(1)}, u32[]{:S(2)}, u32[]{:S(2)}) collective-permute-start(bf16[256,1152]{1,0:T(8,128)(2,1)} %get-tuple-element.1716), channel_id=1, source_target_pairs={{0,4},{1,5},{2,6},{3,7},{8,12},{9,13},{10,14},{11,15},{16,20},{17,... | collective-permute-start | bytes 1769480 | tf_op jit(solution)/shard_map/while/body/eval_jaxpr/ppermute | solution.py:14
  2122.0 165.3 %reduce-scatter.25.cloned.1.call-start = ((), (), s32[]{:S(2)}) async-start(), calls=%async_computation.20 | async-start | bytes 3317760 | tf_op jit(solution)/shard_map/while/body/eval_jaxpr/reduce_scatter | solution.py:395
  2141.0 223.4 %reduce-scatter.21.cloned.1.call-start = ((), (), s32[]{:S(2)}) async-start(), calls=%async_computation.18 | async-start | bytes 1105920 | tf_op jit(solution)/shard_map/while/body/eval_jaxpr/reduce_scatter | solution.py:389
  2195.1 188.9 %all-reduce.8.cloned.1.call-start = ((), (), s32[]{:S(2)}) async-start(), calls=%async_computation.17 | async-start | bytes 3538944 | tf_op jit(solution)/shard_map/while
  2203.5 223.5 %reduce-scatter.19.cloned.1.call-start = ((), (), s32[]{:S(2)}) async-start(), calls=%async_computation.16 | async-start | bytes 3317760 | tf_op jit(solution)/shard_map/while/body/eval_jaxpr/reduce_scatter | solution.py:383
  2214.0 263.0 %reduce-scatter.17.cloned.1.call-start = ((), (), s32[]{:S(2)}) async-start(), calls=%async_computation.15 | async-start | bytes 2949120 | tf_op jit(solution)/shard_map/while/body/eval_jaxpr/reduce_scatter | solution.py:291
  2223.3 261.4 %collective-permute-start = (bf16[256,1152]{1,0:T(8,128)(2,1)}, bf16[256,1152]{1,0:T(8,128)(2,1)S(1)}, u32[]{:S(2)}, u32[]{:S(2)}) collective-permute-start(bf16[256,1152]{1,0:T(8,128)(2,1)} %get-tuple-element.1716), channel_id=1, source_target_pairs={{0,4},{1,5},{2,6},{3,7},{8,12},{9,13},{10,14},{11,15},{16,20},{17,... | collective-permute-start | bytes 1769480 | tf_op jit(solution)/shard_map/while/body/eval_jaxpr/ppermute | solution.py:14
  2824.9 165.0 %reduce-scatter.25.cloned.1.call-start = ((), (), s32[]{:S(2)}) async-start(), calls=%async_computation.20 | async-start | bytes 3317760 | tf_op jit(solution)/shard_map/while/body/eval_jaxpr/reduce_scatter | solution.py:395
  2843.9 223.1 %reduce-scatter.21.cloned.1.call-start = ((), (), s32[]{:S(2)}) async-start(), calls=%async_computation.18 | async-start | bytes 1105920 | tf_op jit(solution)/shard_map/while/body/eval_jaxpr/reduce_scatter | solution.py:389
  2898.0 188.8 %all-reduce.8.cloned.1.call-start = ((), (), s32[]{:S(2)}) async-start(), calls=%async_computation.17 | async-start | bytes 3538944 | tf_op jit(solution)/shard_map/while
  2906.3 223.2 %reduce-scatter.19.cloned.1.call-start = ((), (), s32[]{:S(2)}) async-start(), calls=%async_computation.16 | async-start | bytes 3317760 | tf_op jit(solution)/shard_map/while/body/eval_jaxpr/reduce_scatter | solution.py:383
  2916.9 262.8 %reduce-scatter.17.cloned.1.call-start = ((), (), s32[]{:S(2)}) async-start(), calls=%async_computation.15 | async-start | bytes 2949120 | tf_op jit(solution)/shard_map/while/body/eval_jaxpr/reduce_scatter | solution.py:291
  2926.1 261.3 %collective-permute-start = (bf16[256,1152]{1,0:T(8,128)(2,1)}, bf16[256,1152]{1,0:T(8,128)(2,1)S(1)}, u32[]{:S(2)}, u32[]{:S(2)}) collective-permute-start(bf16[256,1152]{1,0:T(8,128)(2,1)} %get-tuple-element.1716), channel_id=1, source_target_pairs={{0,4},{1,5},{2,6},{3,7},{8,12},{9,13},{10,14},{11,15},{16,20},{17,... | collective-permute-start | bytes 1769480 | tf_op jit(solution)/shard_map/while/body/eval_jaxpr/ppermute | solution.py:14
  (336 other events, 7621.6 us)
Sparse Core Ops, SparseCore 0:
  381.6 52.5 all-gather.4
  525.4 50.0 all-gather.6
  577.0 49.2 all-gather.8
  696.8 50.0 all-gather.10
  914.1 64.1 all-reduce.7
  1023.4 47.8 reduce-scatter.16
  1087.9 49.4 all-gather.4
  1228.6 50.0 all-gather.6
  1280.1 49.2 all-gather.8
  1399.8 50.0 all-gather.10
  1617.0 64.1 all-reduce.7
  1726.3 47.8 reduce-scatter.16
  1790.8 49.4 all-gather.4
  1931.5 50.1 all-gather.6
  1983.1 49.2 all-gather.8
  2102.8 50.0 all-gather.10
  2319.8 64.1 all-reduce.7
  2429.1 47.8 reduce-scatter.16
  2493.6 49.4 all-gather.4
  2634.3 50.0 all-gather.6
  2685.9 49.2 all-gather.8
  2805.6 50.0 all-gather.10
  3022.5 64.1 all-reduce.7
  3131.8 47.8 reduce-scatter.16
  (28 shorter events, 1142.7 us)
where the time goes:
time: 3350 us; the launch traced here: 3320 us
  waiting for transfers between devices  1610 us (48%)
  local copies, waits for them, and re-layouts  640 us (19%)
  matrix products  603 us (18%)
  other arithmetic  321 us (10%)
  blocking collectives  89.6 us (3%)
    all_gather x4, waiting for transfers between devices, forward(): normed_mlp = lax.all_gather(normed_mlp_local, 'tensor', axis=0, tiled=True)  193 us
    reduce_scatter x4, waiting for transfers between devices, backward(): lax.psum_scatter(jnp.einsum('rcn,dcn->rd', row_piece, qkv_weight, preferr...  190 us
    reduce_scatter x4, waiting for transfers between devices, forward(): lax.psum_scatter(jnp.einsum('rn,dn->rd', row_piece, proj_weight, preferre...  186 us
    all_gather x4, waiting for transfers between devices, forward(): normed = lax.all_gather(normed_local, 'tensor', axis=0, tiled=True)  186 us
    reduce_scatter x4, waiting for transfers between devices, backward(): lax.psum_scatter(jnp.einsum('rf,df->rd', row_piece, up_weight, preferred_...  182 us
    reshape x8, local copies, waits for them, and re-layouts, offset_sums(): laid_out = score_grads.reshape(heads_here, extent, extent, extent, extent)  174 us
    reduce_scatter x4, waiting for transfers between devices, one_tick(): lax.psum_scatter(tick_weights[0].astype(jnp.bfloat16), 'dp', scatter_dime...  164 us
    all_gather x4, waiting for transfers between devices, backward(): dout_all = lax.all_gather(dout_low, 'tensor', axis=0, tiled=True)  164 us
  transfers between devices with their start and end apart: 60, of which 48 were waited for; matrix products, arithmetic and copies ran while one was open for 25% of the time, Pallas kernels for 0%

commit v1 on v0

v1 whole, which is shorter than its diff:
```python
import functools
import math

import jax
import jax.numpy as jnp
from jax import lax
from jax.experimental import pallas as pl
from jax.experimental.pallas import tpu as pltpu
from jax.sharding import PartitionSpec as P

LOG2E = 1.4426950408889634
HIGHEST = lax.Precision.HIGHEST
BIGL = 1920
SMALL0 = 4 * BIGL
WALL = SMALL0 + 2304


def _labels_hi_lo(lab):
    hi = lax.shift_right_logical(lab, 6)
    lo = jnp.bitwise_and(lab, 63)
    iota = lax.broadcasted_iota(jnp.int32, (64, lab.shape[1]), 0)
    return iota == hi, jnp.where(iota == lo, 1.0, 0.0)


def bias_kernel(out_lab_ref, lab_ref, table_ref, wall_ref):
    lab = lab_ref[...]
    hi_mask, lo_hot = _labels_hi_lo(lab)
    rows = lax.dot_general(table_ref[0], lo_hot, (((1,), (0,)), ((), ())), precision=HIGHEST, preferred_element_type=jnp.float32)
    flat = jnp.sum(jnp.where(hi_mask, rows, 0.0), axis=0, keepdims=True) * LOG2E
    outside = jnp.sum(jnp.where(lab == out_lab_ref[0], flat, 0.0), axis=1, keepdims=True)
    wide = jnp.broadcast_to(flat, (32, 4096))
    wide = pltpu.roll(wide, 4096 - 31, 1, stride=1, stride_axis=0)
    lane = lax.broadcasted_iota(jnp.int32, (32, 128), 1)
    tight = []
    for g in range(16):
        a = wide[:, 256 * g : 256 * g + 128]
        b = wide[:, 256 * g + 128 : 256 * g + 256]
        piece = jnp.where(lane < 32, a, pltpu.roll(a, 96, 1))
        other = jnp.where(lane < 96, pltpu.roll(b, 64, 1), pltpu.roll(b, 32, 1))
        tight.append(jnp.where(lane < 64, piece, other))
    w0 = jnp.concatenate(tight, axis=1)
    for s in range(4):
        shifted = w0 if s == 0 else pltpu.roll(w0, 2048 - 32 * s, 1)
        wall_ref[0, :, s * BIGL : (s + 1) * BIGL] = shifted[:, :BIGL]
    lane16 = lane[:16]
    tight16 = []
    for g in range(8):
        lo_v = w0[:16, 256 * g : 256 * g + 128]
        hi_v = w0[:16, 256 * g + 128 : 256 * g + 256]
        acc = lo_v
        for k in range(1, 4):
            acc = jnp.where(lane16 >= 16 * k, pltpu.roll(lo_v, 128 - 16 * k, 1), acc)
        for k in range(4):
            acc = jnp.where(lane16 >= 64 + 16 * k, pltpu.roll(hi_v, (64 - 16 * k) % 128, 1), acc)
        tight16.append(acc)
    w16 = jnp.concatenate(tight16, axis=1)
    for j in range(16):
        sl = pltpu.roll(w16, 1024 - 16 * (31 - j), 1)[:, :256]
        wall_ref[0, 16 * (j % 2) : 16 * (j % 2) + 16, SMALL0 + 256 * (j // 2) : SMALL0 + 256 * (j // 2) + 256] = sl
    wall_ref[0, :, SMALL0 + 2048 : WALL] = jnp.broadcast_to(outside, (32, 256))


def bias_tables(out_lab, lab, table):
    heads = table.shape[0]
    return pl.pallas_call(
        bias_kernel,
        grid=(heads,),
        in_specs=[
            pl.BlockSpec(memory_space=pltpu.SMEM),
            pl.BlockSpec((1, 4096), lambda h: (0, 0)),
            pl.BlockSpec((1, 64, 64), lambda h: (h, 0, 0)),
        ],
        out_specs=pl.BlockSpec((1, 32, WALL), lambda h: (h, 0, 0)),
        out_shape=jax.ShapeDtypeStruct((heads, 32, WALL), jnp.float32),
        compiler_params=pltpu.CompilerParams(vmem_limit_bytes=40 << 20),
    )(out_lab, lab, table)


def bias_grad_kernel(out_lab_ref, lab_ref, acc_ref, out_ref):
    lab = lab_ref[...]
    hi_mask, lo_hot = _labels_hi_lo(lab)
    acc = acc_ref[0]
    w0 = jnp.zeros((32, 2048), jnp.float32)
    for s in range(4):
        piece = jnp.concatenate([acc[:, s * BIGL : (s + 1) * BIGL], jnp.zeros((32, 128), jnp.float32)], axis=1)
        w0 = w0 + (piece if s == 0 else pltpu.roll(piece, 32 * s, 1))
    w16 = jnp.zeros((16, 1024), jnp.float32)
    for j in range(16):
        piece = acc[16 * (j % 2) : 16 * (j % 2) + 16, SMALL0 + 256 * (j // 2) : SMALL0 + 256 * (j // 2) + 256]
        piece = jnp.concatenate([piece, jnp.zeros((16, 768), jnp.float32)], axis=1)
        w16 = w16 + pltpu.roll(piece, 16 * (31 - j), 1)
    outside = jnp.sum(jnp.sum(acc[:, SMALL0 + 2048 : WALL], axis=0, keepdims=True), axis=1, keepdims=True)
    lane = lax.broadcasted_iota(jnp.int32, (32, 128), 1)
    lane16 = lane[:16]
    wide = []
    for g in range(32):
        src = w0[:, 128 * (g // 2) : 128 * (g // 2) + 128]
        k = 2 * (g % 2)
        first = src if k == 0 else pltpu.roll(src, 128 - 32 * k, 1)
        second = pltpu.roll(src, (64 - 32 * (k + 1)) % 128, 1)
        piece = jnp.where(lane < 32, first, jnp.where((lane >= 64) & (lane < 96), second, 0.0))
        src16 = w16[:, 128 * (g // 4) : 128 * (g // 4) + 128]
        k = 2 * (g % 4)
        first = src16 if k == 0 else pltpu.roll(src16, 128 - 16 * k, 1)
        second = pltpu.roll(src16, (64 - 16 * (k + 1)) % 128, 1)
        piece16 = jnp.where(lane16 < 16, first, jnp.where((lane16 >= 64) & (lane16 < 80), second, 0.0))
        wide.append(piece + jnp.concatenate([piece16, jnp.zeros((16, 128), jnp.float32)], axis=0))
    wide = jnp.concatenate(wide, axis=1)
    back = 31 - lax.broadcasted_iota(jnp.int32, (32, 4096), 0)
    for k in range(5):
        wide = jnp.where(jnp.bitwise_and(back, 1 << k) > 0, pltpu.roll(wide, 1 << k, 1), wide)
    flat = jnp.sum(wide, axis=0, keepdims=True)
    flat = flat + jnp.where(lab == out_lab_ref[0], outside, 0.0)
    spread = jnp.where(hi_mask, jnp.broadcast_to(flat, (64, 4096)), 0.0)
    out_ref[0] = lax.dot_general(spread, lo_hot, (((1,), (1,)), ((), ())), precision=HIGHEST, preferred_element_type=jnp.float32)


def bias_grads(out_lab, lab, acc):
    heads = acc.shape[0]
    return pl.pallas_call(
        bias_grad_kernel,
        grid=(heads,),
        in_specs=[
            pl.BlockSpec(memory_space=pltpu.SMEM),
            pl.BlockSpec((1, 4096), lambda h: (0, 0)),
            pl.BlockSpec((1, 32, WALL), lambda h: (h, 0, 0)),
        ],
        out_specs=pl.BlockSpec((1, 64, 64), lambda h: (h, 0, 0)),
        out_shape=jax.ShapeDtypeStruct((heads, 64, 64), jnp.float32),
        compiler_params=pltpu.CompilerParams(vmem_limit_bytes=40 << 20),
    )(out_lab, lab, acc)


def label_row(rel_index):
    side = 32
    a = rel_index[0, 1023].reshape(side, side)
    b = rel_index[0, 0].reshape(side, side)
    c = rel_index[0, 992].reshape(side, side)
    d = rel_index[0, 31].reshape(side, side)
    top = jnp.concatenate([a, c[:, 1:]], axis=1)
    low = jnp.concatenate([d[1:], b[1:, 1:]], axis=1)
    grid = jnp.flip(jnp.concatenate([top, low], axis=0), (0, 1))
    return jnp.pad(grid, ((0, 1), (0, 1)), constant_values=4095).reshape(1, 4096)


NT = (((1,), (1,)), ((), ()))
TN = (((0,), (0,)), ((), ()))
NN = (((1,), (0,)), ((), ()))
HD = 72
QB = 256


def dot(a, b, dims):
    return lax.dot_general(a, b, dims, preferred_element_type=jnp.float32)


def head_lanes(x, at, extra=None):
    rows = x.shape[0]
    part = x[:, at : at + HD]
    if extra is None:
        pad = jnp.zeros((rows, 128 - HD), x.dtype)
    else:
        pad = extra
    return jnp.concatenate([part, pad], axis=1)


def strip_start(t, small, q_quarter, jj, rel):
    kq = jnp.bitwise_xor(t, rel)
    big = BIGL * ((31 - jj) % 4) + 128 * ((31 - jj) // 4 - 2 * kq + 2 * q_quarter)
    inner = SMALL0 + 256 * jj
    tiny = jnp.where((kq == 0) & (q_quarter == 0), inner, SMALL0 + 2048)
    return pl.multiple_of(jnp.where(small == 1, tiny, big), 128)


def attn_fwd_kernel(order, scale, sc_ref, q_ref, kv_ref, mask_ref, wall_ref, o_ref, lse_ref, s_scr, p_scr):
    t, small = sc_ref[0], sc_ref[1]
    qq = jnp.bitwise_xor(t, sc_ref[2 + pl.program_id(0)])
    heads = wall_ref.shape[0]
    width = heads * HD
    rows = kv_ref.shape[0]
    nstrip = rows // 32
    k_extra = mask_ref[...]
    lane = lax.broadcasted_iota(jnp.int32, (QB, 128 - HD), 1)
    q_extra = jnp.where(lane == 0, 1.0, 0.0).astype(jnp.bfloat16)
    outs = []
    for h in range(heads):
        kh = head_lanes(kv_ref, width + HD * h, k_extra)
        qh = head_lanes(q_ref, HD * h, q_extra)
        vh = head_lanes(kv_ref, 2 * width + HD * h)
        s_scr[h % 2] = dot(kh, qh, NT)
        top = None
        for st in range(nstrip):
            start = strip_start(t, small, qq, st % 8, order[st // 8])
            s = s_scr[h % 2, 32 * st : 32 * st + 32] * (scale * LOG2E) + wall_ref[h, :, pl.ds(start, QB)]
            s_scr[h % 2, 32 * st : 32 * st + 32] = s
            top = s if top is None else jnp.maximum(top, s)
        row_max = jnp.max(top, axis=0, keepdims=True)
        total = None
        for st in range(nstrip):
            p = jnp.exp2(s_scr[h % 2, 32 * st : 32 * st + 32] - row_max)
            p_scr[h % 2, 32 * st : 32 * st + 32] = p.astype(jnp.bfloat16)
            total = p if total is None else total + p
        row_sum = jnp.sum(total, axis=0, keepdims=True)
        o_t = dot(vh, p_scr[h % 2], TN) * (1.0 / row_sum)
        lse_ref[0, h : h + 1, :] = row_max + jnp.log2(row_sum)
        outs.append(o_t.T[:, :HD].astype(jnp.bfloat16))
    o_ref[...] = jnp.concatenate(outs, axis=1)


def attn_fwd(qkv, mask_pad, wall, scalars, order, scale):
    rows, wide = qkv.shape
    nq = rows // QB
    heads = wall.shape[0]
    width = heads * HD
    return pl.pallas_call(
        functools.partial(attn_fwd_kernel, order, scale),
        grid=(nq,),
        in_specs=[
            pl.BlockSpec(memory_space=pltpu.SMEM),
            pl.BlockSpec((QB, wide), lambda i: (i, 0)),
            pl.BlockSpec((rows, wide), lambda i: (0, 0)),
            pl.BlockSpec((rows, 128 - HD), lambda i: (0, 0)),
            pl.BlockSpec((heads, 32, WALL), lambda i: (0, 0, 0), pipeline_mode=pl.Buffered(1)),
        ],
        out_specs=[pl.BlockSpec((QB, width), lambda i: (i, 0)), pl.BlockSpec((1, heads, QB), lambda i: (i, 0, 0))],
        out_shape=[jax.ShapeDtypeStruct((rows, width), jnp.bfloat16), jax.ShapeDtypeStruct((nq, heads, QB), jnp.float32)],
        scratch_shapes=[pltpu.VMEM((2, rows, QB), jnp.float32), pltpu.VMEM((2, rows, QB), jnp.bfloat16)],
        compiler_params=pltpu.CompilerParams(vmem_limit_bytes=40 << 20),
        cost_estimate=pl.CostEstimate(flops=16 << 30, bytes_accessed=12 << 20, transcendentals=0),
    )(scalars, qkv, qkv, mask_pad, wall)


def attn_bwd_kernel(order, scale, sc_ref, q_ref, kv_ref, do_ref, o_ref, lse_ref, mask_ref, wall_ref,
                    dqkv_ref, acc_ref, p_scr, s_scr, dq_scr, dk_scr, dv_scr):
    step = pl.program_id(0)
    t, small = sc_ref[0], sc_ref[1]
    qq = jnp.bitwise_xor(t, sc_ref[2 + step])
    heads = wall_ref.shape[0]
    width = heads * HD
    rows = kv_ref.shape[0]

    @pl.when(step == 0)
    def _():
        acc_ref[...] = jnp.zeros_like(acc_ref)
        dk_scr[...] = jnp.zeros_like(dk_scr)
        dv_scr[...] = jnp.zeros_like(dv_scr)

    k_extra = mask_ref[...]
    lane = lax.broadcasted_iota(jnp.int32, (QB, 128 - HD), 1)
    q_extra = jnp.where(lane == 0, 1.0, 0.0).astype(jnp.bfloat16)
    dqs = []
    for h in range(heads):
        kh = head_lanes(kv_ref, width + HD * h, k_extra)
        qh = head_lanes(q_ref, HD * h, q_extra)
        vh = head_lanes(kv_ref, 2 * width + HD * h)
        doh = head_lanes(do_ref, HD * h)
        oh = head_lanes(o_ref, HD * h)
        inner = jnp.sum((doh.astype(jnp.float32) * oh.astype(jnp.float32)).T, axis=0, keepdims=True)
        lse = lse_ref[0, h : h + 1, :]
        for kb in range(rows // 256):
            s_t = dot(kh[256 * kb : 256 * kb + 256], qh, NT)
            dp_t = dot(vh[256 * kb : 256 * kb + 256], doh, NT)
            for js in range(8):
                st = 8 * kb + js
                start = strip_start(t, small, qq, js, order[kb])
                s = s_t[32 * js : 32 * js + 32] * (scale * LOG2E) + wall_ref[h, :, pl.ds(start, QB)]
                p = jnp.exp2(s - lse)
                ds = p * (dp_t[32 * js : 32 * js + 32] - inner)
                p_scr[h % 2, 32 * st : 32 * st + 32] = p.astype(jnp.bfloat16)
                s_scr[h % 2, 32 * st : 32 * st + 32] = ds.astype(jnp.bfloat16)
                acc_ref[h, :, pl.ds(start, QB)] += ds
        p_b, ds_b = p_scr[h % 2], s_scr[h % 2]
        dv_scr[h] += dot(p_b, doh, NN)
        dk_scr[h] += dot(ds_b, qh, NN)
        dq_t = dot(kh, ds_b, TN) * scale
        dqs.append(dq_t.T[:, :HD].astype(jnp.bfloat16))
    dq_scr[pl.ds(pl.multiple_of(step * QB, QB), QB)] = jnp.concatenate(dqs, axis=1)

    @pl.when(step == pl.num_programs(0) - 1)
    def _():
        parts = [dq_scr[...]]
        parts += [(dk_scr[h, :, :HD] * scale).astype(jnp.bfloat16) for h in range(heads)]
        parts += [dv_scr[h, :, :HD].astype(jnp.bfloat16) for h in range(heads)]
        dqkv_ref[...] = jnp.concatenate(parts, axis=1)


def attn_bwd(qkv, do, o, lse, mask_pad, wall, scalars, order, scale):
    rows, wide = qkv.shape
    nq = rows // QB
    heads = wall.shape[0]
    width = heads * HD
    row_spec = pl.BlockSpec((QB, width), lambda i: (i, 0))
    return pl.pallas_call(
        functools.partial(attn_bwd_kernel, order, scale),
        grid=(nq,),
        in_specs=[
            pl.BlockSpec(memory_space=pltpu.SMEM),
            pl.BlockSpec((QB, wide), lambda i: (i, 0)),
            pl.BlockSpec((rows, wide), lambda i: (0, 0)),
            row_spec,
            row_spec,
            pl.BlockSpec((1, heads, QB), lambda i: (i, 0, 0)),
            pl.BlockSpec((rows, 128 - HD), lambda i: (0, 0)),
            pl.BlockSpec((heads, 32, WALL), lambda i: (0, 0, 0), pipeline_mode=pl.Buffered(1)),
        ],
        out_specs=[pl.BlockSpec((rows, wide), lambda i: (0, 0)), pl.BlockSpec((heads, 32, WALL), lambda i: (0, 0, 0))],
        out_shape=[jax.ShapeDtypeStruct((rows, wide), jnp.bfloat16), jax.ShapeDtypeStruct((heads, 32, WALL), jnp.float32)],
        scratch_shapes=[
            pltpu.VMEM((2, rows, QB), jnp.bfloat16),
            pltpu.VMEM((2, rows, QB), jnp.bfloat16),
            pltpu.VMEM((rows, width), jnp.bfloat16),
            pltpu.VMEM((heads, rows, 128), jnp.float32),
            pltpu.VMEM((heads, rows, 128), jnp.float32),
        ],
        compiler_params=pltpu.CompilerParams(vmem_limit_bytes=48 << 20),
        cost_estimate=pl.CostEstimate(flops=24 << 30, bytes_accessed=20 << 20, transcendentals=0),
    )(scalars, qkv, qkv, do, o, lse, mask_pad, wall)


EPSILON = 1e-05
AXES = ("dp", "section", "tensor")
ORDER = (0, 2, 1, 3)


def normed(x):
    center = x - jnp.mean(x, axis=-1, keepdims=True)
    spread = jnp.mean(center * center, axis=-1, keepdims=True)
    r = lax.rsqrt(spread + EPSILON)
    return center * r, r


def norm_back(x, dy, gain):
    xhat, r = normed(x)
    dxhat = dy * gain
    dx = r * (
        dxhat
        - jnp.mean(dxhat, axis=-1, keepdims=True)
        - xhat * jnp.mean(dxhat * xhat, axis=-1, keepdims=True)
    )
    return dx, jnp.sum(dy * xhat, axis=0), jnp.sum(dy, axis=0)


def gelu_tanh(values):
    return jax.nn.gelu(values, approximate=True)


def local(
    inputs,
    time_emb,
    lengths,
    key_mask,
    rel_index,
    w_qkv,
    w_time,
    w_proj,
    w_fc1,
    w_fc2,
    rel_table,
    norm_gains,
    norm_biases,
    cotangent,
):
    bf16, f32 = jnp.bfloat16, jnp.float32
    _, rows, width = inputs.shape
    seq_len = key_mask.shape[1]
    heads, buckets = rel_table.shape[1:]
    local_width = w_proj.shape[2]
    scale = 1.0 / math.sqrt(HD)
    ndp = lax.axis_size("dp")
    d = lax.axis_index("dp")
    c = lax.axis_index("section")
    z = lax.axis_index("tensor")
    pair = z // 2
    home = c == pair
    first = c == 0
    t = z % 2 + 2 * c

    def move(x, to):
        pairs = []
        for dd in range(ndp):
            for cc in range(2):
                for zz in range(4):
                    dst = to(dd, cc, zz)
                    if dst is not None:
                        pairs.append(((dd * 2 + cc) * 4 + zz, (dst[0] * 2 + dst[1]) * 4 + dst[2]))
        return lax.ppermute(x, AXES, pairs)

    def partner(x):
        return move(x, lambda dd, cc, zz: (dd, cc, zz ^ 1))

    def sibling(x):
        return move(x, lambda dd, cc, zz: (dd, 1 - cc, zz))

    def across(x):
        return move(x, lambda dd, cc, zz: (dd, cc, zz ^ 2))

    def fetch(x):
        rem = across(x)
        keep = jnp.where(home, x, rem)
        recv = sibling(jnp.where(home, rem, x))
        return jnp.where(first, keep, recv), jnp.where(first, recv, keep)

    def fetch_weight(w):
        part = w.shape[0] // ndp
        rem = lax.all_gather(across(lax.dynamic_slice_in_dim(w, d * part, part, 0)), "dp", axis=0, tiled=True)
        keep = jnp.where(home, w, rem)
        recv = sibling(jnp.where(home, rem, w))
        return jnp.where(first, keep, recv), jnp.where(first, recv, keep)

    time_all = jnp.einsum("id,dcn->icn", time_emb, w_time[0], preferred_element_type=f32)
    table = jnp.pad(rel_table[0], ((0, 0), (0, 4096 - buckets)))
    small_pack = jnp.concatenate(
        [
            table.reshape(-1, 128),
            time_all.reshape(-1, 128),
            norm_gains[0].reshape(-1, 128),
            norm_biases[0].reshape(-1, 128),
        ],
        axis=0,
    )
    cuts = []
    at = 0
    for n in (heads * 32, time_all.size // 128, 2 * width // 128, 2 * width // 128):
        cuts.append((at, at + n))
        at += n
    weights_qkv = fetch_weight(w_qkv[0].reshape(width, 3 * local_width))
    packs = fetch(small_pack)
    weights_proj = fetch_weight(w_proj[0])
    weights_fc1 = fetch_weight(w_fc1[0])
    weights_fc2 = fetch_weight(w_fc2[0])

    def home_rows(x):
        other = lax.dynamic_index_in_dim(x, 1 - pair, 0, keepdims=False)
        got = move(other, lambda dd, cc, zz: (dd, cc, zz ^ 2) if cc == zz // 2 else None)
        return jnp.where(home, lax.dynamic_index_in_dim(x, pair, 0, keepdims=False), got)

    label_lanes = label_row(rel_index)
    out_label = rel_index[1, seq_len - 1, seq_len - 1].reshape(1)
    walls, time_terms, gains, shifts = [], [], [], []
    for pack in packs:
        pieces = [pack[a:b] for a, b in cuts]
        walls.append(bias_tables(out_label, label_lanes, pieces[0].reshape(heads, 64, 64)))
        both = pieces[1].reshape(2, 2, local_width)
        mine = lax.dynamic_index_in_dim(both, pair, 0, keepdims=False)
        time_terms.append(jnp.concatenate([mine[0], jnp.zeros((local_width,), f32), mine[1]]))
        gains.append(pieces[2].reshape(2, width))
        shifts.append(pieces[3].reshape(2, width))

    length = lax.dynamic_index_in_dim(lengths, pair, 0, keepdims=False)
    small = (length < seq_len).astype(jnp.int32)
    scalars = jnp.stack([t, small] + [jnp.int32(j) for j in ORDER])
    mask = lax.dynamic_index_in_dim(key_mask, pair, 0, keepdims=False).reshape(4, rows)
    mask = jnp.concatenate([lax.dynamic_index_in_dim(mask, t ^ j, 0, keepdims=False) for j in ORDER])
    lane = jnp.arange(128 - HD)[None, :]
    mask_pad = jnp.where((lane == 0) & (mask[:, None] == 0), -1e30, 0.0).astype(bf16)

    def gather_rows(x):
        far = partner(x)
        near = sibling(x)
        return jnp.concatenate([x, near, far, sibling(far)], axis=0)

    def scatter_rows(far, near):
        a = sibling(far[rows:].astype(bf16))
        rz = partner((far[:rows] + a.astype(f32)).astype(bf16))
        rs = sibling(near[rows:].astype(bf16))
        return near[:rows] + rs.astype(f32) + rz.astype(f32)

    def times_t(x, w):
        return lax.dot_general(x, w, (((1,), (1,)), ((), ())), preferred_element_type=f32)

    def grad_of(x, y):
        return lax.dot_general(x, y, (((0,), (0,)), ((), ())), preferred_element_type=f32).astype(bf16)

    half = 2 * rows

    def forward(layer, x):
        xhat, _ = normed(x)
        n1 = gather_rows((xhat * gains[layer][0] + shifts[layer][0]).astype(bf16))
        qkv = (jnp.dot(n1, weights_qkv[layer], preferred_element_type=f32) + time_terms[layer]).astype(bf16)
        o, lse = attn_fwd(qkv, mask_pad, walls[layer], scalars, ORDER, scale)
        hidden = x + scatter_rows(
            times_t(o[half:], weights_proj[layer]), times_t(o[:half], weights_proj[layer])
        )
        hhat, _ = normed(hidden)
        n2 = gather_rows((hhat * gains[layer][1] + shifts[layer][1]).astype(bf16))
        u = jnp.dot(n2, weights_fc1[layer], preferred_element_type=f32)
        g = gelu_tanh(u).astype(bf16)
        y = hidden + scatter_rows(
            times_t(g[half:], weights_fc2[layer]), times_t(g[:half], weights_fc2[layer])
        )
        return y, (x, n1, qkv, o, lse, hidden, n2, u, g)

    def backward(layer, dy, kept):
        x, n1, qkv, o, lse, hidden, n2, u, g = kept
        dm = gather_rows(dy.astype(bf16))
        grad_fc2 = grad_of(dm, g)
        dg = jnp.dot(dm, weights_fc2[layer], preferred_element_type=f32)
        du = jax.vjp(gelu_tanh, u)[1](dg)[0].astype(bf16)
        dn2 = scatter_rows(times_t(du[half:], weights_fc1[layer]), times_t(du[:half], weights_fc1[layer]))
        grad_fc1 = grad_of(n2, du)
        dx2, dgain2, dshift2 = norm_back(hidden, dn2, gains[layer][1])
        dh = dy + dx2
        da = gather_rows(dh.astype(bf16))
        do = jnp.dot(da, weights_proj[layer], preferred_element_type=f32).astype(bf16)
        grad_proj = grad_of(da, o)
        dqkv, dwall = attn_bwd(qkv, do, o, lse, mask_pad, walls[layer], scalars, ORDER, scale)
        dn1 = scatter_rows(times_t(dqkv[half:], weights_qkv[layer]), times_t(dqkv[:half], weights_qkv[layer]))
        grad_qkv = grad_of(n1, dqkv)
        sums = jnp.sum(dqkv.astype(f32), axis=0)
        sums = jnp.concatenate([sums[:local_width], sums[2 * local_width :]])
        dx1, dgain1, dshift1 = norm_back(x, dn1, gains[layer][0])
        rel = bias_grads(out_label, label_lanes, dwall)
        norms = jnp.stack([dgain1, dgain2, dshift1, dshift2])
        parts = [lax.psum_scatter(w, "dp", scatter_dimension=0, tiled=True) for w in (grad_fc2, grad_fc1, grad_proj, grad_qkv)]
        return dh + dx1, parts, rel, norms, sums

    def by_core(pairs):
        return jnp.where(first, pairs[0], pairs[1])

    def to_home_core(both):
        return move(
            jnp.where(first, both[1], both[0]),
            lambda dd, cc, zz: (dd, 1 - cc, zz) if cc == zz // 2 else None,
        )

    def deliver(both):
        same = jnp.where(home, by_core(both), to_home_core(both))
        got = [
            move(both[layer], lambda dd, cc, zz, to=layer: (dd, to, zz ^ 2) if cc != zz // 2 else None)
            for layer in range(2)
        ]
        return same, by_core(got)

    x0 = home_rows(inputs).astype(f32)
    y0, kept0 = forward(0, x0)
    act0 = y0.astype(bf16)
    y1, kept1 = forward(1, act0.astype(f32))
    act1 = y1.astype(bf16)
    live = (t * rows + jnp.arange(rows)) < length
    dy1 = home_rows(cotangent).astype(f32) * live.astype(f32)[:, None]
    gin1, parts1, rel1, norms1, sums1 = backward(1, dy1, kept1)
    gin0, parts0, rel0, norms0, sums0 = backward(0, gin1.astype(bf16).astype(f32), kept0)

    def by_image(same, other):
        return jnp.stack([jnp.where(pair == 0, same, other), jnp.where(pair == 0, other, same)])[None]

    acts = by_image(*deliver((act0, act1)))
    same, other = deliver((gin0.astype(bf16), gin1.astype(bf16)))
    same = jnp.where(home, by_core((gin0, gin1)), same.astype(f32))
    input_grads = by_image(same, other.astype(f32))
    grads = []
    for a, b in zip(parts0, parts1):
        same, other = deliver((a, b))
        grads.append(same.astype(f32) + other.astype(f32))

    here = (jnp.arange(2 * ndp) == 2 * d + pair).astype(f32)[:, None]
    pack = jnp.concatenate(
        [
            rel0.reshape(-1, 128),
            rel1.reshape(-1, 128),
            (here * jnp.concatenate([sums0, sums1])[None]).reshape(-1, 128),
            jnp.stack([norms0, norms1]).reshape(-1, 128),
        ],
        axis=0,
    )
    bit = 1
    while bit < ndp:
        pack = pack + move(pack, lambda dd, cc, zz, b=bit: (dd ^ b, cc, zz))
        bit *= 2
    pack = pack + across(pack)
    n_rel = heads * 32
    n_sum = 2 * ndp * 4 * local_width // 128
    rel_both = (pack[:n_rel], pack[n_rel : 2 * n_rel])
    sums_all = pack[2 * n_rel : 2 * n_rel + n_sum].reshape(2 * ndp, 2, 2 * local_width)
    norms_all = pack[2 * n_rel + n_sum :]
    norms_all = norms_all + partner(norms_all)
    norms_all = norms_all + sibling(norms_all)
    norms_all = norms_all.reshape(2, 4, width)
    norms_mine = jnp.where(first, norms_all[0], norms_all[1])
    cols = width // (4 * ndp)
    norms_mine = lax.dynamic_slice_in_dim(norms_mine, (d * 4 + z) * cols, cols, 1)
    rel_mine = jnp.where(home, by_core(rel_both), to_home_core(rel_both))
    rel_grad = rel_mine.reshape(heads, 4096)[:, :buckets]
    sums_both = (sums_all[:, 0], sums_all[:, 1])
    sums_mine = jnp.where(home, by_core(sums_both), to_home_core(sums_both))
    emb_all = lax.all_gather(time_emb, "dp", axis=0, tiled=True)
    emb_mine = lax.dynamic_slice_in_dim(emb_all, d * (width // ndp), width // ndp, 1).astype(f32)
    grad_time = lax.dot_general(
        emb_mine, sums_mine, (((0,), (0,)), ((), ())), precision=lax.Precision.HIGHEST, preferred_element_type=f32
    ).reshape(width // ndp, 2, local_width)
    return (
        acts,
        input_grads,
        grads[3].reshape(width // ndp, 3, local_width)[None],
        grad_time[None],
        grads[2][None],
        grads[1][None],
        grads[0][None],
        rel_grad[None],
        norms_mine[:2][None],
        norms_mine[2:][None],
    )


def solution(mesh):
    return jax.shard_map(
        local,
        mesh=mesh,
        in_specs=(
            P("dp", "tensor", None),
            P("dp", None),
            P("dp"),
            P("dp", None),
            P(),
            P("section", None, None, "tensor"),
            P("section", None, None, "tensor"),
            P("section", None, "tensor"),
            P("section", None, "tensor"),
            P("section", None, "tensor"),
            P("section", "tensor", None),
            P("section", None, None),
            P("section", None, None),
            P("dp", "tensor", None),
        ),
        out_specs=(
            P("section", "dp", "tensor", None),
            P("section", "dp", "tensor", None),
            P("section", "dp", None, "tensor"),
            P("section", "dp", None, "tensor"),
            P("section", "dp", "tensor"),
            P("section", "dp", "tensor"),
            P("section", "dp", "tensor"),
            P("section", "tensor", None),
            P("section", None, ("dp", "tensor")),
            P("section", None, ("dp", "tensor")),
        ),
        check_vma=False,
    )
```

time: 3350 us -> 904 us (0.27)
  waiting for transfers between devices: 1610 us -> 313 us
  local copies, waits for them, and re-layouts: 640 us -> 68.8 us
  matrix products: 603 us -> 118 us
  other arithmetic: 321 us -> 95.8 us
  starting transfers between devices: 21.8 us -> 155 us
  Pallas kernels: 0 us -> 96.5 us
  blocking collectives: 89.6 us -> 24.1 us
    reduce_scatter x32 -> x8, waiting for transfers between devices: 941 us -> 0.03 us  [backward(): lax.psum_scatter(w, 'dp', scatter_dimension=0, tiled=True)]
    all_gather x16 -> x3, waiting for transfers between devices: 590 us -> 0.01 us  [fetch_weight(): lax.all_gather(across(lax.dynamic_slice_in_dim(w, d * part, part, 0)), 'd...]
    dot_general x128 -> x34, matrix products: 603 us -> 118 us  [the longest x8 42.7 us: grad_of(): lax.dot_general(x, y, (((0,), (0,)), ((), ())), preferred_element_type=f32)]
    ppermute x8 -> x85, waiting for transfers between devices: 3.56 us -> 312 us  [move(): return lax.ppermute(x, AXES, pairs)]
    reshape x27 -> x13, local copies, waits for them, and re-layouts: 178 us -> 4.39 us  [the longest x1 1.63 us: local(): rel1.reshape(-1, 128)]
    ppermute x8 -> x85, starting transfers between devices: 16.3 us -> 154 us  [move(): return lax.ppermute(x, AXES, pairs)]
    gather x3 -> x0, local copies, waits for them, and re-layouts: 123 us -> none  [the longest x1 106 us: local(): offset_labels = rel_index[0][query_slot, key_slot]]
    pallas_call x0 -> x8, Pallas kernels: none -> 96.5 us  [the longest x2 39 us: attn_bwd(): pl.pallas_call(functools.partial(attn_bwd_kernel, order, scale), grid=(nq...]
  transfers between devices with their start and end apart: 60 -> 96, of which waited for: 48 -> 32; matrix products, arithmetic and copies ran while one was open for 25% -> 22% of each run, Pallas kernels for 0% -> 7%
where the time goes in v1:
time: 904 us; the launch traced here: 888 us
  waiting for transfers between devices  313 us (35%)
  starting transfers between devices  155 us (17%)
  matrix products  118 us (13%)
  Pallas kernels  96.5 us (11%)
  other arithmetic  95.8 us (11%)
  local copies, waits for them, and re-layouts  68.8 us (8%)
  blocking collectives  24.1 us (3%)
  between operations  17.5 us (2%)
    ppermute x85, waiting for transfers between devices, move(): return lax.ppermute(x, AXES, pairs)  312 us
    ppermute x85, starting transfers between devices, move(): return lax.ppermute(x, AXES, pairs)  154 us
    dot_general x8, matrix products, grad_of(): lax.dot_general(x, y, (((0,), (0,)), ((), ())), preferred_element_type=f32)  42.7 us
    pallas_call x2, Pallas kernels, attn_bwd(): pl.pallas_call(functools.partial(attn_bwd_kernel, order, scale), grid=(nq...  39 us
    dot_general x16, matrix products, times_t(): lax.dot_general(x, w, (((1,), (1,)), ((), ())), preferred_element_type=f32)  30.6 us
    unnamed x346, local copies, waits for them, and re-layouts  26.5 us
    pallas_call x2, Pallas kernels, attn_fwd(): pl.pallas_call(functools.partial(attn_fwd_kernel, order, scale), grid=(nq...  25.3 us
    pallas_call x2, Pallas kernels, bias_grads(): pl.pallas_call(bias_grad_kernel, grid=(heads,), in_specs=[pl.BlockSpec(me...  19.6 us
  transfers between devices with their start and end apart: 96, of which 32 were waited for; matrix products, arithmetic and copies ran while one was open for 22% of the time, Pallas kernels for 7%

profile of v1, /device:TPU:1, one launch (start us, length us, event | category | flops | bytes accessed | tf_op | source)
XLA Modules:
  0.0 888.5 jit_solution(3670915020223720657)
XLA Ops:
  13.0 22.7 %collective-permute-done.6 = bf16[288,864]{1,0:T(8,128)(2,1)S(1)} collective-permute-done((bf16[288,864]{1,0:T(8,128)(2,1)}, bf16[288,864]{1,0:T(8,128)(2,1)S(1)}, u32[]{:S(2)}, u32[]{:S(2)}) %collective-permute-start.6) | collective-permute-done | bytes 497696 | tf_op jit(solution)/shard_map/ppermute | solution.py:386
  55.6 60.4 %collective-permute-done.18 = bf16[288,1152]{1,0:T(8,128)(2,1)S(1)} collective-permute-done((bf16[288,1152]{1,0:T(8,128)(2,1)S(1)}, bf16[288,1152]{1,0:T(8,128)(2,1)S(1)}, u32[]{:S(2)}, u32[]{:S(2)}) %collective-permute-start.18) | collective-permute-done | bytes 663584 | tf_op jit(solution)/shard_map/ppermute | solution.py:386
  118.6 16.7 %all_gather.16 = bf16[1152,288]{1,0:T(8,128)(2,1)S(1)} all-gather(bf16[288,288]{1,0:T(8,128)(2,1)} %collective-permute-done.8), channel_id=1, replica_groups=mesh['dp'=4,'section'=2,'tensor'=4] {'dp'}, dimensions={0}, use_global_device_ids=true | all-gather | bytes 829440 | tf_op jit(solution)/shard_map/all_gather | solution.py:405
  165.8 9.8 %collective-permute-done.4 = bf16[256,1152]{1,0:T(8,128)(2,1)} collective-permute-done((bf16[256,1152]{1,0:T(8,128)(2,1)S(1)}, bf16[256,1152]{1,0:T(8,128)(2,1)}, u32[]{:S(2)}, u32[]{:S(2)}) %collective-permute-start.4) | collective-permute-done | bytes 589856 | tf_op jit(solution)/shard_map/ppermute | solution.py:386
  185.1 12.6 %shard_map.214 = (bf16[1024,288]{1,0:T(8,128)(2,1)S(1)}, f32[4,4,256]{2,1,0:T(4,128)S(1)}) custom-call(s32[6]{0:T(128)S(1)} %stack.72.sc_ref, bf16[1024,864]{1,0:T(8,128)(2,1)S(1)} %add_convert_fusion.1.q_ref.kv_ref, bf16[1024,864]{1,0:T(8,128)(2,1)S(1)} %add_convert_fusion.1.q_ref.kv_ref, bf16[1024,56]{1,0:T(8,128)(2,1)S(1)} %select_convert_fusion.mask_ref, ...), custom_call_target="tpu_custom_call" | custom-call | flops 17179869184 | bytes 12582912 | tf_op jit(solution)/shard_map/pallas_call | solution.py:215
  213.7 10.1 %collective-permute-done.12 = bf16[256,1152]{1,0:T(8,128)(2,1)S(1)} collective-permute-done((bf16[256,1152]{1,0:T(8,128)(2,1)S(1)}, bf16[256,1152]{1,0:T(8,128)(2,1)S(1)}, u32[]{:S(2)}, u32[]{:S(2)}) %collective-permute-start.12) | collective-permute-done | bytes 589856 | tf_op jit(solution)/shard_map/ppermute | solution.py:386
  228.5 11.2 %collective-permute-done.14 = bf16[256,1152]{1,0:T(8,128)(2,1)S(1)} collective-permute-done((bf16[256,1152]{1,0:T(8,128)(2,1)S(1)}, bf16[256,1152]{1,0:T(8,128)(2,1)S(1)}, u32[]{:S(2)}, u32[]{:S(2)}) %collective-permute-start.14) | collective-permute-done | bytes 589856 | tf_op jit(solution)/shard_map/ppermute | solution.py:386
  262.1 13.2 %collective-permute-done.22 = bf16[256,1152]{1,0:T(8,128)(2,1)S(1)} collective-permute-done((bf16[256,1152]{1,0:T(8,128)(2,1)S(1)}, bf16[256,1152]{1,0:T(8,128)(2,1)S(1)}, u32[]{:S(2)}, u32[]{:S(2)}) %collective-permute-start.22) | collective-permute-done | bytes 589856 | tf_op jit(solution)/shard_map/ppermute | solution.py:386
  281.2 11.8 %collective-permute-done.24 = bf16[256,1152]{1,0:T(8,128)(2,1)S(1)} collective-permute-done((bf16[256,1152]{1,0:T(8,128)(2,1)S(1)}, bf16[256,1152]{1,0:T(8,128)(2,1)S(1)}, u32[]{:S(2)}, u32[]{:S(2)}) %collective-permute-start.24) | collective-permute-done | bytes 589856 | tf_op jit(solution)/shard_map/ppermute | solution.py:386
  307.6 12.7 %shard_map.216 = (bf16[1024,288]{1,0:T(8,128)(2,1)S(1)}, f32[4,4,256]{2,1,0:T(4,128)S(1)}) custom-call(s32[6]{0:T(128)S(1)} %stack.72.sc_ref, bf16[1024,864]{1,0:T(8,128)(2,1)S(1)} %add_convert_fusion.q_ref.kv_ref, bf16[1024,864]{1,0:T(8,128)(2,1)S(1)} %add_convert_fusion.q_ref.kv_ref, bf16[1024,56]{1,0:T(8,128)(2,1)S(1)} %select_convert_fusion.mask_ref, ...), custom_call_target="tpu_custom_call" | custom-call | flops 17179869184 | bytes 12582912 | tf_op jit(solution)/shard_map/pallas_call | solution.py:215
  327.2 18.7 %collective-permute-done.28 = bf16[256,1152]{1,0:T(8,128)(2,1)} collective-permute-done((bf16[256,1152]{1,0:T(8,128)(2,1)}, bf16[256,1152]{1,0:T(8,128)(2,1)}, u32[]{:S(2)}, u32[]{:S(2)}) %collective-permute-start.28) | collective-permute-done | bytes 589856 | tf_op jit(solution)/shard_map/ppermute | solution.py:386
  352.5 10.3 %collective-permute-done.30 = bf16[256,1152]{1,0:T(8,128)(2,1)S(1)} collective-permute-done((bf16[256,1152]{1,0:T(8,128)(2,1)S(1)}, bf16[256,1152]{1,0:T(8,128)(2,1)S(1)}, u32[]{:S(2)}, u32[]{:S(2)}) %collective-permute-start.30) | collective-permute-done | bytes 589856 | tf_op jit(solution)/shard_map/ppermute | solution.py:386
  398.7 13.5 %collective-permute-done.44 = bf16[256,1152]{1,0:T(8,128)(2,1)S(1)} collective-permute-done((bf16[256,1152]{1,0:T(8,128)(2,1)S(1)}, bf16[256,1152]{1,0:T(8,128)(2,1)S(1)}, u32[]{:S(2)}, u32[]{:S(2)}) %collective-permute-start.44) | collective-permute-done | bytes 589856 | tf_op jit(solution)/shard_map/ppermute | solution.py:386
  416.2 15.2 %collective-permute-done.46 = bf16[256,1152]{1,0:T(8,128)(2,1)S(1)} collective-permute-done((bf16[256,1152]{1,0:T(8,128)(2,1)S(1)}, bf16[256,1152]{1,0:T(8,128)(2,1)S(1)}, u32[]{:S(2)}, u32[]{:S(2)}) %collective-permute-start.46) | collective-permute-done | bytes 589856 | tf_op jit(solution)/shard_map/ppermute | solution.py:386
  438.3 19.8 %shard_map.217 = (bf16[1024,864]{1,0:T(8,128)(2,1)S(1)}, f32[4,32,9984]{2,1,0:T(8,128)}) custom-call(s32[6]{0:T(128)S(1)} %stack.72.sc_ref, bf16[1024,864]{1,0:T(8,128)(2,1)S(1)} %copy-done.17, bf16[1024,864]{1,0:T(8,128)(2,1)S(1)} %copy-done.17, bf16[1024,288]{1,0:T(8,128)(2,1)S(1)} %copy.104.do_ref, bf16[1024,288]{1,0:T(8,128)(2,1)S(1)} %get-tuple-element.19.o_ref, ...), custom_call_target="tpu_custom_call" | custom-call | flops 25769803776 | bytes 20971520 | tf_op jit(solution)/shard_map/pallas_call | solution.py:293
  463.8 12.9 %collective-permute-done.50 = bf16[256,1152]{1,0:T(8,128)(2,1)S(1)} collective-permute-done((bf16[256,1152]{1,0:T(8,128)(2,1)S(1)}, bf16[256,1152]{1,0:T(8,128)(2,1)S(1)}, u32[]{:S(2)}, u32[]{:S(2)}) %collective-permute-start.50) | collective-permute-done | bytes 589856 | tf_op jit(solution)/shard_map/ppermute | solution.py:386
  483.3 12.1 %collective-permute-done.52 = bf16[256,1152]{1,0:T(8,128)(2,1)S(1)} collective-permute-done((bf16[256,1152]{1,0:T(8,128)(2,1)S(1)}, bf16[256,1152]{1,0:T(8,128)(2,1)S(1)}, u32[]{:S(2)}, u32[]{:S(2)}) %collective-permute-start.52) | collective-permute-done | bytes 589856 | tf_op jit(solution)/shard_map/ppermute | solution.py:386
  514.1 12.9 %collective-permute-done.56 = bf16[256,1152]{1,0:T(8,128)(2,1)S(1)} collective-permute-done((bf16[256,1152]{1,0:T(8,128)(2,1)S(1)}, bf16[256,1152]{1,0:T(8,128)(2,1)S(1)}, u32[]{:S(2)}, u32[]{:S(2)}) %collective-permute-start.56) | collective-permute-done | bytes 589856 | tf_op jit(solution)/shard_map/ppermute | solution.py:386
  534.1 9.9 %collective-permute-done.58 = bf16[256,1152]{1,0:T(8,128)(2,1)} collective-permute-done((bf16[256,1152]{1,0:T(8,128)(2,1)}, bf16[256,1152]{1,0:T(8,128)(2,1)}, u32[]{:S(2)}, u32[]{:S(2)}) %collective-permute-start.58) | collective-permute-done | bytes 589856 | tf_op jit(solution)/shard_map/ppermute | solution.py:386
  597.9 14.1 %collective-permute-done.34 = bf16[256,1152]{1,0:T(8,128)(2,1)S(1)} collective-permute-done((bf16[256,1152]{1,0:T(8,128)(2,1)S(1)}, bf16[256,1152]{1,0:T(8,128)(2,1)S(1)}, u32[]{:S(2)}, u32[]{:S(2)}) %collective-permute-start.34) | collective-permute-done | bytes 589856 | tf_op jit(solution)/shard_map/ppermute | solution.py:386
  671.7 19.3 %shard_map.218 = (bf16[1024,864]{1,0:T(8,128)(2,1)S(1)}, f32[4,32,9984]{2,1,0:T(8,128)}) custom-call(s32[6]{0:T(128)S(1)} %copy-done.13, bf16[1024,864]{1,0:T(8,128)(2,1)S(1)} %copy-done.15, bf16[1024,864]{1,0:T(8,128)(2,1)S(1)} %copy-done.15, bf16[1024,288]{1,0:T(8,128)(2,1)S(1)} %copy.105.do_ref, bf16[1024,288]{1,0:T(8,128)(2,1)S(1)} %copy-done.5, ...), custom_call_target="tpu_custom_call" | custom-call | flops 25769803776 | bytes 20971520 | tf_op jit(solution)/shard_map/pallas_call | solution.py:293
  694.0 10.0 %shard_map.219 = f32[4,64,64]{2,1,0:T(8,128)S(1)} custom-call(s32[1]{0:T(128)} %bitcast.15.out_lab_ref, s32[1,4096]{1,0:T(1,128)S(1)} %copy-done.8, f32[4,32,9984]{2,1,0:T(8,128)S(1)} %bitcast.151), custom_call_target="tpu_custom_call" | custom-call | tf_op jit(solution)/shard_map/pallas_call | solution.py:120
  779.6 35.5 %collective-permute-start.83 = (f32[72,128]{1,0:T(8,128)S(1)}, f32[72,128]{1,0:T(8,128)S(1)}, u32[]{:S(2)}, u32[]{:S(2)}) collective-permute-start(f32[72,128]{1,0:T(8,128)S(1)} %slice.456), channel_id=1, source_target_pairs={{0,1},{1,0},{2,3},{3,2},{4,5},{5,4},{6,7},{7,6},{8,9},{9,8},{10,11... | collective-permute-start | bytes 110600 | tf_op jit(solution)/shard_map/ppermute | solution.py:386
  852.4 17.2 %collective-permute-start.67 = (bf16[288,864]{1,0:T(8,128)(2,1)}, bf16[288,864]{1,0:T(8,128)(2,1)S(1)}, u32[]{:S(2)}, u32[]{:S(2)}) collective-permute-start(bf16[288,864]{1,0:T(8,128)(2,1)} %reduce-scatter.9.cloned.1.call-done), channel_id=1, source_target_pairs={{2,0},{3,1},{4,2},{5,3},{10,8},{11,9},{12,10},{13,11},{18,16},{19,... | collective-permute-start | bytes 1493000 | tf_op jit(solution)/shard_map/ppermute | solution.py:386
  (756 shorter events, 468.4 us)
Async XLA Ops:
  7.2 144.2 %all-gather.5.cloned.1.call-start = ((), (), s32[]{:S(2)}) async-start(), calls=%async_computation.8 | async-start | bytes 2580480 | tf_op jit(solution)/shard_map/all_gather | solution.py:405
  36.6 164.5 %all-gather.9.cloned.1.call-start = ((), (), s32[]{:S(2)}) async-start(), calls=%async_computation.10 | async-start | bytes 3317760 | tf_op jit(solution)/shard_map/all_gather | solution.py:405
  37.5 81.0 %collective-permute-start.1 = (f32[173,128]{1,0:T(8,128)S(1)}, f32[173,128]{1,0:T(8,128)S(1)}, u32[]{:S(2)}, u32[]{:S(2)}) collective-permute-start(f32[173,128]{1,0:T(8,128)S(1)} %pad_maximum_fusion.29), channel_id=1, source_target_pairs={{0,2},{1,3},{2,0},{3,1},{4,6},{5,7},{6,4},{7,5},{8,10},{9,11},{10,... | collective-permute-start | bytes 265736 | tf_op jit(solution)/shard_map/ppermute | solution.py:386
  39.5 79.0 %collective-permute-start.8 = (bf16[288,288]{1,0:T(8,128)(2,1)}, bf16[288,288]{1,0:T(8,128)(2,1)}, u32[]{:S(2)}, u32[]{:S(2)}) collective-permute-start(bf16[288,288]{1,0:T(8,128)(2,1)} %bitcast.17), channel_id=1, source_target_pairs={{0,2},{1,3},{2,0},{3,1},{4,6},{5,7},{6,4},{7,5},{8,10},{9,11},{10,... | collective-permute-start | bytes 497672 | tf_op jit(solution)/shard_map/ppermute | solution.py:386
  42.7 115.5 %collective-permute-start = (bf16[256,1152]{1,0:T(8,128)(2,1)}, bf16[256,1152]{1,0:T(8,128)(2,1)}, u32[]{:S(2)}, u32[]{:S(2)}) collective-permute-start(bf16[256,1152]{1,0:T(8,128)(2,1)} %dynamic-slice_bitcast_fusion.3), channel_id=1, source_target_pairs={{0,2},{1,3},{6,4},{7,5},{8,10},{9,11},{14,12},{15,13},{16,18},{17,... | collective-permute-start | bytes 1769480 | tf_op jit(solution)/shard_map/ppermute | solution.py:386
  45.3 70.6 %collective-permute-start.18 = (bf16[288,1152]{1,0:T(8,128)(2,1)S(1)}, bf16[288,1152]{1,0:T(8,128)(2,1)S(1)}, u32[]{:S(2)}, u32[]{:S(2)}) collective-permute-start(bf16[288,1152]{1,0:T(8,128)(2,1)S(1)} %dynamic-slice_bitcast_fusion), channel_id=1, source_target_pairs={{0,2},{1,3},{2,0},{3,1},{4,6},{5,7},{6,4},{7,5},{8,10},{9,11},{10,... | collective-permute-start | bytes 1990664 | tf_op jit(solution)/shard_map/ppermute | solution.py:386
  51.2 109.8 %collective-permute-start.16 = (bf16[288,1152]{1,0:T(8,128)(2,1)}, bf16[288,1152]{1,0:T(8,128)(2,1)}, u32[]{:S(2)}, u32[]{:S(2)}) collective-permute-start(bf16[288,1152]{1,0:T(8,128)(2,1)} %dynamic-slice_bitcast_fusion.1), channel_id=1, source_target_pairs={{0,2},{1,3},{2,0},{3,1},{4,6},{5,7},{6,4},{7,5},{8,10},{9,11},{10,... | collective-permute-start | bytes 1990664 | tf_op jit(solution)/shard_map/ppermute | solution.py:386
  116.8 93.2 %all-gather.7.cloned.1.call-start = ((), (), s32[]{:S(2)}) async-start(), calls=%async_computation.9 | async-start | bytes 3317760 | tf_op jit(solution)/shard_map/all_gather | solution.py:405
  161.0 502.2 %reduce-scatter.15.cloned.1.call-start = ((), (), s32[]{:S(2)}) async-start(), calls=%async_computation.14 | async-start | bytes 1105920 | tf_op jit(solution)/shard_map/reduce_scatter | solution.py:514
  204.7 37.3 %collective-permute-start.19 = (bf16[1152,1152]{1,0:T(8,128)(2,1)}, bf16[1152,1152]{1,0:T(8,128)(2,1)}, u32[]{:S(2)}, u32[]{:S(2)}) collective-permute-start(bf16[1152,1152]{1,0:T(8,128)(2,1)} %bitcast_select_fusion), channel_id=1, source_target_pairs={{0,4},{1,5},{2,6},{3,7},{4,0},{5,1},{6,2},{7,3},{8,12},{9,13},{10,... | collective-permute-start | bytes 7962632 | tf_op jit(solution)/shard_map/ppermute | solution.py:386
  532.6 214.8 %reduce-scatter.13.cloned.1.call-start = ((), (), s32[]{:S(2)}) async-start(), calls=%async_computation.13 | async-start | bytes 1105920 | tf_op jit(solution)/shard_map/reduce_scatter | solution.py:514
  552.4 202.3 %reduce-scatter.19.cloned.1.call-start = ((), (), s32[]{:S(2)}) async-start(), calls=%async_computation.16 | async-start | bytes 3317760 | tf_op jit(solution)/shard_map/reduce_scatter | solution.py:514
  559.5 199.5 %reduce-scatter.23.cloned.1.call-start = ((), (), s32[]{:S(2)}) async-start(), calls=%async_computation.18 | async-start | bytes 3317760 | tf_op jit(solution)/shard_map/reduce_scatter | solution.py:514
  567.5 198.1 %reduce-scatter.11.cloned.1.call-start = ((), (), s32[]{:S(2)}) async-start(), calls=%async_computation.12 | async-start | bytes 2580480 | tf_op jit(solution)/shard_map/reduce_scatter | solution.py:514
  574.0 257.5 %reduce-scatter.17.cloned.1.call-start = ((), (), s32[]{:S(2)}) async-start(), calls=%async_computation.15 | async-start | bytes 3317760 | tf_op jit(solution)/shard_map/reduce_scatter | solution.py:514
  585.2 252.5 %reduce-scatter.21.cloned.1.call-start = ((), (), s32[]{:S(2)}) async-start(), calls=%async_computation.17 | async-start | bytes 3317760 | tf_op jit(solution)/shard_map/reduce_scatter | solution.py:514
  591.3 41.1 %collective-permute-start.36 = (bf16[256,1152]{1,0:T(8,128)(2,1)}, bf16[256,1152]{1,0:T(8,128)(2,1)}, u32[]{:S(2)}, u32[]{:S(2)}) collective-permute-start(bf16[256,1152]{1,0:T(8,128)(2,1)} %get-tuple-element.131), channel_id=1, source_target_pairs={{2,0},{3,1},{4,2},{5,3},{10,8},{11,9},{12,10},{13,11},{18,16},{19,... | collective-permute-start | bytes 1769480 | tf_op jit(solution)/shard_map/ppermute | solution.py:386
  651.3 114.4 %collective-permute-start.65 = (bf16[256,1152]{1,0:T(8,128)(2,1)}, bf16[256,1152]{1,0:T(8,128)(2,1)}, u32[]{:S(2)}, u32[]{:S(2)}) collective-permute-start(bf16[256,1152]{1,0:T(8,128)(2,1)} %copy-done.33), channel_id=1, source_target_pairs={{2,4},{3,5},{4,6},{5,7},{10,12},{11,13},{12,14},{13,15},{18,20},{1... | collective-permute-start | bytes 1769480 | tf_op jit(solution)/shard_map/ppermute | solution.py:386
  661.9 187.9 %reduce-scatter.9.cloned.1.call-start = ((), (), s32[]{:S(2)}) async-start(), calls=%async_computation.11 | async-start | bytes 2580480 | tf_op jit(solution)/shard_map/reduce_scatter | solution.py:514
  663.1 86.0 %collective-permute-start.75 = (bf16[288,288]{1,0:T(8,128)(2,1)}, bf16[288,288]{1,0:T(8,128)(2,1)}, u32[]{:S(2)}, u32[]{:S(2)}) collective-permute-start(bf16[288,288]{1,0:T(8,128)(2,1)} %reduce-scatter.15.cloned.1.call-done), channel_id=1, source_target_pairs={{2,4},{3,5},{4,6},{5,7},{10,12},{11,13},{12,14},{13,15},{18,20},{1... | collective-permute-start | bytes 497672 | tf_op jit(solution)/shard_map/ppermute | solution.py:386
  754.7 85.1 %collective-permute-start.78 = (bf16[288,1152]{1,0:T(8,128)(2,1)}, bf16[288,1152]{1,0:T(8,128)(2,1)}, u32[]{:S(2)}, u32[]{:S(2)}) collective-permute-start(bf16[288,1152]{1,0:T(8,128)(2,1)} %reduce-scatter.19.cloned.1.call-done), channel_id=1, source_target_pairs={{2,4},{3,5},{4,6},{5,7},{10,12},{11,13},{12,14},{13,15},{18,20},{1... | collective-permute-start | bytes 1990664 | tf_op jit(solution)/shard_map/ppermute | solution.py:386
  762.0 90.3 %collective-permute-start.81 = (bf16[288,1152]{1,0:T(8,128)(2,1)}, bf16[288,1152]{1,0:T(8,128)(2,1)}, u32[]{:S(2)}, u32[]{:S(2)}) collective-permute-start(bf16[288,1152]{1,0:T(8,128)(2,1)} %reduce-scatter.23.cloned.1.call-done), channel_id=1, source_target_pairs={{2,4},{3,5},{4,6},{5,7},{10,12},{11,13},{12,14},{13,15},{18,20},{1... | collective-permute-start | bytes 1990664 | tf_op jit(solution)/shard_map/ppermute | solution.py:386
  765.7 106.5 %collective-permute-start.68 = (bf16[288,864]{1,0:T(8,128)(2,1)}, bf16[288,864]{1,0:T(8,128)(2,1)}, u32[]{:S(2)}, u32[]{:S(2)}) collective-permute-start(bf16[288,864]{1,0:T(8,128)(2,1)} %reduce-scatter.11.cloned.1.call-done), channel_id=1, source_target_pairs={{2,4},{3,5},{4,6},{5,7},{10,12},{11,13},{12,14},{13,15},{18,20},{1... | collective-permute-start | bytes 1493000 | tf_op jit(solution)/shard_map/ppermute | solution.py:386
  779.6 37.3 %collective-permute-start.83 = (f32[72,128]{1,0:T(8,128)S(1)}, f32[72,128]{1,0:T(8,128)S(1)}, u32[]{:S(2)}, u32[]{:S(2)}) collective-permute-start(f32[72,128]{1,0:T(8,128)S(1)} %slice.456), channel_id=1, source_target_pairs={{0,1},{1,0},{2,3},{3,2},{4,5},{5,4},{6,7},{7,6},{8,9},{9,8},{10,11... | collective-permute-start | bytes 110600 | tf_op jit(solution)/shard_map/ppermute | solution.py:386
  (243 other events, 3986.9 us)
Sparse Core Ops, SparseCore 0:
  36.7 36.6 all-gather.4
  116.9 44.8 all-gather.8
  163.6 39.9 all-gather.6
  532.7 27.0 reduce-scatter.14
  563.2 26.6 reduce-scatter.12
  592.8 39.9 reduce-scatter.18
  635.8 39.8 reduce-scatter.22
  678.6 35.0 reduce-scatter.10
  717.0 40.6 reduce-scatter.16
  760.9 41.0 reduce-scatter.20
  805.2 35.1 reduce-scatter.8

commit v2 on v1

--- a/solution.py
+++ b/solution.py
@@ -318,8 +318,8 @@
 
 
 EPSILON = 1e-05
-AXES = ("dp", "section", "tensor")
-ORDER = (0, 2, 1, 3)
+NCH = 2
+GELU_C = math.sqrt(2.0 / math.pi)
 
 
 def normed(x):
@@ -337,11 +337,485 @@
         - jnp.mean(dxhat, axis=-1, keepdims=True)
         - xhat * jnp.mean(dxhat * xhat, axis=-1, keepdims=True)
     )
-    return dx, jnp.sum(dy * xhat, axis=0), jnp.sum(dy, axis=0)
-
-
-def gelu_tanh(values):
-    return jax.nn.gelu(values, approximate=True)
+    return dx, jnp.sum(dy * xhat, axis=0, keepdims=True), jnp.sum(dy, axis=0, keepdims=True)
+
+
+def gelu_both(u):
+    th = jnp.tanh(GELU_C * (u + 0.044715 * u * u * u))
+    half = 0.5 * (1.0 + th)
+    slope = half + 0.5 * u * (1.0 - th * th) * GELU_C * (1.0 + 3 * 0.044715 * u * u)
+    return u * half, slope
+
+
+class Links:
+    def __init__(self, send_sem, recv_sem):
+        z, c = lax.axis_index("tensor"), lax.axis_index("section")
+        self.ids = ({"tensor": z + 1 - 2 * lax.rem(z, 2)}, {"section": 1 - c})
+        self.send_sem, self.recv_sem = send_sem, recv_sem
+        self.used = 0
+        self.started = []
+
+    def enter(self):
+        barrier = pltpu.get_barrier_semaphore()
+        for where in self.ids:
+            pl.semaphore_signal(barrier, inc=1, device_id=where, device_id_type=pl.DeviceIdType.MESH)
+        pl.semaphore_wait(barrier, 2)
+
+    def send(self, src, dst, to):
+        k = self.used
+        self.used += 1
+        copy = pltpu.make_async_remote_copy(
+            src_ref=src,
+            dst_ref=dst,
+            send_sem=self.send_sem.at[k],
+            recv_sem=self.recv_sem.at[k],
+            device_id=self.ids[to],
+            device_id_type=pl.DeviceIdType.MESH,
+        )
+        copy.start()
+        self.started.append(copy)
+        return copy
+
+    def leave(self):
+        for copy in self.started:
+            copy.wait_send()
+
+
+PARTNER, SIBLING = 0, 1
+
+
+def chunk(i, rows):
+    return pl.ds(i * (rows // NCH), rows // NCH)
+
+
+class Scatter:
+    COPIES = 3 * NCH
+
+    def __init__(self, links, low, wide):
+        self.links, self.low, self.wide = links, low, wide
+        self.rows = low.shape[1]
+        self.copies = {}
+
+    def far(self, i, p2, p3):
+        at = chunk(i, self.rows)
+        self.low[0, at] = p3.astype(jnp.bfloat16)
+        self.copies["a", i] = self.links.send(self.low.at[0, at], self.low.at[3, at], SIBLING)
+        self.wide[0, at] = p2
+
+    def middle(self, i):
+        at = chunk(i, self.rows)
+        self.copies["a", i].wait_recv()
+        self.low[1, at] = (self.wide[0, at] + self.low[3, at].astype(jnp.float32)).astype(jnp.bfloat16)
+        self.copies["z", i] = self.links.send(self.low.at[1, at], self.low.at[4, at], PARTNER)
+
+    def near(self, i, p0, p1):
+        at = chunk(i, self.rows)
+        self.low[2, at] = p1.astype(jnp.bfloat16)
+        self.copies["b", i] = self.links.send(self.low.at[2, at], self.low.at[5, at], SIBLING)
+        self.wide[1, at] = p0
+
+    def done(self, i):
+        at = chunk(i, self.rows)
+        self.copies["b", i].wait_recv()
+        self.copies["z", i].wait_recv()
+        return self.wide[1, at] + self.low[5, at].astype(jnp.float32) + self.low[4, at].astype(jnp.float32)
+
+
+class Gather:
+    COPIES = 3 * NCH
+
+    def __init__(self, links, buf):
+        self.links, self.buf = links, buf
+        self.rows = buf.shape[1]
+        self.copies = {}
+
+    def send(self, i, x):
+        at = chunk(i, self.rows)
+        self.buf[0, at] = x
+        self.copies["z", i] = self.links.send(self.buf.at[0, at], self.buf.at[2, at], PARTNER)
+        self.copies["s", i] = self.links.send(self.buf.at[0, at], self.buf.at[1, at], SIBLING)
+
+    def forward(self, i):
+        at = chunk(i, self.rows)
+        self.copies["z", i].wait_recv()
+        self.copies["f", i] = self.links.send(self.buf.at[2, at], self.buf.at[3, at], SIBLING)
+
+    def done(self, i):
+        self.copies["s", i].wait_recv()
+        self.copies["f", i].wait_recv()
+        at = chunk(i, self.rows)
+        n = self.rows // NCH
+        return jnp.concatenate([self.buf[b, at] for b in range(4)], axis=0)
+
+
+def start_load(src, dst, sem):
+    copy = pltpu.make_async_copy(src, dst, sem)
+    copy.start()
+    return copy
+
+
+def block_rows(ref, b, i, rows):
+    n = rows // NCH
+    return ref[pl.ds(b * rows + i * n, n)]
+
+
+def put_rows(ref, value, i, rows):
+    n = rows // NCH
+    for b in range(4):
+        ref[pl.ds(b * rows + i * n, n)] = value[b * n : (b + 1) * n]
+
+
+def weight_grad(out, col, x, y):
+    width = x.shape[1]
+    step = 384
+    for k in range(0, width, step):
+        out[k : k + step, col : col + y.shape[1]] = dot(x[:, k : k + step], y, TN).astype(out.dtype)
+
+
+def flat(ref):
+    return ref[...].reshape(-1, ref.shape[-1])
+
+
+def scatter_product(scatter, i, lhs, weight, rows):
+    p = dot(jnp.concatenate([lhs(2), lhs(3)], axis=0), weight, NT)
+    n = rows // NCH
+    scatter.far(i, p[:n], p[n:])
+    p = dot(jnp.concatenate([lhs(0), lhs(1)], axis=0), weight, NT)
+    scatter.near(i, p[:n], p[n:])
+
+
+def mid_kernel(x_ref, o_ref, ln_ref, wp_hbm, wf_hbm,
+               hid_ref, act_ref, n2_hbm, u_hbm, g_hbm, n1_hbm,
+               wp, wf, u_buf, g_buf, gat1, gat2, low1, wide1, low2, wide2, load_sem, store_sem, send_sem, recv_sem):
+    rows = x_ref.shape[0]
+    n = rows // NCH
+    hidden = wf.shape[1] // 2
+    loads = [start_load(wp_hbm, wp, load_sem.at[0]), start_load(wf_hbm, wf, load_sem.at[1])]
+    links = Links(send_sem, recv_sem)
+    links.enter()
+    s1, s2 = Scatter(links, low1, wide1), Scatter(links, low2, wide2)
+    g1, g2 = Gather(links, gat1), Gather(links, gat2)
+    loads[0].wait()
+    for i in range(NCH):
+        scatter_product(s1, i, lambda b: block_rows(o_ref, b, i, rows), wp[...], rows)
+    for i in range(NCH):
+        s1.middle(i)
+    for i in range(NCH):
+        h = x_ref[chunk(i, rows)] + s1.done(i)
+        hid_ref[chunk(i, rows)] = h
+        g1.send(i, (normed(h)[0] * ln_ref[0:1] + ln_ref[1:2]).astype(jnp.bfloat16))
+    loads[1].wait()
+
+    def mlp(i):
+        u = dot(g1.done(i), wf[:, :hidden], NN)
+        put_rows(u_buf, u.astype(jnp.bfloat16), i, rows)
+        g = gelu_both(u)[0].astype(jnp.bfloat16)
+        put_rows(g_buf, g, i, rows)
+        scatter_product(s2, i, lambda b: g[b * n : (b + 1) * n], wf[:, hidden:], rows)
+
+    g1.forward(0)
+    mlp(0)
+    g1.forward(1)
+    s2.middle(0)
+    mlp(1)
+    s2.middle(1)
+    stores = [
+        start_load(gat1, n2_hbm, store_sem.at[0]),
+        start_load(u_buf, u_hbm, store_sem.at[1]),
+        start_load(g_buf, g_hbm, store_sem.at[2]),
+    ]
+    for i in range(NCH):
+        act = (hid_ref[chunk(i, rows)] + s2.done(i)).astype(jnp.bfloat16)
+        act_ref[chunk(i, rows)] = act
+        g2.send(i, (normed(act.astype(jnp.float32))[0] * ln_ref[2:3] + ln_ref[3:4]).astype(jnp.bfloat16))
+    for i in range(NCH):
+        g2.forward(i)
+    for i in range(NCH):
+        g2.copies["s", i].wait_recv()
+        g2.copies["f", i].wait_recv()
+    stores.append(start_load(gat2, n1_hbm, store_sem.at[3]))
+    links.leave()
+    for store in stores:
+        store.wait()
+
+
+VM = pl.BlockSpec(memory_space=pltpu.VMEM)
+HB = pl.BlockSpec(memory_space=pl.ANY)
+
+
+def comm_scratch(copies):
+    return [pltpu.SemaphoreType.DMA((copies,)), pltpu.SemaphoreType.DMA((copies,))]
+
+
+def scatter_scratch(rows, width):
+    return [pltpu.VMEM((6, rows, width), jnp.bfloat16), pltpu.VMEM((2, rows, width), jnp.float32)]
+
+
+def params(ident):
+    return pltpu.CompilerParams(collective_id=ident, has_side_effects=True, vmem_limit_bytes=60 << 20)
+
+
+def mid_chain(x, o, ln, wp, wf):
+    rows, width = x.shape
+    hidden = wf.shape[1] // 2
+    bf16, f32 = jnp.bfloat16, jnp.float32
+    out = jax.ShapeDtypeStruct
+    res = pl.pallas_call(
+        mid_kernel,
+        in_specs=[VM, VM, VM, HB, HB],
+        out_specs=[VM, VM, HB, HB, HB, HB],
+        out_shape=[
+            out((rows, width), f32),
+            out((rows, width), bf16),
+            out((4, rows, width), bf16),
+            out((4 * rows, hidden), bf16),
+            out((4 * rows, hidden), bf16),
+            out((4, rows, width), bf16),
+        ],
+        scratch_shapes=[
+            pltpu.VMEM(wp.shape, bf16),
+            pltpu.VMEM(wf.shape, bf16),
+            pltpu.VMEM((4 * rows, hidden), bf16),
+            pltpu.VMEM((4 * rows, hidden), bf16),
+            pltpu.VMEM((4, rows, width), bf16),
+            pltpu.VMEM((4, rows, width), bf16),
+            *scatter_scratch(rows, width),
+            *scatter_scratch(rows, width),
+            pltpu.SemaphoreType.DMA((2,)),
+            pltpu.SemaphoreType.DMA((4,)),
+            *comm_scratch(2 * Scatter.COPIES + 2 * Gather.COPIES),
+        ],
+        compiler_params=params(1),
+        cost_estimate=pl.CostEstimate(flops=60 << 30, bytes_accessed=24 << 20, transcendentals=0),
+    )(x, o, ln, wp, wf)
+    hid, act, n2, u, g, n1 = res
+    return hid, act, n2.reshape(4 * rows, width), u, g, n1.reshape(4 * rows, width)
+
+
+def turn_kernel(x_ref, o_ref, dy_ref, ln_ref, dm_hbm, wp_hbm, wf_hbm,
+                dh_ref, norm_ref, y_hbm, hid_ref, do_ref, da_hbm, gfc_hbm,
+                wp, wf, dm, g_buf, du_buf, y_buf, gfc, gat1, gat2, low1, wide1, low2, wide2,
+                load_sem, store_sem, send_sem, recv_sem):
+    rows = x_ref.shape[0]
+    n = rows // NCH
+    hidden = wf.shape[1] // 2
+    loads = [
+        start_load(wp_hbm, wp, load_sem.at[0]),
+        start_load(wf_hbm, wf, load_sem.at[1]),
+        start_load(dm_hbm, dm, load_sem.at[2]),
+    ]
+    links = Links(send_sem, recv_sem)
+    links.enter()
+    s1, s2 = Scatter(links, low1, wide1), Scatter(links, low2, wide2)
+    g1, g2 = Gather(links, gat1), Gather(links, gat2)
+    loads[0].wait()
+    for i in range(NCH):
+        scatter_product(s1, i, lambda b: block_rows(o_ref, b, i, rows), wp[...], rows)
+    for i in range(NCH):
+        s1.middle(i)
+    for i in range(NCH):
+        h = x_ref[chunk(i, rows)].astype(jnp.float32) + s1.done(i)
+        hid_ref[chunk(i, rows)] = h
+        g1.send(i, (normed(h)[0] * ln_ref[0:1] + ln_ref[1:2]).astype(jnp.bfloat16))
+    loads[1].wait()
+    loads[2].wait()
+
+    def mlp(i):
+        u = dot(g1.done(i), wf[:, :hidden], NN)
+        g, slope = gelu_both(u)
+        put_rows(g_buf, g.astype(jnp.bfloat16), i, rows)
+        dmi = jnp.concatenate([block_rows(dm, b, i, rows) for b in range(4)], axis=0)
+        du = (dot(dmi, wf[:, hidden:], NN) * slope).astype(jnp.bfloat16)
+        put_rows(du_buf, du, i, rows)
+        scatter_product(s2, i, lambda b: du[b * n : (b + 1) * n], wf[:, :hidden], rows)
+
+    g1.forward(0)
+    mlp(0)
+    g1.forward(1)
+    s2.middle(0)
+    mlp(1)
+    s2.middle(1)
+    weight_grad(gfc, hidden, dm[...], g_buf[...])
+    sums = None
+    for i in range(NCH):
+        at = chunk(i, rows)
+        dx, dgain, dshift = norm_back(hid_ref[at], s2.done(i), ln_ref[0:1])
+        dh = dy_ref[at] + dx
+        dh_ref[at] = dh
+        g2.send(i, dh.astype(jnp.bfloat16))
+        both = jnp.concatenate([dgain, dshift], axis=0)
+        sums = both if sums is None else sums + both
+    norm_ref[...] = sums
+    weight_grad(gfc, 0, flat(gat1), du_buf[...])
+    stores = [start_load(gfc, gfc_hbm, store_sem.at[0])]
+    for b in range(4):
+        y_buf[pl.ds(b * rows, rows)] = dot(g_buf[pl.ds(b * rows, rows)], wf[:, hidden:], NT).astype(jnp.bfloat16)
+    stores.append(start_load(y_buf, y_hbm, store_sem.at[1]))
+    for i in range(NCH):
+        g2.forward(i)
+        put_rows(do_ref, dot(g2.done(i), wp[...], NN).astype(jnp.bfloat16), i, rows)
+    stores.append(start_load(gat2, da_hbm, store_sem.at[2]))
+    links.leave()
+    for store in stores:
+        store.wait()
+
+
+def turn_chain(x, o, dy, ln, dm, wp, wf):
+    rows, width = x.shape
+    hidden = wf.shape[1] // 2
+    lw = wp.shape[1]
+    bf16, f32 = jnp.bfloat16, jnp.float32
+    out = jax.ShapeDtypeStruct
+    res = pl.pallas_call(
+        turn_kernel,
+        in_specs=[VM, VM, VM, VM, HB, HB, HB],
+        out_specs=[VM, VM, HB, VM, VM, HB, HB],
+        out_shape=[
+            out((rows, width), f32),
+            out((2, width), f32),
+            out((4 * rows, width), bf16),
+            out((rows, width), f32),
+            out((4 * rows, lw), bf16),
+            out((4, rows, width), bf16),
+            out((width, 2 * hidden), bf16),
+        ],
+        scratch_shapes=[
+            pltpu.VMEM(wp.shape, bf16),
+            pltpu.VMEM(wf.shape, bf16),
+            pltpu.VMEM((4 * rows, width), bf16),
+            pltpu.VMEM((4 * rows, hidden), bf16),
+            pltpu.VMEM((4 * rows, hidden), bf16),
+            pltpu.VMEM((4 * rows, width), bf16),
+            pltpu.VMEM((width, 2 * hidden), bf16),
+            pltpu.VMEM((4, rows, width), bf16),
+            pltpu.VMEM((4, rows, width), bf16),
+            *scatter_scratch(rows, width),
+            *scatter_scratch(rows, width),
+            pltpu.SemaphoreType.DMA((3,)),
+            pltpu.SemaphoreType.DMA((3,)),
+            *comm_scratch(2 * Scatter.COPIES + 2 * Gather.COPIES),
+        ],
+        compiler_params=params(2),
+        cost_estimate=pl.CostEstimate(flops=60 << 30, bytes_accessed=24 << 20, transcendentals=0),
+    )(x, o, dy, ln, dm, wp, wf)
+    dh, norms, y, hid, do, da, gfc = res
+    return dh, norms, y, hid, do, da.reshape(4 * rows, width), gfc
+
+
+def back_kernel(x_ref, dh1_ref, hid_ref, ln_ref, dqkv_ref, wq_hbm, wp_hbm, wf_hbm, u_hbm, g_hbm, n2_hbm,
+                gin_ref, dh_ref, norm_ref, do_ref, da_hbm, gfc_hbm,
+                wq, wp, wf, u_buf, g_buf, n2, du_buf, gfc, gat1, gat2, low1, wide1, low2, wide2,
+                load_sem, store_sem, send_sem, recv_sem):
+    rows = x_ref.shape[0]
+    n = rows // NCH
+    hidden = wf.shape[1] // 2
+    loads = [
+        start_load(src, dst, load_sem.at[k])
+        for k, (src, dst) in enumerate(
+            ((wq_hbm, wq), (wf_hbm, wf), (u_hbm, u_buf), (g_hbm, g_buf), (n2_hbm, n2), (wp_hbm, wp))
+        )
+    ]
+    links = Links(send_sem, recv_sem)
+    links.enter()
+    s1, s2 = Scatter(links, low1, wide1), Scatter(links, low2, wide2)
+    g1, g2 = Gather(links, gat1), Gather(links, gat2)
+    loads[0].wait()
+    for i in range(NCH):
+        scatter_product(s1, i, lambda b: block_rows(dqkv_ref, b, i, rows), wq[...], rows)
+        if i:
+            s1.middle(i - 1)
+    s1.middle(NCH - 1)
+    sums1 = None
+    for i in range(NCH):
+        at = chunk(i, rows)
+        dx, dgain, dshift = norm_back(x_ref[at].astype(jnp.float32), s1.done(i), ln_ref[0:1])
+        gin = dh1_ref[at] + dx
+        gin_ref[at] = gin
+        g1.send(i, gin.astype(jnp.bfloat16))
+        both = jnp.concatenate([dgain, dshift], axis=0)
+        sums1 = both if sums1 is None else sums1 + both
+    for load in loads[1:]:
+        load.wait()
+
+    def mlp(i):
+        dmi = g1.done(i)
+        ui = jnp.concatenate([block_rows(u_buf, b, i, rows) for b in range(4)], axis=0).astype(jnp.float32)
+        du = (dot(dmi, wf[:, hidden:], NN) * gelu_both(ui)[1]).astype(jnp.bfloat16)
+        put_rows(du_buf, du, i, rows)
+        scatter_product(s2, i, lambda b: du[b * n : (b + 1) * n], wf[:, :hidden], rows)
+
+    g1.forward(0)
+    mlp(0)
+    g1.forward(1)
+    s2.middle(0)
+    mlp(1)
+    s2.middle(1)
+    weight_grad(gfc, hidden, flat(gat1), g_buf[...])
+    sums2 = None
+    for i in range(NCH):
+        at = chunk(i, rows)
+        dx, dgain, dshift = norm_back(hid_ref[at], s2.done(i), ln_ref[1:2])
+        dh = gin_ref[at].astype(jnp.bfloat16).astype(jnp.float32) + dx
+        dh_ref[at] = dh
+        g2.send(i, dh.astype(jnp.bfloat16))
+        both = jnp.concatenate([dgain, dshift], axis=0)
+        sums2 = both if sums2 is None else sums2 + both
+    norm_ref[...] = jnp.concatenate([sums1, sums2], axis=0)
+    weight_grad(gfc, 0, flat(n2), du_buf[...])
+    stores = [start_load(gfc, gfc_hbm, store_sem.at[0])]
+    for i in range(NCH):
+        g2.forward(i)
+        put_rows(do_ref, dot(g2.done(i), wp[...], NN).astype(jnp.bfloat16), i, rows)
+    stores.append(start_load(gat2, da_hbm, store_sem.at[1]))
+    links.leave()
+    for store in stores:
+        store.wait()
+
+
+def back_chain(x, dh1, hid, ln, dqkv, wq, wp, wf, u, g, n2):
+    rows, width = x.shape
+    hidden = wf.shape[1] // 2
+    lw = wp.shape[1]
+    bf16, f32 = jnp.bfloat16, jnp.float32
+    out = jax.ShapeDtypeStruct
+    res = pl.pallas_call(
+        back_kernel,
+        in_specs=[VM] * 5 + [HB] * 6,
+        out_specs=[VM, VM, VM, VM, HB, HB],
+        out_shape=[
+            out((rows, width), f32),
+            out((rows, width), f32),
+            out((4, width), f32),
+            out((4 * rows, lw), bf16),
+            out((4, rows, width), bf16),
+            out((width, 2 * hidden), bf16),
+        ],
+        scratch_shapes=[
+            pltpu.VMEM(wq.shape, bf16),
+            pltpu.VMEM(wp.shape, bf16),
+            pltpu.VMEM(wf.shape, bf16),
+            pltpu.VMEM((4 * rows, hidden), bf16),
+            pltpu.VMEM((4 * rows, hidden), bf16),
+            pltpu.VMEM((4 * rows, width), bf16),
+            pltpu.VMEM((4 * rows, hidden), bf16),
+            pltpu.VMEM((width, 2 * hidden), bf16),
+            pltpu.VMEM((4, rows, width), bf16),
+            pltpu.VMEM((4, rows, width), bf16),
+            *scatter_scratch(rows, width),
+            *scatter_scratch(rows, width),
+            pltpu.SemaphoreType.DMA((6,)),
+            pltpu.SemaphoreType.DMA((2,)),
+            *comm_scratch(2 * Scatter.COPIES + 2 * Gather.COPIES),
+        ],
+        compiler_params=params(3),
+        cost_estimate=pl.CostEstimate(flops=60 << 30, bytes_accessed=24 << 20, transcendentals=0),
+    )(x, dh1, hid, ln, dqkv, wq, wp, wf, u, g, n2)
+    gin, dh, norms, do, da, gfc = res
+    return gin, dh, norms, do, da.reshape(4 * rows, width), gfc
+
+
+AXES = ("dp", "section", "tensor")
+ORDER = (0, 2, 1, 3)
 
 
 def local(
@@ -375,7 +849,7 @@
     first = c == 0
     t = z % 2 + 2 * c
 
-    def move(x, to):
+    def move(x, to, name="move"):
         pairs = []
         for dd in range(ndp):
             for cc in range(2):
@@ -383,16 +857,17 @@
                     dst = to(dd, cc, zz)
                     if dst is not None:
                         pairs.append(((dd * 2 + cc) * 4 + zz, (dst[0] * 2 + dst[1]) * 4 + dst[2]))
-        return lax.ppermute(x, AXES, pairs)
+        with jax.named_scope(name):
+            return lax.ppermute(x, AXES, pairs)
 
     def partner(x):
-        return move(x, lambda dd, cc, zz: (dd, cc, zz ^ 1))
+        return move(x, lambda dd, cc, zz: (dd, cc, zz ^ 1), "partner")
 
     def sibling(x):
-        return move(x, lambda dd, cc, zz: (dd, 1 - cc, zz))
+        return move(x, lambda dd, cc, zz: (dd, 1 - cc, zz), "sibling")
 
     def across(x):
-        return move(x, lambda dd, cc, zz: (dd, cc, zz ^ 2))
+        return move(x, lambda dd, cc, zz: (dd, cc, zz ^ 2), "across")
 
     def fetch(x):
         rem = across(x)
@@ -400,12 +875,41 @@
         recv = sibling(jnp.where(home, rem, x))
         return jnp.where(first, keep, recv), jnp.where(first, recv, keep)
 
-    def fetch_weight(w):
+    def dp_gather(piece):
+        if ndp != 4:
+            return lax.all_gather(piece, "dp", axis=0, tiled=True)
+        n = piece.shape[0]
+        p1 = move(piece, lambda dd, cc, zz: (dd ^ 1, cc, zz), "w_x")
+        p2 = move(piece, lambda dd, cc, zz: (dd ^ 2, cc, zz), "w_y")
+        p3a = move(p2[: n // 2], lambda dd, cc, zz: (dd ^ 1, cc, zz), "w_yx")
+        p3b = move(p1[n // 2 :], lambda dd, cc, zz: (dd ^ 2, cc, zz), "w_xy")
+        out = jnp.zeros((ndp * n, piece.shape[1]), piece.dtype)
+        for part, at in ((piece, d * n), (p1, (d ^ 1) * n), (p2, (d ^ 2) * n), (p3a, (d ^ 3) * n), (p3b, (d ^ 3) * n + n // 2)):
+            out = lax.dynamic_update_slice_in_dim(out, part, at, 0)
+        return out
+
+    def dp_scatter(x, bits):
+        n = x.shape[1]
+        left = sorted(bits, reverse=True)
+        v = x.reshape((2,) * len(left) + (-1, n))
+        for b in bits:
+            axis = left.index(b)
+            left.remove(b)
+            mine = (d >> b) & 1
+            send = lax.dynamic_index_in_dim(v, 1 - mine, axis, keepdims=False)
+            keep = lax.dynamic_index_in_dim(v, mine, axis, keepdims=False)
+            got = move(send, lambda dd, cc, zz, b=b: (dd ^ (1 << b), cc, zz), "g_dp")
+            v = keep.astype(f32) + got.astype(f32)
+            if left:
+                v = v.astype(bf16)
+        return v
+
+    def piece_of(w, layer):
         part = w.shape[0] // ndp
-        rem = lax.all_gather(across(lax.dynamic_slice_in_dim(w, d * part, part, 0)), "dp", axis=0, tiled=True)
-        keep = jnp.where(home, w, rem)
-        recv = sibling(jnp.where(home, rem, w))
-        return jnp.where(first, keep, recv), jnp.where(first, recv, keep)
+        src = lax.dynamic_slice_in_dim(w, d * part, part, 0)
+        far = move(src, lambda dd, cc, zz: (dd, 1 - (zz ^ 2) // 2, zz ^ 2) if cc == layer else None, "w_far")
+        near = move(src, lambda dd, cc, zz: (dd, zz // 2, zz) if cc == layer else None, "w_near")
+        return jnp.where(home, near, far)
 
     time_all = jnp.einsum("id,dcn->icn", time_emb, w_time[0], preferred_element_type=f32)
     table = jnp.pad(rel_table[0], ((0, 0), (0, 4096 - buckets)))
@@ -423,16 +927,34 @@
     for n in (heads * 32, time_all.size // 128, 2 * width // 128, 2 * width // 128):
         cuts.append((at, at + n))
         at += n
-    weights_qkv = fetch_weight(w_qkv[0].reshape(width, 3 * local_width))
     packs = fetch(small_pack)
-    weights_proj = fetch_weight(w_proj[0])
-    weights_fc1 = fetch_weight(w_fc1[0])
-    weights_fc2 = fetch_weight(w_fc2[0])
-
     def home_rows(x):
         other = lax.dynamic_index_in_dim(x, 1 - pair, 0, keepdims=False)
-        got = move(other, lambda dd, cc, zz: (dd, cc, zz ^ 2) if cc == zz // 2 else None)
+        got = move(other, lambda dd, cc, zz: (dd, cc, zz ^ 2) if cc == zz // 2 else None, "x_rows")
         return jnp.where(home, lax.dynamic_index_in_dim(x, pair, 0, keepdims=False), got)
+
+    def after(x, *first_things):
+        return lax.optimization_barrier((x,) + first_things)[0]
+
+    x0 = home_rows(inputs).astype(f32)
+    own_qp = (w_qkv[0].reshape(width, 3 * local_width), w_proj[0])
+    own_fc = jnp.concatenate([w_fc1[0], w_fc2[0]], axis=1)
+    piece_q0 = piece_of(own_qp[0], 0)
+    piece_p0 = piece_of(after(own_qp[1], piece_q0), 0)
+    piece_f0 = piece_of(after(own_fc, piece_p0), 0)
+    piece_qp1 = piece_of(after(jnp.concatenate(own_qp, axis=1), piece_f0), 1)
+    piece_f1 = piece_of(after(own_fc, piece_qp1), 1)
+    hidden_units = w_fc1.shape[2]
+
+    def sc_gather(piece):
+        return lax.all_gather(piece, "dp", axis=0, tiled=True)
+
+    fc = [sc_gather(piece_f0)]
+    qp1 = sc_gather(after(piece_qp1, fc[0]))
+    fc.append(sc_gather(after(piece_f1, qp1)))
+    weights_qkv = (dp_gather(piece_q0), qp1[:, : 3 * local_width])
+    weights_proj = (dp_gather(piece_p0), qp1[:, 3 * local_width :])
+    weights_fc = fc
 
     label_lanes = label_row(rel_index)
     out_label = rel_index[1, seq_len - 1, seq_len - 1].reshape(1)
@@ -473,85 +995,113 @@
 
     half = 2 * rows
 
-    def forward(layer, x):
-        xhat, _ = normed(x)
-        n1 = gather_rows((xhat * gains[layer][0] + shifts[layer][0]).astype(bf16))
-        qkv = (jnp.dot(n1, weights_qkv[layer], preferred_element_type=f32) + time_terms[layer]).astype(bf16)
-        o, lse = attn_fwd(qkv, mask_pad, walls[layer], scalars, ORDER, scale)
-        hidden = x + scatter_rows(
-            times_t(o[half:], weights_proj[layer]), times_t(o[:half], weights_proj[layer])
-        )
-        hhat, _ = normed(hidden)
-        n2 = gather_rows((hhat * gains[layer][1] + shifts[layer][1]).astype(bf16))
-        u = jnp.dot(n2, weights_fc1[layer], preferred_element_type=f32)
-        g = gelu_tanh(u).astype(bf16)
-        y = hidden + scatter_rows(
-            times_t(g[half:], weights_fc2[layer]), times_t(g[:half], weights_fc2[layer])
-        )
-        return y, (x, n1, qkv, o, lse, hidden, n2, u, g)
-
-    def backward(layer, dy, kept):
-        x, n1, qkv, o, lse, hidden, n2, u, g = kept
-        dm = gather_rows(dy.astype(bf16))
-        grad_fc2 = grad_of(dm, g)
-        dg = jnp.dot(dm, weights_fc2[layer], preferred_element_type=f32)
-        du = jax.vjp(gelu_tanh, u)[1](dg)[0].astype(bf16)
-        dn2 = scatter_rows(times_t(du[half:], weights_fc1[layer]), times_t(du[:half], weights_fc1[layer]))
-        grad_fc1 = grad_of(n2, du)
-        dx2, dgain2, dshift2 = norm_back(hidden, dn2, gains[layer][1])
-        dh = dy + dx2
-        da = gather_rows(dh.astype(bf16))
-        do = jnp.dot(da, weights_proj[layer], preferred_element_type=f32).astype(bf16)
-        grad_proj = grad_of(da, o)
-        dqkv, dwall = attn_bwd(qkv, do, o, lse, mask_pad, walls[layer], scalars, ORDER, scale)
-        dn1 = scatter_rows(times_t(dqkv[half:], weights_qkv[layer]), times_t(dqkv[:half], weights_qkv[layer]))
-        grad_qkv = grad_of(n1, dqkv)
+    def reduced(x):
+        with jax.named_scope("g_sum"):
+            return lax.psum_scatter(x, "dp", scatter_dimension=0, tiled=True)
+
+    def reduced_late(x):
+        if ndp & (ndp - 1):
+            return reduced(x)
+        bits = list(range(ndp.bit_length() - 1))
+        cut = 4 * 128
+        return jnp.concatenate(
+            [dp_scatter(x[:, :cut], bits), dp_scatter(x[:, cut:], bits[::-1])], axis=1
+        ).astype(bf16)
+
+    def scores_in(n1, layer):
+        return (jnp.dot(n1, weights_qkv[layer], preferred_element_type=f32) + time_terms[layer]).astype(bf16)
+
+    def column_sums(dqkv):
         sums = jnp.sum(dqkv.astype(f32), axis=0)
-        sums = jnp.concatenate([sums[:local_width], sums[2 * local_width :]])
-        dx1, dgain1, dshift1 = norm_back(x, dn1, gains[layer][0])
-        rel = bias_grads(out_label, label_lanes, dwall)
-        norms = jnp.stack([dgain1, dgain2, dshift1, dshift2])
-        parts = [lax.psum_scatter(w, "dp", scatter_dimension=0, tiled=True) for w in (grad_fc2, grad_fc1, grad_proj, grad_qkv)]
-        return dh + dx1, parts, rel, norms, sums
+        return jnp.concatenate([sums[:local_width], sums[2 * local_width :]])
+
+    def tie(*values):
+        return lax.optimization_barrier(values)
 
     def by_core(pairs):
         return jnp.where(first, pairs[0], pairs[1])
 
-    def to_home_core(both):
-        return move(
-            jnp.where(first, both[1], both[0]),
-            lambda dd, cc, zz: (dd, 1 - cc, zz) if cc == zz // 2 else None,
-        )
-
-    def deliver(both):
-        same = jnp.where(home, by_core(both), to_home_core(both))
-        got = [
-            move(both[layer], lambda dd, cc, zz, to=layer: (dd, to, zz ^ 2) if cc != zz // 2 else None)
-            for layer in range(2)
-        ]
-        return same, by_core(got)
-
-    x0 = home_rows(inputs).astype(f32)
-    y0, kept0 = forward(0, x0)
-    act0 = y0.astype(bf16)
-    y1, kept1 = forward(1, act0.astype(f32))
-    act1 = y1.astype(bf16)
+    def near_of(x, layer):
+        return move(x, lambda dd, cc, zz: (dd, layer, zz) if cc == zz // 2 and cc != layer else None, "d_near")
+
+    def far_of(x, layer):
+        return move(x, lambda dd, cc, zz: (dd, layer, zz ^ 2) if cc != zz // 2 else None, "d_far")
+
     live = (t * rows + jnp.arange(rows)) < length
-    dy1 = home_rows(cotangent).astype(f32) * live.astype(f32)[:, None]
-    gin1, parts1, rel1, norms1, sums1 = backward(1, dy1, kept1)
-    gin0, parts0, rel0, norms0, sums0 = backward(0, gin1.astype(bf16).astype(f32), kept0)
+
+    n1_0 = gather_rows((normed(x0)[0] * gains[0][0] + shifts[0][0]).astype(bf16))
+    qkv0 = scores_in(n1_0, 0)
+    qkv0, cotangent = tie(qkv0, cotangent)
+    cot = home_rows(cotangent)
+    o0, lse0 = attn_fwd(qkv0, mask_pad, walls[0], scalars, ORDER, scale)
+    o0, cot = tie(o0, cot)
+    ln_mid = jnp.stack([gains[0][1], shifts[0][1], gains[1][0], shifts[1][0]])
+    hid0, act0, n2_0, u0, g0, n1_1 = mid_chain(x0, o0, ln_mid, weights_proj[0], weights_fc[0])
+    qkv1 = scores_in(n1_1, 1)
+    dy1 = cot.astype(f32) * live.astype(f32)[:, None]
+    qkv1, dm1 = tie(qkv1, dy1.astype(bf16))
+    dm1 = gather_rows(dm1)
+    o1, lse1 = attn_fwd(qkv1, mask_pad, walls[1], scalars, ORDER, scale)
+    o1, dm1 = tie(o1, dm1)
+
+    ln_turn = jnp.stack([gains[1][1], shifts[1][1]])
+    dh1, norms1, y1, hid1, do1, da1, gfc1 = turn_chain(act0, o1, dy1, ln_turn, dm1, weights_proj[1], weights_fc[1])
+    sum_fc1 = reduced(gfc1)
+    do1, y1, a0 = tie(do1, y1, act0)
+    act1 = (hid1 + scatter_rows(y1[half:], y1[:half])).astype(bf16)
+    got_acts = [near_of(a0, 0) + near_of(act1, 1), far_of(a0, 0) + far_of(act1, 1)]
+    dqkv1, dwall1 = attn_bwd(qkv1, do1, o1, lse1, mask_pad, walls[1], scalars, ORDER, scale)
+    dqkv1, got_acts = tie(dqkv1, got_acts)
+    ln_back = jnp.stack([gains[1][0], gains[0][1]])
+    gin1, dh0, norms10, do0, da0, gfc0 = back_chain(
+        act0, dh1, hid0, ln_back, dqkv1, weights_qkv[1], weights_proj[0], weights_fc[0], u0, g0, n2_0
+    )
+    sum_fc0 = reduced(gfc0)
+    sum_qp1 = reduced(jnp.concatenate([grad_of(n1_1, dqkv1), grad_of(da1, o1)], axis=1))
+    rel1 = bias_grads(out_label, label_lanes, dwall1)
+    sums1 = column_sums(dqkv1)
+    do0, sum_qp1, rel1, sums1 = tie(do0, sum_qp1, rel1, sums1)
+    g1 = gin1.astype(bf16)
+    w1 = jnp.concatenate([sum_qp1, sum_fc1], axis=1)
+    do0, g1, w1 = tie(do0, g1, w1)
+    got1 = [near_of(g1, 1), far_of(g1, 1), near_of(w1, 1), far_of(w1, 1)]
+    dqkv0, dwall0 = attn_bwd(qkv0, do0, o0, lse0, mask_pad, walls[0], scalars, ORDER, scale)
+    dqkv0, got1 = tie(dqkv0, got1)
+    dn1 = scatter_rows(times_t(dqkv0[half:], weights_qkv[0]), times_t(dqkv0[:half], weights_qkv[0]))
+    grad_qp0 = jnp.concatenate([grad_of(n1_0, dqkv0), grad_of(da0, o0)], axis=1)
+    sum_qp0 = reduced_late(grad_qp0)
+    rel0 = bias_grads(out_label, label_lanes, dwall0)
+    sums0 = column_sums(dqkv0)
+    dn1, grad_qp0, rel0, sums0 = tie(dn1, grad_qp0, rel0, sums0)
+    dx, dgain, dshift = norm_back(x0, dn1, gains[0][0])
+    gin0 = dh0 + dx
+    early0, early1, late1 = norms10[2:], norms1, norms10[:2]
+    late0 = jnp.concatenate([dgain, dshift], axis=0)
+    sums_w0, sums_w1 = (sum_qp0, sum_fc0), (sum_qp1, sum_fc1)
 
     def by_image(same, other):
         return jnp.stack([jnp.where(pair == 0, same, other), jnp.where(pair == 0, other, same)])[None]
 
-    acts = by_image(*deliver((act0, act1)))
-    same, other = deliver((gin0.astype(bf16), gin1.astype(bf16)))
-    same = jnp.where(home, by_core((gin0, gin1)), same.astype(f32))
-    input_grads = by_image(same, other.astype(f32))
-    grads = []
-    for a, b in zip(parts0, parts1):
-        same, other = deliver((a, b))
-        grads.append(same.astype(f32) + other.astype(f32))
+    acts = by_image(jnp.where(home, by_core((act0, act1)), got_acts[0]), got_acts[1])
+    low0 = gin0.astype(bf16)
+    same = jnp.where(home, by_core((gin0, gin1)), (near_of(low0, 0) + got1[0]).astype(f32))
+    input_grads = by_image(same, (far_of(low0, 0) + got1[1]).astype(f32))
+
+    def total(mine, parts):
+        out = jnp.where(home, mine, jnp.zeros_like(mine)).astype(f32)
+        for part in parts:
+            out = out + part.astype(f32)
+        return out
+
+    n_qp = 4 * local_width
+    grad_fc = total(
+        by_core((sums_w0[1], sums_w1[1])),
+        (near_of(sums_w0[1], 0), far_of(sums_w0[1], 0), got1[2][:, n_qp:], got1[3][:, n_qp:]),
+    )
+    grad_qp = total(
+        by_core((sums_w0[0], sums_w1[0])),
+        (near_of(sums_w0[0], 0), far_of(sums_w0[0], 0), got1[2][:, :n_qp], got1[3][:, :n_qp]),
+    )
 
     here = (jnp.arange(2 * ndp) == 2 * d + pair).astype(f32)[:, None]
     pack = jnp.concatenate(
@@ -559,26 +1109,43 @@
             rel0.reshape(-1, 128),
             rel1.reshape(-1, 128),
             (here * jnp.concatenate([sums0, sums1])[None]).reshape(-1, 128),
-            jnp.stack([norms0, norms1]).reshape(-1, 128),
+            jnp.stack([early0, early1, late1]).reshape(-1, 128),
         ],
         axis=0,
     )
-    bit = 1
-    while bit < ndp:
-        pack = pack + move(pack, lambda dd, cc, zz, b=bit: (dd ^ b, cc, zz))
-        bit *= 2
-    pack = pack + across(pack)
+    late = late0.reshape(-1, 128)
+
+    def summed(x):
+        bit = 1
+        while bit < ndp:
+            x = x + move(x, lambda dd, cc, zz, b=bit: (dd ^ b, cc, zz), "pack_dp")
+            bit *= 2
+        return x + across(x)
+
+    pack = summed(pack)
     n_rel = heads * 32
     n_sum = 2 * ndp * 4 * local_width // 128
     rel_both = (pack[:n_rel], pack[n_rel : 2 * n_rel])
     sums_all = pack[2 * n_rel : 2 * n_rel + n_sum].reshape(2 * ndp, 2, 2 * local_width)
-    norms_all = pack[2 * n_rel + n_sum :]
-    norms_all = norms_all + partner(norms_all)
-    norms_all = norms_all + sibling(norms_all)
-    norms_all = norms_all.reshape(2, 4, width)
-    norms_mine = jnp.where(first, norms_all[0], norms_all[1])
+    norms = pack[2 * n_rel + n_sum :]
+    norms = norms + partner(norms)
+    norms = norms + sibling(norms)
+    late = summed(late)
+    late = late + partner(late)
+    late = late + sibling(late)
+    early0, early1, late1 = norms.reshape(3, 2, width)
+    late0 = late.reshape(2, width)
+    norms_mine = jnp.stack([by_core((late0, late1)), by_core((early0, early1))], axis=1)
     cols = width // (4 * ndp)
-    norms_mine = lax.dynamic_slice_in_dim(norms_mine, (d * 4 + z) * cols, cols, 1)
+    norms_mine = lax.dynamic_slice_in_dim(norms_mine, (d * 4 + z) * cols, cols, 2)
+
+    def to_home_core(both):
+        return move(
+            jnp.where(first, both[1], both[0]),
+            lambda dd, cc, zz: (dd, 1 - cc, zz) if cc == zz // 2 else None,
+            "pack_near",
+        )
+
     rel_mine = jnp.where(home, by_core(rel_both), to_home_core(rel_both))
     rel_grad = rel_mine.reshape(heads, 4096)[:, :buckets]
     sums_both = (sums_all[:, 0], sums_all[:, 1])
@@ -591,14 +1158,14 @@
     return (
         acts,
         input_grads,
-        grads[3].reshape(width // ndp, 3, local_width)[None],
+        grad_qp[:, : 3 * local_width].reshape(width // ndp, 3, local_width)[None],
         grad_time[None],
-        grads[2][None],
-        grads[1][None],
-        grads[0][None],
+        grad_qp[:, 3 * local_width :][None],
+        grad_fc[:, :hidden_units][None],
+        grad_fc[:, hidden_units:][None],
         rel_grad[None],
-        norms_mine[:2][None],
-        norms_mine[2:][None],
+        norms_mine[0][None],
+        norms_mine[1][None],
     )
 
 

time: 904 us -> 807 us (0.89)
  Pallas kernels: 96.5 us -> 304 us
  waiting for transfers between devices: 313 us -> 211 us
  matrix products: 118 us -> 26.8 us
  starting transfers between devices: 155 us -> 110 us
  other arithmetic: 95.8 us -> 56.8 us
  blocking collectives: 24.1 us -> 6.85 us
    pallas_call x0 -> x3, Pallas kernels: none -> 200 us  [the longest x1 69.7 us: back_chain(): pl.pallas_call(back_kernel, in_specs=[VM] * 5 + [HB] * 6, out_specs=[VM,...]
    ppermute x85 -> x64, waiting for transfers between devices: 312 us -> 185 us  [move(): return lax.ppermute(x, AXES, pairs)]
    ppermute x85 -> x64, starting transfers between devices: 154 us -> 110 us  [move(): return lax.ppermute(x, AXES, pairs)]
    dot_general x8 -> x2, matrix products: 43.3 us -> 7.31 us  [scores_in(): jnp.dot(n1, weights_qkv[layer], preferred_element_type=f32)]
    dot_general x8 -> x4, matrix products: 42.7 us -> 10.1 us  [grad_of(): lax.dot_general(x, y, (((0,), (0,)), ((), ())), preferred_element_type=f32)]
    reduce_scatter x8 -> x3, waiting for transfers between devices: 0.03 us -> 25 us  [reduced(): return lax.psum_scatter(x, 'dp', scatter_dimension=0, tiled=True)]
    dot_general x16 -> x2, matrix products: 30.6 us -> 7.63 us  [times_t(): lax.dot_general(x, w, (((1,), (1,)), ((), ())), preferred_element_type=f32)]
    select_n x9 -> x5, other arithmetic: 22.9 us -> 4.12 us  [the longest x3 3.34 us: piece_of(): return jnp.where(home, near, far)]
  transfers between devices with their start and end apart: 96 -> 70, of which waited for: 32 -> 23; matrix products, arithmetic and copies ran while one was open for 22% -> 14% of each run, Pallas kernels for 7% -> 30%
where the time goes in v2:
time: 807 us; the launch traced here: 796 us
  Pallas kernels  304 us (38%)
  waiting for transfers between devices  211 us (26%)
  starting transfers between devices  110 us (14%)
  local copies, waits for them, and re-layouts  64 us (8%)
  other arithmetic  56.8 us (7%)
  matrix products  26.8 us (3%)
  between operations  17 us (2%)
    ppermute x64, waiting for transfers between devices, move(): return lax.ppermute(x, AXES, pairs)  185 us
    ppermute x64, starting transfers between devices, move(): return lax.ppermute(x, AXES, pairs)  110 us
    pallas_call x1, Pallas kernels, back_chain(): pl.pallas_call(back_kernel, in_specs=[VM] * 5 + [HB] * 6, out_specs=[VM,...  69.7 us
    pallas_call x1, Pallas kernels, turn_chain(): pl.pallas_call(turn_kernel, in_specs=[VM, VM, VM, VM, HB, HB, HB], out_sp...  66.2 us
    pallas_call x1, Pallas kernels, mid_chain(): pl.pallas_call(mid_kernel, in_specs=[VM, VM, VM, HB, HB], out_specs=[VM,...  63.8 us
    pallas_call x2, Pallas kernels, attn_bwd(): pl.pallas_call(functools.partial(attn_bwd_kernel, order, scale), grid=(nq...  38.8 us
    pallas_call x2, Pallas kernels, attn_fwd(): pl.pallas_call(functools.partial(attn_fwd_kernel, order, scale), grid=(nq...  33.6 us
    reduce_scatter x3, waiting for transfers between devices, reduced(): return lax.psum_scatter(x, 'dp', scatter_dimension=0, tiled=True)  25 us
  transfers between devices with their start and end apart: 70, of which 23 were waited for; matrix products, arithmetic and copies ran while one was open for 14% of the time, Pallas kernels for 30%

profile of v2, /device:TPU:1, one launch (start us, length us, event | category | flops | bytes accessed | tf_op | source)
XLA Modules:
  0.0 795.9 jit_solution(13476331789436910912)
XLA Ops:
  13.1 14.9 %collective-permute-done.7 = bf16[288,864]{1,0:T(8,128)(2,1)S(1)} collective-permute-done((bf16[288,864]{1,0:T(8,128)(2,1)}, bf16[288,864]{1,0:T(8,128)(2,1)S(1)}, u32[]{:S(2)}, u32[]{:S(2)}) %collective-permute-start.7) | collective-permute-done | bytes 497696 | tf_op jit(solution)/shard_map/w_far/ppermute | solution.py:861
  33.4 6.4 collective-permute-done.14
  43.7 40.1 %collective-permute-done.20 = bf16[288,2304]{1,0:T(8,128)(2,1)S(1)} collective-permute-done((bf16[288,2304]{1,0:T(8,128)(2,1)S(1)}, bf16[288,2304]{1,0:T(8,128)(2,1)S(1)}, u32[]{:S(2)}, u32[]{:S(2)}) %collective-permute-start.20) | collective-permute-done | bytes 1327136 | tf_op jit(solution)/shard_map/w_far/ppermute | solution.py:861
  110.9 6.3 shard_map.216.wall_ref
  124.6 27.6 %collective-permute-done.16 = bf16[288,288]{1,0:T(8,128)(2,1)S(1)} collective-permute-done((bf16[288,288]{1,0:T(8,128)(2,1)S(1)}, bf16[288,288]{1,0:T(8,128)(2,1)S(1)}, u32[]{:S(2)}, u32[]{:S(2)}) %collective-permute-start.16) | collective-permute-done | bytes 165920 | tf_op jit(solution)/shard_map/w_y/ppermute | solution.py:861
  171.7 7.8 collective-permute-start.22
  201.8 12.4 %shard_map.214 = (bf16[1024,288]{1,0:T(8,128)(2,1)S(1)}, f32[4,4,256]{2,1,0:T(4,128)S(1)}) custom-call(s32[6]{0:T(128)S(1)} %stack.59.sc_ref, bf16[1024,864]{1,0:T(8,128)(2,1)S(1)} %add_convert_fusion.1.q_ref.kv_ref, bf16[1024,864]{1,0:T(8,128)(2,1)S(1)} %add_convert_fusion.1.q_ref.kv_ref, bf16[1024,56]{1,0:T(8,128)(2,1)S(1)} %select_convert_fusion.mask_ref, ...), custom_call_target="tpu_custom_call" | custom-call | flops 17179869184 | bytes 12582912 | tf_op jit(solution)/shard_map/pallas_call | solution.py:215
  217.9 12.7 %collective-permute-done.27 = bf16[288,2304]{1,0:T(8,128)(2,1)S(1)} collective-permute-done((bf16[288,2304]{1,0:T(8,128)(2,1)S(1)}, bf16[288,2304]{1,0:T(8,128)(2,1)S(1)}, u32[]{:S(2)}, u32[]{:S(2)}) %collective-permute-start.27) | collective-permute-done | bytes 1327136 | tf_op jit(solution)/shard_map/w_far/ppermute | solution.py:861
  231.8 63.8 %shard_map.215 = (f32[256,1152]{1,0:T(8,128)}, bf16[256,1152]{1,0:T(8,128)(2,1)}, bf16[4,256,1152]{2,1,0:T(8,128)(2,1)}, bf16[1024,1152]{1,0:T(8,128)(2,1)}, bf1...) custom-call(f32[256,1152]{1,0:T(8,128)} %convert_element_type.177.x_ref, bf16[1024,288]{1,0:T(8,128)(2,1)} %copy-done.12, ...), custom_call_target="tpu_custom_call" | custom-call | flops 64424509440 | bytes 25165824 | tf_op jit(solution)/shard_map/pallas_call | solution.py:563
  301.4 14.1 %collective-permute-done.24 = bf16[256,1152]{1,0:T(8,128)(2,1)S(1)} collective-permute-done((bf16[256,1152]{1,0:T(8,128)(2,1)S(1)}, bf16[256,1152]{1,0:T(8,128)(2,1)S(1)}, u32[]{:S(2)}, u32[]{:S(2)}) %collective-permute-start.24) | collective-permute-done | bytes 589856 | tf_op jit(solution)/shard_map/partner/ppermute | solution.py:861
  318.4 21.2 %shard_map.217 = (bf16[1024,288]{1,0:T(8,128)(2,1)S(1)}, f32[4,4,256]{2,1,0:T(4,128)S(1)}) custom-call(s32[6]{0:T(128)S(1)} %stack.59.sc_ref, bf16[1024,864]{1,0:T(8,128)(2,1)S(1)} %add_convert_fusion.q_ref.kv_ref, bf16[1024,864]{1,0:T(8,128)(2,1)S(1)} %add_convert_fusion.q_ref.kv_ref, bf16[1024,56]{1,0:T(8,128)(2,1)S(1)} %select_convert_fusion.mask_ref, ...), custom_call_target="tpu_custom_call" | custom-call | flops 17179869184 | bytes 12582912 | tf_op jit(solution)/shard_map/pallas_call | solution.py:215
  342.6 66.2 %shard_map.218 = (f32[256,1152]{1,0:T(8,128)}, f32[2,1152]{1,0:T(2,128)}, bf16[1024,1152]{1,0:T(8,128)(2,1)}, f32[256,1152]{1,0:T(8,128)}, bf16[1024,288]{1,0:T(...) custom-call(bf16[256,1152]{1,0:T(8,128)(2,1)} %get-tuple-element.97.x_ref, ...), custom_call_target="tpu_custom_call" | custom-call | flops 64424509440 | bytes 25165824 | tf_op jit(solution)/shard_map/pallas_call | solution.py:669
  419.1 14.6 %collective-permute-done.30 = bf16[256,1152]{1,0:T(8,128)(2,1)S(1)} collective-permute-done((bf16[256,1152]{1,0:T(8,128)(2,1)S(1)}, bf16[256,1152]{1,0:T(8,128)(2,1)S(1)}, u32[]{:S(2)}, u32[]{:S(2)}) %collective-permute-start.30) | collective-permute-done | bytes 589856 | tf_op jit(solution)/shard_map/partner/ppermute | solution.py:861
  438.0 19.7 %shard_map.219 = (bf16[1024,864]{1,0:T(8,128)(2,1)S(1)}, f32[4,32,9984]{2,1,0:T(8,128)}) custom-call(s32[6]{0:T(128)S(1)} %stack.59.sc_ref, bf16[1024,864]{1,0:T(8,128)(2,1)S(1)} %copy-done.17, bf16[1024,864]{1,0:T(8,128)(2,1)S(1)} %copy-done.17, bf16[1024,288]{1,0:T(8,128)(2,1)S(1)} %copy-done.21, bf16[1024,288]{1,0:T(8,128)(2,1)S(1)} %copy-done.15, ...), custom_call_target="tpu_custom_call" | custom-call | flops 25769803776 | bytes 20971520 | tf_op jit(solution)/shard_map/pallas_call | solution.py:293
  480.3 69.7 %shard_map.220 = (f32[256,1152]{1,0:T(8,128)}, f32[256,1152]{1,0:T(8,128)}, f32[4,1152]{1,0:T(4,128)}, bf16[1024,288]{1,0:T(8,128)(2,1)}, bf16[4,256,1152]{2,1,0:T(8,128)(2,1)}, /*index=5*/bf16[1152,2304]{1,0:T(8,128)(2,1)}) custom-call(bf16[256,1152]{1,0:T(8,128)(2,1)} %get-tuple-element.97.x_ref, f32[256,1152]{1,0:T(8,128)} %get-tuple-element.100.dh1_ref, ...), custom_call_target="tpu_custom_call" | custom-call | flops 64424509440 | bytes 25165824 | tf_op jit(solution)/shard_map/pallas_call | solution.py:781
  550.7 6.8 all-gather
  560.7 9.6 %shard_map.221 = f32[4,64,64]{2,1,0:T(8,128)S(1)} custom-call(s32[1]{0:T(128)} %bitcast.15.out_lab_ref, s32[1,4096]{1,0:T(1,128)S(1)} %copy-done.11, f32[4,32,9984]{2,1,0:T(8,128)S(1)} %copy-done.6), custom_call_target="tpu_custom_call" | custom-call | tf_op jit(solution)/shard_map/pallas_call | solution.py:120
  593.7 19.1 %shard_map.222 = (bf16[1024,864]{1,0:T(8,128)(2,1)S(1)}, f32[4,32,9984]{2,1,0:T(8,128)}) custom-call(s32[6]{0:T(128)S(1)} %stack.59.sc_ref, bf16[1024,864]{1,0:T(8,128)(2,1)S(1)} %copy-done.19, bf16[1024,864]{1,0:T(8,128)(2,1)S(1)} %copy-done.19, bf16[1024,288]{1,0:T(8,128)(2,1)S(1)} %copy-done.20, bf16[1024,288]{1,0:T(8,128)(2,1)S(1)} %copy-done.13, ...), custom_call_target="tpu_custom_call" | custom-call | flops 25769803776 | bytes 20971520 | tf_op jit(solution)/shard_map/pallas_call | solution.py:293
  615.3 9.6 %shard_map.223 = f32[4,64,64]{2,1,0:T(8,128)S(1)} custom-call(s32[1]{0:T(128)} %bitcast.15.out_lab_ref, s32[1,4096]{1,0:T(1,128)S(1)} %copy-done.11, f32[4,32,9984]{2,1,0:T(8,128)S(1)} %copy-done.7), custom_call_target="tpu_custom_call" | custom-call | tf_op jit(solution)/shard_map/pallas_call | solution.py:120
  624.9 22.1 %reduce-scatter.8.cloned.1.call-done = bf16[288,2304]{1,0:T(8,128)(2,1)} async-done(((bf16[1152,2304]{1,0:T(8,128)(2,1)}), bf16[288,2304]{1,0:T(8,128)(2,1)}) %reduce-scatter.8.cloned.1.call-update) | async-done | bytes 1327120 | tf_op jit(solution)/shard_map/g_sum/reduce_scatter | solution.py:1000
  676.1 8.5 %collective-permute-done.44 = bf16[2,288,512]{2,1,0:T(8,128)(2,1)S(1)} collective-permute-done((bf16[2,288,512]{2,1,0:T(8,128)(2,1)S(1)}, bf16[2,288,512]{2,1,0:T(8,128)(2,1)S(1)}, u32[]{:S(2)}, u32[]{:S(2)}) %collective-permute-start.44) | collective-permute-done | bytes 589856 | tf_op jit(solution)/shard_map/g_dp/ppermute | solution.py:861
  725.8 6.8 collective-permute-start.43
  741.2 8.3 %collective-permute-start.49 = (bf16[288,1152]{1,0:T(8,128)(2,1)}, bf16[288,1152]{1,0:T(8,128)(2,1)}, u32[]{:S(2)}, u32[]{:S(2)}) collective-permute-start(bf16[288,1152]{1,0:T(8,128)(2,1)} %pad_maximum_fusion.7), channel_id=1, source_target_pairs={{2,0},{3,1},{4,2},{5,3},{10,8},{11,9},{12,10},{13,11},{18,16},{19,... | collective-permute-start | bytes 1990664 | tf_op jit(solution)/shard_map/d_far/ppermute | solution.py:861
  749.6 9.9 %collective-permute-done.52 = f32[382,128]{1,0:T(8,128)S(1)} collective-permute-done((f32[382,128]{1,0:T(8,128)S(1)}, f32[382,128]{1,0:T(8,128)S(1)}, u32[]{:S(2)}, u32[]{:S(2)}) %collective-permute-start.52) | collective-permute-done | bytes 195616 | tf_op jit(solution)/shard_map/across/ppermute | solution.py:861
  (496 shorter events, 280.8 us)
Async XLA Ops:
  7.2 182.9 %all-gather.5.cloned.1.call-start = ((), (), s32[]{:S(2)}) async-start(), calls=%async_computation.3 | async-start | bytes 6635520 | tf_op jit(solution)/shard_map/all_gather | solution.py:950
  41.6 42.2 %collective-permute-start.20 = (bf16[288,2304]{1,0:T(8,128)(2,1)S(1)}, bf16[288,2304]{1,0:T(8,128)(2,1)S(1)}, u32[]{:S(2)}, u32[]{:S(2)}) collective-permute-start(bf16[288,2304]{1,0:T(8,128)(2,1)S(1)} %constant_dynamic-slice_fusion.6), channel_id=1, source_target_pairs={{0,2},{1,3},{2,4},{3,5},{8,10},{9,11},{10,12},{11,13},{16,18},{17,... | collective-permute-start | bytes 3981320 | tf_op jit(solution)/shard_map/w_far/ppermute | solution.py:861
  42.9 40.9 %collective-permute-start.19 = (bf16[288,2304]{1,0:T(8,128)(2,1)S(1)}, bf16[288,2304]{1,0:T(8,128)(2,1)S(1)}, u32[]{:S(2)}, u32[]{:S(2)}) collective-permute-start(bf16[288,2304]{1,0:T(8,128)(2,1)S(1)} %constant_dynamic-slice_fusion.6), channel_id=1, source_target_pairs={{0,0},{1,1},{2,6},{3,7},{8,8},{9,9},{10,14},{11,15},{16,16},{17,17... | collective-permute-start | bytes 3981320 | tf_op jit(solution)/shard_map/w_near/ppermute | solution.py:861
  85.0 146.7 %all-gather.7.cloned.1.call-start = ((), (), s32[]{:S(2)}) async-start(), calls=%async_computation.4 | async-start | bytes 3317760 | tf_op jit(solution)/shard_map/all_gather | solution.py:950
  118.0 46.6 %collective-permute-start.9 = (bf16[288,864]{1,0:T(8,128)(2,1)S(1)}, bf16[288,864]{1,0:T(8,128)(2,1)S(1)}, u32[]{:S(2)}, u32[]{:S(2)}) collective-permute-start(bf16[288,864]{1,0:T(8,128)(2,1)S(1)} %copy-done.54), channel_id=1, source_target_pairs={{0,16},{1,17},{2,18},{3,19},{4,20},{5,21},{6,22},{7,23},{8,24},{9,... | collective-permute-start | bytes 1493000 | tf_op jit(solution)/shard_map/w_y/ppermute | solution.py:861
  119.3 46.6 %collective-permute-start.8 = (bf16[288,864]{1,0:T(8,128)(2,1)S(1)}, bf16[288,864]{1,0:T(8,128)(2,1)S(1)}, u32[]{:S(2)}, u32[]{:S(2)}) collective-permute-start(bf16[288,864]{1,0:T(8,128)(2,1)S(1)} %copy-done.54), channel_id=1, source_target_pairs={{0,8},{1,9},{2,10},{3,11},{4,12},{5,13},{6,14},{7,15},{8,0},{9,1},... | collective-permute-start | bytes 1493000 | tf_op jit(solution)/shard_map/w_x/ppermute | solution.py:861
  124.6 42.9 %collective-permute-start.4 = (bf16[256,1152]{1,0:T(8,128)(2,1)S(1)}, bf16[256,1152]{1,0:T(8,128)(2,1)S(1)}, u32[]{:S(2)}, u32[]{:S(2)}) collective-permute-start(bf16[256,1152]{1,0:T(8,128)(2,1)S(1)} %add_convert_fusion.4), channel_id=1, source_target_pairs={{0,1},{1,0},{2,3},{3,2},{4,5},{5,4},{6,7},{7,6},{8,9},{9,8},{10,11... | collective-permute-start | bytes 1769480 | tf_op jit(solution)/shard_map/partner/ppermute | solution.py:861
  190.1 152.4 %all-gather.9.cloned.1.call-start = ((), (), s32[]{:S(2)}) async-start(), calls=%async_computation.5 | async-start | bytes 6635520 | tf_op jit(solution)/shard_map/all_gather | solution.py:950
  194.1 36.5 %collective-permute-start.27 = (bf16[288,2304]{1,0:T(8,128)(2,1)S(1)}, bf16[288,2304]{1,0:T(8,128)(2,1)S(1)}, u32[]{:S(2)}, u32[]{:S(2)}) collective-permute-start(bf16[288,2304]{1,0:T(8,128)(2,1)S(1)} %constant_dynamic-slice_fusion.3), channel_id=1, source_target_pairs={{4,2},{5,3},{6,4},{7,5},{12,10},{13,11},{14,12},{15,13},{20,18},{2... | collective-permute-start | bytes 3981320 | tf_op jit(solution)/shard_map/w_far/ppermute | solution.py:861
  197.4 33.2 %collective-permute-start.26 = (bf16[288,2304]{1,0:T(8,128)(2,1)S(1)}, bf16[288,2304]{1,0:T(8,128)(2,1)S(1)}, u32[]{:S(2)}, u32[]{:S(2)}) collective-permute-start(bf16[288,2304]{1,0:T(8,128)(2,1)S(1)} %constant_dynamic-slice_fusion.3), channel_id=1, source_target_pairs={{4,0},{5,1},{6,6},{7,7},{12,8},{13,9},{14,14},{15,15},{20,16},{21,... | collective-permute-start | bytes 3981320 | tf_op jit(solution)/shard_map/w_near/ppermute | solution.py:861
  231.8 347.2 %reduce-scatter.4.cloned.1.call-start = ((), (), s32[]{:S(2)}) async-start(), calls=%async_computation.6 | async-start | bytes 3317760 | tf_op jit(solution)/shard_map/g_sum/reduce_scatter | solution.py:1000
  301.4 39.6 %collective-permute-start.23 = (bf16[256,1152]{1,0:T(8,128)(2,1)S(1)}, bf16[256,1152]{1,0:T(8,128)(2,1)S(1)}, u32[]{:S(2)}, u32[]{:S(2)}) collective-permute-start(bf16[256,1152]{1,0:T(8,128)(2,1)S(1)} %copy-done.36), channel_id=1, source_target_pairs={{0,4},{1,5},{2,6},{3,7},{4,0},{5,1},{6,2},{7,3},{8,12},{9,13},{10,... | collective-permute-start | bytes 1769480 | tf_op jit(solution)/shard_map/sibling/ppermute | solution.py:861
  413.0 48.9 %collective-permute-start.33 = (bf16[256,1152]{1,0:T(8,128)(2,1)}, bf16[256,1152]{1,0:T(8,128)(2,1)}, u32[]{:S(2)}, u32[]{:S(2)}) collective-permute-start(bf16[256,1152]{1,0:T(8,128)(2,1)} %get-tuple-element.97.x_ref), channel_id=1, source_target_pairs={{2,0},{3,1},{4,2},{5,3},{10,8},{11,9},{12,10},{13,11},{18,16},{19,... | collective-permute-start | bytes 1769480 | tf_op jit(solution)/shard_map/d_far/ppermute | solution.py:861
  417.5 45.8 %collective-permute-start.31 = (bf16[256,1152]{1,0:T(8,128)(2,1)}, bf16[256,1152]{1,0:T(8,128)(2,1)}, u32[]{:S(2)}, u32[]{:S(2)}) collective-permute-start(bf16[256,1152]{1,0:T(8,128)(2,1)} %get-tuple-element.97.x_ref), channel_id=1, source_target_pairs={{6,2},{7,3},{14,10},{15,11},{22,18},{23,19},{30,26},{31,27}} | collective-permute-start | bytes 1769480 | tf_op jit(solution)/shard_map/d_near/ppermute | solution.py:861
  475.8 106.2 %reduce-scatter.6.cloned.1.call-start = ((), (), s32[]{:S(2)}) async-start(), calls=%async_computation.7 | async-start | bytes 6635520 | tf_op jit(solution)/shard_map/g_sum/reduce_scatter | solution.py:1000
  476.4 170.6 %reduce-scatter.8.cloned.1.call-start = ((), (), s32[]{:S(2)}) async-start(), calls=%async_computation.8 | async-start | bytes 6635520 | tf_op jit(solution)/shard_map/g_sum/reduce_scatter | solution.py:1000
  585.1 67.5 %collective-permute-start.36 = (bf16[256,1152]{1,0:T(8,128)(2,1)}, bf16[256,1152]{1,0:T(8,128)(2,1)}, u32[]{:S(2)}, u32[]{:S(2)}) collective-permute-start(bf16[256,1152]{1,0:T(8,128)(2,1)} %convert_element_type.195), channel_id=1, source_target_pairs={{2,4},{3,5},{4,6},{5,7},{10,12},{11,13},{12,14},{13,15},{18,20},{1... | collective-permute-start | bytes 1769480 | tf_op jit(solution)/shard_map/d_far/ppermute | solution.py:861
  589.2 65.4 %collective-permute-start.35 = (bf16[256,1152]{1,0:T(8,128)(2,1)}, bf16[256,1152]{1,0:T(8,128)(2,1)}, u32[]{:S(2)}, u32[]{:S(2)}) collective-permute-start(bf16[256,1152]{1,0:T(8,128)(2,1)} %convert_element_type.195), channel_id=1, source_target_pairs={{0,4},{1,5},{8,12},{9,13},{16,20},{17,21},{24,28},{25,29}} | collective-permute-start | bytes 1769480 | tf_op jit(solution)/shard_map/d_near/ppermute | solution.py:861
  590.5 64.1 %collective-permute-start.38 = (bf16[288,3456]{1,0:T(8,128)(2,1)}, bf16[288,3456]{1,0:T(8,128)(2,1)}, u32[]{:S(2)}, u32[]{:S(2)}) collective-permute-start(bf16[288,3456]{1,0:T(8,128)(2,1)} %pad_maximum_fusion.6), channel_id=1, source_target_pairs={{2,4},{3,5},{4,6},{5,7},{10,12},{11,13},{12,14},{13,15},{18,20},{1... | collective-permute-start | bytes 5971976 | tf_op jit(solution)/shard_map/d_far/ppermute | solution.py:861
  592.4 62.2 %collective-permute-start.37 = (bf16[288,3456]{1,0:T(8,128)(2,1)}, bf16[288,3456]{1,0:T(8,128)(2,1)}, u32[]{:S(2)}, u32[]{:S(2)}) collective-permute-start(bf16[288,3456]{1,0:T(8,128)(2,1)} %pad_maximum_fusion.6), channel_id=1, source_target_pairs={{0,4},{1,5},{8,12},{9,13},{16,20},{17,21},{24,28},{25,29}} | collective-permute-start | bytes 5971976 | tf_op jit(solution)/shard_map/d_near/ppermute | solution.py:861
  647.0 53.0 %collective-permute-start.55 = (bf16[288,2304]{1,0:T(8,128)(2,1)}, bf16[288,2304]{1,0:T(8,128)(2,1)}, u32[]{:S(2)}, u32[]{:S(2)}) collective-permute-start(bf16[288,2304]{1,0:T(8,128)(2,1)} %reduce-scatter.8.cloned.1.call-done), channel_id=1, source_target_pairs={{2,0},{3,1},{4,2},{5,3},{10,8},{11,9},{12,10},{13,11},{18,16},{19,... | collective-permute-start | bytes 3981320 | tf_op jit(solution)/shard_map/d_far/ppermute | solution.py:861
  652.7 47.3 %collective-permute-start.54 = (bf16[288,2304]{1,0:T(8,128)(2,1)}, bf16[288,2304]{1,0:T(8,128)(2,1)}, u32[]{:S(2)}, u32[]{:S(2)}) collective-permute-start(bf16[288,2304]{1,0:T(8,128)(2,1)} %reduce-scatter.8.cloned.1.call-done), channel_id=1, source_target_pairs={{6,2},{7,3},{14,10},{15,11},{22,18},{23,19},{30,26},{31,27}} | collective-permute-start | bytes 3981320 | tf_op jit(solution)/shard_map/d_near/ppermute | solution.py:861
  725.8 40.6 %collective-permute-start.43 = (bf16[256,1152]{1,0:T(8,128)(2,1)}, bf16[256,1152]{1,0:T(8,128)(2,1)}, u32[]{:S(2)}, u32[]{:S(2)}) collective-permute-start(bf16[256,1152]{1,0:T(8,128)(2,1)} %get-tuple-element.187), channel_id=1, source_target_pairs={{2,0},{3,1},{4,2},{5,3},{10,8},{11,9},{12,10},{13,11},{18,16},{19,... | collective-permute-start | bytes 1769480 | tf_op jit(solution)/shard_map/d_far/ppermute | solution.py:861
  732.6 35.1 %collective-permute-start.42 = (bf16[256,1152]{1,0:T(8,128)(2,1)}, bf16[256,1152]{1,0:T(8,128)(2,1)}, u32[]{:S(2)}, u32[]{:S(2)}) collective-permute-start(bf16[256,1152]{1,0:T(8,128)(2,1)} %get-tuple-element.187), channel_id=1, source_target_pairs={{6,2},{7,3},{14,10},{15,11},{22,18},{23,19},{30,26},{31,27}} | collective-permute-start | bytes 1769480 | tf_op jit(solution)/shard_map/d_near/ppermute | solution.py:861
  (130 other events, 1896.8 us)
Sparse Core Ops, SparseCore 0:
  85.1 77.7 all-gather.4
  190.2 37.8 all-gather.6
  231.9 60.6 all-gather.8
  475.9 41.1 reduce-scatter.3
  520.0 62.0 reduce-scatter.5
  584.9 62.0 reduce-scatter.7

commit v3 on v2

--- a/solution.py
+++ b/solution.py
@@ -10,9 +10,8 @@
 
 LOG2E = 1.4426950408889634
 HIGHEST = lax.Precision.HIGHEST
-BIGL = 1920
-SMALL0 = 4 * BIGL
-WALL = SMALL0 + 2304
+PLANE = 7 * 256
+WALL = 8 * PLANE
 
 
 def _labels_hi_lo(lab):
@@ -22,12 +21,10 @@
     return iota == hi, jnp.where(iota == lo, 1.0, 0.0)
 
 
-def bias_kernel(out_lab_ref, lab_ref, table_ref, wall_ref):
-    lab = lab_ref[...]
-    hi_mask, lo_hot = _labels_hi_lo(lab)
-    rows = lax.dot_general(table_ref[0], lo_hot, (((1,), (0,)), ((), ())), precision=HIGHEST, preferred_element_type=jnp.float32)
+def build_wall(small, out_lab, lab, hi_mask, lo_hot, table, wall_ref):
+    rows = lax.dot_general(table, lo_hot, (((1,), (0,)), ((), ())), precision=HIGHEST, preferred_element_type=jnp.float32)
     flat = jnp.sum(jnp.where(hi_mask, rows, 0.0), axis=0, keepdims=True) * LOG2E
-    outside = jnp.sum(jnp.where(lab == out_lab_ref[0], flat, 0.0), axis=1, keepdims=True)
+    outside = jnp.sum(jnp.where(lab == out_lab, flat, 0.0), axis=1, keepdims=True)
     wide = jnp.broadcast_to(flat, (32, 4096))
     wide = pltpu.roll(wide, 4096 - 31, 1, stride=1, stride_axis=0)
     lane = lax.broadcasted_iota(jnp.int32, (32, 128), 1)
@@ -39,9 +36,6 @@
         other = jnp.where(lane < 96, pltpu.roll(b, 64, 1), pltpu.roll(b, 32, 1))
         tight.append(jnp.where(lane < 64, piece, other))
     w0 = jnp.concatenate(tight, axis=1)
-    for s in range(4):
-        shifted = w0 if s == 0 else pltpu.roll(w0, 2048 - 32 * s, 1)
-        wall_ref[0, :, s * BIGL : (s + 1) * BIGL] = shifted[:, :BIGL]
     lane16 = lane[:16]
     tight16 = []
     for g in range(8):
@@ -54,13 +48,25 @@
             acc = jnp.where(lane16 >= 64 + 16 * k, pltpu.roll(hi_v, (64 - 16 * k) % 128, 1), acc)
         tight16.append(acc)
     w16 = jnp.concatenate(tight16, axis=1)
-    for j in range(16):
-        sl = pltpu.roll(w16, 1024 - 16 * (31 - j), 1)[:, :256]
-        wall_ref[0, 16 * (j % 2) : 16 * (j % 2) + 16, SMALL0 + 256 * (j // 2) : SMALL0 + 256 * (j // 2) + 256] = sl
-    wall_ref[0, :, SMALL0 + 2048 : WALL] = jnp.broadcast_to(outside, (32, 256))
-
-
-def bias_tables(out_lab, lab, table):
+    beyond = jnp.broadcast_to(outside, (32, 768))
+    tiny = small == 1
+    for j in range(8):
+        big = w0 if j == 7 else pltpu.roll(w0, 2048 - 32 * (7 - j), 1)
+        inner = [pltpu.roll(w16, 1024 - 16 * (31 - 2 * j - k), 1)[:, :256] for k in range(2)]
+        inner = jnp.concatenate(inner, axis=0)
+        at = j * PLANE
+        wall_ref[:, at : at + 768] = jnp.where(tiny, beyond, big[:, :768])
+        wall_ref[:, at + 768 : at + 1024] = jnp.where(tiny, inner, big[:, 768:1024])
+        wall_ref[:, at + 1024 : at + PLANE] = jnp.where(tiny, beyond, big[:, 1024:PLANE])
+
+
+def bias_kernel(flags_ref, lab_ref, table_ref, wall_ref):
+    lab = lab_ref[...]
+    hi_mask, lo_hot = _labels_hi_lo(lab)
+    build_wall(flags_ref[0], flags_ref[1], lab, hi_mask, lo_hot, table_ref[0], wall_ref.at[0])
+
+
+def bias_tables(flags, lab, table):
     heads = table.shape[0]
     return pl.pallas_call(
         bias_kernel,
@@ -73,23 +79,26 @@
         out_specs=pl.BlockSpec((1, 32, WALL), lambda h: (h, 0, 0)),
         out_shape=jax.ShapeDtypeStruct((heads, 32, WALL), jnp.float32),
         compiler_params=pltpu.CompilerParams(vmem_limit_bytes=40 << 20),
-    )(out_lab, lab, table)
-
-
-def bias_grad_kernel(out_lab_ref, lab_ref, acc_ref, out_ref):
-    lab = lab_ref[...]
-    hi_mask, lo_hot = _labels_hi_lo(lab)
-    acc = acc_ref[0]
+    )(flags, lab, table)
+
+
+def wall_grad(small, out_lab, lab, hi_mask, lo_hot, acc_ref):
+    tiny = small == 1
     w0 = jnp.zeros((32, 2048), jnp.float32)
-    for s in range(4):
-        piece = jnp.concatenate([acc[:, s * BIGL : (s + 1) * BIGL], jnp.zeros((32, 128), jnp.float32)], axis=1)
-        w0 = w0 + (piece if s == 0 else pltpu.roll(piece, 32 * s, 1))
     w16 = jnp.zeros((16, 1024), jnp.float32)
-    for j in range(16):
-        piece = acc[16 * (j % 2) : 16 * (j % 2) + 16, SMALL0 + 256 * (j // 2) : SMALL0 + 256 * (j // 2) + 256]
-        piece = jnp.concatenate([piece, jnp.zeros((16, 768), jnp.float32)], axis=1)
-        w16 = w16 + pltpu.roll(piece, 16 * (31 - j), 1)
-    outside = jnp.sum(jnp.sum(acc[:, SMALL0 + 2048 : WALL], axis=0, keepdims=True), axis=1, keepdims=True)
+    beyond = jnp.zeros((32, 768), jnp.float32)
+    for j in range(8):
+        at = j * PLANE
+        piece = jnp.concatenate([acc_ref[:, at : at + PLANE], jnp.zeros((32, 256), jnp.float32)], axis=1)
+        w0 = w0 + (piece if j == 7 else pltpu.roll(piece, 32 * (7 - j), 1))
+        beyond = beyond + acc_ref[:, at + 1024 : at + PLANE]
+        for k in range(2):
+            inner = acc_ref[16 * k : 16 * k + 16, at + 768 : at + 1024]
+            inner = jnp.concatenate([inner, jnp.zeros((16, 768), jnp.float32)], axis=1)
+            w16 = w16 + pltpu.roll(inner, 16 * (31 - 2 * j - k), 1)
+    w0 = jnp.where(tiny, 0.0, w0)
+    w16 = jnp.where(tiny, w16, 0.0)
+    outside = jnp.sum(jnp.sum(jnp.where(tiny, beyond, 0.0), axis=0, keepdims=True), axis=1, keepdims=True)
     lane = lax.broadcasted_iota(jnp.int32, (32, 128), 1)
     lane16 = lane[:16]
     wide = []
@@ -110,12 +119,18 @@
     for k in range(5):
         wide = jnp.where(jnp.bitwise_and(back, 1 << k) > 0, pltpu.roll(wide, 1 << k, 1), wide)
     flat = jnp.sum(wide, axis=0, keepdims=True)
-    flat = flat + jnp.where(lab == out_lab_ref[0], outside, 0.0)
+    flat = flat + jnp.where(lab == out_lab, outside, 0.0)
     spread = jnp.where(hi_mask, jnp.broadcast_to(flat, (64, 4096)), 0.0)
-    out_ref[0] = lax.dot_general(spread, lo_hot, (((1,), (1,)), ((), ())), precision=HIGHEST, preferred_element_type=jnp.float32)
-
-
-def bias_grads(out_lab, lab, acc):
+    return lax.dot_general(spread, lo_hot, (((1,), (1,)), ((), ())), precision=HIGHEST, preferred_element_type=jnp.float32)
+
+
+def bias_grad_kernel(flags_ref, lab_ref, acc_ref, out_ref):
+    lab = lab_ref[...]
+    hi_mask, lo_hot = _labels_hi_lo(lab)
+    out_ref[0] = wall_grad(flags_ref[0], flags_ref[1], lab, hi_mask, lo_hot, acc_ref.at[0])
+
+
+def bias_grads(flags, lab, acc):
     heads = acc.shape[0]
     return pl.pallas_call(
         bias_grad_kernel,
@@ -128,7 +143,7 @@
         out_specs=pl.BlockSpec((1, 64, 64), lambda h: (h, 0, 0)),
         out_shape=jax.ShapeDtypeStruct((heads, 64, 64), jnp.float32),
         compiler_params=pltpu.CompilerParams(vmem_limit_bytes=40 << 20),
-    )(out_lab, lab, acc)
+    )(flags, lab, acc)
 
 
 def label_row(rel_index):
@@ -164,22 +179,18 @@
     return jnp.concatenate([part, pad], axis=1)
 
 
-def strip_start(t, small, q_quarter, jj, rel):
-    kq = jnp.bitwise_xor(t, rel)
-    big = BIGL * ((31 - jj) % 4) + 128 * ((31 - jj) // 4 - 2 * kq + 2 * q_quarter)
-    inner = SMALL0 + 256 * jj
-    tiny = jnp.where((kq == 0) & (q_quarter == 0), inner, SMALL0 + 2048)
-    return pl.multiple_of(jnp.where(small == 1, tiny, big), 128)
-
-
-def attn_fwd_kernel(order, scale, sc_ref, q_ref, kv_ref, mask_ref, wall_ref, o_ref, lse_ref, s_scr, p_scr):
-    t, small = sc_ref[0], sc_ref[1]
-    qq = jnp.bitwise_xor(t, sc_ref[2 + pl.program_id(0)])
+def quarter(r, c, rel):
+    return lax.rem(r + rel % 2, 2) + 2 * lax.rem(c + rel // 2, 2)
+
+
+def strip_start(q_quarter, jj, kq):
+    return pl.multiple_of(PLANE * jj + 256 * (q_quarter - kq + 3), 256)
+
+
+def attn_block(q_quarter, key_quarters, scale, q_ref, kv_ref, k_extra, wall_ref, lse_ref, s_scr, p_scr):
     heads = wall_ref.shape[0]
     width = heads * HD
-    rows = kv_ref.shape[0]
-    nstrip = rows // 32
-    k_extra = mask_ref[...]
+    nstrip = kv_ref.shape[0] // 32
     lane = lax.broadcasted_iota(jnp.int32, (QB, 128 - HD), 1)
     q_extra = jnp.where(lane == 0, 1.0, 0.0).astype(jnp.bfloat16)
     outs = []
@@ -190,7 +201,7 @@
         s_scr[h % 2] = dot(kh, qh, NT)
         top = None
         for st in range(nstrip):
-            start = strip_start(t, small, qq, st % 8, order[st // 8])
+            start = strip_start(q_quarter, st % 8, key_quarters[st // 8])
             s = s_scr[h % 2, 32 * st : 32 * st + 32] * (scale * LOG2E) + wall_ref[h, :, pl.ds(start, QB)]
             s_scr[h % 2, 32 * st : 32 * st + 32] = s
             top = s if top is None else jnp.maximum(top, s)
@@ -202,9 +213,18 @@
             total = p if total is None else total + p
         row_sum = jnp.sum(total, axis=0, keepdims=True)
         o_t = dot(vh, p_scr[h % 2], TN) * (1.0 / row_sum)
-        lse_ref[0, h : h + 1, :] = row_max + jnp.log2(row_sum)
+        lse_ref[h : h + 1, :] = row_max + jnp.log2(row_sum)
         outs.append(o_t.T[:, :HD].astype(jnp.bfloat16))
-    o_ref[...] = jnp.concatenate(outs, axis=1)
+    return jnp.concatenate(outs, axis=1)
+
+
+def attn_fwd_kernel(order, scale, sc_ref, q_ref, kv_ref, mask_ref, wall_ref, o_ref, lse_ref, s_scr, p_scr):
+    r, c = sc_ref[0], sc_ref[1]
+    qq = quarter(r, c, sc_ref[2 + pl.program_id(0)])
+    keys = [quarter(r, c, j) for j in order]
+    o_ref[...] = attn_block(
+        qq, keys, scale, q_ref, kv_ref, mask_ref[...], wall_ref, lse_ref.at[0], s_scr, p_scr
+    )
 
 
 def attn_fwd(qkv, mask_pad, wall, scalars, order, scale):
@@ -233,8 +253,9 @@
 def attn_bwd_kernel(order, scale, sc_ref, q_ref, kv_ref, do_ref, o_ref, lse_ref, mask_ref, wall_ref,
                     dqkv_ref, acc_ref, p_scr, s_scr, dq_scr, dk_scr, dv_scr):
     step = pl.program_id(0)
-    t, small = sc_ref[0], sc_ref[1]
-    qq = jnp.bitwise_xor(t, sc_ref[2 + step])
+    r, c = sc_ref[0], sc_ref[1]
+    qq = quarter(r, c, sc_ref[2 + step])
+    keys = [quarter(r, c, j) for j in order]
     heads = wall_ref.shape[0]
     width = heads * HD
     rows = kv_ref.shape[0]
@@ -262,7 +283,7 @@
             dp_t = dot(vh[256 * kb : 256 * kb + 256], doh, NT)
             for js in range(8):
                 st = 8 * kb + js
-                start = strip_start(t, small, qq, js, order[kb])
+                start = strip_start(qq, js, keys[kb])
                 s = s_t[32 * js : 32 * js + 32] * (scale * LOG2E) + wall_ref[h, :, pl.ds(start, QB)]
                 p = jnp.exp2(s - lse)
                 ds = p * (dp_t[32 * js : 32 * js + 32] - inner)
@@ -348,20 +369,40 @@
 
 
 class Links:
-    def __init__(self, send_sem, recv_sem):
+    def __init__(self, send_sem, recv_sem, bits=0):
         z, c = lax.axis_index("tensor"), lax.axis_index("section")
-        self.ids = ({"tensor": z + 1 - 2 * lax.rem(z, 2)}, {"section": 1 - c})
+        self.z, self.c = z, c
+        self.pair = z // 2
+        self.r = lax.rem(z, 2)
+        self.home = c == self.pair
+        across = z + 2 - 4 * self.pair
+        self.ids = {
+            PARTNER: {"tensor": z + 1 - 2 * self.r},
+            SIBLING: {"section": 1 - c},
+            FAR: {"tensor": across, "section": self.pair},
+            HOME: {"section": self.pair},
+        }
+        self.greet = [self.ids[PARTNER], self.ids[SIBLING]]
+        self.dp_bit = []
+        if bits:
+            d = lax.axis_index("dp")
+            for b in range(bits):
+                bit = lax.rem(d // (1 << b), 2)
+                self.dp_bit.append(bit)
+                self.ids["dp", b] = {"dp": d + (1 - 2 * bit) * (1 << b)}
+                self.greet.append(self.ids["dp", b])
+            self.greet += [{"tensor": across}, {"tensor": across, "section": 1 - c}]
         self.send_sem, self.recv_sem = send_sem, recv_sem
         self.used = 0
         self.started = []
 
     def enter(self):
         barrier = pltpu.get_barrier_semaphore()
-        for where in self.ids:
+        for where in self.greet:
             pl.semaphore_signal(barrier, inc=1, device_id=where, device_id_type=pl.DeviceIdType.MESH)
-        pl.semaphore_wait(barrier, 2)
-
-    def send(self, src, dst, to):
+        pl.semaphore_wait(barrier, len(self.greet))
+
+    def send(self, src, dst, to, cond=None):
         k = self.used
         self.used += 1
         copy = pltpu.make_async_remote_copy(
@@ -372,16 +413,120 @@
             device_id=self.ids[to],
             device_id_type=pl.DeviceIdType.MESH,
         )
-        copy.start()
-        self.started.append(copy)
+        when(cond, copy.start)
+        self.started.append((copy, cond))
         return copy
 
     def leave(self):
-        for copy in self.started:
-            copy.wait_send()
-
-
-PARTNER, SIBLING = 0, 1
+        for copy, cond in self.started:
+            when(cond, copy.wait_send)
+
+
+def when(cond, do):
+    if cond is None:
+        do()
+    else:
+        pl.when(cond)(lambda: do())
+
+
+PARTNER, SIBLING, FAR, HOME = "partner", "sibling", "far", "home"
+
+
+class Spread:
+    COPIES = 2
+
+    def __init__(self, links, layer, src, out, sem):
+        self.links, self.layer, self.src, self.out, self.sem = links, layer, src, out, sem
+
+    def start(self):
+        links = self.links
+        mine = links.c == self.layer
+        keeps = links.pair == self.layer
+        self.local = pltpu.make_async_copy(self.src, self.out, self.sem)
+        when(mine & keeps, self.local.start)
+        self.near = links.send(self.src, self.out, HOME, mine & jnp.logical_not(keeps))
+        self.far = links.send(self.src, self.out, FAR, mine)
+
+    def done(self):
+        links = self.links
+        keeps = links.pair == self.layer
+        when(links.home & keeps, self.local.wait)
+        when(links.home & jnp.logical_not(keeps), self.near.wait_recv)
+        when(jnp.logical_not(links.home), self.far.wait_recv)
+
+
+def bits_region(links, gathered, cols=None):
+    index = []
+    for b in reversed(range(len(links.dp_bit))):
+        index.append(pl.ds(0, 2) if b in gathered else links.dp_bit[b])
+    return tuple(index) + (() if cols is None else (slice(None), cols))
+
+
+class Deliver:
+    COPIES = 2
+
+    def __init__(self, links, layer, src, out, sem):
+        self.links, self.layer, self.src, self.out, self.sem = links, layer, src, out, sem
+
+    def start(self):
+        links = self.links
+        mine = links.c == self.layer
+        keeps = links.pair == self.layer
+        self.local = pltpu.make_async_copy(self.src, self.out, self.sem)
+        when(mine & keeps, self.local.start)
+        at = bits_region(links, ())
+        self.far = links.send(self.src.at[at], self.out.at[at], FAR, mine)
+        self.near = links.send(self.src, self.out, HOME, mine & jnp.logical_not(keeps))
+
+    def done(self):
+        links = self.links
+        keeps = links.pair == self.layer
+        when(links.home & keeps, self.local.wait)
+        when(links.home & jnp.logical_not(keeps), self.near.wait_recv)
+        when(jnp.logical_not(links.home), self.far.wait_recv)
+
+
+class Exchange:
+    def __init__(self, links, buf):
+        self.links, self.buf = links, buf
+        columns = buf.shape[-1]
+        cut = columns // 256 * 128
+        order = list(range(len(links.dp_bit)))
+        self.halves = [(pl.ds(0, cut), order), (pl.ds(cut, columns - cut), order[::-1])]
+        self.away = jnp.logical_not(links.home)
+        self.last = None
+
+    @staticmethod
+    def copies(bits):
+        return 2 * bits
+
+    def step(self, s):
+        self.done()
+        self.last = []
+        for cols, order in self.halves:
+            at = bits_region(self.links, order[:s], cols)
+            self.last.append(self.links.send(self.buf.at[at], self.buf.at[at], ("dp", order[s]), self.away))
+
+    def done(self):
+        for copy in self.last or ():
+            when(self.away, copy.wait_recv)
+
+
+class Part:
+    def __init__(self, links, src, dst, sem):
+        at = bits_region(links, ())
+        self.whole = pltpu.make_async_copy(src, dst, sem)
+        self.piece = pltpu.make_async_copy(src.at[at], dst.at[at], sem)
+        self.home, self.away = links.home, jnp.logical_not(links.home)
+
+    def start(self):
+        when(self.home, self.whole.start)
+        when(self.away, self.piece.start)
+        return self
+
+    def wait(self):
+        when(self.home, self.whole.wait)
+        when(self.away, self.piece.wait)
 
 
 def chunk(i, rows):
@@ -484,56 +629,95 @@
     scatter.near(i, p[:n], p[n:])
 
 
-def mid_kernel(x_ref, o_ref, ln_ref, wp_hbm, wf_hbm,
-               hid_ref, act_ref, n2_hbm, u_hbm, g_hbm, n1_hbm,
-               wp, wf, u_buf, g_buf, gat1, gat2, low1, wide1, low2, wide2, load_sem, store_sem, send_sem, recv_sem):
-    rows = x_ref.shape[0]
+def mid_kernel(bits, x_ref, o_ref, ln_ref, live_ref, cot_hbm, wp_hbm, w1_hbm, w2_hbm, own_q, own_p, own_1, own_2,
+               hid_ref, act_ref, dy_ref, n2_hbm, u_hbm, g_hbm, n1_hbm, w1_out, w2_out, next_q, next_p, next_1, next_2,
+               wp, w1, w2, got_q, got_p, got_1, got_2, cot, u_buf, g_buf, gat1, gat2, low1, wide1, low2, wide2,
+               load_sem, store_sem, send_sem, recv_sem):
+    rows, width = x_ref.shape
     n = rows // NCH
-    hidden = wf.shape[1] // 2
-    loads = [start_load(wp_hbm, wp, load_sem.at[0]), start_load(wf_hbm, wf, load_sem.at[1])]
-    links = Links(send_sem, recv_sem)
+    links = Links(send_sem, recv_sem, bits)
+    load_p = start_load(wp_hbm, wp, load_sem.at[0])
+    load_1 = Part(links, w1_hbm, w1, load_sem.at[1]).start()
+    load_2 = Part(links, w2_hbm, w2, load_sem.at[2]).start()
+    own_cot = pltpu.make_async_copy(cot_hbm.at[links.pair], cot, load_sem.at[3])
+    when(links.home, own_cot.start)
     links.enter()
+    ex1, ex2 = Exchange(links, w1), Exchange(links, w2)
+    got = (got_q, got_p, got_1, got_2)
+    delivers = [
+        Deliver(links, 1, src, dst, load_sem.at[4 + k]) for k, (src, dst) in enumerate(zip((own_q, own_p, own_1, own_2), got))
+    ]
     s1, s2 = Scatter(links, low1, wide1), Scatter(links, low2, wide2)
     g1, g2 = Gather(links, gat1), Gather(links, gat2)
-    loads[0].wait()
+    load_p.wait()
     for i in range(NCH):
         scatter_product(s1, i, lambda b: block_rows(o_ref, b, i, rows), wp[...], rows)
+    load_1.wait()
+    ex1.step(0)
+    load_2.wait()
+    ex2.step(0)
     for i in range(NCH):
         s1.middle(i)
-    for i in range(NCH):
-        h = x_ref[chunk(i, rows)] + s1.done(i)
+    for s in range(1, bits):
+        ex1.step(s)
+    for i in range(NCH):
+        h = x_ref[chunk(i, rows)].astype(jnp.float32) + s1.done(i)
         hid_ref[chunk(i, rows)] = h
         g1.send(i, (normed(h)[0] * ln_ref[0:1] + ln_ref[1:2]).astype(jnp.bfloat16))
-    loads[1].wait()
+        if i == 0:
+            for s in range(1, bits):
+                ex2.step(s)
+    for deliver in delivers:
+        deliver.start()
+    far_cot = links.send(cot_hbm.at[1 - links.pair], cot, FAR, links.home)
 
     def mlp(i):
-        u = dot(g1.done(i), wf[:, :hidden], NN)
+        u = dot(g1.done(i), w1[...].reshape(width, -1), NN)
         put_rows(u_buf, u.astype(jnp.bfloat16), i, rows)
         g = gelu_both(u)[0].astype(jnp.bfloat16)
         put_rows(g_buf, g, i, rows)
-        scatter_product(s2, i, lambda b: g[b * n : (b + 1) * n], wf[:, hidden:], rows)
+        if i == 0:
+            ex2.done()
+        scatter_product(s2, i, lambda b: g[b * n : (b + 1) * n], w2[...].reshape(width, -1), rows)
 
     g1.forward(0)
+    ex1.done()
     mlp(0)
     g1.forward(1)
     s2.middle(0)
     mlp(1)
     s2.middle(1)
     stores = [
-        start_load(gat1, n2_hbm, store_sem.at[0]),
-        start_load(u_buf, u_hbm, store_sem.at[1]),
-        start_load(g_buf, g_hbm, store_sem.at[2]),
+        start_load(src, dst, store_sem.at[k])
+        for k, (src, dst) in enumerate(((gat1, n2_hbm), (u_buf, u_hbm), (g_buf, g_hbm), (w1, w1_out), (w2, w2_out)))
     ]
+    exq, exp = Exchange(links, got_q), Exchange(links, got_p)
     for i in range(NCH):
         act = (hid_ref[chunk(i, rows)] + s2.done(i)).astype(jnp.bfloat16)
         act_ref[chunk(i, rows)] = act
         g2.send(i, (normed(act.astype(jnp.float32))[0] * ln_ref[2:3] + ln_ref[3:4]).astype(jnp.bfloat16))
+    delivers[0].done()
+    exq.step(0)
+    delivers[1].done()
+    exp.step(0)
     for i in range(NCH):
         g2.forward(i)
+    for s in range(1, bits):
+        exq.step(s)
+        exp.step(s)
     for i in range(NCH):
         g2.copies["s", i].wait_recv()
         g2.copies["f", i].wait_recv()
-    stores.append(start_load(gat2, n1_hbm, store_sem.at[3]))
+    stores.append(start_load(gat2, n1_hbm, store_sem.at[5]))
+    for k, (ex, buf, dst) in enumerate(((exq, got_q, next_q), (exp, got_p, next_p))):
+        ex.done()
+        stores.append(start_load(buf, dst, store_sem.at[6 + k]))
+    for k, (buf, dst) in enumerate(((got_1, next_1), (got_2, next_2))):
+        delivers[2 + k].done()
+        stores.append(Part(links, buf, dst, store_sem.at[8 + k]).start())
+    when(links.home, own_cot.wait)
+    when(jnp.logical_not(links.home), far_cot.wait_recv)
+    dy_ref[...] = cot[...].astype(jnp.float32) * live_ref[...]
     links.leave()
     for store in stores:
         store.wait()
@@ -555,81 +739,98 @@
     return pltpu.CompilerParams(collective_id=ident, has_side_effects=True, vmem_limit_bytes=60 << 20)
 
 
-def mid_chain(x, o, ln, wp, wf):
+def mid_chain(x, o, ln, live, cot, wp, w1, w2, own):
     rows, width = x.shape
-    hidden = wf.shape[1] // 2
+    hidden = w1.shape[-1]
+    bits = w1.ndim - 2
     bf16, f32 = jnp.bfloat16, jnp.float32
     out = jax.ShapeDtypeStruct
     res = pl.pallas_call(
-        mid_kernel,
-        in_specs=[VM, VM, VM, HB, HB],
-        out_specs=[VM, VM, HB, HB, HB, HB],
+        functools.partial(mid_kernel, bits),
+        in_specs=[VM] * 4 + [HB] * 8,
+        out_specs=[VM] * 3 + [HB] * 10,
         out_shape=[
             out((rows, width), f32),
             out((rows, width), bf16),
+            out((rows, width), f32),
             out((4, rows, width), bf16),
             out((4 * rows, hidden), bf16),
             out((4 * rows, hidden), bf16),
             out((4, rows, width), bf16),
-        ],
+        ]
+        + [out(w.shape, bf16) for w in (w1, w2, *own)],
         scratch_shapes=[
-            pltpu.VMEM(wp.shape, bf16),
-            pltpu.VMEM(wf.shape, bf16),
+            *[pltpu.VMEM(w.shape, bf16) for w in (wp, w1, w2, *own)],
+            pltpu.VMEM((rows, width), bf16),
             pltpu.VMEM((4 * rows, hidden), bf16),
             pltpu.VMEM((4 * rows, hidden), bf16),
             pltpu.VMEM((4, rows, width), bf16),
             pltpu.VMEM((4, rows, width), bf16),
             *scatter_scratch(rows, width),
             *scatter_scratch(rows, width),
-            pltpu.SemaphoreType.DMA((2,)),
-            pltpu.SemaphoreType.DMA((4,)),
-            *comm_scratch(2 * Scatter.COPIES + 2 * Gather.COPIES),
+            pltpu.SemaphoreType.DMA((8,)),
+            pltpu.SemaphoreType.DMA((10,)),
+            *comm_scratch(
+                2 * Scatter.COPIES + 2 * Gather.COPIES + 4 * Deliver.COPIES + 4 * Exchange.copies(bits) + 1
+            ),
         ],
         compiler_params=params(1),
         cost_estimate=pl.CostEstimate(flops=60 << 30, bytes_accessed=24 << 20, transcendentals=0),
-    )(x, o, ln, wp, wf)
-    hid, act, n2, u, g, n1 = res
-    return hid, act, n2.reshape(4 * rows, width), u, g, n1.reshape(4 * rows, width)
-
-
-def turn_kernel(x_ref, o_ref, dy_ref, ln_ref, dm_hbm, wp_hbm, wf_hbm,
+    )(x, o, ln, live, cot, wp, w1, w2, *own)
+    hid, act, dy, n2, u, g, n1 = res[:7]
+    return hid, act, dy, n2.reshape(4 * rows, width), u, g, n1.reshape(4 * rows, width), res[7:9], res[9:]
+
+
+def turn_kernel(bits, x_ref, o_ref, dy_ref, ln_ref, dm_hbm, wp_hbm, w1_hbm, w2_hbm,
                 dh_ref, norm_ref, y_hbm, hid_ref, do_ref, da_hbm, gfc_hbm,
-                wp, wf, dm, g_buf, du_buf, y_buf, gfc, gat1, gat2, low1, wide1, low2, wide2,
+                wp, w1, w2, dm, g_buf, du_buf, y_buf, gfc, gat1, gat2, low1, wide1, low2, wide2,
                 load_sem, store_sem, send_sem, recv_sem):
-    rows = x_ref.shape[0]
+    rows, width = x_ref.shape
     n = rows // NCH
-    hidden = wf.shape[1] // 2
+    hidden = w1.shape[-1]
+    links = Links(send_sem, recv_sem, bits)
     loads = [
         start_load(wp_hbm, wp, load_sem.at[0]),
-        start_load(wf_hbm, wf, load_sem.at[1]),
-        start_load(dm_hbm, dm, load_sem.at[2]),
+        Part(links, w1_hbm, w1, load_sem.at[1]).start(),
+        Part(links, w2_hbm, w2, load_sem.at[2]).start(),
+        start_load(dm_hbm, dm, load_sem.at[3]),
     ]
-    links = Links(send_sem, recv_sem)
     links.enter()
+    ex1, ex2 = Exchange(links, w1), Exchange(links, w2)
     s1, s2 = Scatter(links, low1, wide1), Scatter(links, low2, wide2)
     g1, g2 = Gather(links, gat1), Gather(links, gat2)
     loads[0].wait()
     for i in range(NCH):
         scatter_product(s1, i, lambda b: block_rows(o_ref, b, i, rows), wp[...], rows)
+    loads[1].wait()
+    ex1.step(0)
+    loads[2].wait()
+    ex2.step(0)
     for i in range(NCH):
         s1.middle(i)
+    for s in range(1, bits):
+        ex1.step(s)
     for i in range(NCH):
         h = x_ref[chunk(i, rows)].astype(jnp.float32) + s1.done(i)
         hid_ref[chunk(i, rows)] = h
         g1.send(i, (normed(h)[0] * ln_ref[0:1] + ln_ref[1:2]).astype(jnp.bfloat16))
-    loads[1].wait()
-    loads[2].wait()
+        if i == 0:
+            for s in range(1, bits):
+                ex2.step(s)
+    loads[3].wait()
 
     def mlp(i):
-        u = dot(g1.done(i), wf[:, :hidden], NN)
+        u = dot(g1.done(i), w1[...].reshape(width, -1), NN)
         g, slope = gelu_both(u)
         put_rows(g_buf, g.astype(jnp.bfloat16), i, rows)
         dmi = jnp.concatenate([block_rows(dm, b, i, rows) for b in range(4)], axis=0)
-        du = (dot(dmi, wf[:, hidden:], NN) * slope).astype(jnp.bfloat16)
+        du = (dot(dmi, w2[...].reshape(width, -1), NN) * slope).astype(jnp.bfloat16)
         put_rows(du_buf, du, i, rows)
-        scatter_product(s2, i, lambda b: du[b * n : (b + 1) * n], wf[:, :hidden], rows)
+        scatter_product(s2, i, lambda b: du[b * n : (b + 1) * n], w1[...].reshape(width, -1), rows)
 
     g1.forward(0)
+    ex1.done()
+    ex2.done()
     mlp(0)
     g1.forward(1)
     s2.middle(0)
@@ -649,7 +850,7 @@
     weight_grad(gfc, 0, flat(gat1), du_buf[...])
     stores = [start_load(gfc, gfc_hbm, store_sem.at[0])]
     for b in range(4):
-        y_buf[pl.ds(b * rows, rows)] = dot(g_buf[pl.ds(b * rows, rows)], wf[:, hidden:], NT).astype(jnp.bfloat16)
+        y_buf[pl.ds(b * rows, rows)] = dot(g_buf[pl.ds(b * rows, rows)], w2[...].reshape(width, -1), NT).astype(jnp.bfloat16)
     stores.append(start_load(y_buf, y_hbm, store_sem.at[1]))
     for i in range(NCH):
         g2.forward(i)
@@ -660,15 +861,16 @@
         store.wait()
 
 
-def turn_chain(x, o, dy, ln, dm, wp, wf):
+def turn_chain(x, o, dy, ln, dm, wp, w1, w2):
     rows, width = x.shape
-    hidden = wf.shape[1] // 2
+    hidden = w1.shape[-1]
+    bits = w1.ndim - 2
     lw = wp.shape[1]
     bf16, f32 = jnp.bfloat16, jnp.float32
     out = jax.ShapeDtypeStruct
     res = pl.pallas_call(
-        turn_kernel,
-        in_specs=[VM, VM, VM, VM, HB, HB, HB],
+        functools.partial(turn_kernel, bits),
+        in_specs=[VM, VM, VM, VM, HB, HB, HB, HB],
         out_specs=[VM, VM, HB, VM, VM, HB, HB],
         out_shape=[
             out((rows, width), f32),
@@ -681,7 +883,8 @@
         ],
         scratch_shapes=[
             pltpu.VMEM(wp.shape, bf16),
-            pltpu.VMEM(wf.shape, bf16),
+            pltpu.VMEM(w1.shape, bf16),
+            pltpu.VMEM(w2.shape, bf16),
             pltpu.VMEM((4 * rows, width), bf16),
             pltpu.VMEM((4 * rows, hidden), bf16),
             pltpu.VMEM((4 * rows, hidden), bf16),
@@ -691,28 +894,28 @@
             pltpu.VMEM((4, rows, width), bf16),
             *scatter_scratch(rows, width),
             *scatter_scratch(rows, width),
+            pltpu.SemaphoreType.DMA((4,)),
             pltpu.SemaphoreType.DMA((3,)),
-            pltpu.SemaphoreType.DMA((3,)),
-            *comm_scratch(2 * Scatter.COPIES + 2 * Gather.COPIES),
+            *comm_scratch(2 * Scatter.COPIES + 2 * Gather.COPIES + 2 * Exchange.copies(bits)),
         ],
         compiler_params=params(2),
         cost_estimate=pl.CostEstimate(flops=60 << 30, bytes_accessed=24 << 20, transcendentals=0),
-    )(x, o, dy, ln, dm, wp, wf)
+    )(x, o, dy, ln, dm, wp, w1, w2)
     dh, norms, y, hid, do, da, gfc = res
     return dh, norms, y, hid, do, da.reshape(4 * rows, width), gfc
 
 
-def back_kernel(x_ref, dh1_ref, hid_ref, ln_ref, dqkv_ref, wq_hbm, wp_hbm, wf_hbm, u_hbm, g_hbm, n2_hbm,
+def back_kernel(x_ref, dh1_ref, hid_ref, ln_ref, dqkv_ref, wq_hbm, wp_hbm, w1_hbm, w2_hbm, u_hbm, g_hbm, n2_hbm,
                 gin_ref, dh_ref, norm_ref, do_ref, da_hbm, gfc_hbm,
-                wq, wp, wf, u_buf, g_buf, n2, du_buf, gfc, gat1, gat2, low1, wide1, low2, wide2,
+                wq, wp, w1, w2, u_buf, g_buf, n2, du_buf, gfc, gat1, gat2, low1, wide1, low2, wide2,
                 load_sem, store_sem, send_sem, recv_sem):
     rows = x_ref.shape[0]
     n = rows // NCH
-    hidden = wf.shape[1] // 2
+    hidden = w1.shape[1]
     loads = [
         start_load(src, dst, load_sem.at[k])
         for k, (src, dst) in enumerate(
-            ((wq_hbm, wq), (wf_hbm, wf), (u_hbm, u_buf), (g_hbm, g_buf), (n2_hbm, n2), (wp_hbm, wp))
+            ((wq_hbm, wq), (w1_hbm, w1), (w2_hbm, w2), (u_hbm, u_buf), (g_hbm, g_buf), (n2_hbm, n2), (wp_hbm, wp))
         )
     ]
     links = Links(send_sem, recv_sem)
@@ -740,9 +943,9 @@
     def mlp(i):
         dmi = g1.done(i)
         ui = jnp.concatenate([block_rows(u_buf, b, i, rows) for b in range(4)], axis=0).astype(jnp.float32)
-        du = (dot(dmi, wf[:, hidden:], NN) * gelu_both(ui)[1]).astype(jnp.bfloat16)
+        du = (dot(dmi, w2[...], NN) * gelu_both(ui)[1]).astype(jnp.bfloat16)
         put_rows(du_buf, du, i, rows)
-        scatter_product(s2, i, lambda b: du[b * n : (b + 1) * n], wf[:, :hidden], rows)
+        scatter_product(s2, i, lambda b: du[b * n : (b + 1) * n], w1[...], rows)
 
     g1.forward(0)
     mlp(0)
@@ -772,15 +975,15 @@
         store.wait()
 
 
-def back_chain(x, dh1, hid, ln, dqkv, wq, wp, wf, u, g, n2):
+def back_chain(x, dh1, hid, ln, dqkv, wq, wp, w1, w2, u, g, n2):
     rows, width = x.shape
-    hidden = wf.shape[1] // 2
+    hidden = w1.shape[1]
     lw = wp.shape[1]
     bf16, f32 = jnp.bfloat16, jnp.float32
     out = jax.ShapeDtypeStruct
     res = pl.pallas_call(
         back_kernel,
-        in_specs=[VM] * 5 + [HB] * 6,
+        in_specs=[VM] * 5 + [HB] * 7,
         out_specs=[VM, VM, VM, VM, HB, HB],
         out_shape=[
             out((rows, width), f32),
@@ -793,7 +996,8 @@
         scratch_shapes=[
             pltpu.VMEM(wq.shape, bf16),
             pltpu.VMEM(wp.shape, bf16),
-            pltpu.VMEM(wf.shape, bf16),
+            pltpu.VMEM(w1.shape, bf16),
+            pltpu.VMEM(w2.shape, bf16),
             pltpu.VMEM((4 * rows, hidden), bf16),
             pltpu.VMEM((4 * rows, hidden), bf16),
             pltpu.VMEM((4 * rows, width), bf16),
@@ -803,15 +1007,150 @@
             pltpu.VMEM((4, rows, width), bf16),
             *scatter_scratch(rows, width),
             *scatter_scratch(rows, width),
-            pltpu.SemaphoreType.DMA((6,)),
+            pltpu.SemaphoreType.DMA((7,)),
             pltpu.SemaphoreType.DMA((2,)),
             *comm_scratch(2 * Scatter.COPIES + 2 * Gather.COPIES),
         ],
         compiler_params=params(3),
         cost_estimate=pl.CostEstimate(flops=60 << 30, bytes_accessed=24 << 20, transcendentals=0),
-    )(x, dh1, hid, ln, dqkv, wq, wp, wf, u, g, n2)
+    )(x, dh1, hid, ln, dqkv, wq, wp, w1, w2, u, g, n2)
     gin, dh, norms, do, da, gfc = res
     return gin, dh, norms, do, da.reshape(4 * rows, width), gfc
+
+
+def start_kernel(order, scale, bits, flags_ref, x_hbm, mask_ref, lab_ref, tab_hbm, pack_hbm,
+                 wq_hbm, wp_hbm, w1_hbm, w2_hbm,
+                 x_ref, pack_ref, lse_ref, o_ref, n1_hbm, qkv_hbm, wall0_hbm, wall1_hbm,
+                 wq0_hbm, wp0_hbm, w10_hbm, w20_hbm,
+                 tab, wq, wp, w1, w2, qkv, wall, gat1, s_scr, p_scr, load_sem, store_sem, send_sem, recv_sem):
+    small, out_lab = flags_ref[0], flags_ref[1]
+    rows, width = x_ref.shape
+    wide = qkv.shape[1]
+    heads = wall.shape[1]
+    links = Links(send_sem, recv_sem, bits)
+    pair, home = links.pair, links.home
+    own_x = pltpu.make_async_copy(x_hbm.at[pair], x_ref, load_sem.at[0])
+    when(home, own_x.start)
+    links.enter()
+    far_x = links.send(x_hbm.at[1 - pair], x_ref, FAR, home)
+    packs = [Spread(links, l, pack_hbm, pack_ref.at[l], load_sem.at[1 + l]) for l in range(2)]
+    tabs = [Spread(links, l, tab_hbm, tab.at[l], load_sem.at[3 + l]) for l in range(2)]
+    for spread in packs + tabs:
+        spread.start()
+    get_q = Deliver(links, 0, wq_hbm, wq, load_sem.at[5])
+    get_p = Deliver(links, 0, wp_hbm, wp, load_sem.at[6])
+    get_1 = Deliver(links, 0, w1_hbm, w1, load_sem.at[7])
+    get_2 = Deliver(links, 0, w2_hbm, w2, load_sem.at[8])
+    ex_q, ex_p = Exchange(links, wq), Exchange(links, wp)
+    get_q.start()
+    packs[0].done()
+    when(home, own_x.wait)
+    when(jnp.logical_not(home), far_x.wait_recv)
+    g1 = Gather(links, gat1)
+    for i in range(NCH):
+        at = chunk(i, rows)
+        xhat = normed(x_ref[at].astype(jnp.float32))[0]
+        g1.send(i, (xhat * pack_ref[0, 0:1] + pack_ref[0, 2:3]).astype(jnp.bfloat16))
+    get_p.start()
+    get_1.start()
+    get_2.start()
+    lab = lab_ref[...]
+    hi_mask, lo_hot = _labels_hi_lo(lab)
+
+    def build(l):
+        def one(h, carry):
+            build_wall(small, out_lab, lab, hi_mask, lo_hot, tab[l, h], wall.at[l, h])
+            return carry
+
+        lax.fori_loop(0, heads, one, 0)
+
+    tabs[0].done()
+    build(0)
+    stores = [start_load(wall.at[0], wall0_hbm, store_sem.at[0])]
+    get_q.done()
+    ex_q.step(0)
+    for i in range(NCH):
+        g1.forward(i)
+    for s in range(1, bits):
+        ex_q.step(s)
+    for i in range(NCH):
+        g1.copies["s", i].wait_recv()
+        g1.copies["f", i].wait_recv()
+    stores.append(start_load(gat1, n1_hbm, store_sem.at[1]))
+    packs[1].done()
+    get_p.done()
+    ex_q.done()
+    ex_p.step(0)
+    stores.append(start_load(wq, wq0_hbm, store_sem.at[2]))
+    term = pack_ref[0, pl.ds(4 + pair, 1)][:, :wide]
+    weight = wq[...].reshape(width, wide)
+    for b in range(4):
+        qkv[pl.ds(b * rows, rows)] = (dot(gat1[b], weight, NN) + term).astype(jnp.bfloat16)
+    stores.append(start_load(qkv, qkv_hbm, store_sem.at[3]))
+    for s in range(1, bits):
+        ex_p.step(s)
+    keys = [quarter(links.r, links.c, j) for j in order]
+
+    def block(i, carry):
+        at = pl.ds(pl.multiple_of(i * QB, QB), QB)
+        qq = lax.rem(links.r + i // 2, 2) + 2 * lax.rem(links.c + lax.rem(i, 2), 2)
+        o_ref[at] = attn_block(
+            qq, keys, scale, qkv.at[at], qkv, mask_ref[...], wall.at[0], lse_ref.at[i], s_scr, p_scr
+        )
+        return carry
+
+    lax.fori_loop(0, 4, block, 0)
+    ex_p.done()
+    stores.append(start_load(wp, wp0_hbm, store_sem.at[4]))
+    tabs[1].done()
+    build(1)
+    stores.append(start_load(wall.at[1], wall1_hbm, store_sem.at[5]))
+    for k, (get, src, dst) in enumerate(((get_1, w1, w10_hbm), (get_2, w2, w20_hbm))):
+        get.done()
+        stores.append(Part(links, src, dst, store_sem.at[6 + k]).start())
+    links.leave()
+    for store in stores:
+        store.wait()
+
+
+def start_chain(flags, x, mask_pad, lab, table, pack, wq, wp, w1, w2, order, scale):
+    bits = wq.ndim - 2
+    _, rows, width = x.shape
+    heads = table.shape[0]
+    wide = wq.shape[-1]
+    bf16, f32 = jnp.bfloat16, jnp.float32
+    out = jax.ShapeDtypeStruct
+    copies = 1 + 4 * Spread.COPIES + 4 * Deliver.COPIES + 2 * Exchange.copies(bits) + Gather.COPIES
+    return pl.pallas_call(
+        functools.partial(start_kernel, order, scale, bits),
+        in_specs=[pl.BlockSpec(memory_space=pltpu.SMEM), HB, VM, VM, HB, HB, HB, HB, HB, HB],
+        out_specs=[VM] * 4 + [HB] * 8,
+        out_shape=[
+            out((rows, width), bf16),
+            out((2,) + pack.shape, f32),
+            out((4, heads, QB), f32),
+            out((4 * rows, heads * HD), bf16),
+            out((4, rows, width), bf16),
+            out((4 * rows, wide), bf16),
+            out((heads, 32, WALL), f32),
+            out((heads, 32, WALL), f32),
+            *[out(w.shape, bf16) for w in (wq, wp, w1, w2)],
+        ],
+        scratch_shapes=[
+            pltpu.VMEM((2,) + table.shape, f32),
+            *[pltpu.VMEM(w.shape, bf16) for w in (wq, wp, w1, w2)],
+            pltpu.VMEM((4 * rows, wide), bf16),
+            pltpu.VMEM((2, heads, 32, WALL), f32),
+            pltpu.VMEM((4, rows, width), bf16),
+            pltpu.VMEM((2, 4 * rows, QB), f32),
+            pltpu.VMEM((2, 4 * rows, QB), bf16),
+            pltpu.SemaphoreType.DMA((9,)),
+            pltpu.SemaphoreType.DMA((8,)),
+            *comm_scratch(copies),
+        ],
+        compiler_params=params(0),
+        cost_estimate=pl.CostEstimate(flops=80 << 30, bytes_accessed=24 << 20, transcendentals=0),
+    )(flags, x, mask_pad, lab, table, pack, wq, wp, w1, w2)
 
 
 AXES = ("dp", "section", "tensor")
@@ -869,25 +1208,6 @@
     def across(x):
         return move(x, lambda dd, cc, zz: (dd, cc, zz ^ 2), "across")
 
-    def fetch(x):
-        rem = across(x)
-        keep = jnp.where(home, x, rem)
-        recv = sibling(jnp.where(home, rem, x))
-        return jnp.where(first, keep, recv), jnp.where(first, recv, keep)
-
-    def dp_gather(piece):
-        if ndp != 4:
-            return lax.all_gather(piece, "dp", axis=0, tiled=True)
-        n = piece.shape[0]
-        p1 = move(piece, lambda dd, cc, zz: (dd ^ 1, cc, zz), "w_x")
-        p2 = move(piece, lambda dd, cc, zz: (dd ^ 2, cc, zz), "w_y")
-        p3a = move(p2[: n // 2], lambda dd, cc, zz: (dd ^ 1, cc, zz), "w_yx")
-        p3b = move(p1[n // 2 :], lambda dd, cc, zz: (dd ^ 2, cc, zz), "w_xy")
-        out = jnp.zeros((ndp * n, piece.shape[1]), piece.dtype)
-        for part, at in ((piece, d * n), (p1, (d ^ 1) * n), (p2, (d ^ 2) * n), (p3a, (d ^ 3) * n), (p3b, (d ^ 3) * n + n // 2)):
-            out = lax.dynamic_update_slice_in_dim(out, part, at, 0)
-        return out
-
     def dp_scatter(x, bits):
         n = x.shape[1]
         left = sorted(bits, reverse=True)
@@ -904,73 +1224,22 @@
                 v = v.astype(bf16)
         return v
 
-    def piece_of(w, layer):
-        part = w.shape[0] // ndp
-        src = lax.dynamic_slice_in_dim(w, d * part, part, 0)
-        far = move(src, lambda dd, cc, zz: (dd, 1 - (zz ^ 2) // 2, zz ^ 2) if cc == layer else None, "w_far")
-        near = move(src, lambda dd, cc, zz: (dd, zz // 2, zz) if cc == layer else None, "w_near")
-        return jnp.where(home, near, far)
-
+    def by_bits(w):
+        return w.reshape(2, 2, -1, w.shape[-1])
+
+    table = jnp.pad(rel_table[0], ((0, 0), (0, 4096 - buckets))).reshape(heads, 64, 64)
     time_all = jnp.einsum("id,dcn->icn", time_emb, w_time[0], preferred_element_type=f32)
-    table = jnp.pad(rel_table[0], ((0, 0), (0, 4096 - buckets)))
-    small_pack = jnp.concatenate(
-        [
-            table.reshape(-1, 128),
-            time_all.reshape(-1, 128),
-            norm_gains[0].reshape(-1, 128),
-            norm_biases[0].reshape(-1, 128),
-        ],
-        axis=0,
-    )
-    cuts = []
-    at = 0
-    for n in (heads * 32, time_all.size // 128, 2 * width // 128, 2 * width // 128):
-        cuts.append((at, at + n))
-        at += n
-    packs = fetch(small_pack)
-    def home_rows(x):
-        other = lax.dynamic_index_in_dim(x, 1 - pair, 0, keepdims=False)
-        got = move(other, lambda dd, cc, zz: (dd, cc, zz ^ 2) if cc == zz // 2 else None, "x_rows")
-        return jnp.where(home, lax.dynamic_index_in_dim(x, pair, 0, keepdims=False), got)
-
-    def after(x, *first_things):
-        return lax.optimization_barrier((x,) + first_things)[0]
-
-    x0 = home_rows(inputs).astype(f32)
-    own_qp = (w_qkv[0].reshape(width, 3 * local_width), w_proj[0])
-    own_fc = jnp.concatenate([w_fc1[0], w_fc2[0]], axis=1)
-    piece_q0 = piece_of(own_qp[0], 0)
-    piece_p0 = piece_of(after(own_qp[1], piece_q0), 0)
-    piece_f0 = piece_of(after(own_fc, piece_p0), 0)
-    piece_qp1 = piece_of(after(jnp.concatenate(own_qp, axis=1), piece_f0), 1)
-    piece_f1 = piece_of(after(own_fc, piece_qp1), 1)
-    hidden_units = w_fc1.shape[2]
-
-    def sc_gather(piece):
-        return lax.all_gather(piece, "dp", axis=0, tiled=True)
-
-    fc = [sc_gather(piece_f0)]
-    qp1 = sc_gather(after(piece_qp1, fc[0]))
-    fc.append(sc_gather(after(piece_f1, qp1)))
-    weights_qkv = (dp_gather(piece_q0), qp1[:, : 3 * local_width])
-    weights_proj = (dp_gather(piece_p0), qp1[:, 3 * local_width :])
-    weights_fc = fc
-
+    gap = jnp.zeros((2, local_width), f32)
+    time_rows = jnp.concatenate([time_all[:, 0], gap, time_all[:, 1], gap], axis=1)
+    small_pack = jnp.concatenate([norm_gains[0], norm_biases[0], time_rows, jnp.zeros((2, width), f32)], axis=0)
+    own = [by_bits(w) for w in (jnp.concatenate([w_qkv[0, :, j] for j in range(3)], axis=1), w_proj[0], w_fc1[0], w_fc2[0])]
     label_lanes = label_row(rel_index)
     out_label = rel_index[1, seq_len - 1, seq_len - 1].reshape(1)
-    walls, time_terms, gains, shifts = [], [], [], []
-    for pack in packs:
-        pieces = [pack[a:b] for a, b in cuts]
-        walls.append(bias_tables(out_label, label_lanes, pieces[0].reshape(heads, 64, 64)))
-        both = pieces[1].reshape(2, 2, local_width)
-        mine = lax.dynamic_index_in_dim(both, pair, 0, keepdims=False)
-        time_terms.append(jnp.concatenate([mine[0], jnp.zeros((local_width,), f32), mine[1]]))
-        gains.append(pieces[2].reshape(2, width))
-        shifts.append(pieces[3].reshape(2, width))
 
     length = lax.dynamic_index_in_dim(lengths, pair, 0, keepdims=False)
     small = (length < seq_len).astype(jnp.int32)
-    scalars = jnp.stack([t, small] + [jnp.int32(j) for j in ORDER])
+    scalars = jnp.stack([z % 2, c] + [jnp.int32(j) for j in ORDER])
+    flags = jnp.concatenate([small.reshape(1), out_label])
     mask = lax.dynamic_index_in_dim(key_mask, pair, 0, keepdims=False).reshape(4, rows)
     mask = jnp.concatenate([lax.dynamic_index_in_dim(mask, t ^ j, 0, keepdims=False) for j in ORDER])
     lane = jnp.arange(128 - HD)[None, :]
@@ -1008,9 +1277,6 @@
             [dp_scatter(x[:, :cut], bits), dp_scatter(x[:, cut:], bits[::-1])], axis=1
         ).astype(bf16)
 
-    def scores_in(n1, layer):
-        return (jnp.dot(n1, weights_qkv[layer], preferred_element_type=f32) + time_terms[layer]).astype(bf16)
-
     def column_sums(dqkv):
         sums = jnp.sum(dqkv.astype(f32), axis=0)
         return jnp.concatenate([sums[:local_width], sums[2 * local_width :]])
@@ -1027,25 +1293,34 @@
     def far_of(x, layer):
         return move(x, lambda dd, cc, zz: (dd, layer, zz ^ 2) if cc != zz // 2 else None, "d_far")
 
-    live = (t * rows + jnp.arange(rows)) < length
-
-    n1_0 = gather_rows((normed(x0)[0] * gains[0][0] + shifts[0][0]).astype(bf16))
-    qkv0 = scores_in(n1_0, 0)
-    qkv0, cotangent = tie(qkv0, cotangent)
-    cot = home_rows(cotangent)
-    o0, lse0 = attn_fwd(qkv0, mask_pad, walls[0], scalars, ORDER, scale)
-    o0, cot = tie(o0, cot)
+    live = ((t * rows + jnp.arange(rows)) < length).astype(f32)[:, None]
+    res = start_chain(flags, inputs, mask_pad, label_lanes, table, small_pack, *own, ORDER, scale)
+    x0, packs, lse0, o0, n1_0, qkv0 = res[:6]
+    walls, weights0 = res[6:8], res[8:]
+    n1_0 = n1_0.reshape(seq_len, width)
+
+    def whole(w):
+        return w.reshape(width, w.shape[-1])
+
+    gains = [packs[l, 0:2] for l in range(2)]
+    shifts = [packs[l, 2:4] for l in range(2)]
     ln_mid = jnp.stack([gains[0][1], shifts[0][1], gains[1][0], shifts[1][0]])
-    hid0, act0, n2_0, u0, g0, n1_1 = mid_chain(x0, o0, ln_mid, weights_proj[0], weights_fc[0])
-    qkv1 = scores_in(n1_1, 1)
-    dy1 = cot.astype(f32) * live.astype(f32)[:, None]
+    wq0, wp0 = whole(weights0[0]), whole(weights0[1])
+    hid0, act0, dy1, n2_0, u0, g0, n1_1, weights0, weights1 = mid_chain(
+        x0, o0, ln_mid, live, cotangent, wp0, weights0[2], weights0[3], own
+    )
+    w10, w20 = whole(weights0[0]), whole(weights0[1])
+    wq1, wp1 = whole(weights1[0]), whole(weights1[1])
+    term1 = lax.dynamic_index_in_dim(packs[1], 4 + pair, 0, keepdims=False)[: 3 * local_width]
+    qkv1 = (jnp.dot(n1_1, wq1, preferred_element_type=f32) + term1).astype(bf16)
     qkv1, dm1 = tie(qkv1, dy1.astype(bf16))
-    dm1 = gather_rows(dm1)
+    dm_far, dm_near = partner(dm1), sibling(dm1)
     o1, lse1 = attn_fwd(qkv1, mask_pad, walls[1], scalars, ORDER, scale)
-    o1, dm1 = tie(o1, dm1)
+    o1, dm1, dm_far, dm_near = tie(o1, dm1, dm_far, dm_near)
+    dm1 = jnp.concatenate([dm1, dm_near, dm_far, sibling(dm_far)], axis=0)
 
     ln_turn = jnp.stack([gains[1][1], shifts[1][1]])
-    dh1, norms1, y1, hid1, do1, da1, gfc1 = turn_chain(act0, o1, dy1, ln_turn, dm1, weights_proj[1], weights_fc[1])
+    dh1, norms1, y1, hid1, do1, da1, gfc1 = turn_chain(act0, o1, dy1, ln_turn, dm1, wp1, weights1[2], weights1[3])
     sum_fc1 = reduced(gfc1)
     do1, y1, a0 = tie(do1, y1, act0)
     act1 = (hid1 + scatter_rows(y1[half:], y1[:half])).astype(bf16)
@@ -1054,11 +1329,11 @@
     dqkv1, got_acts = tie(dqkv1, got_acts)
     ln_back = jnp.stack([gains[1][0], gains[0][1]])
     gin1, dh0, norms10, do0, da0, gfc0 = back_chain(
-        act0, dh1, hid0, ln_back, dqkv1, weights_qkv[1], weights_proj[0], weights_fc[0], u0, g0, n2_0
+        act0, dh1, hid0, ln_back, dqkv1, wq1, wp0, w10, w20, u0, g0, n2_0
     )
     sum_fc0 = reduced(gfc0)
     sum_qp1 = reduced(jnp.concatenate([grad_of(n1_1, dqkv1), grad_of(da1, o1)], axis=1))
-    rel1 = bias_grads(out_label, label_lanes, dwall1)
+    rel1 = bias_grads(flags, label_lanes, dwall1)
     sums1 = column_sums(dqkv1)
     do0, sum_qp1, rel1, sums1 = tie(do0, sum_qp1, rel1, sums1)
     g1 = gin1.astype(bf16)
@@ -1067,13 +1342,13 @@
     got1 = [near_of(g1, 1), far_of(g1, 1), near_of(w1, 1), far_of(w1, 1)]
     dqkv0, dwall0 = attn_bwd(qkv0, do0, o0, lse0, mask_pad, walls[0], scalars, ORDER, scale)
     dqkv0, got1 = tie(dqkv0, got1)
-    dn1 = scatter_rows(times_t(dqkv0[half:], weights_qkv[0]), times_t(dqkv0[:half], weights_qkv[0]))
+    dn1 = scatter_rows(times_t(dqkv0[half:], wq0), times_t(dqkv0[:half], wq0))
     grad_qp0 = jnp.concatenate([grad_of(n1_0, dqkv0), grad_of(da0, o0)], axis=1)
     sum_qp0 = reduced_late(grad_qp0)
-    rel0 = bias_grads(out_label, label_lanes, dwall0)
+    rel0 = bias_grads(flags, label_lanes, dwall0)
     sums0 = column_sums(dqkv0)
     dn1, grad_qp0, rel0, sums0 = tie(dn1, grad_qp0, rel0, sums0)
-    dx, dgain, dshift = norm_back(x0, dn1, gains[0][0])
+    dx, dgain, dshift = norm_back(x0.astype(f32), dn1, gains[0][0])
     gin0 = dh0 + dx
     early0, early1, late1 = norms10[2:], norms1, norms10[:2]
     late0 = jnp.concatenate([dgain, dshift], axis=0)
@@ -1094,6 +1369,7 @@
         return out
 
     n_qp = 4 * local_width
+    hidden_units = w_fc1.shape[2]
     grad_fc = total(
         by_core((sums_w0[1], sums_w1[1])),
         (near_of(sums_w0[1], 0), far_of(sums_w0[1], 0), got1[2][:, n_qp:], got1[3][:, n_qp:]),

time: 807 us -> 733 us (0.908); the launches traced: 796 us -> 732 us
  waiting for transfers between devices: 211 us -> 82 us
  Pallas kernels: 304 us -> 412 us
  starting transfers between devices: 110 us -> 69.4 us
  matrix products: 26.8 us -> 35.5 us
    ppermute x64 -> x39, waiting for transfers between devices: 185 us -> 59 us  [move(): return lax.ppermute(x, AXES, pairs)]
    pallas_call x5 -> x4, Pallas kernels: 212 us -> 336 us  [the longest x1 107 us: mid_chain(): pl.pallas_call(functools.partial(mid_kernel, bits), in_specs=[VM] * 4 + [...]
    ppermute x64 -> x39, starting transfers between devices: 110 us -> 69.2 us  [move(): return lax.ppermute(x, AXES, pairs)]
    pallas_call x2 -> x1, Pallas kernels: 33.6 us -> 12.5 us  [attn_fwd(): pl.pallas_call(functools.partial(attn_fwd_kernel, order, scale), grid=(nq...]
    dot_general x2 -> x1, matrix products: 7.31 us -> 15.9 us  [local(): qkv1 = (jnp.dot(n1_1, wq1, preferred_element_type=f32) + term1).astype(bf16)]
    unnamed x178 -> x112, local copies, waits for them, and re-layouts: 18.1 us -> 18.9 us
  transfers between devices with their start and end apart: 70 -> 42, of which waited for: 23 -> 14; matrix products, arithmetic and copies ran while one was open for 14% -> 10% of each run, Pallas kernels for 30% -> 20%
where the time goes in v3:
time: 733 us; the launch traced here: 732 us
  Pallas kernels  412 us (56%)
  waiting for transfers between devices  82 us (11%)
  starting transfers between devices  69.4 us (9%)
  local copies, waits for them, and re-layouts  60.6 us (8%)
  other arithmetic  51.1 us (7%)
  matrix products  35.5 us (5%)
  between operations  15.9 us (2%)
    pallas_call x1, Pallas kernels, mid_chain(): pl.pallas_call(functools.partial(mid_kernel, bits), in_specs=[VM] * 4 + [...  107 us
    pallas_call x1, Pallas kernels, start_chain(): pl.pallas_call(functools.partial(start_kernel, order, scale, bits), in_sp...  90.9 us
    pallas_call x1, Pallas kernels, back_chain(): pl.pallas_call(back_kernel, in_specs=[VM] * 5 + [HB] * 7, out_specs=[VM,...  69.7 us
    ppermute x39, starting transfers between devices, move(): return lax.ppermute(x, AXES, pairs)  69.2 us
    pallas_call x1, Pallas kernels, turn_chain(): pl.pallas_call(functools.partial(turn_kernel, bits), in_specs=[VM, VM, VM...  68.6 us
    ppermute x39, waiting for transfers between devices, move(): return lax.ppermute(x, AXES, pairs)  59 us
    pallas_call x2, Pallas kernels, attn_bwd(): pl.pallas_call(functools.partial(attn_bwd_kernel, order, scale), grid=(nq...  42.7 us
    reduce_scatter x3, waiting for transfers between devices, reduced(): return lax.psum_scatter(x, 'dp', scatter_dimension=0, tiled=True)  22.3 us
  transfers between devices with their start and end apart: 42, of which 14 were waited for; matrix products, arithmetic and copies ran while one was open for 10% of the time, Pallas kernels for 20%

profile of v3, /device:TPU:1, one launch (start us, length us, event | category | flops | bytes accessed | tf_op | source)
XLA Modules:
  0.0 732.3 jit_solution(11977566679008548639)
XLA Ops:
  30.4 90.9 %shard_map.213 = (bf16[256,1152]{1,0:T(8,128)(2,1)}, f32[2,8,1152]{2,1,0:T(8,128)}, f32[4,4,256]{2,1,0:T(4,128)}, bf16[1024,288]{1,0:T(8,128)(2,1)}, bf16[4,256,...) custom-call(s32[2]{0:T(128)} %pad_add_fusion.flags_ref, ...), custom_call_target="tpu_custom_call" | custom-call | flops 85899345920 | bytes 25165824 | tf_op jit(solution)/shard_map/pallas_call | solution.py:1124
  125.6 107.0 %shard_map.214 = (f32[256,1152]{1,0:T(8,128)}, bf16[256,1152]{1,0:T(8,128)(2,1)}, f32[256,1152]{1,0:T(8,128)}, bf16[4,256,1152]{2,1,0:T(8,128)(2,1)}, bf16[1024,...) custom-call(bf16[256,1152]{1,0:T(8,128)(2,1)} %get-tuple-element.81., ...), custom_call_target="tpu_custom_call" | custom-call | flops 64424509440 | bytes 25165824 | tf_op jit(solution)/shard_map/pallas_call | solution.py:748
  234.8 15.9 %add_convert_fusion.q_ref.kv_ref = bf16[1024,864]{1,0:T(8,128)(2,1)S(1)} fusion(f32[864]{0:T(1024)S(1)} %fusion.38, bf16[1024,1152]{1,0:T(8,128)(2,1)} %bitcast.155, bf16[1152,864]{1,0:T(8,128)(2,1)} %bitcast.161), kind=kOutput, calls=%fused_computation.2 | convolution fusion | flops 2040201216 | bytes 6122880 | tf_op jit(solution)/shard_map/dot_general | solution.py:1315
  254.5 12.5 %shard_map.215 = (bf16[1024,288]{1,0:T(8,128)(2,1)S(1)}, f32[4,4,256]{2,1,0:T(4,128)S(1)}) custom-call(s32[6]{0:T(128)S(1)} %stack.56.sc_ref, bf16[1024,864]{1,0:T(8,128)(2,1)S(1)} %add_convert_fusion.q_ref.kv_ref, bf16[1024,864]{1,0:T(8,128)(2,1)S(1)} %add_convert_fusion.q_ref.kv_ref, bf16[1024,56]{1,0:T(8,128)(2,1)S(1)} %copy-done.6, ...), custom_call_target="tpu_custom_call" | custom-call | flops 17179869184 | bytes 12582912 | tf_op jit(solution)/shard_map/pallas_call | solution.py:235
  272.3 68.6 %shard_map.216 = (f32[256,1152]{1,0:T(8,128)}, f32[2,1152]{1,0:T(2,128)}, bf16[1024,1152]{1,0:T(8,128)(2,1)}, f32[256,1152]{1,0:T(8,128)}, bf16[1024,288]{1,0:T(...) custom-call(bf16[256,1152]{1,0:T(8,128)(2,1)} %get-tuple-element.109.x_ref, ...), custom_call_target="tpu_custom_call" | custom-call | flops 64424509440 | bytes 25165824 | tf_op jit(solution)/shard_map/pallas_call | solution.py:871
  345.1 5.5 collective-permute-start.8
  352.1 13.8 %collective-permute-done.5 = bf16[256,1152]{1,0:T(8,128)(2,1)S(1)} collective-permute-done((bf16[256,1152]{1,0:T(8,128)(2,1)S(1)}, bf16[256,1152]{1,0:T(8,128)(2,1)S(1)}, u32[]{:S(2)}, u32[]{:S(2)}) %collective-permute-start.5) | collective-permute-done | bytes 589856 | tf_op jit(solution)/shard_map/partner/ppermute | solution.py:1200
  370.7 21.6 %shard_map.217 = (bf16[1024,864]{1,0:T(8,128)(2,1)S(1)}, f32[4,32,14336]{2,1,0:T(8,128)}) custom-call(s32[6]{0:T(128)S(1)} %stack.56.sc_ref, bf16[1024,864]{1,0:T(8,128)(2,1)S(1)} %copy-done.13, bf16[1024,864]{1,0:T(8,128)(2,1)S(1)} %copy-done.13, bf16[1024,288]{1,0:T(8,128)(2,1)S(1)} %copy-done.17, bf16[1024,288]{1,0:T(8,128)(2,1)S(1)} %copy-done.11, ...), custom_call_target="tpu_custom_call" | custom-call | flops 25769803776 | bytes 20971520 | tf_op jit(solution)/shard_map/pallas_call | solution.py:314
  410.7 69.7 %shard_map.218 = (f32[256,1152]{1,0:T(8,128)}, f32[256,1152]{1,0:T(8,128)}, f32[4,1152]{1,0:T(4,128)}, bf16[1024,288]{1,0:T(8,128)(2,1)}, bf16[4,256,1152]{2,1,0:T(8,128)(2,1)}, /*index=5*/bf16[1152,2304]{1,0:T(8,128)(2,1)}) custom-call(bf16[256,1152]{1,0:T(8,128)(2,1)} %get-tuple-element.109.x_ref, f32[256,1152]{1,0:T(8,128)} %get-tuple-element.112.dh1_ref, ...), custom_call_target="tpu_custom_call" | custom-call | flops 64424509440 | bytes 25165824 | tf_op jit(solution)/shard_map/pallas_call | solution.py:984
  481.2 6.3 all-gather
  491.8 10.1 %shard_map.219 = f32[4,64,64]{2,1,0:T(8,128)S(1)} custom-call(s32[2]{0:T(128)S(1)} %copy-done.8, s32[1,4096]{1,0:T(1,128)S(1)} %copy-done.7, f32[4,32,14336]{2,1,0:T(8,128)S(1)} %copy-done.2), custom_call_target="tpu_custom_call" | custom-call | tf_op jit(solution)/shard_map/pallas_call | solution.py:135
  518.7 4.7 collective-permute-start.13
  527.1 21.0 %shard_map.220 = (bf16[1024,864]{1,0:T(8,128)(2,1)S(1)}, f32[4,32,14336]{2,1,0:T(8,128)}) custom-call(s32[6]{0:T(128)S(1)} %stack.56.sc_ref, bf16[1024,864]{1,0:T(8,128)(2,1)S(1)} %copy-done.15, bf16[1024,864]{1,0:T(8,128)(2,1)S(1)} %copy-done.15, bf16[1024,288]{1,0:T(8,128)(2,1)S(1)} %copy-done.16, bf16[1024,288]{1,0:T(8,128)(2,1)S(1)} %copy-done.9, ...), custom_call_target="tpu_custom_call" | custom-call | flops 25769803776 | bytes 20971520 | tf_op jit(solution)/shard_map/pallas_call | solution.py:314
  551.2 10.1 %shard_map.221 = f32[4,64,64]{2,1,0:T(8,128)S(1)} custom-call(s32[2]{0:T(128)S(1)} %copy-done.8, s32[1,4096]{1,0:T(1,128)S(1)} %copy-done.7, f32[4,32,14336]{2,1,0:T(8,128)S(1)} %copy-done.3), custom_call_target="tpu_custom_call" | custom-call | tf_op jit(solution)/shard_map/pallas_call | solution.py:135
  561.3 18.0 %reduce-scatter.8.cloned.1.call-done = bf16[288,2304]{1,0:T(8,128)(2,1)} async-done(((bf16[1152,2304]{1,0:T(8,128)(2,1)}), bf16[288,2304]{1,0:T(8,128)(2,1)}) %reduce-scatter.8.cloned.1.call-update) | async-done | bytes 1327120 | tf_op jit(solution)/shard_map/g_sum/reduce_scatter | solution.py:1269
  581.1 5.3 collective-permute-start.30
  586.5 4.7 fusion.20
  615.6 10.3 %collective-permute-done.21 = bf16[2,288,640]{2,1,0:T(8,128)(2,1)S(1)} collective-permute-done((bf16[2,288,640]{2,1,0:T(8,128)(2,1)S(1)}, bf16[2,288,640]{2,1,0:T(8,128)(2,1)S(1)}, u32[]{:S(2)}, u32[]{:S(2)}) %collective-permute-start.21) | collective-permute-done | bytes 737312 | tf_op jit(solution)/shard_map/g_dp/ppermute | solution.py:1200
  627.8 5.7 collective-permute-done.20
  641.6 6.3 collective-permute-done.16
  661.3 7.6 %collective-permute-start.18 = (bf16[256,1152]{1,0:T(8,128)(2,1)}, bf16[256,1152]{1,0:T(8,128)(2,1)}, u32[]{:S(2)}, u32[]{:S(2)}) collective-permute-start(bf16[256,1152]{1,0:T(8,128)(2,1)} %get-tuple-element.201), channel_id=1, source_target_pairs={{2,0},{3,1},{4,2},{5,3},{10,8},{11,9},{12,10},{13,11},{18,16},{19,... | collective-permute-start | bytes 1769480 | tf_op jit(solution)/shard_map/d_far/ppermute | solution.py:1200
  676.7 9.2 %collective-permute-start.24 = (bf16[288,1152]{1,0:T(8,128)(2,1)}, bf16[288,1152]{1,0:T(8,128)(2,1)}, u32[]{:S(2)}, u32[]{:S(2)}) collective-permute-start(bf16[288,1152]{1,0:T(8,128)(2,1)} %pad_maximum_fusion.5), channel_id=1, source_target_pairs={{2,0},{3,1},{4,2},{5,3},{10,8},{11,9},{12,10},{13,11},{18,16},{19,... | collective-permute-start | bytes 1990664 | tf_op jit(solution)/shard_map/d_far/ppermute | solution.py:1200
  686.0 9.9 %collective-permute-done.27 = f32[382,128]{1,0:T(8,128)S(1)} collective-permute-done((f32[382,128]{1,0:T(8,128)S(1)}, f32[382,128]{1,0:T(8,128)S(1)}, u32[]{:S(2)}, u32[]{:S(2)}) %collective-permute-start.27) | collective-permute-done | bytes 195616 | tf_op jit(solution)/shard_map/across/ppermute | solution.py:1200
  695.9 5.7 collective-permute-start.36
  (330 shorter events, 176.0 us)
Async XLA Ops:
  7.2 502.7 %reduce-scatter.4.cloned.1.call-start = ((), (), s32[]{:S(2)}) async-start(), calls=%async_computation.3 | async-start | bytes 3317760 | tf_op jit(solution)/shard_map/g_sum/reduce_scatter | solution.py:1269
  250.7 16.3 %collective-permute-start = (bf16[256,1152]{1,0:T(8,128)(2,1)}, bf16[256,1152]{1,0:T(8,128)(2,1)}, u32[]{:S(2)}, u32[]{:S(2)}) collective-permute-start(bf16[256,1152]{1,0:T(8,128)(2,1)} %convert_element_type.174), channel_id=1, source_target_pairs={{0,1},{1,0},{2,3},{3,2},{4,5},{5,4},{6,7},{7,6},{8,9},{9,8},{10,11... | collective-permute-start | bytes 1769480 | tf_op jit(solution)/shard_map/partner/ppermute | solution.py:1200
  250.8 16.2 %collective-permute-start.1 = (bf16[256,1152]{1,0:T(8,128)(2,1)}, bf16[256,1152]{1,0:T(8,128)(2,1)}, u32[]{:S(2)}, u32[]{:S(2)}) collective-permute-start(bf16[256,1152]{1,0:T(8,128)(2,1)} %convert_element_type.174), channel_id=1, source_target_pairs={{0,4},{1,5},{2,6},{3,7},{4,0},{5,1},{6,2},{7,3},{8,12},{9,13},{10,... | collective-permute-start | bytes 1769480 | tf_op jit(solution)/shard_map/sibling/ppermute | solution.py:1200
  344.7 21.2 %collective-permute-start.5 = (bf16[256,1152]{1,0:T(8,128)(2,1)S(1)}, bf16[256,1152]{1,0:T(8,128)(2,1)S(1)}, u32[]{:S(2)}, u32[]{:S(2)}) collective-permute-start(bf16[256,1152]{1,0:T(8,128)(2,1)S(1)} %add_convert_fusion.2), channel_id=1, source_target_pairs={{0,1},{1,0},{2,3},{3,2},{4,5},{5,4},{6,7},{7,6},{8,9},{9,8},{10,11... | collective-permute-start | bytes 1769480 | tf_op jit(solution)/shard_map/partner/ppermute | solution.py:1200
  345.1 50.5 %collective-permute-start.8 = (bf16[256,1152]{1,0:T(8,128)(2,1)}, bf16[256,1152]{1,0:T(8,128)(2,1)}, u32[]{:S(2)}, u32[]{:S(2)}) collective-permute-start(bf16[256,1152]{1,0:T(8,128)(2,1)} %get-tuple-element.109.x_ref), channel_id=1, source_target_pairs={{2,0},{3,1},{4,2},{5,3},{10,8},{11,9},{12,10},{13,11},{18,16},{19,... | collective-permute-start | bytes 1769480 | tf_op jit(solution)/shard_map/d_far/ppermute | solution.py:1200
  350.6 47.4 %collective-permute-start.6 = (bf16[256,1152]{1,0:T(8,128)(2,1)}, bf16[256,1152]{1,0:T(8,128)(2,1)}, u32[]{:S(2)}, u32[]{:S(2)}) collective-permute-start(bf16[256,1152]{1,0:T(8,128)(2,1)} %get-tuple-element.109.x_ref), channel_id=1, source_target_pairs={{6,2},{7,3},{14,10},{15,11},{22,18},{23,19},{30,26},{31,27}} | collective-permute-start | bytes 1769480 | tf_op jit(solution)/shard_map/d_near/ppermute | solution.py:1200
  367.0 28.7 %collective-permute-start.9 = (bf16[256,1152]{1,0:T(8,128)(2,1)}, bf16[256,1152]{1,0:T(8,128)(2,1)}, u32[]{:S(2)}, u32[]{:S(2)}) collective-permute-start(bf16[256,1152]{1,0:T(8,128)(2,1)} %add_convert_fusion.1), channel_id=1, source_target_pairs={{2,4},{3,5},{4,6},{5,7},{10,12},{11,13},{12,14},{13,15},{18,20},{1... | collective-permute-start | bytes 1769480 | tf_op jit(solution)/shard_map/d_far/ppermute | solution.py:1200
  369.3 28.7 %collective-permute-start.7 = (bf16[256,1152]{1,0:T(8,128)(2,1)}, bf16[256,1152]{1,0:T(8,128)(2,1)}, u32[]{:S(2)}, u32[]{:S(2)}) collective-permute-start(bf16[256,1152]{1,0:T(8,128)(2,1)} %add_convert_fusion.1), channel_id=1, source_target_pairs={{0,4},{1,5},{8,12},{9,13},{16,20},{17,21},{24,28},{25,29}} | collective-permute-start | bytes 1769480 | tf_op jit(solution)/shard_map/d_near/ppermute | solution.py:1200
  409.1 105.2 %reduce-scatter.6.cloned.1.call-start = ((), (), s32[]{:S(2)}) async-start(), calls=%async_computation.4 | async-start | bytes 6635520 | tf_op jit(solution)/shard_map/g_sum/reduce_scatter | solution.py:1269
  409.9 169.4 %reduce-scatter.8.cloned.1.call-start = ((), (), s32[]{:S(2)}) async-start(), calls=%async_computation.5 | async-start | bytes 6635520 | tf_op jit(solution)/shard_map/g_sum/reduce_scatter | solution.py:1269
  517.4 69.1 %collective-permute-start.12 = (bf16[288,3456]{1,0:T(8,128)(2,1)}, bf16[288,3456]{1,0:T(8,128)(2,1)}, u32[]{:S(2)}, u32[]{:S(2)}) collective-permute-start(bf16[288,3456]{1,0:T(8,128)(2,1)} %pad_maximum_fusion.4), channel_id=1, source_target_pairs={{0,4},{1,5},{8,12},{9,13},{16,20},{17,21},{24,28},{25,29}} | collective-permute-start | bytes 5971976 | tf_op jit(solution)/shard_map/d_near/ppermute | solution.py:1200
  518.7 67.8 %collective-permute-start.13 = (bf16[288,3456]{1,0:T(8,128)(2,1)}, bf16[288,3456]{1,0:T(8,128)(2,1)}, u32[]{:S(2)}, u32[]{:S(2)}) collective-permute-start(bf16[288,3456]{1,0:T(8,128)(2,1)} %pad_maximum_fusion.4), channel_id=1, source_target_pairs={{2,4},{3,5},{4,6},{5,7},{10,12},{11,13},{12,14},{13,15},{18,20},{1... | collective-permute-start | bytes 5971976 | tf_op jit(solution)/shard_map/d_far/ppermute | solution.py:1200
  523.4 57.7 %collective-permute-start.10 = (bf16[256,1152]{1,0:T(8,128)(2,1)}, bf16[256,1152]{1,0:T(8,128)(2,1)}, u32[]{:S(2)}, u32[]{:S(2)}) collective-permute-start(bf16[256,1152]{1,0:T(8,128)(2,1)} %convert_element_type.186), channel_id=1, source_target_pairs={{0,4},{1,5},{8,12},{9,13},{16,20},{17,21},{24,28},{25,29}} | collective-permute-start | bytes 1769480 | tf_op jit(solution)/shard_map/d_near/ppermute | solution.py:1200
  524.7 61.8 %collective-permute-start.11 = (bf16[256,1152]{1,0:T(8,128)(2,1)}, bf16[256,1152]{1,0:T(8,128)(2,1)}, u32[]{:S(2)}, u32[]{:S(2)}) collective-permute-start(bf16[256,1152]{1,0:T(8,128)(2,1)} %convert_element_type.186), channel_id=1, source_target_pairs={{2,4},{3,5},{4,6},{5,7},{10,12},{11,13},{12,14},{13,15},{18,20},{1... | collective-permute-start | bytes 1769480 | tf_op jit(solution)/shard_map/d_far/ppermute | solution.py:1200
  579.3 56.9 %collective-permute-start.29 = (bf16[288,2304]{1,0:T(8,128)(2,1)}, bf16[288,2304]{1,0:T(8,128)(2,1)}, u32[]{:S(2)}, u32[]{:S(2)}) collective-permute-start(bf16[288,2304]{1,0:T(8,128)(2,1)} %reduce-scatter.8.cloned.1.call-done), channel_id=1, source_target_pairs={{6,2},{7,3},{14,10},{15,11},{22,18},{23,19},{30,26},{31,27}} | collective-permute-start | bytes 3981320 | tf_op jit(solution)/shard_map/d_near/ppermute | solution.py:1200
  581.1 55.1 %collective-permute-start.30 = (bf16[288,2304]{1,0:T(8,128)(2,1)}, bf16[288,2304]{1,0:T(8,128)(2,1)}, u32[]{:S(2)}, u32[]{:S(2)}) collective-permute-start(bf16[288,2304]{1,0:T(8,128)(2,1)} %reduce-scatter.8.cloned.1.call-done), channel_id=1, source_target_pairs={{2,0},{3,1},{4,2},{5,3},{10,8},{11,9},{12,10},{13,11},{18,16},{19,... | collective-permute-start | bytes 3981320 | tf_op jit(solution)/shard_map/d_far/ppermute | solution.py:1200
  614.3 27.3 %collective-permute-start.14 = (bf16[256,1152]{1,0:T(8,128)(2,1)S(1)}, bf16[256,1152]{1,0:T(8,128)(2,1)S(1)}, u32[]{:S(2)}, u32[]{:S(2)}) collective-permute-start(bf16[256,1152]{1,0:T(8,128)(2,1)S(1)} %slice.355), channel_id=1, source_target_pairs={{0,4},{1,5},{2,6},{3,7},{4,0},{5,1},{6,2},{7,3},{8,12},{9,13},{10,... | collective-permute-start | bytes 1769480 | tf_op jit(solution)/shard_map/sibling/ppermute | solution.py:1200
  659.7 43.2 %collective-permute-start.17 = (bf16[256,1152]{1,0:T(8,128)(2,1)}, bf16[256,1152]{1,0:T(8,128)(2,1)}, u32[]{:S(2)}, u32[]{:S(2)}) collective-permute-start(bf16[256,1152]{1,0:T(8,128)(2,1)} %get-tuple-element.201), channel_id=1, source_target_pairs={{6,2},{7,3},{14,10},{15,11},{22,18},{23,19},{30,26},{31,27}} | collective-permute-start | bytes 1769480 | tf_op jit(solution)/shard_map/d_near/ppermute | solution.py:1200
  661.3 41.7 %collective-permute-start.18 = (bf16[256,1152]{1,0:T(8,128)(2,1)}, bf16[256,1152]{1,0:T(8,128)(2,1)}, u32[]{:S(2)}, u32[]{:S(2)}) collective-permute-start(bf16[256,1152]{1,0:T(8,128)(2,1)} %get-tuple-element.201), channel_id=1, source_target_pairs={{2,0},{3,1},{4,2},{5,3},{10,8},{11,9},{12,10},{13,11},{18,16},{19,... | collective-permute-start | bytes 1769480 | tf_op jit(solution)/shard_map/d_far/ppermute | solution.py:1200
  670.3 25.6 %collective-permute-start.27 = (f32[382,128]{1,0:T(8,128)S(1)}, f32[382,128]{1,0:T(8,128)S(1)}, u32[]{:S(2)}, u32[]{:S(2)}) collective-permute-start(f32[382,128]{1,0:T(8,128)S(1)} %add.260), channel_id=1, source_target_pairs={{0,2},{1,3},{2,0},{3,1},{4,6},{5,7},{6,4},{7,5},{8,10},{9,11},{10,... | collective-permute-start | bytes 586760 | tf_op jit(solution)/shard_map/across/ppermute | solution.py:1200
  671.6 37.8 %collective-permute-start.23 = (bf16[288,1152]{1,0:T(8,128)(2,1)}, bf16[288,1152]{1,0:T(8,128)(2,1)}, u32[]{:S(2)}, u32[]{:S(2)}) collective-permute-start(bf16[288,1152]{1,0:T(8,128)(2,1)} %pad_maximum_fusion.5), channel_id=1, source_target_pairs={{6,2},{7,3},{14,10},{15,11},{22,18},{23,19},{30,26},{31,27}} | collective-permute-start | bytes 1990664 | tf_op jit(solution)/shard_map/d_near/ppermute | solution.py:1200
  676.7 33.9 %collective-permute-start.24 = (bf16[288,1152]{1,0:T(8,128)(2,1)}, bf16[288,1152]{1,0:T(8,128)(2,1)}, u32[]{:S(2)}, u32[]{:S(2)}) collective-permute-start(bf16[288,1152]{1,0:T(8,128)(2,1)} %pad_maximum_fusion.5), channel_id=1, source_target_pairs={{2,0},{3,1},{4,2},{5,3},{10,8},{11,9},{12,10},{13,11},{18,16},{19,... | collective-permute-start | bytes 1990664 | tf_op jit(solution)/shard_map/d_far/ppermute | solution.py:1200
  695.9 27.6 %collective-permute-start.36 = (f32[18,128]{1,0:T(8,128)S(1)}, f32[18,128]{1,0:T(8,128)}, u32[]{:S(2)}, u32[]{:S(2)}) collective-permute-start(f32[18,128]{1,0:T(8,128)S(1)} %add.269), channel_id=1, source_target_pairs={{0,4},{1,5},{2,6},{3,7},{4,0},{5,1},{6,2},{7,3},{8,12},{9,13},{10,... | collective-permute-start | bytes 27656 | tf_op jit(solution)/shard_map/sibling/ppermute | solution.py:1200
  703.1 21.8 %collective-permute-start.31 = (f32[128,128]{1,0:T(8,128)S(1)}, f32[128,128]{1,0:T(8,128)S(1)}, u32[]{:S(2)}, u32[]{:S(2)}) collective-permute-start(f32[128,128]{1,0:T(8,128)S(1)} %slice_select_fusion), channel_id=1, source_target_pairs={{0,4},{1,5},{6,2},{7,3},{8,12},{9,13},{14,10},{15,11},{16,20},{17,... | collective-permute-start | bytes 196616 | tf_op jit(solution)/shard_map/pack_near/ppermute | solution.py:1200
  (72 other events, 893.7 us)
Sparse Core Ops, SparseCore 0:
  409.3 39.7 reduce-scatter.3
  452.1 62.1 reduce-scatter.5
  517.3 61.9 reduce-scatter.7

commit v4 on v3

--- a/solution.py
+++ b/solution.py
@@ -392,6 +392,9 @@
                 self.ids["dp", b] = {"dp": d + (1 - 2 * bit) * (1 << b)}
                 self.greet.append(self.ids["dp", b])
             self.greet += [{"tensor": across}, {"tensor": across, "section": 1 - c}]
+        self.ids[ACROSS] = {"tensor": across}
+        for layer in range(2):
+            self.ids["return", layer] = {"tensor": across, "section": layer}
         self.send_sem, self.recv_sem = send_sem, recv_sem
         self.used = 0
         self.started = []
@@ -402,7 +405,7 @@
             pl.semaphore_signal(barrier, inc=1, device_id=where, device_id_type=pl.DeviceIdType.MESH)
         pl.semaphore_wait(barrier, len(self.greet))
 
-    def send(self, src, dst, to, cond=None):
+    def make(self, src, dst, to, cond=None, track=True):
         k = self.used
         self.used += 1
         copy = pltpu.make_async_remote_copy(
@@ -413,8 +416,13 @@
             device_id=self.ids[to],
             device_id_type=pl.DeviceIdType.MESH,
         )
+        if track:
+            self.started.append((copy, cond))
+        return copy
+
+    def send(self, src, dst, to, cond=None, track=True):
+        copy = self.make(src, dst, to, cond, track)
         when(cond, copy.start)
-        self.started.append((copy, cond))
         return copy
 
     def leave(self):
@@ -429,7 +437,7 @@
         pl.when(cond)(lambda: do())
 
 
-PARTNER, SIBLING, FAR, HOME = "partner", "sibling", "far", "home"
+PARTNER, SIBLING, FAR, HOME, ACROSS = "partner", "sibling", "far", "home", "across"
 
 
 class Spread:
@@ -465,15 +473,16 @@
 class Deliver:
     COPIES = 2
 
-    def __init__(self, links, layer, src, out, sem):
+    def __init__(self, links, layer, src, out, sem=None):
         self.links, self.layer, self.src, self.out, self.sem = links, layer, src, out, sem
 
     def start(self):
         links = self.links
         mine = links.c == self.layer
         keeps = links.pair == self.layer
-        self.local = pltpu.make_async_copy(self.src, self.out, self.sem)
-        when(mine & keeps, self.local.start)
+        if self.sem is not None:
+            self.local = pltpu.make_async_copy(self.src, self.out, self.sem)
+            when(mine & keeps, self.local.start)
         at = bits_region(links, ())
         self.far = links.send(self.src.at[at], self.out.at[at], FAR, mine)
         self.near = links.send(self.src, self.out, HOME, mine & jnp.logical_not(keeps))
@@ -481,7 +490,8 @@
     def done(self):
         links = self.links
         keeps = links.pair == self.layer
-        when(links.home & keeps, self.local.wait)
+        if self.sem is not None:
+            when(links.home & keeps, self.local.wait)
         when(links.home & jnp.logical_not(keeps), self.near.wait_recv)
         when(jnp.logical_not(links.home), self.far.wait_recv)
 
@@ -513,20 +523,23 @@
 
 
 class Part:
-    def __init__(self, links, src, dst, sem):
+    def __init__(self, links, layer, own, got, dst, sem):
         at = bits_region(links, ())
-        self.whole = pltpu.make_async_copy(src, dst, sem)
-        self.piece = pltpu.make_async_copy(src.at[at], dst.at[at], sem)
-        self.home, self.away = links.home, jnp.logical_not(links.home)
+        keeps = links.pair == layer
+        self.ways = (
+            (links.home & keeps, pltpu.make_async_copy(own, dst, sem)),
+            (links.home & jnp.logical_not(keeps), pltpu.make_async_copy(got, dst, sem)),
+            (jnp.logical_not(links.home), pltpu.make_async_copy(got.at[at], dst.at[at], sem)),
+        )
 
     def start(self):
-        when(self.home, self.whole.start)
-        when(self.away, self.piece.start)
+        for cond, copy in self.ways:
+            when(cond, copy.start)
         return self
 
     def wait(self):
-        when(self.home, self.whole.wait)
-        when(self.away, self.piece.wait)
+        for cond, copy in self.ways:
+            when(cond, copy.wait)
 
 
 def chunk(i, rows):
@@ -558,6 +571,12 @@
         self.low[2, at] = p1.astype(jnp.bfloat16)
         self.copies["b", i] = self.links.send(self.low.at[2, at], self.low.at[5, at], SIBLING)
         self.wide[1, at] = p0
+
+    def release(self):
+        for copy in self.copies.values():
+            copy.wait_send()
+        self.links.started = [s for s in self.links.started if all(s[0] is not c for c in self.copies.values())]
+        self.copies = {}
 
     def done(self, i):
         at = chunk(i, self.rows)
@@ -593,6 +612,74 @@
         return jnp.concatenate([self.buf[b, at] for b in range(4)], axis=0)
 
 
+class DpReduce:
+    COPIES = 4
+
+    def __init__(self, links, buf, land0, land1, sent):
+        self.links, self.buf, self.land0, self.land1, self.sent = links, buf, land0, land1, sent
+        columns = buf.shape[-1]
+        cut = columns // 256 * 128
+        self.cols = (pl.ds(0, cut), pl.ds(cut, columns - cut))
+        self.orders = ((0, 1), (1, 0))
+        self.mine = links.dp_bit
+        self.other = [1 - bit for bit in links.dp_bit]
+        self.first, self.second = [], []
+        for (b0, b1), h, cols in zip(self.orders, range(2), self.cols):
+            at = self.place(h, self.other[b0], pl.ds(0, 2))
+            self.first.append(links.make(buf.at[at + (slice(None), cols)], land0.at[:, :, cols], ("dp", b0)))
+            self.second.append(links.make(sent.at[0, :, cols], land1.at[0, :, cols], ("dp", b1)))
+
+    @staticmethod
+    def scratch(n, columns):
+        return [pltpu.VMEM((k, n, columns), jnp.bfloat16) for k in (2, 1, 1)]
+
+    def place(self, h, first, second):
+        return (second, first) if self.orders[h][0] == 0 else (first, second)
+
+    def start(self):
+        for copy in self.first:
+            copy.start()
+
+    def middle(self):
+        for h, cols in enumerate(self.cols):
+            b0, b1 = self.orders[h]
+            self.first[h].wait_recv()
+            sums = []
+            for second in (self.other[b1], self.mine[b1]):
+                own = self.buf[self.place(h, self.mine[b0], second) + (slice(None), cols)]
+                sums.append(own.astype(jnp.float32) + self.land0[second, :, cols].astype(jnp.float32))
+            self.sent[0, :, cols] = sums[0].astype(jnp.bfloat16)
+            self.buf[self.place(h, self.mine[b0], self.mine[b1]) + (slice(None), cols)] = sums[1].astype(jnp.bfloat16)
+            self.second[h].start()
+
+    def done(self, out):
+        for h, cols in enumerate(self.cols):
+            self.second[h].wait_recv()
+            b0, b1 = self.orders[h]
+            own = self.buf[self.place(h, self.mine[b0], self.mine[b1]) + (slice(None), cols)]
+            out[:, cols] = (own.astype(jnp.float32) + self.land1[0, :, cols].astype(jnp.float32)).astype(out.dtype)
+
+
+class Return:
+    COPIES = 2
+
+    def __init__(self, links, layer, src, near, far):
+        self.links, self.layer = links, layer
+        self.home, self.away = links.home, jnp.logical_not(links.home)
+        self.here = links.c == layer
+        self.near_cond = self.home & jnp.logical_not(self.here)
+        self.near = links.make(src, near, SIBLING, self.near_cond)
+        self.far = links.make(src, far, ("return", layer), self.away)
+
+    def start(self):
+        when(self.near_cond, self.near.start)
+        when(self.away, self.far.start)
+
+    def done(self):
+        when(self.here & self.away, self.near.wait_recv)
+        when(self.here, self.far.wait_recv)
+
+
 def start_load(src, dst, sem):
     copy = pltpu.make_async_copy(src, dst, sem)
     copy.start()
@@ -629,26 +716,44 @@
     scatter.near(i, p[:n], p[n:])
 
 
-def mid_kernel(bits, x_ref, o_ref, ln_ref, live_ref, cot_hbm, wp_hbm, w1_hbm, w2_hbm, own_q, own_p, own_1, own_2,
-               hid_ref, act_ref, dy_ref, n2_hbm, u_hbm, g_hbm, n1_hbm, w1_out, w2_out, next_q, next_p, next_1, next_2,
-               wp, w1, w2, got_q, got_p, got_1, got_2, cot, u_buf, g_buf, gat1, gat2, low1, wide1, low2, wide2,
+def slab_grad(out, col, x, y):
+    n = out.shape[2]
+    width = x.shape[1]
+    step = 384
+    for k in range(0, width, step):
+        res = dot(x[:, k : k + step], y, TN).astype(out.dtype)
+        at = k
+        while at < k + step:
+            slab = at // n
+            stop = min(k + step, (slab + 1) * n)
+            out[slab // 2, slab % 2, at - slab * n : stop - slab * n, col : col + y.shape[1]] = res[at - k : stop - k]
+            at = stop
+
+
+def block_quarter(links, i):
+    return lax.rem(links.r + i // 2, 2) + 2 * lax.rem(links.c + lax.rem(i, 2), 2)
+
+
+def mid_kernel(order, scale, bits, x_ref, o_ref, ln_ref, cot_ref, live_ref, term_ref, mask_ref,
+               wp_hbm, got1_hbm, got2_hbm, wall_hbm, own_q, own_p, own_1, own_2,
+               hid_ref, act_ref, dy_ref, o1_ref, lse_ref,
+               n2_hbm, u_hbm, g_hbm, n1_hbm, qkv_hbm, dm_hbm, w1_out, w2_out, next_q, next_p, next_1, next_2,
+               wp, w1, w2, got_q, got_p, wall, u_buf, g_buf, qkv, gat1, gat2, gat3, low, wide, s_scr, p_scr,
                load_sem, store_sem, send_sem, recv_sem):
     rows, width = x_ref.shape
     n = rows // NCH
     links = Links(send_sem, recv_sem, bits)
     load_p = start_load(wp_hbm, wp, load_sem.at[0])
-    load_1 = Part(links, w1_hbm, w1, load_sem.at[1]).start()
-    load_2 = Part(links, w2_hbm, w2, load_sem.at[2]).start()
-    own_cot = pltpu.make_async_copy(cot_hbm.at[links.pair], cot, load_sem.at[3])
-    when(links.home, own_cot.start)
+    load_1 = Part(links, 0, own_1, got1_hbm, w1, load_sem.at[1]).start()
+    load_2 = Part(links, 0, own_2, got2_hbm, w2, load_sem.at[2]).start()
+    load_w = start_load(wall_hbm, wall, load_sem.at[3])
     links.enter()
     ex1, ex2 = Exchange(links, w1), Exchange(links, w2)
-    got = (got_q, got_p, got_1, got_2)
-    delivers = [
-        Deliver(links, 1, src, dst, load_sem.at[4 + k]) for k, (src, dst) in enumerate(zip((own_q, own_p, own_1, own_2), got))
-    ]
-    s1, s2 = Scatter(links, low1, wide1), Scatter(links, low2, wide2)
-    g1, g2 = Gather(links, gat1), Gather(links, gat2)
+    exq, exp = Exchange(links, got_q), Exchange(links, got_p)
+    get_q, get_p = Deliver(links, 1, own_q, got_q, load_sem.at[4]), Deliver(links, 1, own_p, got_p, load_sem.at[5])
+    get_1, get_2 = Deliver(links, 1, own_1, next_1), Deliver(links, 1, own_2, next_2)
+    s1, s2 = Scatter(links, low, wide), Scatter(links, low, wide)
+    g1, g2, g3 = Gather(links, gat1), Gather(links, gat2), Gather(links, gat3)
     load_p.wait()
     for i in range(NCH):
         scatter_product(s1, i, lambda b: block_rows(o_ref, b, i, rows), wp[...], rows)
@@ -660,6 +765,8 @@
         s1.middle(i)
     for s in range(1, bits):
         ex1.step(s)
+    get_q.start()
+    get_p.start()
     for i in range(NCH):
         h = x_ref[chunk(i, rows)].astype(jnp.float32) + s1.done(i)
         hid_ref[chunk(i, rows)] = h
@@ -667,9 +774,7 @@
         if i == 0:
             for s in range(1, bits):
                 ex2.step(s)
-    for deliver in delivers:
-        deliver.start()
-    far_cot = links.send(cot_hbm.at[1 - links.pair], cot, FAR, links.home)
+    s1.release()
 
     def mlp(i):
         u = dot(g1.done(i), w1[...].reshape(width, -1), NN)
@@ -691,33 +796,57 @@
         start_load(src, dst, store_sem.at[k])
         for k, (src, dst) in enumerate(((gat1, n2_hbm), (u_buf, u_hbm), (g_buf, g_hbm), (w1, w1_out), (w2, w2_out)))
     ]
-    exq, exp = Exchange(links, got_q), Exchange(links, got_p)
+    get_q.done()
+    exq.step(0)
     for i in range(NCH):
         act = (hid_ref[chunk(i, rows)] + s2.done(i)).astype(jnp.bfloat16)
         act_ref[chunk(i, rows)] = act
         g2.send(i, (normed(act.astype(jnp.float32))[0] * ln_ref[2:3] + ln_ref[3:4]).astype(jnp.bfloat16))
-    delivers[0].done()
-    exq.step(0)
-    delivers[1].done()
+    for i in range(NCH):
+        at = chunk(i, rows)
+        dy = cot_ref[at].astype(jnp.float32) * live_ref[at]
+        dy_ref[at] = dy
+        g3.send(i, dy.astype(jnp.bfloat16))
+    get_1.start()
+    get_2.start()
+    for s in range(1, bits):
+        exq.step(s)
+    get_p.done()
     exp.step(0)
     for i in range(NCH):
         g2.forward(i)
+    exq.done()
+    weight = got_q[...].reshape(width, -1)
+    for i in range(NCH):
+        part = (dot(g2.done(i), weight, NN) + term_ref[0:1]).astype(jnp.bfloat16)
+        put_rows(qkv, part, i, rows)
     for s in range(1, bits):
-        exq.step(s)
         exp.step(s)
+    stores += [
+        start_load(src, dst, store_sem.at[5 + k])
+        for k, (src, dst) in enumerate(((gat2, n1_hbm), (qkv, qkv_hbm), (got_q, next_q)))
+    ]
+    load_w.wait()
+    keys = [quarter(links.r, links.c, j) for j in order]
+
+    def block(i, carry):
+        at = pl.ds(pl.multiple_of(i * QB, QB), QB)
+        o1_ref[at] = attn_block(
+            block_quarter(links, i), keys, scale, qkv.at[at], qkv, mask_ref[...], wall, lse_ref.at[i], s_scr, p_scr
+        )
+        return carry
+
+    lax.fori_loop(0, 4, block, 0)
     for i in range(NCH):
-        g2.copies["s", i].wait_recv()
-        g2.copies["f", i].wait_recv()
-    stores.append(start_load(gat2, n1_hbm, store_sem.at[5]))
-    for k, (ex, buf, dst) in enumerate(((exq, got_q, next_q), (exp, got_p, next_p))):
-        ex.done()
-        stores.append(start_load(buf, dst, store_sem.at[6 + k]))
-    for k, (buf, dst) in enumerate(((got_1, next_1), (got_2, next_2))):
-        delivers[2 + k].done()
-        stores.append(Part(links, buf, dst, store_sem.at[8 + k]).start())
-    when(links.home, own_cot.wait)
-    when(jnp.logical_not(links.home), far_cot.wait_recv)
-    dy_ref[...] = cot[...].astype(jnp.float32) * live_ref[...]
+        g3.forward(i)
+    exp.done()
+    stores.append(start_load(got_p, next_p, store_sem.at[8]))
+    for i in range(NCH):
+        g3.copies["s", i].wait_recv()
+        g3.copies["f", i].wait_recv()
+    stores.append(start_load(gat3, dm_hbm, store_sem.at[9]))
+    get_1.done()
+    get_2.done()
     links.leave()
     for store in stores:
         store.wait()
@@ -736,68 +865,75 @@
 
 
 def params(ident):
-    return pltpu.CompilerParams(collective_id=ident, has_side_effects=True, vmem_limit_bytes=60 << 20)
-
-
-def mid_chain(x, o, ln, live, cot, wp, w1, w2, own):
+    return pltpu.CompilerParams(collective_id=ident, has_side_effects=True, vmem_limit_bytes=52 << 20)
+
+
+def mid_chain(x, o, ln, cot, live, term, mask_pad, wp, w1, w2, wall, own, order, scale):
     rows, width = x.shape
     hidden = w1.shape[-1]
     bits = w1.ndim - 2
+    heads = wall.shape[0]
+    wide = own[0].shape[-1]
     bf16, f32 = jnp.bfloat16, jnp.float32
     out = jax.ShapeDtypeStruct
     res = pl.pallas_call(
-        functools.partial(mid_kernel, bits),
-        in_specs=[VM] * 4 + [HB] * 8,
-        out_specs=[VM] * 3 + [HB] * 10,
+        functools.partial(mid_kernel, order, scale, bits),
+        in_specs=[VM] * 7 + [HB] * 8,
+        out_specs=[VM] * 5 + [HB] * 12,
         out_shape=[
             out((rows, width), f32),
             out((rows, width), bf16),
             out((rows, width), f32),
+            out((4 * rows, heads * HD), bf16),
+            out((4, heads, QB), f32),
             out((4, rows, width), bf16),
             out((4 * rows, hidden), bf16),
             out((4 * rows, hidden), bf16),
             out((4, rows, width), bf16),
+            out((4 * rows, wide), bf16),
+            out((4, rows, width), bf16),
         ]
         + [out(w.shape, bf16) for w in (w1, w2, *own)],
         scratch_shapes=[
-            *[pltpu.VMEM(w.shape, bf16) for w in (wp, w1, w2, *own)],
-            pltpu.VMEM((rows, width), bf16),
+            *[pltpu.VMEM(w.shape, bf16) for w in (wp, w1, w2, *own[:2])],
+            pltpu.VMEM(wall.shape, f32),
             pltpu.VMEM((4 * rows, hidden), bf16),
             pltpu.VMEM((4 * rows, hidden), bf16),
+            pltpu.VMEM((4 * rows, wide), bf16),
+            pltpu.VMEM((4, rows, width), bf16),
             pltpu.VMEM((4, rows, width), bf16),
             pltpu.VMEM((4, rows, width), bf16),
             *scatter_scratch(rows, width),
-            *scatter_scratch(rows, width),
-            pltpu.SemaphoreType.DMA((8,)),
+            pltpu.VMEM((2, 4 * rows, QB), f32),
+            pltpu.VMEM((2, 4 * rows, QB), bf16),
+            pltpu.SemaphoreType.DMA((6,)),
             pltpu.SemaphoreType.DMA((10,)),
-            *comm_scratch(
-                2 * Scatter.COPIES + 2 * Gather.COPIES + 4 * Deliver.COPIES + 4 * Exchange.copies(bits) + 1
-            ),
+            *comm_scratch(2 * Scatter.COPIES + 3 * Gather.COPIES + 4 * Deliver.COPIES + 4 * Exchange.copies(bits)),
         ],
         compiler_params=params(1),
         cost_estimate=pl.CostEstimate(flops=60 << 30, bytes_accessed=24 << 20, transcendentals=0),
-    )(x, o, ln, live, cot, wp, w1, w2, *own)
-    hid, act, dy, n2, u, g, n1 = res[:7]
-    return hid, act, dy, n2.reshape(4 * rows, width), u, g, n1.reshape(4 * rows, width), res[7:9], res[9:]
-
-
-def turn_kernel(bits, x_ref, o_ref, dy_ref, ln_ref, dm_hbm, wp_hbm, w1_hbm, w2_hbm,
-                dh_ref, norm_ref, y_hbm, hid_ref, do_ref, da_hbm, gfc_hbm,
-                wp, w1, w2, dm, g_buf, du_buf, y_buf, gfc, gat1, gat2, low1, wide1, low2, wide2,
-                load_sem, store_sem, send_sem, recv_sem):
+    )(x, o, ln, cot, live, term, mask_pad, wp, w1, w2, wall, *own)
+    hid, act, dy, o1, lse, n2, u, g, n1, qkv, dm = res[:11]
+    rest = lambda v: v.reshape(4 * rows, width)
+    return hid, act, dy, o1, lse, rest(n2), u, g, rest(n1), qkv, rest(dm), res[11:13], res[13:]
+
+
+def turn_kernel(bits, fold, x_ref, o_ref, dy_ref, ln_ref, dm_hbm, wp_hbm, own1, own2, got1, got2,
+                dh_ref, norm_ref, hid_ref, do_ref, fc2_ref, y_hbm, da_hbm, fc1_hbm,
+                wp, w1, w2, dm, g_buf, du_buf, y_buf, fc1, fc2, gat1, gat2, low, wide, *refs):
+    lands, (load_sem, store_sem, send_sem, recv_sem) = refs[:-4], refs[-4:]
     rows, width = x_ref.shape
     n = rows // NCH
-    hidden = w1.shape[-1]
     links = Links(send_sem, recv_sem, bits)
     loads = [
         start_load(wp_hbm, wp, load_sem.at[0]),
-        Part(links, w1_hbm, w1, load_sem.at[1]).start(),
-        Part(links, w2_hbm, w2, load_sem.at[2]).start(),
+        Part(links, 1, own1, got1, w1, load_sem.at[1]).start(),
+        Part(links, 1, own2, got2, w2, load_sem.at[2]).start(),
         start_load(dm_hbm, dm, load_sem.at[3]),
     ]
     links.enter()
     ex1, ex2 = Exchange(links, w1), Exchange(links, w2)
-    s1, s2 = Scatter(links, low1, wide1), Scatter(links, low2, wide2)
+    s1, s2 = Scatter(links, low, wide), Scatter(links, low, wide)
     g1, g2 = Gather(links, gat1), Gather(links, gat2)
     loads[0].wait()
     for i in range(NCH):
@@ -817,6 +953,7 @@
         if i == 0:
             for s in range(1, bits):
                 ex2.step(s)
+    s1.release()
     loads[3].wait()
 
     def mlp(i):
@@ -836,7 +973,10 @@
     s2.middle(0)
     mlp(1)
     s2.middle(1)
-    weight_grad(gfc, hidden, dm[...], g_buf[...])
+    slab_grad(fc2, 0, dm[...], g_buf[...])
+    if fold:
+        reduce = DpReduce(links, fc2, *lands)
+        reduce.start()
     sums = None
     for i in range(NCH):
         at = chunk(i, rows)
@@ -847,104 +987,153 @@
         both = jnp.concatenate([dgain, dshift], axis=0)
         sums = both if sums is None else sums + both
     norm_ref[...] = sums
-    weight_grad(gfc, 0, flat(gat1), du_buf[...])
-    stores = [start_load(gfc, gfc_hbm, store_sem.at[0])]
+    slab_grad(fc1, 0, flat(gat1), du_buf[...])
+    stores = [start_load(fc1, fc1_hbm, store_sem.at[0])]
+    g2.forward(0)
     for b in range(4):
-        y_buf[pl.ds(b * rows, rows)] = dot(g_buf[pl.ds(b * rows, rows)], w2[...].reshape(width, -1), NT).astype(jnp.bfloat16)
+        y = dot(g_buf[pl.ds(b * rows, rows)], w2[...].reshape(width, -1), NT)
+        y_buf[pl.ds(b * rows, rows)] = y.astype(jnp.bfloat16)
     stores.append(start_load(y_buf, y_hbm, store_sem.at[1]))
+    if fold:
+        reduce.middle()
+    g2.forward(1)
     for i in range(NCH):
-        g2.forward(i)
         put_rows(do_ref, dot(g2.done(i), wp[...], NN).astype(jnp.bfloat16), i, rows)
     stores.append(start_load(gat2, da_hbm, store_sem.at[2]))
+    if fold:
+        reduce.done(fc2_ref)
+    else:
+        fc2_ref[...] = fc2[...]
     links.leave()
     for store in stores:
         store.wait()
 
 
-def turn_chain(x, o, dy, ln, dm, wp, w1, w2):
+def turn_chain(ndp, x, o, dy, ln, dm, wp, own, got):
     rows, width = x.shape
-    hidden = w1.shape[-1]
-    bits = w1.ndim - 2
+    hidden = own[0].shape[-1]
+    bits = own[0].ndim - 2
+    fold = ndp == 4
     lw = wp.shape[1]
+    n = width // 4
     bf16, f32 = jnp.bfloat16, jnp.float32
     out = jax.ShapeDtypeStruct
     res = pl.pallas_call(
-        functools.partial(turn_kernel, bits),
-        in_specs=[VM, VM, VM, VM, HB, HB, HB, HB],
-        out_specs=[VM, VM, HB, VM, VM, HB, HB],
+        functools.partial(turn_kernel, bits, fold),
+        in_specs=[VM, VM, VM, VM] + [HB] * 6,
+        out_specs=[VM] * 5 + [HB] * 3,
         out_shape=[
             out((rows, width), f32),
             out((2, width), f32),
-            out((4 * rows, width), bf16),
             out((rows, width), f32),
             out((4 * rows, lw), bf16),
+            out((n, hidden) if fold else (2, 2, n, hidden), bf16),
+            out((4 * rows, width), bf16),
             out((4, rows, width), bf16),
-            out((width, 2 * hidden), bf16),
+            out((2, 2, n, hidden), bf16),
         ],
         scratch_shapes=[
             pltpu.VMEM(wp.shape, bf16),
-            pltpu.VMEM(w1.shape, bf16),
-            pltpu.VMEM(w2.shape, bf16),
+            pltpu.VMEM(own[0].shape, bf16),
+            pltpu.VMEM(own[1].shape, bf16),
             pltpu.VMEM((4 * rows, width), bf16),
             pltpu.VMEM((4 * rows, hidden), bf16),
             pltpu.VMEM((4 * rows, hidden), bf16),
             pltpu.VMEM((4 * rows, width), bf16),
-            pltpu.VMEM((width, 2 * hidden), bf16),
+            pltpu.VMEM((2, 2, n, hidden), bf16),
+            pltpu.VMEM((2, 2, n, hidden), bf16),
             pltpu.VMEM((4, rows, width), bf16),
             pltpu.VMEM((4, rows, width), bf16),
             *scatter_scratch(rows, width),
-            *scatter_scratch(rows, width),
+            *(DpReduce.scratch(n, hidden) if fold else []),
             pltpu.SemaphoreType.DMA((4,)),
             pltpu.SemaphoreType.DMA((3,)),
-            *comm_scratch(2 * Scatter.COPIES + 2 * Gather.COPIES + 2 * Exchange.copies(bits)),
+            *comm_scratch(2 * Scatter.COPIES + 2 * Gather.COPIES + 2 * Exchange.copies(bits) + DpReduce.COPIES),
         ],
         compiler_params=params(2),
         cost_estimate=pl.CostEstimate(flops=60 << 30, bytes_accessed=24 << 20, transcendentals=0),
-    )(x, o, dy, ln, dm, wp, w1, w2)
-    dh, norms, y, hid, do, da, gfc = res
-    return dh, norms, y, hid, do, da.reshape(4 * rows, width), gfc
-
-
-def back_kernel(x_ref, dh1_ref, hid_ref, ln_ref, dqkv_ref, wq_hbm, wp_hbm, w1_hbm, w2_hbm, u_hbm, g_hbm, n2_hbm,
-                gin_ref, dh_ref, norm_ref, do_ref, da_hbm, gfc_hbm,
-                wq, wp, w1, w2, u_buf, g_buf, n2, du_buf, gfc, gat1, gat2, low1, wide1, low2, wide2,
-                load_sem, store_sem, send_sem, recv_sem):
-    rows = x_ref.shape[0]
+    )(x, o, dy, ln, dm, wp, *own, *got)
+    dh, norms, hid, do, fc2, y, da, fc1 = res
+    return dh, norms, y, hid, do, da.reshape(4 * rows, width), fc1, fc2
+
+
+def back_kernel(bits, fold, layers, flags_ref, x_ref, dh1_ref, hid_ref, ln_ref, dqkv_ref, o1_ref, lab_ref,
+                wq_hbm, wp_hbm, w1_hbm, w2_hbm, u_hbm, g_hbm, n2_hbm, n1_hbm, da1_hbm, dwall_hbm, *refs):
+    refs = list(refs)
+    take = lambda k: [refs.pop(0) for _ in range(k)]
+    blocks = take(len(layers))
+    gin_ref, dh_ref, norm_ref, do_ref, da_hbm, fc1_hbm, fc2_out, qp_out, rel_out, sum_out = take(10)
+    places = [take(2) for _ in range(len(layers) + 1)]
+    wq, wp, w1, w2, u_buf, g_buf, fc2, gqp, strips, gin_low, gat1, gat2, low, wide = take(14)
+    if fold:
+        lands_qp, lands_fc = take(3), take(3)
+    load_sem, store_sem, send_sem, recv_sem = refs
+    small, out_lab = flags_ref[0], flags_ref[1]
+    rows, width = x_ref.shape
     n = rows // NCH
     hidden = w1.shape[1]
-    loads = [
-        start_load(src, dst, load_sem.at[k])
-        for k, (src, dst) in enumerate(
-            ((wq_hbm, wq), (w1_hbm, w1), (w2_hbm, w2), (u_hbm, u_buf), (g_hbm, g_buf), (n2_hbm, n2), (wp_hbm, wp))
-        )
-    ]
-    links = Links(send_sem, recv_sem)
+    heads = rel_out.shape[0]
+    lw = o1_ref.shape[1]
+    load = lambda k, src, dst: start_load(src, dst, load_sem.at[k])
+    load_q, load_n1, load_da = load(0, wq_hbm, wq), load(1, n1_hbm, u_buf), load(2, da1_hbm, g_buf)
+    load_1, load_2, load_p = load(3, w1_hbm, w1), load(4, w2_hbm, w2), load(5, wp_hbm, wp)
+    load_strip = load(6, dwall_hbm.at[0], strips)
+    links = Links(send_sem, recv_sem, bits)
     links.enter()
-    s1, s2 = Scatter(links, low1, wide1), Scatter(links, low2, wide2)
+    blocks.append(gin_low)
+    layers = layers + [1]
+    returns = [Return(links, layer, src, *at) for layer, src, at in zip(layers, blocks, places)]
+    for back in returns[:-1]:
+        back.start()
+    s1, s2 = Scatter(links, low, wide), Scatter(links, low, wide)
     g1, g2 = Gather(links, gat1), Gather(links, gat2)
-    loads[0].wait()
+    load_q.wait()
     for i in range(NCH):
         scatter_product(s1, i, lambda b: block_rows(dqkv_ref, b, i, rows), wq[...], rows)
         if i:
             s1.middle(i - 1)
     s1.middle(NCH - 1)
+    load_n1.wait()
+    slab_grad(gqp, 0, u_buf[...], dqkv_ref[...])
+    load_da.wait()
+    slab_grad(gqp, dqkv_ref.shape[1], g_buf[...], o1_ref[...])
+    load_u, load_g = load(8, u_hbm, u_buf), load(9, g_hbm, g_buf)
+    if fold:
+        reduce = DpReduce(links, gqp, *lands_qp)
+        reduce.start()
+    cols = jnp.sum(dqkv_ref[...].astype(jnp.float32), axis=0, keepdims=True)
+    sum_out[...] = jnp.concatenate([cols[:, :lw], cols[:, 2 * lw :]], axis=1)
     sums1 = None
     for i in range(NCH):
         at = chunk(i, rows)
         dx, dgain, dshift = norm_back(x_ref[at].astype(jnp.float32), s1.done(i), ln_ref[0:1])
         gin = dh1_ref[at] + dx
         gin_ref[at] = gin
-        g1.send(i, gin.astype(jnp.bfloat16))
+        gin_low[at] = gin.astype(jnp.bfloat16)
+        g1.send(i, gin_low[at])
         both = jnp.concatenate([dgain, dshift], axis=0)
         sums1 = both if sums1 is None else sums1 + both
-    for load in loads[1:]:
-        load.wait()
+    returns[-1].start()
+    lab = lab_ref[...]
+    hi_mask, lo_hot = _labels_hi_lo(lab)
+
+    def bias_head(h, load_strip):
+        load_strip.wait()
+        rel_out[h] = wall_grad(small, out_lab, lab, hi_mask, lo_hot, strips)
+        return load(6, dwall_hbm.at[h + 1], strips) if h + 1 < heads else None
+
+    load_strip = bias_head(0, load_strip)
+    load_strip = bias_head(1, load_strip)
+    s1.release()
+    load_1.wait()
+    load_2.wait()
+    load_u.wait()
 
     def mlp(i):
         dmi = g1.done(i)
         ui = jnp.concatenate([block_rows(u_buf, b, i, rows) for b in range(4)], axis=0).astype(jnp.float32)
         du = (dot(dmi, w2[...], NN) * gelu_both(ui)[1]).astype(jnp.bfloat16)
-        put_rows(du_buf, du, i, rows)
+        put_rows(u_buf, du, i, rows)
         scatter_product(s2, i, lambda b: du[b * n : (b + 1) * n], w1[...], rows)
 
     g1.forward(0)
@@ -953,7 +1142,14 @@
     s2.middle(0)
     mlp(1)
     s2.middle(1)
-    weight_grad(gfc, hidden, flat(gat1), g_buf[...])
+    if fold:
+        reduce.middle()
+    load_g.wait()
+    slab_grad(fc2, 0, flat(gat1), g_buf[...])
+    if fold:
+        reduce_2 = DpReduce(links, fc2, *lands_fc)
+        reduce_2.start()
+    load_n2 = load(10, n2_hbm, g_buf)
     sums2 = None
     for i in range(NCH):
         at = chunk(i, rows)
@@ -964,35 +1160,63 @@
         both = jnp.concatenate([dgain, dshift], axis=0)
         sums2 = both if sums2 is None else sums2 + both
     norm_ref[...] = jnp.concatenate([sums1, sums2], axis=0)
-    weight_grad(gfc, 0, flat(n2), du_buf[...])
-    stores = [start_load(gfc, gfc_hbm, store_sem.at[0])]
+    load_n2.wait()
+    weight_grad(w2, 0, g_buf[...], u_buf[...])
+    stores = [start_load(w2, fc1_hbm, store_sem.at[0])]
+    load_strip = bias_head(2, load_strip)
+    load_p.wait()
+    g2.forward(0)
+    bias_head(3, load_strip)
+    g2.forward(1)
     for i in range(NCH):
-        g2.forward(i)
         put_rows(do_ref, dot(g2.done(i), wp[...], NN).astype(jnp.bfloat16), i, rows)
-    stores.append(start_load(gat2, da_hbm, store_sem.at[1]))
+    stores.append(start_load(gat2, da_hbm, store_sem.at[2]))
+    if fold:
+        reduce_2.middle()
+        reduce.done(qp_out)
+        reduce_2.done(fc2_out)
+    else:
+        qp_out[...] = gqp[...]
+        fc2_out[...] = fc2[...]
+    for back in returns:
+        back.done()
     links.leave()
     for store in stores:
         store.wait()
 
 
-def back_chain(x, dh1, hid, ln, dqkv, wq, wp, w1, w2, u, g, n2):
+def back_chain(ndp, flags, x, dh1, hid, ln, dqkv, o1, lab, wq, wp, w1, w2, u, g, n2, n1, da1, dwall, returns):
     rows, width = x.shape
     hidden = w1.shape[1]
     lw = wp.shape[1]
+    heads = dwall.shape[0]
+    fold = ndp == 4
+    bits = 2
+    n = width // 4
+    qp_cols = wq.shape[1] + lw
     bf16, f32 = jnp.bfloat16, jnp.float32
     out = jax.ShapeDtypeStruct
+    layers = [layer for layer, _ in returns]
+    blocks = [block for _, block in returns]
+    copies = 2 * Scatter.COPIES + 2 * Gather.COPIES + 2 * DpReduce.COPIES + (len(layers) + 1) * Return.COPIES
     res = pl.pallas_call(
-        back_kernel,
-        in_specs=[VM] * 5 + [HB] * 7,
-        out_specs=[VM, VM, VM, VM, HB, HB],
+        functools.partial(back_kernel, bits, fold, layers),
+        in_specs=[pl.BlockSpec(memory_space=pltpu.SMEM)] + [VM] * 7 + [HB] * (10 + len(blocks)),
+        out_specs=[VM, VM, VM, VM, HB, HB, VM, VM, VM, VM] + [HB] * (2 * len(blocks) + 2),
         out_shape=[
             out((rows, width), f32),
             out((rows, width), f32),
             out((4, width), f32),
             out((4 * rows, lw), bf16),
             out((4, rows, width), bf16),
-            out((width, 2 * hidden), bf16),
-        ],
+            out((width, hidden), bf16),
+            out((n, hidden) if fold else (2, 2, n, hidden), bf16),
+            out((n, qp_cols) if fold else (2, 2, n, qp_cols), bf16),
+            out((heads, 64, 64), f32),
+            out((1, 2 * lw), f32),
+        ]
+        + [out(block.shape, block.dtype) for block in blocks for _ in range(2)]
+        + [out((rows, width), bf16)] * 2,
         scratch_shapes=[
             pltpu.VMEM(wq.shape, bf16),
             pltpu.VMEM(wp.shape, bf16),
@@ -1000,29 +1224,31 @@
             pltpu.VMEM(w2.shape, bf16),
             pltpu.VMEM((4 * rows, hidden), bf16),
             pltpu.VMEM((4 * rows, hidden), bf16),
-            pltpu.VMEM((4 * rows, width), bf16),
-            pltpu.VMEM((4 * rows, hidden), bf16),
-            pltpu.VMEM((width, 2 * hidden), bf16),
+            pltpu.VMEM((2, 2, n, hidden), bf16),
+            pltpu.VMEM((2, 2, n, qp_cols), bf16),
+            pltpu.VMEM(dwall.shape[1:], f32),
+            pltpu.VMEM((rows, width), bf16),
             pltpu.VMEM((4, rows, width), bf16),
             pltpu.VMEM((4, rows, width), bf16),
             *scatter_scratch(rows, width),
-            *scatter_scratch(rows, width),
-            pltpu.SemaphoreType.DMA((7,)),
-            pltpu.SemaphoreType.DMA((2,)),
-            *comm_scratch(2 * Scatter.COPIES + 2 * Gather.COPIES),
+            *(DpReduce.scratch(n, qp_cols) + DpReduce.scratch(n, hidden) if fold else []),
+            pltpu.SemaphoreType.DMA((11,)),
+            pltpu.SemaphoreType.DMA((3,)),
+            *comm_scratch(copies),
         ],
         compiler_params=params(3),
         cost_estimate=pl.CostEstimate(flops=60 << 30, bytes_accessed=24 << 20, transcendentals=0),
-    )(x, dh1, hid, ln, dqkv, wq, wp, w1, w2, u, g, n2)
-    gin, dh, norms, do, da, gfc = res
-    return gin, dh, norms, do, da.reshape(4 * rows, width), gfc
-
-
-def start_kernel(order, scale, bits, flags_ref, x_hbm, mask_ref, lab_ref, tab_hbm, pack_hbm,
+    )(flags, x, dh1, hid, ln, dqkv, o1, lab, wq, wp, w1, w2, u, g, n2, n1, da1, dwall, *blocks)
+    gin, dh, norms, do, da, fc1, fc2, qp, rel, sums = res[:10]
+    got = [(res[10 + 2 * k], res[11 + 2 * k]) for k in range(len(layers) + 1)]
+    return gin, dh, norms, do, da.reshape(4 * rows, width), fc1, fc2, qp, rel, sums, got
+
+
+def start_kernel(order, scale, bits, flags_ref, x_hbm, cot_hbm, mask_ref, lab_ref, tab_hbm, pack_hbm,
                  wq_hbm, wp_hbm, w1_hbm, w2_hbm,
-                 x_ref, pack_ref, lse_ref, o_ref, n1_hbm, qkv_hbm, wall0_hbm, wall1_hbm,
+                 x_ref, cot_ref, pack_ref, lse_ref, o_ref, n1_hbm, qkv_hbm, wall0_hbm, wall1_hbm,
                  wq0_hbm, wp0_hbm, w10_hbm, w20_hbm,
-                 tab, wq, wp, w1, w2, qkv, wall, gat1, s_scr, p_scr, load_sem, store_sem, send_sem, recv_sem):
+                 tab, wq, wp, qkv, wall, gat1, s_scr, p_scr, load_sem, store_sem, send_sem, recv_sem):
     small, out_lab = flags_ref[0], flags_ref[1]
     rows, width = x_ref.shape
     wide = qkv.shape[1]
@@ -1031,18 +1257,34 @@
     pair, home = links.pair, links.home
     own_x = pltpu.make_async_copy(x_hbm.at[pair], x_ref, load_sem.at[0])
     when(home, own_x.start)
+    own_cot = pltpu.make_async_copy(cot_hbm.at[pair], cot_ref, load_sem.at[7])
+    when(home, own_cot.start)
     links.enter()
-    far_x = links.send(x_hbm.at[1 - pair], x_ref, FAR, home)
     packs = [Spread(links, l, pack_hbm, pack_ref.at[l], load_sem.at[1 + l]) for l in range(2)]
     tabs = [Spread(links, l, tab_hbm, tab.at[l], load_sem.at[3 + l]) for l in range(2)]
-    for spread in packs + tabs:
-        spread.start()
+    tabs[0].start()
+    packs[0].start()
+    far_x = links.send(x_hbm.at[1 - pair], x_ref, FAR, home)
+    tabs[1].start()
+    packs[1].start()
     get_q = Deliver(links, 0, wq_hbm, wq, load_sem.at[5])
     get_p = Deliver(links, 0, wp_hbm, wp, load_sem.at[6])
-    get_1 = Deliver(links, 0, w1_hbm, w1, load_sem.at[7])
-    get_2 = Deliver(links, 0, w2_hbm, w2, load_sem.at[8])
+    get_1, get_2 = Deliver(links, 0, w1_hbm, w10_hbm), Deliver(links, 0, w2_hbm, w20_hbm)
     ex_q, ex_p = Exchange(links, wq), Exchange(links, wp)
     get_q.start()
+    lab = lab_ref[...]
+    hi_mask, lo_hot = _labels_hi_lo(lab)
+
+    def build(l):
+        def one(h, carry):
+            build_wall(small, out_lab, lab, hi_mask, lo_hot, tab[l, h], wall.at[l, h])
+            return carry
+
+        lax.fori_loop(0, heads, one, 0)
+
+    tabs[0].done()
+    build(0)
+    stores = [start_load(wall.at[0], wall0_hbm, store_sem.at[0])]
     packs[0].done()
     when(home, own_x.wait)
     when(jnp.logical_not(home), far_x.wait_recv)
@@ -1054,19 +1296,10 @@
     get_p.start()
     get_1.start()
     get_2.start()
-    lab = lab_ref[...]
-    hi_mask, lo_hot = _labels_hi_lo(lab)
-
-    def build(l):
-        def one(h, carry):
-            build_wall(small, out_lab, lab, hi_mask, lo_hot, tab[l, h], wall.at[l, h])
-            return carry
-
-        lax.fori_loop(0, heads, one, 0)
-
-    tabs[0].done()
-    build(0)
-    stores = [start_load(wall.at[0], wall0_hbm, store_sem.at[0])]
+    far_cot = links.send(cot_hbm.at[1 - pair], cot_ref, FAR, home)
+    tabs[1].done()
+    build(1)
+    stores.append(start_load(wall.at[1], wall1_hbm, store_sem.at[5]))
     get_q.done()
     ex_q.step(0)
     for i in range(NCH):
@@ -1102,30 +1335,29 @@
     lax.fori_loop(0, 4, block, 0)
     ex_p.done()
     stores.append(start_load(wp, wp0_hbm, store_sem.at[4]))
-    tabs[1].done()
-    build(1)
-    stores.append(start_load(wall.at[1], wall1_hbm, store_sem.at[5]))
-    for k, (get, src, dst) in enumerate(((get_1, w1, w10_hbm), (get_2, w2, w20_hbm))):
-        get.done()
-        stores.append(Part(links, src, dst, store_sem.at[6 + k]).start())
+    get_1.done()
+    get_2.done()
+    when(home, own_cot.wait)
+    when(jnp.logical_not(home), far_cot.wait_recv)
     links.leave()
     for store in stores:
         store.wait()
 
 
-def start_chain(flags, x, mask_pad, lab, table, pack, wq, wp, w1, w2, order, scale):
+def start_chain(flags, x, cot, mask_pad, lab, table, pack, wq, wp, w1, w2, order, scale):
     bits = wq.ndim - 2
     _, rows, width = x.shape
     heads = table.shape[0]
     wide = wq.shape[-1]
     bf16, f32 = jnp.bfloat16, jnp.float32
     out = jax.ShapeDtypeStruct
-    copies = 1 + 4 * Spread.COPIES + 4 * Deliver.COPIES + 2 * Exchange.copies(bits) + Gather.COPIES
+    copies = 2 + 4 * Spread.COPIES + 4 * Deliver.COPIES + 2 * Exchange.copies(bits) + Gather.COPIES
     return pl.pallas_call(
         functools.partial(start_kernel, order, scale, bits),
-        in_specs=[pl.BlockSpec(memory_space=pltpu.SMEM), HB, VM, VM, HB, HB, HB, HB, HB, HB],
-        out_specs=[VM] * 4 + [HB] * 8,
+        in_specs=[pl.BlockSpec(memory_space=pltpu.SMEM), HB, HB, VM, VM, HB, HB, HB, HB, HB, HB],
+        out_specs=[VM] * 5 + [HB] * 8,
         out_shape=[
+            out((rows, width), bf16),
             out((rows, width), bf16),
             out((2,) + pack.shape, f32),
             out((4, heads, QB), f32),
@@ -1138,19 +1370,428 @@
         ],
         scratch_shapes=[
             pltpu.VMEM((2,) + table.shape, f32),
-            *[pltpu.VMEM(w.shape, bf16) for w in (wq, wp, w1, w2)],
+            *[pltpu.VMEM(w.shape, bf16) for w in (wq, wp)],
             pltpu.VMEM((4 * rows, wide), bf16),
             pltpu.VMEM((2, heads, 32, WALL), f32),
             pltpu.VMEM((4, rows, width), bf16),
             pltpu.VMEM((2, 4 * rows, QB), f32),
             pltpu.VMEM((2, 4 * rows, QB), bf16),
-            pltpu.SemaphoreType.DMA((9,)),
             pltpu.SemaphoreType.DMA((8,)),
+            pltpu.SemaphoreType.DMA((6,)),
             *comm_scratch(copies),
         ],
         compiler_params=params(0),
         cost_estimate=pl.CostEstimate(flops=80 << 30, bytes_accessed=24 << 20, transcendentals=0),
-    )(flags, x, mask_pad, lab, table, pack, wq, wp, w1, w2)
+    )(flags, x, cot, mask_pad, lab, table, pack, wq, wp, w1, w2)
+
+
+def attn_back(links, order, scale, qkv_ref, do_ref, o_ref, lse_ref, k_extra, wall, acc, p_scr, s_scr, dq_scr, dk_scr, dv_scr,
+              dqkv_ref, event):
+    heads = wall.shape[0]
+    width = heads * HD
+    total = qkv_ref.shape[0]
+    keys = [quarter(links.r, links.c, j) for j in order]
+    lane = lax.broadcasted_iota(jnp.int32, (QB, 128 - HD), 1)
+    q_extra = jnp.where(lane == 0, 1.0, 0.0).astype(jnp.bfloat16)
+
+    def block(i, carry):
+        at = pl.ds(pl.multiple_of(i * QB, QB), QB)
+        q_ref, d_ref, out_ref = qkv_ref.at[at], do_ref.at[at], o_ref.at[at]
+        qq = block_quarter(links, i)
+        dqs = []
+        for h in range(heads):
+            kh = head_lanes(qkv_ref, width + HD * h, k_extra)
+            qh = head_lanes(q_ref, HD * h, q_extra)
+            vh = head_lanes(qkv_ref, 2 * width + HD * h)
+            doh = head_lanes(d_ref, HD * h)
+            oh = head_lanes(out_ref, HD * h)
+            inner = jnp.sum((doh.astype(jnp.float32) * oh.astype(jnp.float32)).T, axis=0, keepdims=True)
+            lse = lse_ref[i, h : h + 1, :]
+            for kb in range(total // 256):
+                s_t = dot(kh[256 * kb : 256 * kb + 256], qh, NT)
+                dp_t = dot(vh[256 * kb : 256 * kb + 256], doh, NT)
+                for js in range(8):
+                    st = 8 * kb + js
+                    start = strip_start(qq, js, keys[kb])
+                    s = s_t[32 * js : 32 * js + 32] * (scale * LOG2E) + wall[h, :, pl.ds(start, QB)]
+                    p = jnp.exp2(s - lse)
+                    ds = p * (dp_t[32 * js : 32 * js + 32] - inner)
+                    p_scr[h % 2, 32 * st : 32 * st + 32] = p.astype(jnp.bfloat16)
+                    s_scr[h % 2, 32 * st : 32 * st + 32] = ds.astype(jnp.bfloat16)
+                    acc[h, :, pl.ds(start, QB)] += ds
+            p_b, ds_b = p_scr[h % 2], s_scr[h % 2]
+            dv_scr[h] += dot(p_b, doh, NN)
+            dk_scr[h] += dot(ds_b, qh, NN)
+            dq_t = dot(kh, ds_b, TN) * scale
+            dqs.append(dq_t.T[:, :HD].astype(jnp.bfloat16))
+        dq_scr[at] = jnp.concatenate(dqs, axis=1)
+        event(i)
+        return carry
+
+    lax.fori_loop(0, total // QB, block, 0)
+    parts = [dq_scr[...]]
+    parts += [(dk_scr[h, :, :HD] * scale).astype(jnp.bfloat16) for h in range(heads)]
+    parts += [dv_scr[h, :, :HD].astype(jnp.bfloat16) for h in range(heads)]
+    dqkv_ref[...] = jnp.concatenate(parts, axis=1)
+
+
+def bwd_kernel(order, scale, bits, fold, layers, summed, qkv_ref, do_ref, o_ref, lse_ref, mask_ref, wall_hbm, gfc_hbm, *refs):
+    refs = list(refs)
+    take = lambda k: [refs.pop(0) for _ in range(k)]
+    blocks = take(len(layers))
+    y_ref, hid_ref = take(2) if summed else (None, None)
+    dqkv_ref, acc_hbm = take(2)
+    (fc_out,) = take(1) if fold else (None,)
+    places = [take(2) for _ in layers]
+    (act_ref,) = take(1) if summed else (None,)
+    wall, acc, p_scr, s_scr, dq_scr, dk_scr, dv_scr = take(7)
+    if fold:
+        gfc, land0, land1, sent = take(4)
+    if summed:
+        (low,) = take(1)
+    load_sem, store_sem, send_sem, recv_sem = refs
+    loads = [start_load(wall_hbm, wall, load_sem.at[0])]
+    if fold:
+        loads.append(start_load(gfc_hbm, gfc, load_sem.at[1]))
+    links = Links(send_sem, recv_sem, bits)
+    links.enter()
+    returns = [Return(links, layer, src, *at) for layer, src, at in zip(layers, blocks, places)]
+    if fold:
+        reduce = DpReduce(links, gfc, land0, land1, sent)
+    if summed:
+        rows = hid_ref.shape[0]
+        part = lambda b: y_ref.at[pl.ds(b * rows, rows)]
+        to_sib = links.make(part(3), low.at[0], SIBLING)
+        near = links.make(part(1), low.at[1], SIBLING)
+        to_partner = links.make(low.at[2], low.at[3], PARTNER)
+        to_sib.start()
+        near.start()
+    acc[...] = jnp.zeros_like(acc)
+    dk_scr[...] = jnp.zeros_like(dk_scr)
+    dv_scr[...] = jnp.zeros_like(dv_scr)
+    if fold:
+        loads[1].wait()
+        reduce.start()
+    if summed:
+        to_sib.wait_recv()
+        low[2] = (part(2)[...].astype(jnp.float32) + low[0].astype(jnp.float32)).astype(jnp.bfloat16)
+        to_partner.start()
+    for back in returns:
+        back.start()
+    loads[0].wait()
+
+    def event(i):
+        if fold:
+            pl.when(i == 2)(lambda: reduce.middle())
+
+    attn_back(
+        links, order, scale, qkv_ref, do_ref, o_ref, lse_ref, mask_ref[...], wall, acc, p_scr, s_scr, dq_scr, dk_scr, dv_scr,
+        dqkv_ref, event,
+    )
+    stores = [start_load(acc, acc_hbm, store_sem.at[0])]
+    if summed:
+        near.wait_recv()
+        to_partner.wait_recv()
+        act = hid_ref[...] + part(0)[...].astype(jnp.float32) + low[1].astype(jnp.float32) + low[3].astype(jnp.float32)
+        act_ref[...] = act.astype(jnp.bfloat16)
+    if fold:
+        reduce.done(fc_out)
+    for back in returns:
+        back.done()
+    links.leave()
+    for store in stores:
+        store.wait()
+
+
+def bwd_chain(ident, fold, qkv, do, o, lse, mask_pad, wall, gfc, returns, order, scale, summed=None):
+    total, wide = qkv.shape
+    heads = wall.shape[0]
+    bits = 2
+    n, columns = gfc.shape[2:]
+    bf16, f32 = jnp.bfloat16, jnp.float32
+    out = jax.ShapeDtypeStruct
+    layers = [layer for layer, _ in returns]
+    blocks = [block for _, block in returns]
+    outs = [out((total, wide), bf16), out(wall.shape, f32)]
+    specs = [VM, HB]
+    if fold:
+        outs.append(out((n, columns), bf16))
+        specs.append(VM)
+    for block in blocks:
+        outs += [out(block.shape, block.dtype)] * 2
+        specs += [VM] * 2
+    scratch = [
+        pltpu.VMEM(wall.shape, f32),
+        pltpu.VMEM(wall.shape, f32),
+        pltpu.VMEM((2, total, QB), bf16),
+        pltpu.VMEM((2, total, QB), bf16),
+        pltpu.VMEM((total, heads * HD), bf16),
+        pltpu.VMEM((heads, total, 128), f32),
+        pltpu.VMEM((heads, total, 128), f32),
+    ]
+    if fold:
+        scratch += [pltpu.VMEM(gfc.shape, bf16), *DpReduce.scratch(n, columns)]
+    more = []
+    if summed is not None:
+        more = list(summed)
+        rows, width = summed[1].shape
+        outs.append(out((rows, width), bf16))
+        specs.append(VM)
+        scratch.append(pltpu.VMEM((4, rows, width), bf16))
+    copies = len(layers) * Return.COPIES + (DpReduce.COPIES if fold else 0) + (3 if more else 0)
+    res = pl.pallas_call(
+        functools.partial(bwd_kernel, order, scale, bits, fold, layers, bool(more)),
+        in_specs=[VM] * 5 + [HB] * 2 + [VM] * (len(blocks) + len(more)),
+        out_specs=specs,
+        out_shape=outs,
+        scratch_shapes=scratch
+        + [pltpu.SemaphoreType.DMA((2,)), pltpu.SemaphoreType.DMA((1,)), *comm_scratch(max(copies, 1))],
+        compiler_params=params(ident),
+        cost_estimate=pl.CostEstimate(flops=24 << 30, bytes_accessed=20 << 20, transcendentals=0),
+    )(qkv, do, o, lse, mask_pad, wall, gfc, *blocks, *more)
+    res = list(res)
+    dqkv, acc = res[:2]
+    res = res[2:]
+    fc = res.pop(0) if fold else None
+    got = [(res[2 * k], res[2 * k + 1]) for k in range(len(layers))]
+    act = res[-1] if more else None
+    return dqkv, acc, fc, got, act
+
+
+class SumHops:
+    def __init__(self, links, buf, land, hops):
+        self.links, self.buf, self.land, self.hops, self.k = links, buf, land, hops, 0
+
+    def send(self):
+        if self.k < len(self.hops):
+            self.copy = self.links.send(self.buf, self.land.at[self.k], self.hops[self.k], track=False)
+
+    def take(self):
+        self.copy.wait_recv()
+        self.copy.wait_send()
+        self.buf[...] = self.buf[...] + self.land[self.k]
+        self.k += 1
+        self.send()
+
+
+def end_kernel(order, scale, bits, fold, layers, flags_ref, qkv_ref, do_ref, o_ref, lse_ref, mask_ref,
+               x_ref, dh_ref, ln_ref, lab_ref, small_ref, rel1_ref,
+               wall_hbm, wq_hbm, n1_hbm, da_hbm, fc_hbm, *refs):
+    refs = list(refs)
+    take = lambda k: [refs.pop(0) for _ in range(k)]
+    blocks = take(len(layers))
+    gin_ref, norm_out, rel_out, sum_out, qp_out = take(5)
+    (fc_out,) = take(1) if fold else (None,)
+    places = [take(2) for _ in range(len(layers) + (3 if fold else 1))]
+    acc, dqkv_ref, gqp, gin_low, low1 = take(5)
+    rel, rel_land, rel_near, norms, norm_land, sums, sum_land, sum_near = take(8)
+    if fold:
+        fc, lands_q, lands_f = take(1)[0], take(3), take(3)
+    load_sem, send_sem, recv_sem = refs
+    small, out_lab = flags_ref[0], flags_ref[1]
+    rows, width = x_ref.shape
+    heads = rel.shape[1]
+    if fold:
+        load_f = start_load(fc_hbm, fc, load_sem.at[1])
+    links = Links(send_sem, recv_sem, bits)
+    home, away = links.home, jnp.logical_not(links.home)
+    links.enter()
+    give = list(zip(layers, blocks)) + [(0, gin_low)] + ([(0, fc_out), (0, qp_out)] if fold else [])
+    returns = [Return(links, layer, src, *at) for (layer, src), at in zip(give, places)]
+    early = len(layers)
+    for back in returns[:early]:
+        back.start()
+    if fold:
+        reduce_f = DpReduce(links, fc, *lands_f)
+        reduce_q = DpReduce(links, gqp, *lands_q)
+        load_f.wait()
+        reduce_f.start()
+    acc[...] = jnp.zeros_like(acc)
+
+    def event(i):
+        if fold:
+            pl.when(i == 2)(lambda: reduce_f.middle())
+
+    def attention(wall, p_scr, s_scr, dq_scr, dk_scr, dv_scr):
+        load_w = start_load(wall_hbm, wall, load_sem.at[0])
+        dk_scr[...] = jnp.zeros_like(dk_scr)
+        dv_scr[...] = jnp.zeros_like(dv_scr)
+        load_w.wait()
+        attn_back(
+            links, order, scale, qkv_ref, do_ref, o_ref, lse_ref, mask_ref[...], wall, acc, p_scr, s_scr, dq_scr, dk_scr,
+            dv_scr, dqkv_ref, event,
+        )
+
+    total = qkv_ref.shape[0]
+    vmem, bf16, f32 = pltpu.VMEM, jnp.bfloat16, jnp.float32
+    pl.run_scoped(
+        attention,
+        vmem(wall_hbm.shape, f32),
+        vmem((2, total, QB), bf16),
+        vmem((2, total, QB), bf16),
+        vmem((total, heads * HD), bf16),
+        vmem((heads, total, 128), f32),
+        vmem((heads, total, 128), f32),
+    )
+    lw = o_ref.shape[1]
+
+    def rest(wq, rows_buf, wide1):
+        s1 = Scatter(links, low1, wide1)
+        load_q = start_load(wq_hbm, wq, load_sem.at[2])
+        load_n = start_load(n1_hbm, rows_buf, load_sem.at[3])
+        load_q.wait()
+        for i in range(NCH):
+            scatter_product(s1, i, lambda b: block_rows(dqkv_ref, b, i, rows), wq[...], rows)
+            if i:
+                s1.middle(i - 1)
+        s1.middle(NCH - 1)
+        if fold:
+            reduce_f.done(fc_out)
+            returns[early + 1].start()
+        load_n.wait()
+        slab_grad(gqp, 0, rows_buf[...], dqkv_ref[...])
+        load_d = start_load(da_hbm, rows_buf, load_sem.at[4])
+        load_d.wait()
+        slab_grad(gqp, dqkv_ref.shape[1], rows_buf[...], o_ref[...])
+
+        if fold:
+            reduce_q.start()
+        hops = [("dp", b) for b in range(bits)] + [ACROSS]
+        cols = jnp.sum(dqkv_ref[...].astype(jnp.float32), axis=0, keepdims=True)
+        mine = jnp.concatenate([cols[:, :lw], cols[:, 2 * lw :]], axis=1)
+        images = sums.shape[0] // 2
+        number = 2 * lax.axis_index("dp") + links.pair
+        here = lax.broadcasted_iota(jnp.int32, (images, 2 * lw), 0) == number
+        sums[...] = small_ref[8:]
+        sums[0:images, 0 : 2 * lw] = jnp.where(here, jnp.broadcast_to(mine, (images, 2 * lw)), 0.0)
+        sum_hops = SumHops(links, sums, sum_land, hops)
+        sum_hops.send()
+        late = None
+        for i in range(NCH):
+            at = chunk(i, rows)
+            dx, dgain, dshift = norm_back(x_ref[at].astype(jnp.float32), s1.done(i), ln_ref[0:1])
+            gin = dh_ref[at] + dx
+            gin_ref[at] = gin
+            gin_low[at] = gin.astype(jnp.bfloat16)
+            both = jnp.concatenate([dgain, dshift], axis=0)
+            late = both if late is None else late + both
+        returns[early].start()
+        norms[...] = small_ref[0:8]
+        norms[0:2] = late
+        norm_hops = SumHops(links, norms, norm_land, hops + [PARTNER, SIBLING])
+        norm_hops.send()
+        lab = lab_ref[...]
+        hi_mask, lo_hot = _labels_hi_lo(lab)
+        rel[1] = rel1_ref[...]
+
+        def heads_of(a, b):
+            def one(h, carry):
+                rel[0, h] = wall_grad(small, out_lab, lab, hi_mask, lo_hot, acc.at[h])
+                return carry
+
+            lax.fori_loop(a, b, one, 0)
+
+        heads_of(0, heads // 2)
+        sum_hops.take()
+        norm_hops.take()
+        heads_of(heads // 2, heads)
+        rel_hops = SumHops(links, rel, rel_land, hops)
+        rel_hops.send()
+        if fold:
+            reduce_q.middle()
+        norm_hops.take()
+        sum_hops.take()
+        rel_hops.take()
+        if fold:
+            reduce_q.done(qp_out)
+            returns[early + 2].start()
+        else:
+            qp_out[...] = gqp[...]
+        for k in range(1, len(hops)):
+            if k + 1 < len(hops):
+                sum_hops.take()
+            rel_hops.take()
+            norm_hops.take()
+        norm_hops.take()
+        norm_out[...] = norms[...]
+        rel_copy = links.send(rel.at[1 - links.c], rel_near, SIBLING, home)
+        sum_copy = links.send(sums, sum_near, SIBLING, home)
+
+        @pl.when(home)
+        def _():
+            rel_out[...] = rel[links.c]
+            sum_out[...] = sums[...]
+
+        @pl.when(away)
+        def _():
+            rel_copy.wait_recv()
+            sum_copy.wait_recv()
+            rel_out[...] = rel_near[...]
+            sum_out[...] = sum_near[...]
+
+        for back in returns:
+            back.done()
+        links.leave()
+
+    pl.run_scoped(rest, vmem(wq_hbm.shape, bf16), vmem(n1_hbm.shape, bf16), vmem((2, rows, width), f32))
+
+
+def end_chain(ndp, flags, qkv, do, o, lse, mask_pad, x, dh, ln, lab, smalls, rel1, wall, wq, n1, da, fc, returns, order, scale):
+    rows, width = x.shape
+    heads = wall.shape[0]
+    total, wide = qkv.shape
+    bits = ndp.bit_length() - 1
+    fold = bits == 2
+    n, fc_cols = fc.shape[2:]
+    qp_cols = wide + o.shape[1]
+    images = smalls.shape[0] - 8
+    hops = bits + 1
+    bf16, f32 = jnp.bfloat16, jnp.float32
+    out = jax.ShapeDtypeStruct
+    layers = [layer for layer, _ in returns]
+    blocks = [block for _, block in returns]
+    landed = [out(block.shape, bf16) for block in blocks] + [out((rows, width), bf16)]
+    outs = [
+        out((rows, width), f32),
+        out((8, width), f32),
+        out((heads, 64, 64), f32),
+        out((images, width), f32),
+        out((n, qp_cols) if fold else (2, 2, n, qp_cols), bf16),
+    ]
+    if fold:
+        outs.append(out((n, fc_cols), bf16))
+        landed += [out((n, fc_cols), bf16), out((n, qp_cols), bf16)]
+    copies = Scatter.COPIES + (len(landed)) * Return.COPIES + 2 * DpReduce.COPIES + 3 * hops + 4
+    res = pl.pallas_call(
+        functools.partial(end_kernel, order, scale, bits, fold, layers),
+        in_specs=[pl.BlockSpec(memory_space=pltpu.SMEM)] + [VM] * 11 + [HB] * (5 + len(blocks)),
+        out_specs=[VM] * len(outs) + [HB] * (2 * len(landed)),
+        out_shape=outs + [shape for shape in landed for _ in range(2)],
+        scratch_shapes=[
+            pltpu.VMEM(wall.shape, f32),
+            pltpu.VMEM((total, wide), bf16),
+            pltpu.VMEM((2, 2, n, qp_cols), bf16),
+            pltpu.VMEM((rows, width), bf16),
+            pltpu.VMEM((6, rows, width), bf16),
+            pltpu.VMEM((2, heads, 64, 64), f32),
+            pltpu.VMEM((hops, 2, heads, 64, 64), f32),
+            pltpu.VMEM((heads, 64, 64), f32),
+            pltpu.VMEM((8, width), f32),
+            pltpu.VMEM((hops + 2, 8, width), f32),
+            pltpu.VMEM((images, width), f32),
+            pltpu.VMEM((hops, images, width), f32),
+            pltpu.VMEM((images, width), f32),
+            *([pltpu.VMEM(fc.shape, bf16)] if fold else []),
+            *(DpReduce.scratch(n, qp_cols) + DpReduce.scratch(n, fc_cols) if fold else []),
+            pltpu.SemaphoreType.DMA((5,)),
+            *comm_scratch(copies),
+        ],
+        compiler_params=params(4),
+        cost_estimate=pl.CostEstimate(flops=90 << 30, bytes_accessed=24 << 20, transcendentals=0),
+    )(flags, qkv, do, o, lse, mask_pad, x, dh, ln, lab, smalls, rel1, wall, wq, n1, da, fc, *blocks)
+    res = list(res)
+    got = [(res[len(outs) + 2 * k], res[len(outs) + 2 * k + 1]) for k in range(len(landed))]
+    return res[: len(outs)], got
 
 
 AXES = ("dp", "section", "tensor")
@@ -1294,9 +1935,9 @@
         return move(x, lambda dd, cc, zz: (dd, layer, zz ^ 2) if cc != zz // 2 else None, "d_far")
 
     live = ((t * rows + jnp.arange(rows)) < length).astype(f32)[:, None]
-    res = start_chain(flags, inputs, mask_pad, label_lanes, table, small_pack, *own, ORDER, scale)
-    x0, packs, lse0, o0, n1_0, qkv0 = res[:6]
-    walls, weights0 = res[6:8], res[8:]
+    res = start_chain(flags, inputs, cotangent, mask_pad, label_lanes, table, small_pack, *own, ORDER, scale)
+    x0, cot, packs, lse0, o0, n1_0, qkv0 = res[:7]
+    walls, got0 = res[7:9], res[9:]
     n1_0 = n1_0.reshape(seq_len, width)
 
     def whole(w):
@@ -1305,129 +1946,80 @@
     gains = [packs[l, 0:2] for l in range(2)]
     shifts = [packs[l, 2:4] for l in range(2)]
     ln_mid = jnp.stack([gains[0][1], shifts[0][1], gains[1][0], shifts[1][0]])
-    wq0, wp0 = whole(weights0[0]), whole(weights0[1])
-    hid0, act0, dy1, n2_0, u0, g0, n1_1, weights0, weights1 = mid_chain(
-        x0, o0, ln_mid, live, cotangent, wp0, weights0[2], weights0[3], own
+    wq0, wp0 = whole(got0[0]), whole(got0[1])
+    term1 = lax.dynamic_index_in_dim(packs[1], 4 + pair, 0, keepdims=True)[:, : 3 * local_width]
+    hid0, act0, dy1, o1, lse1, n2_0, u0, g0, n1_1, qkv1, dm1, fc_w0, got1 = mid_chain(
+        x0, o0, ln_mid, cot, live, term1, mask_pad, wp0, got0[2], got0[3], walls[1], own, ORDER, scale
     )
-    w10, w20 = whole(weights0[0]), whole(weights0[1])
-    wq1, wp1 = whole(weights1[0]), whole(weights1[1])
-    term1 = lax.dynamic_index_in_dim(packs[1], 4 + pair, 0, keepdims=False)[: 3 * local_width]
-    qkv1 = (jnp.dot(n1_1, wq1, preferred_element_type=f32) + term1).astype(bf16)
-    qkv1, dm1 = tie(qkv1, dy1.astype(bf16))
-    dm_far, dm_near = partner(dm1), sibling(dm1)
-    o1, lse1 = attn_fwd(qkv1, mask_pad, walls[1], scalars, ORDER, scale)
-    o1, dm1, dm_far, dm_near = tie(o1, dm1, dm_far, dm_near)
-    dm1 = jnp.concatenate([dm1, dm_near, dm_far, sibling(dm_far)], axis=0)
-
+    w10, w20 = whole(fc_w0[0]), whole(fc_w0[1])
+    wq1, wp1 = whole(got1[0]), whole(got1[1])
+
+    fold = ndp == 4
     ln_turn = jnp.stack([gains[1][1], shifts[1][1]])
-    dh1, norms1, y1, hid1, do1, da1, gfc1 = turn_chain(act0, o1, dy1, ln_turn, dm1, wp1, weights1[2], weights1[3])
-    sum_fc1 = reduced(gfc1)
-    do1, y1, a0 = tie(do1, y1, act0)
-    act1 = (hid1 + scatter_rows(y1[half:], y1[:half])).astype(bf16)
-    got_acts = [near_of(a0, 0) + near_of(act1, 1), far_of(a0, 0) + far_of(act1, 1)]
-    dqkv1, dwall1 = attn_bwd(qkv1, do1, o1, lse1, mask_pad, walls[1], scalars, ORDER, scale)
-    dqkv1, got_acts = tie(dqkv1, got_acts)
+    dh1, norms1, y1, hid1, do1, da1, fc1_1, fc2_1 = turn_chain(
+        ndp, act0, o1, dy1, ln_turn, dm1, wp1, own[2:], got1[2:]
+    )
+    give = [(0, act0)] + ([(1, fc2_1)] if fold else [])
+    dqkv1, dwall1, sum_fc1_1, landed, act1 = bwd_chain(
+        6, fold, qkv1, do1, o1, lse1, mask_pad, walls[1], fc1_1, give, ORDER, scale, (y1, hid1)
+    )
+    got_act0, got_fc2_1 = landed[0], landed[-1]
     ln_back = jnp.stack([gains[1][0], gains[0][1]])
-    gin1, dh0, norms10, do0, da0, gfc0 = back_chain(
-        act0, dh1, hid0, ln_back, dqkv1, wq1, wp0, w10, w20, u0, g0, n2_0
+    give = [(1, act1)] + ([(1, sum_fc1_1)] if fold else [])
+    gin1, dh0, norms10, do0, da0, fc1_0, fc2_0, qp1, rel1, sums1, landed = back_chain(
+        ndp, flags, act0, dh1, hid0, ln_back, dqkv1, o1, label_lanes,
+        wq1, wp0, w10, w20, u0, g0, n2_0, n1_1, da1, dwall1, give,
     )
-    sum_fc0 = reduced(gfc0)
-    sum_qp1 = reduced(jnp.concatenate([grad_of(n1_1, dqkv1), grad_of(da1, o1)], axis=1))
-    rel1 = bias_grads(flags, label_lanes, dwall1)
-    sums1 = column_sums(dqkv1)
-    do0, sum_qp1, rel1, sums1 = tie(do0, sum_qp1, rel1, sums1)
-    g1 = gin1.astype(bf16)
-    w1 = jnp.concatenate([sum_qp1, sum_fc1], axis=1)
-    do0, g1, w1 = tie(do0, g1, w1)
-    got1 = [near_of(g1, 1), far_of(g1, 1), near_of(w1, 1), far_of(w1, 1)]
-    dqkv0, dwall0 = attn_bwd(qkv0, do0, o0, lse0, mask_pad, walls[0], scalars, ORDER, scale)
-    dqkv0, got1 = tie(dqkv0, got1)
-    dn1 = scatter_rows(times_t(dqkv0[half:], wq0), times_t(dqkv0[:half], wq0))
-    grad_qp0 = jnp.concatenate([grad_of(n1_0, dqkv0), grad_of(da0, o0)], axis=1)
-    sum_qp0 = reduced_late(grad_qp0)
-    rel0 = bias_grads(flags, label_lanes, dwall0)
-    sums0 = column_sums(dqkv0)
-    dn1, grad_qp0, rel0, sums0 = tie(dn1, grad_qp0, rel0, sums0)
-    dx, dgain, dshift = norm_back(x0.astype(f32), dn1, gains[0][0])
-    gin0 = dh0 + dx
-    early0, early1, late1 = norms10[2:], norms1, norms10[:2]
-    late0 = jnp.concatenate([dgain, dshift], axis=0)
-    sums_w0, sums_w1 = (sum_qp0, sum_fc0), (sum_qp1, sum_fc1)
+    got_act1, got_fc1_1, got_gin1 = landed[0], landed[len(landed) - 2], landed[-1]
+    number = 2 * d + pair
+    sums_rows = lax.dynamic_update_slice(
+        jnp.zeros((2 * ndp, width), f32), sums1, (number, jnp.int32(width - 2 * local_width))
+    )
+    mine = lax.dynamic_index_in_dim(time_emb, pair, 0, keepdims=True).astype(f32)
+    emb_rows = lax.dynamic_update_slice(jnp.zeros((2 * ndp, width), f32), mine, (number, jnp.int32(0)))
+    smalls = jnp.concatenate(
+        [jnp.zeros((2, width), f32), norms10[2:], norms10[:2], norms1, sums_rows, emb_rows], axis=0
+    )
+    give = [(1, qp1), (0, fc2_0)] if fold else []
+    (gin0, norms, rel, sums_all, qp0, *more), landed = end_chain(
+        ndp, flags, qkv0, do0, o0, lse0, mask_pad, x0, dh0, gains[0][0:1], label_lanes, smalls, rel1,
+        walls[0], wq0, n1_0, da0, by_bits(fc1_0), give, ORDER, scale,
+    )
+    if fold:
+        got_qp1, got_fc2_0, got_gin0, got_fc1_0, got_qp0 = landed
+        parts = (
+            (qp0, got_qp0, qp1, got_qp1),
+            (more[0], got_fc1_0, sum_fc1_1, got_fc1_1),
+            (fc2_0, got_fc2_0, fc2_1, got_fc2_1),
+        )
+    else:
+        (got_gin0,) = landed
+        parts = []
+        for x0_, x1_ in ((qp0, qp1), (by_bits(fc1_0), fc1_1), (fc2_0, fc2_1)):
+            a, b = reduced(whole(x0_)), reduced(whole(x1_))
+            parts.append((a, (near_of(a, 0), far_of(a, 0)), b, (near_of(b, 1), far_of(b, 1))))
 
     def by_image(same, other):
         return jnp.stack([jnp.where(pair == 0, same, other), jnp.where(pair == 0, other, same)])[None]
 
-    acts = by_image(jnp.where(home, by_core((act0, act1)), got_acts[0]), got_acts[1])
-    low0 = gin0.astype(bf16)
-    same = jnp.where(home, by_core((gin0, gin1)), (near_of(low0, 0) + got1[0]).astype(f32))
-    input_grads = by_image(same, (far_of(low0, 0) + got1[1]).astype(f32))
-
-    def total(mine, parts):
-        out = jnp.where(home, mine, jnp.zeros_like(mine)).astype(f32)
-        for part in parts:
-            out = out + part.astype(f32)
-        return out
-
-    n_qp = 4 * local_width
-    hidden_units = w_fc1.shape[2]
-    grad_fc = total(
-        by_core((sums_w0[1], sums_w1[1])),
-        (near_of(sums_w0[1], 0), far_of(sums_w0[1], 0), got1[2][:, n_qp:], got1[3][:, n_qp:]),
+    acts = by_image(
+        jnp.where(home, by_core((act0, act1)), by_core((got_act0[0], got_act1[0]))), by_core((got_act0[1], got_act1[1]))
     )
-    grad_qp = total(
-        by_core((sums_w0[0], sums_w1[0])),
-        (near_of(sums_w0[0], 0), far_of(sums_w0[0], 0), got1[2][:, :n_qp], got1[3][:, :n_qp]),
-    )
-
-    here = (jnp.arange(2 * ndp) == 2 * d + pair).astype(f32)[:, None]
-    pack = jnp.concatenate(
-        [
-            rel0.reshape(-1, 128),
-            rel1.reshape(-1, 128),
-            (here * jnp.concatenate([sums0, sums1])[None]).reshape(-1, 128),
-            jnp.stack([early0, early1, late1]).reshape(-1, 128),
-        ],
-        axis=0,
-    )
-    late = late0.reshape(-1, 128)
-
-    def summed(x):
-        bit = 1
-        while bit < ndp:
-            x = x + move(x, lambda dd, cc, zz, b=bit: (dd ^ b, cc, zz), "pack_dp")
-            bit *= 2
-        return x + across(x)
-
-    pack = summed(pack)
-    n_rel = heads * 32
-    n_sum = 2 * ndp * 4 * local_width // 128
-    rel_both = (pack[:n_rel], pack[n_rel : 2 * n_rel])
-    sums_all = pack[2 * n_rel : 2 * n_rel + n_sum].reshape(2 * ndp, 2, 2 * local_width)
-    norms = pack[2 * n_rel + n_sum :]
-    norms = norms + partner(norms)
-    norms = norms + sibling(norms)
-    late = summed(late)
-    late = late + partner(late)
-    late = late + sibling(late)
-    early0, early1, late1 = norms.reshape(3, 2, width)
-    late0 = late.reshape(2, width)
-    norms_mine = jnp.stack([by_core((late0, late1)), by_core((early0, early1))], axis=1)
+    same = jnp.where(home, by_core((gin0, gin1)), by_core((got_gin0[0], got_gin1[0])).astype(f32))
+    input_grads = by_image(same, by_core((got_gin0[1], got_gin1[1])).astype(f32))
+
+    def total(mine, got):
+        return jnp.where(home, mine, got[0]).astype(f32) + got[1].astype(f32)
+
+    grad_qp, grad_fc1, grad_fc2 = [by_core((total(a, x), total(b, y))) for a, x, b, y in parts]
+
+    rel_grad = rel.reshape(heads, 4096)[:, :buckets]
+    norms_mine = jnp.where(first, norms[:4], norms[4:]).reshape(2, 2, width)
     cols = width // (4 * ndp)
     norms_mine = lax.dynamic_slice_in_dim(norms_mine, (d * 4 + z) * cols, cols, 2)
-
-    def to_home_core(both):
-        return move(
-            jnp.where(first, both[1], both[0]),
-            lambda dd, cc, zz: (dd, 1 - cc, zz) if cc == zz // 2 else None,
-            "pack_near",
-        )
-
-    rel_mine = jnp.where(home, by_core(rel_both), to_home_core(rel_both))
-    rel_grad = rel_mine.reshape(heads, 4096)[:, :buckets]
-    sums_both = (sums_all[:, 0], sums_all[:, 1])
-    sums_mine = jnp.where(home, by_core(sums_both), to_home_core(sums_both))
-    emb_all = lax.all_gather(time_emb, "dp", axis=0, tiled=True)
-    emb_mine = lax.dynamic_slice_in_dim(emb_all, d * (width // ndp), width // ndp, 1).astype(f32)
+    sums_of, emb_of = sums_all[: 2 * ndp], sums_all[2 * ndp :]
+    sums_mine = jnp.where(first, sums_of[:, : 2 * local_width], sums_of[:, 2 * local_width :])
+    emb_mine = lax.dynamic_slice_in_dim(emb_of, d * (width // ndp), width // ndp, 1)
     grad_time = lax.dot_general(
         emb_mine, sums_mine, (((0,), (0,)), ((), ())), precision=lax.Precision.HIGHEST, preferred_element_type=f32
     ).reshape(width // ndp, 2, local_width)
@@ -1437,11 +2029,11 @@
         grad_qp[:, : 3 * local_width].reshape(width // ndp, 3, local_width)[None],
         grad_time[None],
         grad_qp[:, 3 * local_width :][None],
-        grad_fc[:, :hidden_units][None],
-        grad_fc[:, hidden_units:][None],
+        grad_fc1[None],
+        grad_fc2[None],
         rel_grad[None],
-        norms_mine[0][None],
-        norms_mine[1][None],
+        norms_mine[:, 0][None],
+        norms_mine[:, 1][None],
     )
 
 

time: 733 us -> 582 us (0.79)
  Pallas kernels: 412 us -> 522 us
  waiting for transfers between devices: 82 us -> 0 us
  starting transfers between devices: 69.4 us -> 0 us
  matrix products: 35.5 us -> 1.39 us
  other arithmetic: 51.1 us -> 19.5 us
  local copies, waits for them, and re-layouts: 60.6 us -> 33 us
  between operations: 15.9 us -> 2.18 us
    pallas_call x8 -> x5, Pallas kernels: 321 us -> 437 us  [the longest x1 112 us: mid_chain(): pl.pallas_call(functools.partial(mid_kernel, order, scale, bits), in_spec...]
    ppermute x39 -> x0, starting transfers between devices: 69.2 us -> none  [move(): return lax.ppermute(x, AXES, pairs)]
    ppermute x39 -> x0, waiting for transfers between devices: 59 us -> none  [move(): return lax.ppermute(x, AXES, pairs)]
    dot_general x7 -> x0, matrix products: 33.6 us -> none  [the longest x1 15.9 us: local(): qkv1 = (jnp.dot(n1_1, wq1, preferred_element_type=f32) + term1).astype(bf16)]
    reduce_scatter x3 -> x0, waiting for transfers between devices: 22.3 us -> none  [reduced(): return lax.psum_scatter(x, 'dp', scatter_dimension=0, tiled=True)]
    concatenate x9 -> x0, other arithmetic: 11.9 us -> none  [the longest x1 3.06 us: local(): w1 = jnp.concatenate([sum_qp1, sum_fc1], axis=1)]
    add x14 -> x0, other arithmetic: 11.5 us -> none  [the longest x2 5.93 us: total(): out = out + part.astype(f32)]
    slice x13 -> x5, local copies, waits for them, and re-layouts: 10.9 us -> 0.68 us  [the longest x1 0.65 us: local(): norms_mine[:, 1][None]]
  transfers between devices with their start and end apart: 42 -> 0, of which waited for: 14 -> 0; matrix products, arithmetic and copies ran while one was open for 10% -> 0% of each run, Pallas kernels for 20% -> 0%
where the time goes in v4:
time: 582 us; the launch traced here: 578 us
  Pallas kernels  522 us (90%)
  local copies, waits for them, and re-layouts  33 us (6%)
  other arithmetic  19.5 us (3%)
    pallas_call x1, Pallas kernels, mid_chain(): pl.pallas_call(functools.partial(mid_kernel, order, scale, bits), in_spec...  112 us
    pallas_call x1, Pallas kernels, end_chain(): pl.pallas_call(functools.partial(end_kernel, order, scale, bits, fold, la...  110 us
    pallas_call x1, Pallas kernels, back_chain(): pl.pallas_call(functools.partial(back_kernel, bits, fold, layers), in_spe...  95.7 us
    pallas_call x1, Pallas kernels, start_chain(): pl.pallas_call(functools.partial(start_kernel, order, scale, bits), in_sp...  84.7 us
    pallas_call x1, Pallas kernels, turn_chain(): pl.pallas_call(functools.partial(turn_kernel, bits, fold), in_specs=[VM,...  79 us
    pallas_call x1, Pallas kernels, bwd_chain(): pl.pallas_call(functools.partial(bwd_kernel, order, scale, bits, fold, la...  40.1 us
    unnamed x82, local copies, waits for them, and re-layouts  11.8 us

profile of v4, /device:TPU:1, one launch (start us, length us, event | category | flops | bytes accessed | tf_op | source)
XLA Modules:
  0.0 578.3 jit_solution(5405456485933397147)
XLA Ops:
  1.8 1.2 dynamic_slice.37
  3.7 1.3 slice.141
  8.1 2.7 fusion.13
  11.2 1.5 copy.38
  12.7 2.3 copy.39
  15.0 3.5 pad_maximum_fusion.wq_hbm.own_q
  19.7 1.2 copy.40
  21.0 84.7 %shard_map.213 = (bf16[256,1152]{1,0:T(8,128)(2,1)S(1)}, bf16[256,1152]{1,0:T(8,128)(2,1)S(1)}, f32[2,8,1152]{2,1,0:T(8,128)S(1)}, f32[4,4,256]{2,1,0:T(4,128)S(...) custom-call(s32[2]{0:T(128)S(1)} %pad_add_fusion.flags_ref, ...), custom_call_target="tpu_custom_call" | custom-call | flops 85899345920 | bytes 25165824 | tf_op jit(solution)/shard_map/pallas_call | solution.py:1355
  107.4 112.3 %shard_map.214 = (f32[256,1152]{1,0:T(8,128)}, bf16[256,1152]{1,0:T(8,128)(2,1)S(1)}, f32[256,1152]{1,0:T(8,128)}, bf16[1024,288]{1,0:T(8,128)(2,1)}, f32[4,4,25...) custom-call(bf16[256,1152]{1,0:T(8,128)(2,1)S(1)} %get-tuple-element, ...), custom_call_target="tpu_custom_call" | custom-call | flops 64424509440 | bytes 25165824 | tf_op jit(solution)/shard_map/pallas_call | solution.py:879
  219.7 79.0 %shard_map.215 = (f32[256,1152]{1,0:T(8,128)}, f32[2,1152]{1,0:T(2,128)S(1)}, f32[256,1152]{1,0:T(8,128)}, bf16[1024,288]{1,0:T(8,128)(2,1)}, bf16[288,1152]{1,0...) custom-call(bf16[256,1152]{1,0:T(8,128)(2,1)S(1)} %get-tuple-element, ...), custom_call_target="tpu_custom_call" | custom-call | flops 64424509440 | bytes 25165824 | tf_op jit(solution)/shard_map/pallas_call | solution.py:1021
  299.5 40.1 %shard_map.216 = (bf16[1024,864]{1,0:T(8,128)(2,1)}, f32[4,32,14336]{2,1,0:T(8,128)}, bf16[288,1152]{1,0:T(8,128)(2,1)}, bf16[256,1152]{1,0:T(8,128)(2,1)S(1)}, ...) custom-call(bf16[1024,864]{1,0:T(8,128)(2,1)} %get-tuple-element.97., ...), custom_call_target="tpu_custom_call" | custom-call | flops 25769803776 | bytes 20971520 | tf_op jit(solution)/shard_map/pallas_call | solution.py:1542
  339.7 95.7 %shard_map.217 = (f32[256,1152]{1,0:T(8,128)}, f32[256,1152]{1,0:T(8,128)}, f32[4,1152]{1,0:T(4,128)S(1)}, bf16[1024,288]{1,0:T(8,128)(2,1)}, bf16[4,256,1152]{2...) custom-call(s32[2]{0:T(128)S(1)} %copy-done.20, ...), custom_call_target="tpu_custom_call" | custom-call | flops 64424509440 | bytes 25165824 | tf_op jit(solution)/shard_map/pallas_call | solution.py:1202
  438.4 110.4 %shard_map.218 = (f32[256,1152]{1,0:T(8,128)}, f32[8,1152]{1,0:T(8,128)S(1)}, f32[4,64,64]{2,1,0:T(8,128)S(1)}, f32[16,1152]{1,0:T(8,128)S(1)}, bf16[288,1152]{1...) custom-call(s32[2]{0:T(128)S(1)} %copy-done.20, ...), custom_call_target="tpu_custom_call" | custom-call | flops 96636764160 | bytes 25165824 | tf_op jit(solution)/shard_map/pallas_call | solution.py:1765
  551.6 3.4 select_bitcast_fusion
  555.1 1.5 select_bitcast_fusion.1
  557.5 1.6 broadcast_in_dim_reshape.7
  559.1 3.2 add_select_fusion
  562.3 1.3 slice.187
  563.6 1.5 copy.42
  565.1 3.0 copy.44
  568.1 2.0 slice_bitcast_fusion
  570.0 1.9 fusion.2
  572.1 1.6 maximum_bitcast_fusion
  575.1 1.2 select_bitcast_fusion.3
  (132 shorter events, 18.1 us)
Async XLA Ops:
  0.6 17.9 %copy-start = (bf16[1,1152,2,288]{1,3,2,0:T(8,128)(2,1)S(1)}, bf16[1,1152,2,288]{1,3,2,0:T(8,128)(2,1)}, u32[]{:S(2)}) copy-start(bf16[1,1152,2,288]{1,3,2,0:T(8,128)(2,1)} %param.20) | copy-start | bytes 3981316
  5.7 15.3 %copy-start.19 = (s32[2]{0:T(128)}, s32[2]{0:T(128)S(1)}, u32[]{:S(2)}) copy-start(s32[2]{0:T(128)S(1)} %pad_add_fusion.flags_ref) | copy-start | bytes 28
  8.1 12.9 %copy-start.17 = (s32[1,4096]{1,0:T(1,128)}, s32[1,4096]{1,0:T(1,128)S(1)}, u32[]{:S(2)}) copy-start(s32[1,4096]{1,0:T(1,128)S(1)} %reshape.152.lab_ref) | copy-start | bytes 49156
  15.0 3.5 copy-start.36
  18.6 2.3 copy-start.35
  19.2 86.5 %copy-start.33 = (f32[2,1152]{1,0:T(2,128)}, f32[2,1152]{1,0:T(2,128)S(1)}, u32[]{:S(2)}) copy-start(f32[2,1152]{1,0:T(2,128)S(1)} %broadcast.36) | copy-start | bytes 27652
  106.6 113.1 %copy-start.21 = (bf16[256,1152]{1,0:T(8,128)(2,1)}, bf16[256,1152]{1,0:T(8,128)(2,1)S(1)}, u32[]{:S(2)}) copy-start(bf16[256,1152]{1,0:T(8,128)(2,1)S(1)} %get-tuple-element.88.x_ref) | copy-start | bytes 1769476
  106.6 113.1 %copy-start.23 = (f32[4,4,256]{2,1,0:T(4,128)}, f32[4,4,256]{2,1,0:T(4,128)S(1)}, u32[]{:S(2)}) copy-start(f32[4,4,256]{2,1,0:T(4,128)S(1)} %get-tuple-element.130.lse_ref) | copy-start | bytes 49156
  219.7 79.0 %copy-start.4 = (bf16[256,1152]{1,0:T(8,128)(2,1)}, bf16[256,1152]{1,0:T(8,128)(2,1)S(1)}, u32[]{:S(2)}) copy-start(bf16[256,1152]{1,0:T(8,128)(2,1)S(1)} %get-tuple-element.96.x_ref.refs_0_) | copy-start | bytes 1769476
  299.5 40.1 %copy-start.18 = (s32[1,4096]{1,0:T(1,128)S(1)}, s32[1,4096]{1,0:T(1,128)}, u32[]{:S(2)}) copy-start(s32[1,4096]{1,0:T(1,128)} %copy-done.17) | copy-start | bytes 49156
  299.5 40.1 %copy-start.20 = (s32[2]{0:T(128)S(1)}, s32[2]{0:T(128)}, u32[]{:S(2)}) copy-start(s32[2]{0:T(128)} %copy-done.19) | copy-start | bytes 28
  339.7 97.8 %copy-start.37 = (bf16[2,1152]{1,0:T(2,128)(2,1)S(1)}, bf16[2,1152]{1,0:T(2,128)(2,1)}, u32[]{:S(2)}) copy-start(bf16[2,1152]{1,0:T(2,128)(2,1)} %param.15) | copy-start | bytes 13828
  339.7 98.0 %copy-start.34 = (f32[2,1152]{1,0:T(2,128)S(1)}, f32[2,1152]{1,0:T(2,128)}, u32[]{:S(2)}) copy-start(f32[2,1152]{1,0:T(2,128)} %copy-done.33) | copy-start | bytes 27652
  438.4 113.2 %copy-start.3 = (bf16[288,1152]{1,0:T(8,128)(2,1)S(1)}, bf16[288,1152]{1,0:T(8,128)(2,1)}, u32[]{:S(2)}) copy-start(bf16[288,1152]{1,0:T(8,128)(2,1)} %copy-done.2) | copy-start | bytes 1990660
  551.6 3.4 copy-start.27
  551.6 3.4 copy-start.28
  551.6 3.4 copy-start.29
  551.6 3.4 copy-start.30
  551.6 3.4 copy-start.31
  551.6 3.4 copy-start.32
  565.1 4.9 copy-start.9
  572.1 2.3 copy-start.16
  572.1 3.0 copy-start.5
  572.1 3.0 copy-start.7
  (16 other events, 16.0 us)

commit v5 on v4

--- a/solution.py
+++ b/solution.py
@@ -615,7 +615,7 @@
 class DpReduce:
     COPIES = 4
 
-    def __init__(self, links, buf, land0, land1, sent):
+    def __init__(self, links, buf, land0, land1=None, sent=None):
         self.links, self.buf, self.land0, self.land1, self.sent = links, buf, land0, land1, sent
         columns = buf.shape[-1]
         cut = columns // 256 * 128
@@ -627,7 +627,8 @@
         for (b0, b1), h, cols in zip(self.orders, range(2), self.cols):
             at = self.place(h, self.other[b0], pl.ds(0, 2))
             self.first.append(links.make(buf.at[at + (slice(None), cols)], land0.at[:, :, cols], ("dp", b0)))
-            self.second.append(links.make(sent.at[0, :, cols], land1.at[0, :, cols], ("dp", b1)))
+            if land1 is not None:
+                self.second.append(links.make(sent.at[0, :, cols], land1.at[0, :, cols], ("dp", b1)))
 
     @staticmethod
     def scratch(n, columns):
@@ -640,14 +641,25 @@
         for copy in self.first:
             copy.start()
 
+    def half(self, h, cols):
+        b0, b1 = self.orders[h]
+        self.first[h].wait_recv()
+        sums = []
+        for second in (self.other[b1], self.mine[b1]):
+            own = self.buf[self.place(h, self.mine[b0], second) + (slice(None), cols)]
+            sums.append(own.astype(jnp.float32) + self.land0[second, :, cols].astype(jnp.float32))
+        return sums
+
+    def split(self, sent, kept):
+        for h, cols in enumerate(self.cols):
+            sums = self.half(h, cols)
+            sent[:, cols] = sums[0].astype(jnp.bfloat16)
+            kept[:, cols] = sums[1].astype(jnp.bfloat16)
+
     def middle(self):
         for h, cols in enumerate(self.cols):
             b0, b1 = self.orders[h]
-            self.first[h].wait_recv()
-            sums = []
-            for second in (self.other[b1], self.mine[b1]):
-                own = self.buf[self.place(h, self.mine[b0], second) + (slice(None), cols)]
-                sums.append(own.astype(jnp.float32) + self.land0[second, :, cols].astype(jnp.float32))
+            sums = self.half(h, cols)
             self.sent[0, :, cols] = sums[0].astype(jnp.bfloat16)
             self.buf[self.place(h, self.mine[b0], self.mine[b1]) + (slice(None), cols)] = sums[1].astype(jnp.bfloat16)
             self.second[h].start()
@@ -658,6 +670,28 @@
             b0, b1 = self.orders[h]
             own = self.buf[self.place(h, self.mine[b0], self.mine[b1]) + (slice(None), cols)]
             out[:, cols] = (own.astype(jnp.float32) + self.land1[0, :, cols].astype(jnp.float32)).astype(out.dtype)
+
+
+class DpFinish:
+    COPIES = 2
+
+    def __init__(self, links, sent, kept, land):
+        self.kept, self.land = kept, land
+        columns = sent.shape[-1]
+        cut = columns // 256 * 128
+        self.cols = (pl.ds(0, cut), pl.ds(cut, columns - cut))
+        self.copies = [
+            links.make(sent.at[:, cols], land.at[:, cols], ("dp", b)) for cols, b in zip(self.cols, (1, 0))
+        ]
+
+    def start(self):
+        for copy in self.copies:
+            copy.start()
+
+    def done(self, out):
+        for copy, cols in zip(self.copies, self.cols):
+            copy.wait_recv()
+            out[:, cols] = (self.kept[:, cols].astype(jnp.float32) + self.land[:, cols].astype(jnp.float32)).astype(out.dtype)
 
 
 class Return:
@@ -919,7 +953,7 @@
 
 
 def turn_kernel(bits, fold, x_ref, o_ref, dy_ref, ln_ref, dm_hbm, wp_hbm, own1, own2, got1, got2,
-                dh_ref, norm_ref, hid_ref, do_ref, fc2_ref, y_hbm, da_hbm, fc1_hbm,
+                dh_ref, norm_ref, hid_ref, do_ref, fc2_sent, fc2_ref, y_hbm, da_hbm, fc1_hbm,
                 wp, w1, w2, dm, g_buf, du_buf, y_buf, fc1, fc2, gat1, gat2, low, wide, *refs):
     lands, (load_sem, store_sem, send_sem, recv_sem) = refs[:-4], refs[-4:]
     rows, width = x_ref.shape
@@ -975,7 +1009,7 @@
     s2.middle(1)
     slab_grad(fc2, 0, dm[...], g_buf[...])
     if fold:
-        reduce = DpReduce(links, fc2, *lands)
+        reduce = DpReduce(links, fc2, lands[0])
         reduce.start()
     sums = None
     for i in range(NCH):
@@ -994,14 +1028,12 @@
         y = dot(g_buf[pl.ds(b * rows, rows)], w2[...].reshape(width, -1), NT)
         y_buf[pl.ds(b * rows, rows)] = y.astype(jnp.bfloat16)
     stores.append(start_load(y_buf, y_hbm, store_sem.at[1]))
-    if fold:
-        reduce.middle()
     g2.forward(1)
     for i in range(NCH):
         put_rows(do_ref, dot(g2.done(i), wp[...], NN).astype(jnp.bfloat16), i, rows)
     stores.append(start_load(gat2, da_hbm, store_sem.at[2]))
     if fold:
-        reduce.done(fc2_ref)
+        reduce.split(fc2_sent, fc2_ref)
     else:
         fc2_ref[...] = fc2[...]
     links.leave()
@@ -1021,12 +1053,13 @@
     res = pl.pallas_call(
         functools.partial(turn_kernel, bits, fold),
         in_specs=[VM, VM, VM, VM] + [HB] * 6,
-        out_specs=[VM] * 5 + [HB] * 3,
+        out_specs=[VM] * 6 + [HB] * 3,
         out_shape=[
             out((rows, width), f32),
             out((2, width), f32),
             out((rows, width), f32),
             out((4 * rows, lw), bf16),
+            out((n, hidden), bf16),
             out((n, hidden) if fold else (2, 2, n, hidden), bf16),
             out((4 * rows, width), bf16),
             out((4, rows, width), bf16),
@@ -1045,7 +1078,7 @@
             pltpu.VMEM((4, rows, width), bf16),
             pltpu.VMEM((4, rows, width), bf16),
             *scatter_scratch(rows, width),
-            *(DpReduce.scratch(n, hidden) if fold else []),
+            *(DpReduce.scratch(n, hidden)[:1] if fold else []),
             pltpu.SemaphoreType.DMA((4,)),
             pltpu.SemaphoreType.DMA((3,)),
             *comm_scratch(2 * Scatter.COPIES + 2 * Gather.COPIES + 2 * Exchange.copies(bits) + DpReduce.COPIES),
@@ -1053,8 +1086,8 @@
         compiler_params=params(2),
         cost_estimate=pl.CostEstimate(flops=60 << 30, bytes_accessed=24 << 20, transcendentals=0),
     )(x, o, dy, ln, dm, wp, *own, *got)
-    dh, norms, hid, do, fc2, y, da, fc1 = res
-    return dh, norms, y, hid, do, da.reshape(4 * rows, width), fc1, fc2
+    dh, norms, hid, do, sent, fc2, y, da, fc1 = res
+    return dh, norms, y, hid, do, da.reshape(4 * rows, width), fc1, (sent, fc2)
 
 
 def back_kernel(bits, fold, layers, flags_ref, x_ref, dh1_ref, hid_ref, ln_ref, dqkv_ref, o1_ref, lab_ref,
@@ -1062,11 +1095,11 @@
     refs = list(refs)
     take = lambda k: [refs.pop(0) for _ in range(k)]
     blocks = take(len(layers))
-    gin_ref, dh_ref, norm_ref, do_ref, da_hbm, fc1_hbm, fc2_out, qp_out, rel_out, sum_out = take(10)
+    gin_ref, dh_ref, norm_ref, do_ref, da_hbm, fc1_hbm, fc2_sent, fc2_out, qp_out, rel_out, sum_out = take(11)
     places = [take(2) for _ in range(len(layers) + 1)]
     wq, wp, w1, w2, u_buf, g_buf, fc2, gqp, strips, gin_low, gat1, gat2, low, wide = take(14)
     if fold:
-        lands_qp, lands_fc = take(3), take(3)
+        lands_qp, lands_fc = take(3), take(1)
     load_sem, store_sem, send_sem, recv_sem = refs
     small, out_lab = flags_ref[0], flags_ref[1]
     rows, width = x_ref.shape
@@ -1172,9 +1205,8 @@
         put_rows(do_ref, dot(g2.done(i), wp[...], NN).astype(jnp.bfloat16), i, rows)
     stores.append(start_load(gat2, da_hbm, store_sem.at[2]))
     if fold:
-        reduce_2.middle()
         reduce.done(qp_out)
-        reduce_2.done(fc2_out)
+        reduce_2.split(fc2_sent, fc2_out)
     else:
         qp_out[...] = gqp[...]
         fc2_out[...] = fc2[...]
@@ -1202,7 +1234,7 @@
     res = pl.pallas_call(
         functools.partial(back_kernel, bits, fold, layers),
         in_specs=[pl.BlockSpec(memory_space=pltpu.SMEM)] + [VM] * 7 + [HB] * (10 + len(blocks)),
-        out_specs=[VM, VM, VM, VM, HB, HB, VM, VM, VM, VM] + [HB] * (2 * len(blocks) + 2),
+        out_specs=[VM, VM, VM, VM, HB, HB, VM, VM, VM, VM, VM] + [HB] * (2 * len(blocks) + 2),
         out_shape=[
             out((rows, width), f32),
             out((rows, width), f32),
@@ -1210,6 +1242,7 @@
             out((4 * rows, lw), bf16),
             out((4, rows, width), bf16),
             out((width, hidden), bf16),
+            out((n, hidden), bf16),
             out((n, hidden) if fold else (2, 2, n, hidden), bf16),
             out((n, qp_cols) if fold else (2, 2, n, qp_cols), bf16),
             out((heads, 64, 64), f32),
@@ -1231,7 +1264,7 @@
             pltpu.VMEM((4, rows, width), bf16),
             pltpu.VMEM((4, rows, width), bf16),
             *scatter_scratch(rows, width),
-            *(DpReduce.scratch(n, qp_cols) + DpReduce.scratch(n, hidden) if fold else []),
+            *(DpReduce.scratch(n, qp_cols) + DpReduce.scratch(n, hidden)[:1] if fold else []),
             pltpu.SemaphoreType.DMA((11,)),
             pltpu.SemaphoreType.DMA((3,)),
             *comm_scratch(copies),
@@ -1239,9 +1272,9 @@
         compiler_params=params(3),
         cost_estimate=pl.CostEstimate(flops=60 << 30, bytes_accessed=24 << 20, transcendentals=0),
     )(flags, x, dh1, hid, ln, dqkv, o1, lab, wq, wp, w1, w2, u, g, n2, n1, da1, dwall, *blocks)
-    gin, dh, norms, do, da, fc1, fc2, qp, rel, sums = res[:10]
-    got = [(res[10 + 2 * k], res[11 + 2 * k]) for k in range(len(layers) + 1)]
-    return gin, dh, norms, do, da.reshape(4 * rows, width), fc1, fc2, qp, rel, sums, got
+    gin, dh, norms, do, da, fc1, sent, fc2, qp, rel, sums = res[:11]
+    got = [(res[11 + 2 * k], res[12 + 2 * k]) for k in range(len(layers) + 1)]
+    return gin, dh, norms, do, da.reshape(4 * rows, width), fc1, (sent, fc2), qp, rel, sums, got
 
 
 def start_kernel(order, scale, bits, flags_ref, x_hbm, cot_hbm, mask_ref, lab_ref, tab_hbm, pack_hbm,
@@ -1439,14 +1472,15 @@
     refs = list(refs)
     take = lambda k: [refs.pop(0) for _ in range(k)]
     blocks = take(len(layers))
+    sent_2, kept_2 = take(2) if fold else (None, None)
     y_ref, hid_ref = take(2) if summed else (None, None)
     dqkv_ref, acc_hbm = take(2)
-    (fc_out,) = take(1) if fold else (None,)
-    places = [take(2) for _ in layers]
+    fc_out, fin_out = take(2) if fold else (None, None)
+    places = [take(2) for _ in range(len(layers) + (1 if fold else 0))]
     (act_ref,) = take(1) if summed else (None,)
     wall, acc, p_scr, s_scr, dq_scr, dk_scr, dv_scr = take(7)
     if fold:
-        gfc, land0, land1, sent = take(4)
+        gfc, land0, land1, sent, land_2 = take(5)
     if summed:
         (low,) = take(1)
     load_sem, store_sem, send_sem, recv_sem = refs
@@ -1457,6 +1491,9 @@
     links.enter()
     returns = [Return(links, layer, src, *at) for layer, src, at in zip(layers, blocks, places)]
     if fold:
+        finish = DpFinish(links, sent_2, kept_2, land_2)
+        finish.start()
+        last = Return(links, 1, fin_out, *places[-1])
         reduce = DpReduce(links, gfc, land0, land1, sent)
     if summed:
         rows = hid_ref.shape[0]
@@ -1480,8 +1517,13 @@
         back.start()
     loads[0].wait()
 
+    def finished():
+        finish.done(fin_out)
+        last.start()
+
     def event(i):
         if fold:
+            pl.when(i == 0)(finished)
             pl.when(i == 2)(lambda: reduce.middle())
 
     attn_back(
@@ -1496,6 +1538,7 @@
         act_ref[...] = act.astype(jnp.bfloat16)
     if fold:
         reduce.done(fc_out)
+        last.done()
     for back in returns:
         back.done()
     links.leave()
@@ -1503,7 +1546,7 @@
         store.wait()
 
 
-def bwd_chain(ident, fold, qkv, do, o, lse, mask_pad, wall, gfc, returns, order, scale, summed=None):
+def bwd_chain(ident, fold, qkv, do, o, lse, mask_pad, wall, gfc, finish, returns, order, scale, summed=None):
     total, wide = qkv.shape
     heads = wall.shape[0]
     bits = 2
@@ -1515,11 +1558,11 @@
     outs = [out((total, wide), bf16), out(wall.shape, f32)]
     specs = [VM, HB]
     if fold:
-        outs.append(out((n, columns), bf16))
-        specs.append(VM)
-    for block in blocks:
+        outs += [out((n, columns), bf16)] * 2
+        specs += [VM] * 2
+    for block in blocks + ([finish[0]] if fold else []):
         outs += [out(block.shape, block.dtype)] * 2
-        specs += [VM] * 2
+        specs += [HB] * 2
     scratch = [
         pltpu.VMEM(wall.shape, f32),
         pltpu.VMEM(wall.shape, f32),
@@ -1530,17 +1573,17 @@
         pltpu.VMEM((heads, total, 128), f32),
     ]
     if fold:
-        scratch += [pltpu.VMEM(gfc.shape, bf16), *DpReduce.scratch(n, columns)]
-    more = []
+        scratch += [pltpu.VMEM(gfc.shape, bf16), *DpReduce.scratch(n, columns), pltpu.VMEM((n, columns), bf16)]
+    more = list(finish) if fold else []
     if summed is not None:
-        more = list(summed)
+        more += list(summed)
         rows, width = summed[1].shape
         outs.append(out((rows, width), bf16))
         specs.append(VM)
         scratch.append(pltpu.VMEM((4, rows, width), bf16))
-    copies = len(layers) * Return.COPIES + (DpReduce.COPIES if fold else 0) + (3 if more else 0)
+    copies = len(layers) * Return.COPIES + (DpReduce.COPIES + DpFinish.COPIES + Return.COPIES if fold else 0) + (3 if summed else 0)
     res = pl.pallas_call(
-        functools.partial(bwd_kernel, order, scale, bits, fold, layers, bool(more)),
+        functools.partial(bwd_kernel, order, scale, bits, fold, layers, summed is not None),
         in_specs=[VM] * 5 + [HB] * 2 + [VM] * (len(blocks) + len(more)),
         out_specs=specs,
         out_shape=outs,
@@ -1552,10 +1595,10 @@
     res = list(res)
     dqkv, acc = res[:2]
     res = res[2:]
-    fc = res.pop(0) if fold else None
-    got = [(res[2 * k], res[2 * k + 1]) for k in range(len(layers))]
-    act = res[-1] if more else None
-    return dqkv, acc, fc, got, act
+    fc, fin = (res.pop(0), res.pop(0)) if fold else (None, None)
+    got = [(res[2 * k], res[2 * k + 1]) for k in range(len(layers) + (1 if fold else 0))]
+    act = res[-1] if summed is not None else None
+    return dqkv, acc, fc, fin, got, act
 
 
 class SumHops:
@@ -1580,36 +1623,52 @@
     refs = list(refs)
     take = lambda k: [refs.pop(0) for _ in range(k)]
     blocks = take(len(layers))
-    gin_ref, norm_out, rel_out, sum_out, qp_out = take(5)
-    (fc_out,) = take(1) if fold else (None,)
-    places = [take(2) for _ in range(len(layers) + (3 if fold else 1))]
-    acc, dqkv_ref, gqp, gin_low, low1 = take(5)
-    rel, rel_land, rel_near, norms, norm_land, sums, sum_land, sum_near = take(8)
+    sent_2, kept_2 = take(2) if fold else (None, None)
+    gin_ref, small_out, rel_out, q_out = take(4)
+    fc_out, fin_out = take(2) if fold else (None, None)
+    (all_fc,) = (None,) if fold else take(1)
+    places = [take(2) for _ in range(len(layers) + (4 if fold else 1))]
+    acc, dqkv_ref, gq, fc, gin_low, low1 = take(6)
+    rel, rel_land, rel_near, smalls, small_land, norm_land, small_near = take(7)
     if fold:
-        fc, lands_q, lands_f = take(1)[0], take(3), take(3)
+        lands_q, lands_f, (land_2,) = take(3), take(3), take(1)
     load_sem, send_sem, recv_sem = refs
     small, out_lab = flags_ref[0], flags_ref[1]
     rows, width = x_ref.shape
     heads = rel.shape[1]
-    if fold:
-        load_f = start_load(fc_hbm, fc, load_sem.at[1])
+    hidden = fc_hbm.shape[-1]
+    load_f = start_load(fc_hbm, fc.at[:, :, :, pl.ds(0, hidden)], load_sem.at[1])
     links = Links(send_sem, recv_sem, bits)
     home, away = links.home, jnp.logical_not(links.home)
     links.enter()
-    give = list(zip(layers, blocks)) + [(0, gin_low)] + ([(0, fc_out), (0, qp_out)] if fold else [])
+    give = list(zip(layers, blocks)) + [(0, gin_low)] + ([(0, fc_out), (0, q_out), (0, fin_out)] if fold else [])
     returns = [Return(links, layer, src, *at) for (layer, src), at in zip(give, places)]
     early = len(layers)
     for back in returns[:early]:
         back.start()
     if fold:
+        finish = DpFinish(links, sent_2, kept_2, land_2)
+        finish.start()
         reduce_f = DpReduce(links, fc, *lands_f)
-        reduce_q = DpReduce(links, gqp, *lands_q)
-        load_f.wait()
+        reduce_q = DpReduce(links, gq, *lands_q)
+
+    def proj_grad(rows_buf):
+        start_load(da_hbm, rows_buf, load_sem.at[4]).wait()
+        slab_grad(fc, hidden, rows_buf[...], o_ref[...])
+
+    pl.run_scoped(proj_grad, pltpu.VMEM(da_hbm.shape, jnp.bfloat16))
+    load_f.wait()
+    if fold:
         reduce_f.start()
     acc[...] = jnp.zeros_like(acc)
 
+    def finished():
+        finish.done(fin_out)
+        returns[early + 3].start()
+
     def event(i):
         if fold:
+            pl.when(i == 0)(finished)
             pl.when(i == 2)(lambda: reduce_f.middle())
 
     def attention(wall, p_scr, s_scr, dq_scr, dk_scr, dv_scr):
@@ -1637,8 +1696,12 @@
 
     def rest(wq, rows_buf, wide1):
         s1 = Scatter(links, low1, wide1)
+        load_n = start_load(n1_hbm, rows_buf, load_sem.at[3])
         load_q = start_load(wq_hbm, wq, load_sem.at[2])
-        load_n = start_load(n1_hbm, rows_buf, load_sem.at[3])
+        load_n.wait()
+        slab_grad(gq, 0, rows_buf[...], dqkv_ref[...])
+        if fold:
+            reduce_q.start()
         load_q.wait()
         for i in range(NCH):
             scatter_product(s1, i, lambda b: block_rows(dqkv_ref, b, i, rows), wq[...], rows)
@@ -1648,24 +1711,25 @@
         if fold:
             reduce_f.done(fc_out)
             returns[early + 1].start()
-        load_n.wait()
-        slab_grad(gqp, 0, rows_buf[...], dqkv_ref[...])
-        load_d = start_load(da_hbm, rows_buf, load_sem.at[4])
-        load_d.wait()
-        slab_grad(gqp, dqkv_ref.shape[1], rows_buf[...], o_ref[...])
-
-        if fold:
-            reduce_q.start()
-        hops = [("dp", b) for b in range(bits)] + [ACROSS]
         cols = jnp.sum(dqkv_ref[...].astype(jnp.float32), axis=0, keepdims=True)
         mine = jnp.concatenate([cols[:, :lw], cols[:, 2 * lw :]], axis=1)
-        images = sums.shape[0] // 2
+        images = (smalls.shape[0] - 8) // 2
         number = 2 * lax.axis_index("dp") + links.pair
         here = lax.broadcasted_iota(jnp.int32, (images, 2 * lw), 0) == number
-        sums[...] = small_ref[8:]
-        sums[0:images, 0 : 2 * lw] = jnp.where(here, jnp.broadcast_to(mine, (images, 2 * lw)), 0.0)
-        sum_hops = SumHops(links, sums, sum_land, hops)
-        sum_hops.send()
+        smalls[...] = small_ref[...]
+        smalls[8 : 8 + images, 0 : 2 * lw] = jnp.where(here, jnp.broadcast_to(mine, (images, 2 * lw)), 0.0)
+        lab = lab_ref[...]
+        hi_mask, lo_hot = _labels_hi_lo(lab)
+        rel[1] = rel1_ref[...]
+
+        def heads_of(a, b):
+            def one(h, carry):
+                rel[0, h] = wall_grad(small, out_lab, lab, hi_mask, lo_hot, acc.at[h])
+                return carry
+
+            lax.fori_loop(a, b, one, 0)
+
+        heads_of(0, heads // 2)
         late = None
         for i in range(NCH):
             at = chunk(i, rows)
@@ -1675,60 +1739,48 @@
             gin_low[at] = gin.astype(jnp.bfloat16)
             both = jnp.concatenate([dgain, dshift], axis=0)
             late = both if late is None else late + both
+        smalls[0:2] = late
+        hops = [ACROSS] + [("dp", b) for b in range(bits)]
+        small_hops = SumHops(links, smalls, small_land, hops)
+        small_hops.send()
         returns[early].start()
-        norms[...] = small_ref[0:8]
-        norms[0:2] = late
-        norm_hops = SumHops(links, norms, norm_land, hops + [PARTNER, SIBLING])
-        norm_hops.send()
-        lab = lab_ref[...]
-        hi_mask, lo_hot = _labels_hi_lo(lab)
-        rel[1] = rel1_ref[...]
-
-        def heads_of(a, b):
-            def one(h, carry):
-                rel[0, h] = wall_grad(small, out_lab, lab, hi_mask, lo_hot, acc.at[h])
-                return carry
-
-            lax.fori_loop(a, b, one, 0)
-
-        heads_of(0, heads // 2)
-        sum_hops.take()
-        norm_hops.take()
         heads_of(heads // 2, heads)
         rel_hops = SumHops(links, rel, rel_land, hops)
         rel_hops.send()
         if fold:
             reduce_q.middle()
-        norm_hops.take()
-        sum_hops.take()
+        small_hops.take()
         rel_hops.take()
         if fold:
-            reduce_q.done(qp_out)
+            reduce_q.done(q_out)
             returns[early + 2].start()
         else:
-            qp_out[...] = gqp[...]
-        for k in range(1, len(hops)):
-            if k + 1 < len(hops):
-                sum_hops.take()
+            q_out[...] = gq[...]
+            all_fc[...] = fc[...]
+        for _ in range(bits):
+            small_hops.take()
             rel_hops.take()
-            norm_hops.take()
-        norm_hops.take()
-        norm_out[...] = norms[...]
+        images_at = pl.ds(8, smalls.shape[0] - 8)
         rel_copy = links.send(rel.at[1 - links.c], rel_near, SIBLING, home)
-        sum_copy = links.send(sums, sum_near, SIBLING, home)
+        small_copy = links.send(smalls.at[images_at], small_near, SIBLING, home)
+        norm_hops = SumHops(links, smalls.at[pl.ds(0, 8)], norm_land, [PARTNER, SIBLING])
+        norm_hops.send()
 
         @pl.when(home)
         def _():
             rel_out[...] = rel[links.c]
-            sum_out[...] = sums[...]
+            small_out[images_at] = smalls[images_at]
 
         @pl.when(away)
         def _():
             rel_copy.wait_recv()
-            sum_copy.wait_recv()
+            small_copy.wait_recv()
             rel_out[...] = rel_near[...]
-            sum_out[...] = sum_near[...]
-
+            small_out[images_at] = small_near[...]
+
+        norm_hops.take()
+        norm_hops.take()
+        small_out[0:8] = smalls[0:8]
         for back in returns:
             back.done()
         links.leave()
@@ -1736,15 +1788,15 @@
     pl.run_scoped(rest, vmem(wq_hbm.shape, bf16), vmem(n1_hbm.shape, bf16), vmem((2, rows, width), f32))
 
 
-def end_chain(ndp, flags, qkv, do, o, lse, mask_pad, x, dh, ln, lab, smalls, rel1, wall, wq, n1, da, fc, returns, order, scale):
+def end_chain(ndp, flags, qkv, do, o, lse, mask_pad, x, dh, ln, lab, smalls, rel1, wall, wq, n1, da, fc, finish, returns, order, scale):
     rows, width = x.shape
     heads = wall.shape[0]
     total, wide = qkv.shape
     bits = ndp.bit_length() - 1
     fold = bits == 2
-    n, fc_cols = fc.shape[2:]
-    qp_cols = wide + o.shape[1]
-    images = smalls.shape[0] - 8
+    n, hidden = fc.shape[2:]
+    fc_cols = hidden + o.shape[1]
+    count = smalls.shape[0]
     hops = bits + 1
     bf16, f32 = jnp.bfloat16, jnp.float32
     out = jax.ShapeDtypeStruct
@@ -1753,36 +1805,41 @@
     landed = [out(block.shape, bf16) for block in blocks] + [out((rows, width), bf16)]
     outs = [
         out((rows, width), f32),
-        out((8, width), f32),
+        out((count, width), f32),
         out((heads, 64, 64), f32),
-        out((images, width), f32),
-        out((n, qp_cols) if fold else (2, 2, n, qp_cols), bf16),
+        out((n, wide) if fold else (2, 2, n, wide), bf16),
     ]
     if fold:
-        outs.append(out((n, fc_cols), bf16))
-        landed += [out((n, fc_cols), bf16), out((n, qp_cols), bf16)]
-    copies = Scatter.COPIES + (len(landed)) * Return.COPIES + 2 * DpReduce.COPIES + 3 * hops + 4
+        outs += [out((n, fc_cols), bf16), out((n, hidden), bf16)]
+        landed += [out((n, fc_cols), bf16), out((n, wide), bf16), out((n, hidden), bf16)]
+        blocks += list(finish)
+    else:
+        outs.append(out((2, 2, n, fc_cols), bf16))
+    copies = Scatter.COPIES + len(landed) * Return.COPIES + 2 * DpReduce.COPIES + DpFinish.COPIES + 2 * hops + 4
     res = pl.pallas_call(
         functools.partial(end_kernel, order, scale, bits, fold, layers),
-        in_specs=[pl.BlockSpec(memory_space=pltpu.SMEM)] + [VM] * 11 + [HB] * (5 + len(blocks)),
+        in_specs=[pl.BlockSpec(memory_space=pltpu.SMEM)] + [VM] * 11 + [HB] * (5 + len(layers)) + ([VM] * 2 if fold else []),
         out_specs=[VM] * len(outs) + [HB] * (2 * len(landed)),
         out_shape=outs + [shape for shape in landed for _ in range(2)],
         scratch_shapes=[
             pltpu.VMEM(wall.shape, f32),
             pltpu.VMEM((total, wide), bf16),
-            pltpu.VMEM((2, 2, n, qp_cols), bf16),
+            pltpu.VMEM((2, 2, n, wide), bf16),
+            pltpu.VMEM((2, 2, n, fc_cols), bf16),
             pltpu.VMEM((rows, width), bf16),
             pltpu.VMEM((6, rows, width), bf16),
             pltpu.VMEM((2, heads, 64, 64), f32),
             pltpu.VMEM((hops, 2, heads, 64, 64), f32),
             pltpu.VMEM((heads, 64, 64), f32),
-            pltpu.VMEM((8, width), f32),
-            pltpu.VMEM((hops + 2, 8, width), f32),
-            pltpu.VMEM((images, width), f32),
-            pltpu.VMEM((hops, images, width), f32),
-            pltpu.VMEM((images, width), f32),
-            *([pltpu.VMEM(fc.shape, bf16)] if fold else []),
-            *(DpReduce.scratch(n, qp_cols) + DpReduce.scratch(n, fc_cols) if fold else []),
+            pltpu.VMEM((count, width), f32),
+            pltpu.VMEM((hops, count, width), f32),
+            pltpu.VMEM((2, 8, width), f32),
+            pltpu.VMEM((count - 8, width), f32),
+            *(
+                DpReduce.scratch(n, wide) + DpReduce.scratch(n, fc_cols) + [pltpu.VMEM((n, hidden), bf16)]
+                if fold
+                else []
+            ),
             pltpu.SemaphoreType.DMA((5,)),
             *comm_scratch(copies),
         ],
@@ -1959,9 +2016,8 @@
     dh1, norms1, y1, hid1, do1, da1, fc1_1, fc2_1 = turn_chain(
         ndp, act0, o1, dy1, ln_turn, dm1, wp1, own[2:], got1[2:]
     )
-    give = [(0, act0)] + ([(1, fc2_1)] if fold else [])
-    dqkv1, dwall1, sum_fc1_1, landed, act1 = bwd_chain(
-        6, fold, qkv1, do1, o1, lse1, mask_pad, walls[1], fc1_1, give, ORDER, scale, (y1, hid1)
+    dqkv1, dwall1, sum_fc1_1, sum_fc2_1, landed, act1 = bwd_chain(
+        6, fold, qkv1, do1, o1, lse1, mask_pad, walls[1], fc1_1, fc2_1, [(0, act0)], ORDER, scale, (y1, hid1)
     )
     got_act0, got_fc2_1 = landed[0], landed[-1]
     ln_back = jnp.stack([gains[1][0], gains[0][1]])
@@ -1980,24 +2036,35 @@
     smalls = jnp.concatenate(
         [jnp.zeros((2, width), f32), norms10[2:], norms10[:2], norms1, sums_rows, emb_rows], axis=0
     )
-    give = [(1, qp1), (0, fc2_0)] if fold else []
-    (gin0, norms, rel, sums_all, qp0, *more), landed = end_chain(
+    give = [(1, qp1)] if fold else []
+    (gin0, smalls, rel, q0, *more), landed = end_chain(
         ndp, flags, qkv0, do0, o0, lse0, mask_pad, x0, dh0, gains[0][0:1], label_lanes, smalls, rel1,
-        walls[0], wq0, n1_0, da0, by_bits(fc1_0), give, ORDER, scale,
+        walls[0], wq0, n1_0, da0, by_bits(fc1_0), fc2_0, give, ORDER, scale,
     )
+    norms, sums_all = smalls[:8], smalls[8:]
+
+    def total(mine, got):
+        return jnp.where(home, mine, got[0]).astype(f32) + got[1].astype(f32)
+
+    hidden_units = w_fc1.shape[2]
+    wide = 3 * local_width
     if fold:
-        got_qp1, got_fc2_0, got_gin0, got_fc1_0, got_qp0 = landed
-        parts = (
-            (qp0, got_qp0, qp1, got_qp1),
-            (more[0], got_fc1_0, sum_fc1_1, got_fc1_1),
-            (fc2_0, got_fc2_0, fc2_1, got_fc2_1),
-        )
+        got_qp1, got_gin0, got_f0, got_q0, got_fc2_0 = landed
+        f0, sum_fc2_0 = more
+        f0, qp1 = total(f0, got_f0), total(qp1, got_qp1)
+        layer0 = (total(q0, got_q0), f0[:, hidden_units:], f0[:, :hidden_units], total(sum_fc2_0, got_fc2_0))
+        layer1 = (qp1[:, :wide], qp1[:, wide:], total(sum_fc1_1, got_fc1_1), total(sum_fc2_1, got_fc2_1))
     else:
         (got_gin0,) = landed
-        parts = []
-        for x0_, x1_ in ((qp0, qp1), (by_bits(fc1_0), fc1_1), (fc2_0, fc2_1)):
-            a, b = reduced(whole(x0_)), reduced(whole(x1_))
-            parts.append((a, (near_of(a, 0), far_of(a, 0)), b, (near_of(b, 1), far_of(b, 1))))
+
+        def summed(x, layer):
+            x = reduced(whole(x))
+            return total(x, (near_of(x, layer), far_of(x, layer)))
+
+        f0, qp1 = summed(more[0], 0), summed(qp1, 1)
+        layer0 = (summed(q0, 0), f0[:, hidden_units:], f0[:, :hidden_units], summed(fc2_0[1], 0))
+        layer1 = (qp1[:, :wide], qp1[:, wide:], summed(fc1_1, 1), summed(fc2_1[1], 1))
+    grad_q, grad_p, grad_fc1, grad_fc2 = [by_core(pair_of) for pair_of in zip(layer0, layer1)]
 
     def by_image(same, other):
         return jnp.stack([jnp.where(pair == 0, same, other), jnp.where(pair == 0, other, same)])[None]
@@ -2007,11 +2074,6 @@
     )
     same = jnp.where(home, by_core((gin0, gin1)), by_core((got_gin0[0], got_gin1[0])).astype(f32))
     input_grads = by_image(same, by_core((got_gin0[1], got_gin1[1])).astype(f32))
-
-    def total(mine, got):
-        return jnp.where(home, mine, got[0]).astype(f32) + got[1].astype(f32)
-
-    grad_qp, grad_fc1, grad_fc2 = [by_core((total(a, x), total(b, y))) for a, x, b, y in parts]
 
     rel_grad = rel.reshape(heads, 4096)[:, :buckets]
     norms_mine = jnp.where(first, norms[:4], norms[4:]).reshape(2, 2, width)
@@ -2026,9 +2088,9 @@
     return (
         acts,
         input_grads,
-        grad_qp[:, : 3 * local_width].reshape(width // ndp, 3, local_width)[None],
+        grad_q.reshape(width // ndp, 3, local_width)[None],
         grad_time[None],
-        grad_qp[:, 3 * local_width :][None],
+        grad_p[None],
         grad_fc1[None],
         grad_fc2[None],
         rel_grad[None],

time: 582 us -> 595 us (1.022)
  Pallas kernels: 522 us -> 530 us
    pallas_call x1, Pallas kernels: 110 us -> 122 us  [end_chain(): pl.pallas_call(functools.partial(end_kernel, order, scale, bits, fold, la...]
    pallas_call x1, Pallas kernels: 112 us -> 122 us  [mid_chain(): pl.pallas_call(functools.partial(mid_kernel, order, scale, bits), in_spec...]
    pallas_call x1, Pallas kernels: 95.7 us -> 88.2 us  [back_chain(): pl.pallas_call(functools.partial(back_kernel, bits, fold, layers), in_spe...]
    pallas_call x1, Pallas kernels: 79 us -> 71.7 us  [turn_chain(): pl.pallas_call(functools.partial(turn_kernel, bits, fold), in_specs=[VM,...]
    unnamed x82 -> x76, local copies, waits for them, and re-layouts: 11.8 us -> 12.4 us
where the time goes in v5:
time: 595 us; the launch traced here: 591 us
  Pallas kernels  530 us (89%)
  local copies, waits for them, and re-layouts  35.3 us (6%)
  other arithmetic  20.7 us (3%)
    pallas_call x1, Pallas kernels, mid_chain(): pl.pallas_call(functools.partial(mid_kernel, order, scale, bits), in_spec...  122 us
    pallas_call x1, Pallas kernels, end_chain(): pl.pallas_call(functools.partial(end_kernel, order, scale, bits, fold, la...  122 us
    pallas_call x1, Pallas kernels, back_chain(): pl.pallas_call(functools.partial(back_kernel, bits, fold, layers), in_spe...  88.2 us
    pallas_call x1, Pallas kernels, start_chain(): pl.pallas_call(functools.partial(start_kernel, order, scale, bits), in_sp...  84.7 us
    pallas_call x1, Pallas kernels, turn_chain(): pl.pallas_call(functools.partial(turn_kernel, bits, fold), in_specs=[VM,...  71.7 us
    pallas_call x1, Pallas kernels, bwd_chain(): pl.pallas_call(functools.partial(bwd_kernel, order, scale, bits, fold, la...  41.2 us
    unnamed x76, local copies, waits for them, and re-layouts  12.4 us

profile of v5, /device:TPU:1, one launch (start us, length us, event | category | flops | bytes accessed | tf_op | source)
XLA Modules:
  0.0 591.1 jit_solution(7648020266872892792)
XLA Ops:
  1.8 1.2 dynamic_slice.37
  3.7 1.3 slice.153
  8.1 2.7 fusion.15
  10.8 1.5 copy.37
  12.3 2.3 copy.38
  14.6 1.2 copy.39
  15.9 3.7 pad_maximum_fusion.wq_hbm.own_q
  22.1 84.7 %shard_map.213 = (bf16[256,1152]{1,0:T(8,128)(2,1)S(1)}, bf16[256,1152]{1,0:T(8,128)(2,1)S(1)}, f32[2,8,1152]{2,1,0:T(8,128)S(1)}, f32[4,4,256]{2,1,0:T(4,128)S(...) custom-call(s32[2]{0:T(128)S(1)} %pad_add_fusion.flags_ref, ...), custom_call_target="tpu_custom_call" | custom-call | flops 85899345920 | bytes 25165824 | tf_op jit(solution)/shard_map/pallas_call | solution.py:1388
  108.5 122.4 %shard_map.214 = (f32[256,1152]{1,0:T(8,128)}, bf16[256,1152]{1,0:T(8,128)(2,1)S(1)}, f32[256,1152]{1,0:T(8,128)}, bf16[1024,288]{1,0:T(8,128)(2,1)}, f32[4,4,25...) custom-call(bf16[256,1152]{1,0:T(8,128)(2,1)S(1)} %get-tuple-element, ...), custom_call_target="tpu_custom_call" | custom-call | flops 64424509440 | bytes 25165824 | tf_op jit(solution)/shard_map/pallas_call | solution.py:913
  230.9 71.7 %shard_map.215 = (f32[256,1152]{1,0:T(8,128)}, f32[2,1152]{1,0:T(2,128)S(1)}, f32[256,1152]{1,0:T(8,128)}, bf16[1024,288]{1,0:T(8,128)(2,1)}, bf16[288,1152]{1,0...) custom-call(bf16[256,1152]{1,0:T(8,128)(2,1)S(1)} %get-tuple-element, ...), custom_call_target="tpu_custom_call" | custom-call | flops 64424509440 | bytes 25165824 | tf_op jit(solution)/shard_map/pallas_call | solution.py:1053
  304.3 41.2 %shard_map.216 = (bf16[1024,864]{1,0:T(8,128)(2,1)}, f32[4,32,14336]{2,1,0:T(8,128)}, bf16[288,1152]{1,0:T(8,128)(2,1)}, bf16[288,1152]{1,0:T(8,128)(2,1)}, bf16...) custom-call(bf16[1024,864]{1,0:T(8,128)(2,1)} %get-tuple-element.100, ...), custom_call_target="tpu_custom_call" | custom-call | flops 25769803776 | bytes 20971520 | tf_op jit(solution)/shard_map/pallas_call | solution.py:1585
  345.6 88.2 %shard_map.217 = (f32[256,1152]{1,0:T(8,128)}, f32[256,1152]{1,0:T(8,128)}, f32[4,1152]{1,0:T(4,128)S(1)}, bf16[1024,288]{1,0:T(8,128)(2,1)}, bf16[4,256,1152]{2...) custom-call(s32[2]{0:T(128)S(1)} %copy-done.12, ...), custom_call_target="tpu_custom_call" | custom-call | flops 64424509440 | bytes 25165824 | tf_op jit(solution)/shard_map/pallas_call | solution.py:1234
  434.4 1.9 concatenate.61.small_ref
  437.2 122.3 %shard_map.218 = (f32[256,1152]{1,0:T(8,128)}, f32[24,1152]{1,0:T(8,128)S(1)}, f32[4,64,64]{2,1,0:T(8,128)S(1)}, bf16[288,864]{1,0:T(8,128)(2,1)S(1)}, bf16[288,...) custom-call(s32[2]{0:T(128)S(1)} %copy-done.12, ...), custom_call_target="tpu_custom_call" | custom-call | flops 96636764160 | bytes 25165824 | tf_op jit(solution)/shard_map/pallas_call | solution.py:1819
  561.7 3.4 select_bitcast_fusion
  566.6 1.3 fusion
  570.0 1.7 fusion.7
  571.8 2.7 broadcast_in_dim_reshape.7
  574.4 2.7 slice_select_fusion.1
  577.1 2.7 copy.42
  579.8 2.9 copy.44
  582.7 1.9 fusion.3
  584.8 1.6 maximum_bitcast_fusion
  587.8 1.2 select_bitcast_fusion.2
  (127 shorter events, 20.3 us)
Async XLA Ops:
  0.6 18.9 %copy-start = (bf16[1,1152,2,288]{1,3,2,0:T(8,128)(2,1)S(1)}, bf16[1,1152,2,288]{1,3,2,0:T(8,128)(2,1)}, u32[]{:S(2)}) copy-start(bf16[1,1152,2,288]{1,3,2,0:T(8,128)(2,1)} %param.20) | copy-start | bytes 3981316
  5.7 16.4 %copy-start.11 = (s32[2]{0:T(128)}, s32[2]{0:T(128)S(1)}, u32[]{:S(2)}) copy-start(s32[2]{0:T(128)S(1)} %pad_add_fusion.flags_ref) | copy-start | bytes 28
  8.1 14.0 %copy-start.9 = (s32[1,4096]{1,0:T(1,128)}, s32[1,4096]{1,0:T(1,128)S(1)}, u32[]{:S(2)}) copy-start(s32[1,4096]{1,0:T(1,128)S(1)} %reshape.152.lab_ref) | copy-start | bytes 49156
  15.9 3.7 copy-start.33
  19.6 2.3 copy-start.32
  20.3 1.7 copy-start.30
  107.6 123.3 %copy-start.15 = (bf16[256,1152]{1,0:T(8,128)(2,1)}, bf16[256,1152]{1,0:T(8,128)(2,1)S(1)}, u32[]{:S(2)}) copy-start(bf16[256,1152]{1,0:T(8,128)(2,1)S(1)} %get-tuple-element.91.x_ref) | copy-start | bytes 1769476
  230.9 71.7 %copy-start.2 = (bf16[256,1152]{1,0:T(8,128)(2,1)}, bf16[256,1152]{1,0:T(8,128)(2,1)S(1)}, u32[]{:S(2)}) copy-start(bf16[256,1152]{1,0:T(8,128)(2,1)S(1)} %get-tuple-element.99.x_ref.refs_0_) | copy-start | bytes 1769476
  304.3 41.2 %copy-start.10 = (s32[1,4096]{1,0:T(1,128)S(1)}, s32[1,4096]{1,0:T(1,128)}, u32[]{:S(2)}) copy-start(s32[1,4096]{1,0:T(1,128)} %copy-done.9) | copy-start | bytes 49156
  304.3 41.2 %copy-start.12 = (s32[2]{0:T(128)S(1)}, s32[2]{0:T(128)}, u32[]{:S(2)}) copy-start(s32[2]{0:T(128)} %copy-done.11) | copy-start | bytes 28
  345.5 88.7 %copy-start.34 = (bf16[2,1152]{1,0:T(2,128)(2,1)S(1)}, bf16[2,1152]{1,0:T(2,128)(2,1)}, u32[]{:S(2)}) copy-start(bf16[2,1152]{1,0:T(2,128)(2,1)} %param.15) | copy-start | bytes 13828
  345.5 88.9 %copy-start.31 = (f32[2,1152]{1,0:T(2,128)S(1)}, f32[2,1152]{1,0:T(2,128)}, u32[]{:S(2)}) copy-start(f32[2,1152]{1,0:T(2,128)} %copy-done.30) | copy-start | bytes 27652
  561.7 3.4 copy-start.20
  561.7 3.4 copy-start.21
  561.7 3.4 copy-start.22
  565.1 1.3 copy-start.24
  565.1 1.5 copy-start.25
  566.6 1.4 copy-start.27
  566.6 1.5 copy-start.28
  566.6 2.0 copy-start.29
  582.7 1.9 copy-start.18
  582.7 1.9 copy-start.19
  584.8 3.0 copy-start.3
  589.0 1.6 copy-start.1
  (13 other events, 11.7 us)

commit v6 on v5

--- a/solution.py
+++ b/solution.py
@@ -18,10 +18,12 @@
     hi = lax.shift_right_logical(lab, 6)
     lo = jnp.bitwise_and(lab, 63)
     iota = lax.broadcasted_iota(jnp.int32, (64, lab.shape[1]), 0)
-    return iota == hi, jnp.where(iota == lo, 1.0, 0.0)
+    group = 2 * jnp.bitwise_and(iota, 31) + lax.shift_right_logical(iota, 5)
+    return group == hi, jnp.where(iota == lo, 1.0, 0.0)
 
 
 def build_wall(small, out_lab, lab, hi_mask, lo_hot, table, wall_ref):
+    table = jnp.concatenate([table[:, :64], table[:, 64:]], axis=0)
     rows = lax.dot_general(table, lo_hot, (((1,), (0,)), ((), ())), precision=HIGHEST, preferred_element_type=jnp.float32)
     flat = jnp.sum(jnp.where(hi_mask, rows, 0.0), axis=0, keepdims=True) * LOG2E
     outside = jnp.sum(jnp.where(lab == out_lab, flat, 0.0), axis=1, keepdims=True)
@@ -58,28 +60,6 @@
         wall_ref[:, at : at + 768] = jnp.where(tiny, beyond, big[:, :768])
         wall_ref[:, at + 768 : at + 1024] = jnp.where(tiny, inner, big[:, 768:1024])
         wall_ref[:, at + 1024 : at + PLANE] = jnp.where(tiny, beyond, big[:, 1024:PLANE])
-
-
-def bias_kernel(flags_ref, lab_ref, table_ref, wall_ref):
-    lab = lab_ref[...]
-    hi_mask, lo_hot = _labels_hi_lo(lab)
-    build_wall(flags_ref[0], flags_ref[1], lab, hi_mask, lo_hot, table_ref[0], wall_ref.at[0])
-
-
-def bias_tables(flags, lab, table):
-    heads = table.shape[0]
-    return pl.pallas_call(
-        bias_kernel,
-        grid=(heads,),
-        in_specs=[
-            pl.BlockSpec(memory_space=pltpu.SMEM),
-            pl.BlockSpec((1, 4096), lambda h: (0, 0)),
-            pl.BlockSpec((1, 64, 64), lambda h: (h, 0, 0)),
-        ],
-        out_specs=pl.BlockSpec((1, 32, WALL), lambda h: (h, 0, 0)),
-        out_shape=jax.ShapeDtypeStruct((heads, 32, WALL), jnp.float32),
-        compiler_params=pltpu.CompilerParams(vmem_limit_bytes=40 << 20),
-    )(flags, lab, table)
 
 
 def wall_grad(small, out_lab, lab, hi_mask, lo_hot, acc_ref):
@@ -121,29 +101,8 @@
     flat = jnp.sum(wide, axis=0, keepdims=True)
     flat = flat + jnp.where(lab == out_lab, outside, 0.0)
     spread = jnp.where(hi_mask, jnp.broadcast_to(flat, (64, 4096)), 0.0)
-    return lax.dot_general(spread, lo_hot, (((1,), (1,)), ((), ())), precision=HIGHEST, preferred_element_type=jnp.float32)
-
-
-def bias_grad_kernel(flags_ref, lab_ref, acc_ref, out_ref):
-    lab = lab_ref[...]
-    hi_mask, lo_hot = _labels_hi_lo(lab)
-    out_ref[0] = wall_grad(flags_ref[0], flags_ref[1], lab, hi_mask, lo_hot, acc_ref.at[0])
-
-
-def bias_grads(flags, lab, acc):
-    heads = acc.shape[0]
-    return pl.pallas_call(
-        bias_grad_kernel,
-        grid=(heads,),
-        in_specs=[
-            pl.BlockSpec(memory_space=pltpu.SMEM),
-            pl.BlockSpec((1, 4096), lambda h: (0, 0)),
-            pl.BlockSpec((1, 32, WALL), lambda h: (h, 0, 0)),
-        ],
-        out_specs=pl.BlockSpec((1, 64, 64), lambda h: (h, 0, 0)),
-        out_shape=jax.ShapeDtypeStruct((heads, 64, 64), jnp.float32),
-        compiler_params=pltpu.CompilerParams(vmem_limit_bytes=40 << 20),
-    )(flags, lab, acc)
+    res = lax.dot_general(spread, lo_hot, (((1,), (1,)), ((), ())), precision=HIGHEST, preferred_element_type=jnp.float32)
+    return jnp.concatenate([res[:32], res[32:]], axis=1)
 
 
 def label_row(rel_index):
@@ -216,126 +175,6 @@
         lse_ref[h : h + 1, :] = row_max + jnp.log2(row_sum)
         outs.append(o_t.T[:, :HD].astype(jnp.bfloat16))
     return jnp.concatenate(outs, axis=1)
-
-
-def attn_fwd_kernel(order, scale, sc_ref, q_ref, kv_ref, mask_ref, wall_ref, o_ref, lse_ref, s_scr, p_scr):
-    r, c = sc_ref[0], sc_ref[1]
-    qq = quarter(r, c, sc_ref[2 + pl.program_id(0)])
-    keys = [quarter(r, c, j) for j in order]
-    o_ref[...] = attn_block(
-        qq, keys, scale, q_ref, kv_ref, mask_ref[...], wall_ref, lse_ref.at[0], s_scr, p_scr
-    )
-
-
-def attn_fwd(qkv, mask_pad, wall, scalars, order, scale):
-    rows, wide = qkv.shape
-    nq = rows // QB
-    heads = wall.shape[0]
-    width = heads * HD
-    return pl.pallas_call(
-        functools.partial(attn_fwd_kernel, order, scale),
-        grid=(nq,),
-        in_specs=[
-            pl.BlockSpec(memory_space=pltpu.SMEM),
-            pl.BlockSpec((QB, wide), lambda i: (i, 0)),
-            pl.BlockSpec((rows, wide), lambda i: (0, 0)),
-            pl.BlockSpec((rows, 128 - HD), lambda i: (0, 0)),
-            pl.BlockSpec((heads, 32, WALL), lambda i: (0, 0, 0), pipeline_mode=pl.Buffered(1)),
-        ],
-        out_specs=[pl.BlockSpec((QB, width), lambda i: (i, 0)), pl.BlockSpec((1, heads, QB), lambda i: (i, 0, 0))],
-        out_shape=[jax.ShapeDtypeStruct((rows, width), jnp.bfloat16), jax.ShapeDtypeStruct((nq, heads, QB), jnp.float32)],
-        scratch_shapes=[pltpu.VMEM((2, rows, QB), jnp.float32), pltpu.VMEM((2, rows, QB), jnp.bfloat16)],
-        compiler_params=pltpu.CompilerParams(vmem_limit_bytes=40 << 20),
-        cost_estimate=pl.CostEstimate(flops=16 << 30, bytes_accessed=12 << 20, transcendentals=0),
-    )(scalars, qkv, qkv, mask_pad, wall)
-
-
-def attn_bwd_kernel(order, scale, sc_ref, q_ref, kv_ref, do_ref, o_ref, lse_ref, mask_ref, wall_ref,
-                    dqkv_ref, acc_ref, p_scr, s_scr, dq_scr, dk_scr, dv_scr):
-    step = pl.program_id(0)
-    r, c = sc_ref[0], sc_ref[1]
-    qq = quarter(r, c, sc_ref[2 + step])
-    keys = [quarter(r, c, j) for j in order]
-    heads = wall_ref.shape[0]
-    width = heads * HD
-    rows = kv_ref.shape[0]
-
-    @pl.when(step == 0)
-    def _():
-        acc_ref[...] = jnp.zeros_like(acc_ref)
-        dk_scr[...] = jnp.zeros_like(dk_scr)
-        dv_scr[...] = jnp.zeros_like(dv_scr)
-
-    k_extra = mask_ref[...]
-    lane = lax.broadcasted_iota(jnp.int32, (QB, 128 - HD), 1)
-    q_extra = jnp.where(lane == 0, 1.0, 0.0).astype(jnp.bfloat16)
-    dqs = []
-    for h in range(heads):
-        kh = head_lanes(kv_ref, width + HD * h, k_extra)
-        qh = head_lanes(q_ref, HD * h, q_extra)
-        vh = head_lanes(kv_ref, 2 * width + HD * h)
-        doh = head_lanes(do_ref, HD * h)
-        oh = head_lanes(o_ref, HD * h)
-        inner = jnp.sum((doh.astype(jnp.float32) * oh.astype(jnp.float32)).T, axis=0, keepdims=True)
-        lse = lse_ref[0, h : h + 1, :]
-        for kb in range(rows // 256):
-            s_t = dot(kh[256 * kb : 256 * kb + 256], qh, NT)
-            dp_t = dot(vh[256 * kb : 256 * kb + 256], doh, NT)
-            for js in range(8):
-                st = 8 * kb + js
-                start = strip_start(qq, js, keys[kb])
-                s = s_t[32 * js : 32 * js + 32] * (scale * LOG2E) + wall_ref[h, :, pl.ds(start, QB)]
-                p = jnp.exp2(s - lse)
-                ds = p * (dp_t[32 * js : 32 * js + 32] - inner)
-                p_scr[h % 2, 32 * st : 32 * st + 32] = p.astype(jnp.bfloat16)
-                s_scr[h % 2, 32 * st : 32 * st + 32] = ds.astype(jnp.bfloat16)
-                acc_ref[h, :, pl.ds(start, QB)] += ds
-        p_b, ds_b = p_scr[h % 2], s_scr[h % 2]
-        dv_scr[h] += dot(p_b, doh, NN)
-        dk_scr[h] += dot(ds_b, qh, NN)
-        dq_t = dot(kh, ds_b, TN) * scale
-        dqs.append(dq_t.T[:, :HD].astype(jnp.bfloat16))
-    dq_scr[pl.ds(pl.multiple_of(step * QB, QB), QB)] = jnp.concatenate(dqs, axis=1)
-
-    @pl.when(step == pl.num_programs(0) - 1)
-    def _():
-        parts = [dq_scr[...]]
-        parts += [(dk_scr[h, :, :HD] * scale).astype(jnp.bfloat16) for h in range(heads)]
-        parts += [dv_scr[h, :, :HD].astype(jnp.bfloat16) for h in range(heads)]
-        dqkv_ref[...] = jnp.concatenate(parts, axis=1)
-
-
-def attn_bwd(qkv, do, o, lse, mask_pad, wall, scalars, order, scale):
-    rows, wide = qkv.shape
-    nq = rows // QB
-    heads = wall.shape[0]
-    width = heads * HD
-    row_spec = pl.BlockSpec((QB, width), lambda i: (i, 0))
-    return pl.pallas_call(
-        functools.partial(attn_bwd_kernel, order, scale),
-        grid=(nq,),
-        in_specs=[
-            pl.BlockSpec(memory_space=pltpu.SMEM),
-            pl.BlockSpec((QB, wide), lambda i: (i, 0)),
-            pl.BlockSpec((rows, wide), lambda i: (0, 0)),
-            row_spec,
-            row_spec,
-            pl.BlockSpec((1, heads, QB), lambda i: (i, 0, 0)),
-            pl.BlockSpec((rows, 128 - HD), lambda i: (0, 0)),
-            pl.BlockSpec((heads, 32, WALL), lambda i: (0, 0, 0), pipeline_mode=pl.Buffered(1)),
-        ],
-        out_specs=[pl.BlockSpec((rows, wide), lambda i: (0, 0)), pl.BlockSpec((heads, 32, WALL), lambda i: (0, 0, 0))],
-        out_shape=[jax.ShapeDtypeStruct((rows, wide), jnp.bfloat16), jax.ShapeDtypeStruct((heads, 32, WALL), jnp.float32)],
-        scratch_shapes=[
-            pltpu.VMEM((2, rows, QB), jnp.bfloat16),
-            pltpu.VMEM((2, rows, QB), jnp.bfloat16),
-            pltpu.VMEM((rows, width), jnp.bfloat16),
-            pltpu.VMEM((heads, rows, 128), jnp.float32),
-            pltpu.VMEM((heads, rows, 128), jnp.float32),
-        ],
-        compiler_params=pltpu.CompilerParams(vmem_limit_bytes=48 << 20),
-        cost_estimate=pl.CostEstimate(flops=24 << 30, bytes_accessed=20 << 20, transcendentals=0),
-    )(scalars, qkv, qkv, do, o, lse, mask_pad, wall)
 
 
 EPSILON = 1e-05
@@ -408,6 +247,7 @@
     def make(self, src, dst, to, cond=None, track=True):
         k = self.used
         self.used += 1
+        assert k < self.send_sem.shape[0]
         copy = pltpu.make_async_remote_copy(
             src_ref=src,
             dst_ref=dst,
@@ -821,11 +661,11 @@
 
     g1.forward(0)
     ex1.done()
-    mlp(0)
-    g1.forward(1)
-    s2.middle(0)
-    mlp(1)
-    s2.middle(1)
+    for i in range(NCH):
+        mlp(i)
+        if i + 1 < NCH:
+            g1.forward(i + 1)
+        s2.middle(i)
     stores = [
         start_load(src, dst, store_sem.at[k])
         for k, (src, dst) in enumerate(((gat1, n2_hbm), (u_buf, u_hbm), (g_buf, g_hbm), (w1, w1_out), (w2, w2_out)))
@@ -1002,11 +842,11 @@
     g1.forward(0)
     ex1.done()
     ex2.done()
-    mlp(0)
-    g1.forward(1)
-    s2.middle(0)
-    mlp(1)
-    s2.middle(1)
+    for i in range(NCH):
+        mlp(i)
+        if i + 1 < NCH:
+            g1.forward(i + 1)
+        s2.middle(i)
     slab_grad(fc2, 0, dm[...], g_buf[...])
     if fold:
         reduce = DpReduce(links, fc2, lands[0])
@@ -1028,7 +868,8 @@
         y = dot(g_buf[pl.ds(b * rows, rows)], w2[...].reshape(width, -1), NT)
         y_buf[pl.ds(b * rows, rows)] = y.astype(jnp.bfloat16)
     stores.append(start_load(y_buf, y_hbm, store_sem.at[1]))
-    g2.forward(1)
+    for i in range(1, NCH):
+        g2.forward(i)
     for i in range(NCH):
         put_rows(do_ref, dot(g2.done(i), wp[...], NN).astype(jnp.bfloat16), i, rows)
     stores.append(start_load(gat2, da_hbm, store_sem.at[2]))
@@ -1170,11 +1011,11 @@
         scatter_product(s2, i, lambda b: du[b * n : (b + 1) * n], w1[...], rows)
 
     g1.forward(0)
-    mlp(0)
-    g1.forward(1)
-    s2.middle(0)
-    mlp(1)
-    s2.middle(1)
+    for i in range(NCH):
+        mlp(i)
+        if i + 1 < NCH:
+            g1.forward(i + 1)
+        s2.middle(i)
     if fold:
         reduce.middle()
     load_g.wait()
@@ -1200,7 +1041,8 @@
     load_p.wait()
     g2.forward(0)
     bias_head(3, load_strip)
-    g2.forward(1)
+    for i in range(1, NCH):
+        g2.forward(i)
     for i in range(NCH):
         put_rows(do_ref, dot(g2.done(i), wp[...], NN).astype(jnp.bfloat16), i, rows)
     stores.append(start_load(gat2, da_hbm, store_sem.at[2]))
@@ -1245,7 +1087,7 @@
             out((n, hidden), bf16),
             out((n, hidden) if fold else (2, 2, n, hidden), bf16),
             out((n, qp_cols) if fold else (2, 2, n, qp_cols), bf16),
-            out((heads, 64, 64), f32),
+            out((heads, 32, 128), f32),
             out((1, 2 * lw), f32),
         ]
         + [out(block.shape, block.dtype) for block in blocks for _ in range(2)]
@@ -1524,13 +1366,14 @@
     def event(i):
         if fold:
             pl.when(i == 0)(finished)
-            pl.when(i == 2)(lambda: reduce.middle())
 
     attn_back(
         links, order, scale, qkv_ref, do_ref, o_ref, lse_ref, mask_ref[...], wall, acc, p_scr, s_scr, dq_scr, dk_scr, dv_scr,
         dqkv_ref, event,
     )
     stores = [start_load(acc, acc_hbm, store_sem.at[0])]
+    if fold:
+        reduce.middle()
     if summed:
         near.wait_recv()
         to_partner.wait_recv()
@@ -1669,7 +1512,6 @@
     def event(i):
         if fold:
             pl.when(i == 0)(finished)
-            pl.when(i == 2)(lambda: reduce_f.middle())
 
     def attention(wall, p_scr, s_scr, dq_scr, dk_scr, dv_scr):
         load_w = start_load(wall_hbm, wall, load_sem.at[0])
@@ -1696,21 +1538,19 @@
 
     def rest(wq, rows_buf, wide1):
         s1 = Scatter(links, low1, wide1)
+        load_q = start_load(wq_hbm, wq, load_sem.at[2])
         load_n = start_load(n1_hbm, rows_buf, load_sem.at[3])
-        load_q = start_load(wq_hbm, wq, load_sem.at[2])
-        load_n.wait()
-        slab_grad(gq, 0, rows_buf[...], dqkv_ref[...])
-        if fold:
-            reduce_q.start()
         load_q.wait()
         for i in range(NCH):
             scatter_product(s1, i, lambda b: block_rows(dqkv_ref, b, i, rows), wq[...], rows)
             if i:
                 s1.middle(i - 1)
         s1.middle(NCH - 1)
+        load_n.wait()
+        slab_grad(gq, 0, rows_buf[...], dqkv_ref[...])
         if fold:
-            reduce_f.done(fc_out)
-            returns[early + 1].start()
+            reduce_f.middle()
+            reduce_q.start()
         cols = jnp.sum(dqkv_ref[...].astype(jnp.float32), axis=0, keepdims=True)
         mine = jnp.concatenate([cols[:, :lw], cols[:, 2 * lw :]], axis=1)
         images = (smalls.shape[0] - 8) // 2
@@ -1729,7 +1569,13 @@
 
             lax.fori_loop(a, b, one, 0)
 
+        hops = [ACROSS] + [("dp", b) for b in range(bits)]
+        small_hops = SumHops(links, smalls, small_land, hops)
+        rel_hops = SumHops(links, rel, rel_land, hops)
         heads_of(0, heads // 2)
+        if fold:
+            reduce_f.done(fc_out)
+            returns[early + 1].start()
         late = None
         for i in range(NCH):
             at = chunk(i, rows)
@@ -1740,24 +1586,18 @@
             both = jnp.concatenate([dgain, dshift], axis=0)
             late = both if late is None else late + both
         smalls[0:2] = late
-        hops = [ACROSS] + [("dp", b) for b in range(bits)]
-        small_hops = SumHops(links, smalls, small_land, hops)
         small_hops.send()
+        heads_of(heads // 2, heads)
+        rel_hops.send()
         returns[early].start()
-        heads_of(heads // 2, heads)
-        rel_hops = SumHops(links, rel, rel_land, hops)
-        rel_hops.send()
         if fold:
             reduce_q.middle()
-        small_hops.take()
-        rel_hops.take()
-        if fold:
             reduce_q.done(q_out)
             returns[early + 2].start()
         else:
             q_out[...] = gq[...]
             all_fc[...] = fc[...]
-        for _ in range(bits):
+        for _ in range(bits + 1):
             small_hops.take()
             rel_hops.take()
         images_at = pl.ds(8, smalls.shape[0] - 8)
@@ -1806,7 +1646,7 @@
     outs = [
         out((rows, width), f32),
         out((count, width), f32),
-        out((heads, 64, 64), f32),
+        out((heads, 32, 128), f32),
         out((n, wide) if fold else (2, 2, n, wide), bf16),
     ]
     if fold:
@@ -1828,9 +1668,9 @@
             pltpu.VMEM((2, 2, n, fc_cols), bf16),
             pltpu.VMEM((rows, width), bf16),
             pltpu.VMEM((6, rows, width), bf16),
-            pltpu.VMEM((2, heads, 64, 64), f32),
-            pltpu.VMEM((hops, 2, heads, 64, 64), f32),
-            pltpu.VMEM((heads, 64, 64), f32),
+            pltpu.VMEM((2, heads, 32, 128), f32),
+            pltpu.VMEM((hops, 2, heads, 32, 128), f32),
+            pltpu.VMEM((heads, 32, 128), f32),
             pltpu.VMEM((count, width), f32),
             pltpu.VMEM((hops, count, width), f32),
             pltpu.VMEM((2, 8, width), f32),
@@ -1925,7 +1765,7 @@
     def by_bits(w):
         return w.reshape(2, 2, -1, w.shape[-1])
 
-    table = jnp.pad(rel_table[0], ((0, 0), (0, 4096 - buckets))).reshape(heads, 64, 64)
+    table = jnp.pad(rel_table[0], ((0, 0), (0, 4096 - buckets))).reshape(heads, 32, 128)
     time_all = jnp.einsum("id,dcn->icn", time_emb, w_time[0], preferred_element_type=f32)
     gap = jnp.zeros((2, local_width), f32)
     time_rows = jnp.concatenate([time_all[:, 0], gap, time_all[:, 1], gap], axis=1)
@@ -2079,8 +1919,8 @@
     norms_mine = jnp.where(first, norms[:4], norms[4:]).reshape(2, 2, width)
     cols = width // (4 * ndp)
     norms_mine = lax.dynamic_slice_in_dim(norms_mine, (d * 4 + z) * cols, cols, 2)
-    sums_of, emb_of = sums_all[: 2 * ndp], sums_all[2 * ndp :]
-    sums_mine = jnp.where(first, sums_of[:, : 2 * local_width], sums_of[:, 2 * local_width :])
+    emb_of = sums_all[2 * ndp :]
+    sums_mine = jnp.where(first, sums_all[: 2 * ndp, : 2 * local_width], sums_all[: 2 * ndp, 2 * local_width :])
     emb_mine = lax.dynamic_slice_in_dim(emb_of, d * (width // ndp), width // ndp, 1)
     grad_time = lax.dot_general(
         emb_mine, sums_mine, (((0,), (0,)), ((), ())), precision=lax.Precision.HIGHEST, preferred_element_type=f32

time: 595 us -> 578 us (0.971)
  Pallas kernels: 530 us -> 515 us
    pallas_call x1, Pallas kernels: 122 us -> 109 us  [end_chain(): pl.pallas_call(functools.partial(end_kernel, order, scale, bits, fold, la...]
    unnamed x76 -> x83, local copies, waits for them, and re-layouts: 12.4 us -> 13.3 us
where the time goes in v6:
time: 578 us; the launch traced here: 574 us
  Pallas kernels  515 us (89%)
  local copies, waits for them, and re-layouts  34 us (6%)
  other arithmetic  20.4 us (4%)
    pallas_call x1, Pallas kernels, mid_chain(): pl.pallas_call(functools.partial(mid_kernel, order, scale, bits), in_spec...  122 us
    pallas_call x1, Pallas kernels, end_chain(): pl.pallas_call(functools.partial(end_kernel, order, scale, bits, fold, la...  109 us
    pallas_call x1, Pallas kernels, back_chain(): pl.pallas_call(functools.partial(back_kernel, bits, fold, layers), in_spe...  88 us
    pallas_call x1, Pallas kernels, start_chain(): pl.pallas_call(functools.partial(start_kernel, order, scale, bits), in_sp...  81.9 us
    pallas_call x1, Pallas kernels, turn_chain(): pl.pallas_call(functools.partial(turn_kernel, bits, fold), in_specs=[VM,...  72 us
    pallas_call x1, Pallas kernels, bwd_chain(): pl.pallas_call(functools.partial(bwd_kernel, order, scale, bits, fold, la...  41 us
    unnamed x83, local copies, waits for them, and re-layouts  13.3 us

profile of v6, /device:TPU:1, one launch (start us, length us, event | category | flops | bytes accessed | tf_op | source)
XLA Modules:
  0.0 573.8 jit_solution(11899730665325662674)
XLA Ops:
  1.8 1.2 dynamic_slice.37
  3.7 1.3 slice.151
  8.1 2.7 fusion.15
  11.2 1.5 copy.38
  12.8 2.3 copy.39
  15.1 3.5 pad_maximum_fusion.wq_hbm.own_q
  19.7 1.2 copy.40
  21.0 81.9 %shard_map.213 = (bf16[256,1152]{1,0:T(8,128)(2,1)S(1)}, bf16[256,1152]{1,0:T(8,128)(2,1)S(1)}, f32[2,8,1152]{2,1,0:T(8,128)S(1)}, f32[4,4,256]{2,1,0:T(4,128)S(...) custom-call(s32[2]{0:T(128)S(1)} %pad_add_fusion.flags_ref, ...), custom_call_target="tpu_custom_call" | custom-call | flops 85899345920 | bytes 25165824 | tf_op jit(solution)/shard_map/pallas_call | solution.py:1230
  105.1 122.4 %shard_map.214 = (f32[256,1152]{1,0:T(8,128)}, bf16[256,1152]{1,0:T(8,128)(2,1)S(1)}, f32[256,1152]{1,0:T(8,128)}, bf16[1024,288]{1,0:T(8,128)(2,1)}, f32[4,4,25...) custom-call(bf16[256,1152]{1,0:T(8,128)(2,1)S(1)} %get-tuple-element, ...), custom_call_target="tpu_custom_call" | custom-call | flops 64424509440 | bytes 25165824 | tf_op jit(solution)/shard_map/pallas_call | solution.py:753
  227.6 72.0 %shard_map.215 = (f32[256,1152]{1,0:T(8,128)}, f32[2,1152]{1,0:T(2,128)S(1)}, f32[256,1152]{1,0:T(8,128)}, bf16[1024,288]{1,0:T(8,128)(2,1)}, bf16[288,1152]{1,0...) custom-call(bf16[256,1152]{1,0:T(8,128)(2,1)S(1)} %get-tuple-element, ...), custom_call_target="tpu_custom_call" | custom-call | flops 64424509440 | bytes 25165824 | tf_op jit(solution)/shard_map/pallas_call | solution.py:894
  301.3 41.0 %shard_map.216 = (bf16[1024,864]{1,0:T(8,128)(2,1)}, f32[4,32,14336]{2,1,0:T(8,128)}, bf16[288,1152]{1,0:T(8,128)(2,1)}, bf16[288,1152]{1,0:T(8,128)(2,1)}, bf16...) custom-call(bf16[1024,864]{1,0:T(8,128)(2,1)} %get-tuple-element.100, ...), custom_call_target="tpu_custom_call" | custom-call | flops 25769803776 | bytes 20971520 | tf_op jit(solution)/shard_map/pallas_call | solution.py:1428
  342.3 88.0 %shard_map.217 = (f32[256,1152]{1,0:T(8,128)}, f32[256,1152]{1,0:T(8,128)}, f32[4,1152]{1,0:T(4,128)S(1)}, bf16[1024,288]{1,0:T(8,128)(2,1)}, bf16[4,256,1152]{2...) custom-call(s32[2]{0:T(128)S(1)} %copy-done.10, ...), custom_call_target="tpu_custom_call" | custom-call | flops 64424509440 | bytes 25165824 | tf_op jit(solution)/shard_map/pallas_call | solution.py:1076
  433.4 109.5 %shard_map.218 = (f32[256,1152]{1,0:T(8,128)}, f32[24,1152]{1,0:T(8,128)S(1)}, f32[4,32,128]{2,1,0:T(8,128)S(1)}, bf16[288,864]{1,0:T(8,128)(2,1)S(1)}, bf16[288...) custom-call(s32[2]{0:T(128)S(1)} %copy-done.10, ...), custom_call_target="tpu_custom_call" | custom-call | flops 96636764160 | bytes 25165824 | tf_op jit(solution)/shard_map/pallas_call | solution.py:1659
  544.5 3.4 select_bitcast_fusion
  549.4 1.3 fusion
  551.6 1.1 fusion.5
  552.8 1.7 fusion.7
  554.5 2.7 broadcast_in_dim_reshape.7
  557.2 2.7 slice_select_fusion.1
  559.9 2.7 copy.42
  562.6 2.9 copy.44
  565.5 1.9 fusion.3
  567.5 1.6 maximum_bitcast_fusion
  570.5 1.2 select_bitcast_fusion.2
  (131 shorter events, 19.6 us)
Async XLA Ops:
  0.6 17.9 %copy-start = (bf16[1,1152,2,288]{1,3,2,0:T(8,128)(2,1)S(1)}, bf16[1,1152,2,288]{1,3,2,0:T(8,128)(2,1)}, u32[]{:S(2)}) copy-start(bf16[1,1152,2,288]{1,3,2,0:T(8,128)(2,1)} %param.20) | copy-start | bytes 3981316
  5.7 15.3 %copy-start.9 = (s32[2]{0:T(128)}, s32[2]{0:T(128)S(1)}, u32[]{:S(2)}) copy-start(s32[2]{0:T(128)S(1)} %pad_add_fusion.flags_ref) | copy-start | bytes 28
  8.1 12.9 %copy-start.6 = (s32[1,4096]{1,0:T(1,128)}, s32[1,4096]{1,0:T(1,128)S(1)}, u32[]{:S(2)}) copy-start(s32[1,4096]{1,0:T(1,128)S(1)} %reshape.152.lab_ref) | copy-start | bytes 49156
  15.1 3.5 copy-start.35
  18.6 2.3 copy-start.34
  19.3 1.6 copy-start.32
  103.7 123.9 %copy-start.13 = (bf16[256,1152]{1,0:T(8,128)(2,1)}, bf16[256,1152]{1,0:T(8,128)(2,1)S(1)}, u32[]{:S(2)}) copy-start(bf16[256,1152]{1,0:T(8,128)(2,1)S(1)} %get-tuple-element.91.x_ref) | copy-start | bytes 1769476
  103.7 123.9 %copy-start.17 = (f32[4,4,256]{2,1,0:T(4,128)}, f32[4,4,256]{2,1,0:T(4,128)S(1)}, u32[]{:S(2)}) copy-start(f32[4,4,256]{2,1,0:T(4,128)S(1)} %get-tuple-element.134.lse_ref) | copy-start | bytes 49156
  227.6 72.0 %copy-start.2 = (bf16[256,1152]{1,0:T(8,128)(2,1)}, bf16[256,1152]{1,0:T(8,128)(2,1)S(1)}, u32[]{:S(2)}) copy-start(bf16[256,1152]{1,0:T(8,128)(2,1)S(1)} %get-tuple-element.99.x_ref.refs_0_) | copy-start | bytes 1769476
  301.3 41.0 %copy-start.7 = (s32[1,4096]{1,0:T(1,128)S(1)}, s32[1,4096]{1,0:T(1,128)}, u32[]{:S(2)}) copy-start(s32[1,4096]{1,0:T(1,128)} %copy-done.6) | copy-start | bytes 49156
  301.3 41.0 %copy-start.10 = (s32[2]{0:T(128)S(1)}, s32[2]{0:T(128)}, u32[]{:S(2)}) copy-start(s32[2]{0:T(128)} %copy-done.9) | copy-start | bytes 28
  342.3 88.6 %copy-start.36 = (bf16[2,1152]{1,0:T(2,128)(2,1)S(1)}, bf16[2,1152]{1,0:T(2,128)(2,1)}, u32[]{:S(2)}) copy-start(bf16[2,1152]{1,0:T(2,128)(2,1)} %param.15) | copy-start | bytes 13828
  342.3 88.8 %copy-start.33 = (f32[2,1152]{1,0:T(2,128)S(1)}, f32[2,1152]{1,0:T(2,128)}, u32[]{:S(2)}) copy-start(f32[2,1152]{1,0:T(2,128)} %copy-done.32) | copy-start | bytes 27652
  544.5 3.4 copy-start.22
  544.5 3.4 copy-start.23
  544.5 3.4 copy-start.24
  547.9 1.5 copy-start.27
  549.4 1.4 copy-start.29
  549.4 1.5 copy-start.30
  549.4 2.0 copy-start.31
  565.5 1.9 copy-start.20
  565.5 1.9 copy-start.21
  567.5 2.9 copy-start.3
  571.7 1.6 copy-start.1
  (15 other events, 13.1 us)

commit v7 on v6

--- a/solution.py
+++ b/solution.py
@@ -382,6 +382,24 @@
             when(cond, copy.wait)
 
 
+class PartStore:
+    def __init__(self, links, layer, src, dst, sem):
+        at = bits_region(links, ())
+        self.ways = (
+            (links.home & (links.pair != layer), pltpu.make_async_copy(src, dst, sem)),
+            (jnp.logical_not(links.home), pltpu.make_async_copy(src.at[at], dst.at[at], sem)),
+        )
+
+    def start(self):
+        for cond, copy in self.ways:
+            when(cond, copy.start)
+        return self
+
+    def wait(self):
+        for cond, copy in self.ways:
+            when(cond, copy.wait)
+
+
 def chunk(i, rows):
     return pl.ds(i * (rows // NCH), rows // NCH)
 
@@ -612,7 +630,7 @@
                wp_hbm, got1_hbm, got2_hbm, wall_hbm, own_q, own_p, own_1, own_2,
                hid_ref, act_ref, dy_ref, o1_ref, lse_ref,
                n2_hbm, u_hbm, g_hbm, n1_hbm, qkv_hbm, dm_hbm, w1_out, w2_out, next_q, next_p, next_1, next_2,
-               wp, w1, w2, got_q, got_p, wall, u_buf, g_buf, qkv, gat1, gat2, gat3, low, wide, s_scr, p_scr,
+               wp, w1, w2, got_q, got_p, got_1, got_2, wall, u_buf, g_buf, qkv, gat1, gat2, gat3, low, wide, s_scr, p_scr,
                load_sem, store_sem, send_sem, recv_sem):
     rows, width = x_ref.shape
     n = rows // NCH
@@ -625,7 +643,7 @@
     ex1, ex2 = Exchange(links, w1), Exchange(links, w2)
     exq, exp = Exchange(links, got_q), Exchange(links, got_p)
     get_q, get_p = Deliver(links, 1, own_q, got_q, load_sem.at[4]), Deliver(links, 1, own_p, got_p, load_sem.at[5])
-    get_1, get_2 = Deliver(links, 1, own_1, next_1), Deliver(links, 1, own_2, next_2)
+    get_1, get_2 = Deliver(links, 1, own_1, got_1), Deliver(links, 1, own_2, got_2)
     s1, s2 = Scatter(links, low, wide), Scatter(links, low, wide)
     g1, g2, g3 = Gather(links, gat1), Gather(links, gat2), Gather(links, gat3)
     load_p.wait()
@@ -719,8 +737,9 @@
         g3.copies["s", i].wait_recv()
         g3.copies["f", i].wait_recv()
     stores.append(start_load(gat3, dm_hbm, store_sem.at[9]))
-    get_1.done()
-    get_2.done()
+    for k, (get, src, dst) in enumerate(((get_1, got_1, next_1), (get_2, got_2, next_2))):
+        get.done()
+        stores.append(PartStore(links, 1, src, dst, store_sem.at[10 + k]).start())
     links.leave()
     for store in stores:
         store.wait()
@@ -769,7 +788,7 @@
         ]
         + [out(w.shape, bf16) for w in (w1, w2, *own)],
         scratch_shapes=[
-            *[pltpu.VMEM(w.shape, bf16) for w in (wp, w1, w2, *own[:2])],
+            *[pltpu.VMEM(w.shape, bf16) for w in (wp, w1, w2, *own)],
             pltpu.VMEM(wall.shape, f32),
             pltpu.VMEM((4 * rows, hidden), bf16),
             pltpu.VMEM((4 * rows, hidden), bf16),
@@ -781,7 +800,7 @@
             pltpu.VMEM((2, 4 * rows, QB), f32),
             pltpu.VMEM((2, 4 * rows, QB), bf16),
             pltpu.SemaphoreType.DMA((6,)),
-            pltpu.SemaphoreType.DMA((10,)),
+            pltpu.SemaphoreType.DMA((12,)),
             *comm_scratch(2 * Scatter.COPIES + 3 * Gather.COPIES + 4 * Deliver.COPIES + 4 * Exchange.copies(bits)),
         ],
         compiler_params=params(1),
@@ -1928,7 +1947,7 @@
     return (
         acts,
         input_grads,
-        grad_q.reshape(width // ndp, 3, local_width)[None],
+        jnp.stack([grad_q[:, j * local_width : (j + 1) * local_width] for j in range(3)], axis=1)[None],
         grad_time[None],
         grad_p[None],
         grad_fc1[None],

time: 578 us -> 573 us (level)
    unnamed x83 -> x82, local copies, waits for them, and re-layouts: 13.3 us -> 10.4 us
where the time goes in v7:
time: 573 us; the launch traced here: 569 us
  Pallas kernels  515 us (90%)
  local copies, waits for them, and re-layouts  28.6 us (5%)
  other arithmetic  20.6 us (4%)
    pallas_call x1, Pallas kernels, mid_chain(): pl.pallas_call(functools.partial(mid_kernel, order, scale, bits), in_spec...  123 us
    pallas_call x1, Pallas kernels, end_chain(): pl.pallas_call(functools.partial(end_kernel, order, scale, bits, fold, la...  109 us
    pallas_call x1, Pallas kernels, back_chain(): pl.pallas_call(functools.partial(back_kernel, bits, fold, layers), in_spe...  88.1 us
    pallas_call x1, Pallas kernels, start_chain(): pl.pallas_call(functools.partial(start_kernel, order, scale, bits), in_sp...  81.9 us
    pallas_call x1, Pallas kernels, turn_chain(): pl.pallas_call(functools.partial(turn_kernel, bits, fold), in_specs=[VM,...  72.1 us
    pallas_call x1, Pallas kernels, bwd_chain(): pl.pallas_call(functools.partial(bwd_kernel, order, scale, bits, fold, la...  40.8 us

profile of v7, /device:TPU:1, one launch (start us, length us, event | category | flops | bytes accessed | tf_op | source)
XLA Modules:
  0.0 569.0 jit_solution(14583466407664903639)
XLA Ops:
  1.8 1.2 dynamic_slice.37
  3.7 1.3 slice.160
  8.1 2.7 fusion.15
  11.2 1.5 copy.30
  12.8 2.3 copy.31
  15.1 3.5 pad_maximum_fusion.wq_hbm.own_q
  19.7 1.2 copy.32
  21.0 81.9 %shard_map.213 = (bf16[256,1152]{1,0:T(8,128)(2,1)S(1)}, bf16[256,1152]{1,0:T(8,128)(2,1)S(1)}, f32[2,8,1152]{2,1,0:T(8,128)S(1)}, f32[4,4,256]{2,1,0:T(4,128)S(...) custom-call(s32[2]{0:T(128)S(1)} %pad_add_fusion.flags_ref, ...), custom_call_target="tpu_custom_call" | custom-call | flops 85899345920 | bytes 25165824 | tf_op jit(solution)/shard_map/pallas_call | solution.py:1249
  105.1 122.9 %shard_map.214 = (f32[256,1152]{1,0:T(8,128)}, bf16[256,1152]{1,0:T(8,128)(2,1)S(1)}, f32[256,1152]{1,0:T(8,128)}, bf16[1024,288]{1,0:T(8,128)(2,1)}, f32[4,4,25...) custom-call(bf16[256,1152]{1,0:T(8,128)(2,1)S(1)} %get-tuple-element, ...), custom_call_target="tpu_custom_call" | custom-call | flops 64424509440 | bytes 25165824 | tf_op jit(solution)/shard_map/pallas_call | solution.py:772
  228.1 72.1 %shard_map.215 = (f32[256,1152]{1,0:T(8,128)}, f32[2,1152]{1,0:T(2,128)S(1)}, f32[256,1152]{1,0:T(8,128)}, bf16[1024,288]{1,0:T(8,128)(2,1)}, bf16[288,1152]{1,0...) custom-call(bf16[256,1152]{1,0:T(8,128)(2,1)S(1)} %get-tuple-element, ...), custom_call_target="tpu_custom_call" | custom-call | flops 64424509440 | bytes 25165824 | tf_op jit(solution)/shard_map/pallas_call | solution.py:913
  301.9 40.8 %shard_map.216 = (bf16[1024,864]{1,0:T(8,128)(2,1)}, f32[4,32,14336]{2,1,0:T(8,128)}, bf16[288,1152]{1,0:T(8,128)(2,1)}, bf16[288,1152]{1,0:T(8,128)(2,1)}, bf16...) custom-call(bf16[1024,864]{1,0:T(8,128)(2,1)} %get-tuple-element.100, ...), custom_call_target="tpu_custom_call" | custom-call | flops 25769803776 | bytes 20971520 | tf_op jit(solution)/shard_map/pallas_call | solution.py:1447
  342.7 88.1 %shard_map.217 = (f32[256,1152]{1,0:T(8,128)}, f32[256,1152]{1,0:T(8,128)}, f32[4,1152]{1,0:T(4,128)S(1)}, bf16[1024,288]{1,0:T(8,128)(2,1)}, bf16[4,256,1152]{2...) custom-call(s32[2]{0:T(128)S(1)} %copy-done.10, ...), custom_call_target="tpu_custom_call" | custom-call | flops 64424509440 | bytes 25165824 | tf_op jit(solution)/shard_map/pallas_call | solution.py:1095
  433.8 109.4 %shard_map.218 = (f32[256,1152]{1,0:T(8,128)}, f32[24,1152]{1,0:T(8,128)S(1)}, f32[4,32,128]{2,1,0:T(8,128)S(1)}, bf16[288,864]{1,0:T(8,128)(2,1)S(1)}, bf16[288...) custom-call(s32[2]{0:T(128)S(1)} %copy-done.10, ...), custom_call_target="tpu_custom_call" | custom-call | flops 96636764160 | bytes 25165824 | tf_op jit(solution)/shard_map/pallas_call | solution.py:1678
  544.8 3.4 select_bitcast_fusion
  549.7 1.3 fusion
  551.9 1.1 fusion.5
  553.1 1.7 fusion.7
  554.9 2.7 broadcast_in_dim_reshape.3
  557.5 1.7 slice_select_fusion.1
  559.5 1.2 maximum_bitcast_fusion.1
  560.7 1.9 fusion.3
  562.8 1.6 maximum_bitcast_fusion
  565.7 1.2 select_bitcast_fusion.2
  567.1 1.1 maximum_bitcast_fusion.2
  (131 shorter events, 18.8 us)
Async XLA Ops:
  0.6 17.9 %copy-start = (bf16[1,1152,2,288]{1,3,2,0:T(8,128)(2,1)S(1)}, bf16[1,1152,2,288]{1,3,2,0:T(8,128)(2,1)}, u32[]{:S(2)}) copy-start(bf16[1,1152,2,288]{1,3,2,0:T(8,128)(2,1)} %param.20) | copy-start | bytes 3981316
  5.7 15.3 %copy-start.9 = (s32[2]{0:T(128)}, s32[2]{0:T(128)S(1)}, u32[]{:S(2)}) copy-start(s32[2]{0:T(128)S(1)} %pad_add_fusion.flags_ref) | copy-start | bytes 28
  8.1 12.9 %copy-start.6 = (s32[1,4096]{1,0:T(1,128)}, s32[1,4096]{1,0:T(1,128)S(1)}, u32[]{:S(2)}) copy-start(s32[1,4096]{1,0:T(1,128)S(1)} %reshape.152.lab_ref) | copy-start | bytes 49156
  15.1 3.5 copy-start.35
  18.6 2.3 copy-start.34
  19.3 1.6 copy-start.32
  103.7 124.4 %copy-start.13 = (bf16[256,1152]{1,0:T(8,128)(2,1)}, bf16[256,1152]{1,0:T(8,128)(2,1)S(1)}, u32[]{:S(2)}) copy-start(bf16[256,1152]{1,0:T(8,128)(2,1)S(1)} %get-tuple-element.91.x_ref) | copy-start | bytes 1769476
  103.7 124.4 %copy-start.17 = (f32[4,4,256]{2,1,0:T(4,128)}, f32[4,4,256]{2,1,0:T(4,128)S(1)}, u32[]{:S(2)}) copy-start(f32[4,4,256]{2,1,0:T(4,128)S(1)} %get-tuple-element.134.lse_ref) | copy-start | bytes 49156
  228.1 72.1 %copy-start.2 = (bf16[256,1152]{1,0:T(8,128)(2,1)}, bf16[256,1152]{1,0:T(8,128)(2,1)S(1)}, u32[]{:S(2)}) copy-start(bf16[256,1152]{1,0:T(8,128)(2,1)S(1)} %get-tuple-element.99.x_ref.refs_0_) | copy-start | bytes 1769476
  301.9 40.8 %copy-start.7 = (s32[1,4096]{1,0:T(1,128)S(1)}, s32[1,4096]{1,0:T(1,128)}, u32[]{:S(2)}) copy-start(s32[1,4096]{1,0:T(1,128)} %copy-done.6) | copy-start | bytes 49156
  301.9 40.8 %copy-start.10 = (s32[2]{0:T(128)S(1)}, s32[2]{0:T(128)}, u32[]{:S(2)}) copy-start(s32[2]{0:T(128)} %copy-done.9) | copy-start | bytes 28
  342.7 88.6 %copy-start.36 = (bf16[2,1152]{1,0:T(2,128)(2,1)S(1)}, bf16[2,1152]{1,0:T(2,128)(2,1)}, u32[]{:S(2)}) copy-start(bf16[2,1152]{1,0:T(2,128)(2,1)} %param.15) | copy-start | bytes 13828
  342.7 88.8 %copy-start.33 = (f32[2,1152]{1,0:T(2,128)S(1)}, f32[2,1152]{1,0:T(2,128)}, u32[]{:S(2)}) copy-start(f32[2,1152]{1,0:T(2,128)} %copy-done.32) | copy-start | bytes 27652
  544.8 3.4 copy-start.22
  544.8 3.4 copy-start.23
  544.8 3.4 copy-start.24
  548.2 1.5 copy-start.27
  549.7 1.4 copy-start.29
  549.7 1.5 copy-start.30
  549.7 2.0 copy-start.31
  560.7 1.9 copy-start.20
  560.7 1.9 copy-start.21
  562.8 2.9 copy-start.3
  567.0 1.6 copy-start.1
  (15 other events, 13.1 us)

commit v8 on v7

--- a/solution.py
+++ b/solution.py
@@ -1941,9 +1941,19 @@
     emb_of = sums_all[2 * ndp :]
     sums_mine = jnp.where(first, sums_all[: 2 * ndp, : 2 * local_width], sums_all[: 2 * ndp, 2 * local_width :])
     emb_mine = lax.dynamic_slice_in_dim(emb_of, d * (width // ndp), width // ndp, 1)
-    grad_time = lax.dot_general(
-        emb_mine, sums_mine, (((0,), (0,)), ((), ())), precision=lax.Precision.HIGHEST, preferred_element_type=f32
-    ).reshape(width // ndp, 2, local_width)
+    grad_time = jnp.stack(
+        [
+            lax.dot_general(
+                emb_mine,
+                sums_mine[:, j * local_width : (j + 1) * local_width],
+                (((0,), (0,)), ((), ())),
+                precision=lax.Precision.HIGHEST,
+                preferred_element_type=f32,
+            )
+            for j in range(2)
+        ],
+        axis=1,
+    )
     return (
         acts,
         input_grads,

time: 573 us -> 571 us (level)
  no operation moved by 1% of the time
where the time goes in v8:
time: 571 us; the launch traced here: 567 us
  Pallas kernels  515 us (90%)
  local copies, waits for them, and re-layouts  27.7 us (5%)
  other arithmetic  19.5 us (3%)
    pallas_call x1, Pallas kernels, mid_chain(): pl.pallas_call(functools.partial(mid_kernel, order, scale, bits), in_spec...  123 us
    pallas_call x1, Pallas kernels, end_chain(): pl.pallas_call(functools.partial(end_kernel, order, scale, bits, fold, la...  109 us
    pallas_call x1, Pallas kernels, back_chain(): pl.pallas_call(functools.partial(back_kernel, bits, fold, layers), in_spe...  88.1 us
    pallas_call x1, Pallas kernels, start_chain(): pl.pallas_call(functools.partial(start_kernel, order, scale, bits), in_sp...  81.9 us
    pallas_call x1, Pallas kernels, turn_chain(): pl.pallas_call(functools.partial(turn_kernel, bits, fold), in_specs=[VM,...  72.1 us
    pallas_call x1, Pallas kernels, bwd_chain(): pl.pallas_call(functools.partial(bwd_kernel, order, scale, bits, fold, la...  40.8 us

profile of v8, /device:TPU:1, one launch (start us, length us, event | category | flops | bytes accessed | tf_op | source)
XLA Modules:
  0.0 566.8 jit_solution(12086613657054140808)
XLA Ops:
  1.8 1.2 dynamic_slice.37
  3.7 1.3 slice.166
  6.9 0.8 slice_reduce_fusion.1
  8.1 2.7 fusion.14
  10.8 1.5 copy.30
  12.3 2.3 copy.31
  14.6 1.2 copy.32
  15.9 3.7 pad_maximum_fusion.wq_hbm.own_q
  20.7 1.2 copy.33
  22.0 81.9 %shard_map.213 = (bf16[256,1152]{1,0:T(8,128)(2,1)S(1)}, bf16[256,1152]{1,0:T(8,128)(2,1)S(1)}, f32[2,8,1152]{2,1,0:T(8,128)S(1)}, f32[4,4,256]{2,1,0:T(4,128)S(...) custom-call(s32[2]{0:T(128)S(1)} %pad_add_fusion.flags_ref, ...), custom_call_target="tpu_custom_call" | custom-call | flops 85899345920 | bytes 25165824 | tf_op jit(solution)/shard_map/pallas_call | solution.py:1249
  105.6 122.9 %shard_map.214 = (f32[256,1152]{1,0:T(8,128)}, bf16[256,1152]{1,0:T(8,128)(2,1)S(1)}, f32[256,1152]{1,0:T(8,128)}, bf16[1024,288]{1,0:T(8,128)(2,1)}, f32[4,4,25...) custom-call(bf16[256,1152]{1,0:T(8,128)(2,1)S(1)} %get-tuple-element, ...), custom_call_target="tpu_custom_call" | custom-call | flops 64424509440 | bytes 25165824 | tf_op jit(solution)/shard_map/pallas_call | solution.py:772
  228.5 72.1 %shard_map.215 = (f32[256,1152]{1,0:T(8,128)}, f32[2,1152]{1,0:T(2,128)S(1)}, f32[256,1152]{1,0:T(8,128)}, bf16[1024,288]{1,0:T(8,128)(2,1)}, bf16[288,1152]{1,0...) custom-call(bf16[256,1152]{1,0:T(8,128)(2,1)S(1)} %get-tuple-element, ...), custom_call_target="tpu_custom_call" | custom-call | flops 64424509440 | bytes 25165824 | tf_op jit(solution)/shard_map/pallas_call | solution.py:913
  302.3 40.8 %shard_map.216 = (bf16[1024,864]{1,0:T(8,128)(2,1)}, f32[4,32,14336]{2,1,0:T(8,128)}, bf16[288,1152]{1,0:T(8,128)(2,1)}, bf16[288,1152]{1,0:T(8,128)(2,1)}, bf16...) custom-call(bf16[1024,864]{1,0:T(8,128)(2,1)} %get-tuple-element.100, ...), custom_call_target="tpu_custom_call" | custom-call | flops 25769803776 | bytes 20971520 | tf_op jit(solution)/shard_map/pallas_call | solution.py:1447
  343.2 88.1 %shard_map.217 = (f32[256,1152]{1,0:T(8,128)}, f32[256,1152]{1,0:T(8,128)}, f32[4,1152]{1,0:T(4,128)S(1)}, bf16[1024,288]{1,0:T(8,128)(2,1)}, bf16[4,256,1152]{2...) custom-call(s32[2]{0:T(128)S(1)} %copy-done.11, ...), custom_call_target="tpu_custom_call" | custom-call | flops 64424509440 | bytes 25165824 | tf_op jit(solution)/shard_map/pallas_call | solution.py:1095
  434.1 109.4 %shard_map.218 = (f32[256,1152]{1,0:T(8,128)}, f32[24,1152]{1,0:T(8,128)S(1)}, f32[4,32,128]{2,1,0:T(8,128)S(1)}, bf16[288,864]{1,0:T(8,128)(2,1)S(1)}, bf16[288...) custom-call(s32[2]{0:T(128)S(1)} %copy-done.11, ...), custom_call_target="tpu_custom_call" | custom-call | flops 96636764160 | bytes 25165824 | tf_op jit(solution)/shard_map/pallas_call | solution.py:1678
  545.1 3.4 select_bitcast_fusion
  550.0 1.3 fusion
  552.2 1.1 fusion.5
  555.0 1.6 copy.36
  557.3 1.2 maximum_bitcast_fusion.1
  558.5 1.9 fusion.3
  560.6 1.6 maximum_bitcast_fusion
  563.5 1.2 select_bitcast_fusion.2
  564.9 1.1 maximum_bitcast_fusion.2
  (136 shorter events, 18.7 us)
Async XLA Ops:
  0.6 19.0 %copy-start = (bf16[1,1152,2,288]{1,3,2,0:T(8,128)(2,1)S(1)}, bf16[1,1152,2,288]{1,3,2,0:T(8,128)(2,1)}, u32[]{:S(2)}) copy-start(bf16[1,1152,2,288]{1,3,2,0:T(8,128)(2,1)} %param.20) | copy-start | bytes 3981316
  5.7 16.3 %copy-start.10 = (s32[2]{0:T(128)}, s32[2]{0:T(128)S(1)}, u32[]{:S(2)}) copy-start(s32[2]{0:T(128)S(1)} %pad_add_fusion.flags_ref) | copy-start | bytes 28
  8.1 13.9 %copy-start.8 = (s32[1,4096]{1,0:T(1,128)}, s32[1,4096]{1,0:T(1,128)S(1)}, u32[]{:S(2)}) copy-start(s32[1,4096]{1,0:T(1,128)S(1)} %reshape.152.lab_ref) | copy-start | bytes 49156
  15.9 3.7 copy-start.36
  19.6 2.3 copy-start.35
  20.3 83.6 %copy-start.33 = (f32[2,1152]{1,0:T(2,128)}, f32[2,1152]{1,0:T(2,128)S(1)}, u32[]{:S(2)}) copy-start(f32[2,1152]{1,0:T(2,128)S(1)} %broadcast.36) | copy-start | bytes 27652
  104.7 123.8 %copy-start.14 = (bf16[256,1152]{1,0:T(8,128)(2,1)}, bf16[256,1152]{1,0:T(8,128)(2,1)S(1)}, u32[]{:S(2)}) copy-start(bf16[256,1152]{1,0:T(8,128)(2,1)S(1)} %get-tuple-element.91.x_ref) | copy-start | bytes 1769476
  228.5 72.1 %copy-start.2 = (bf16[256,1152]{1,0:T(8,128)(2,1)}, bf16[256,1152]{1,0:T(8,128)(2,1)S(1)}, u32[]{:S(2)}) copy-start(bf16[256,1152]{1,0:T(8,128)(2,1)S(1)} %get-tuple-element.99.x_ref.refs_0_) | copy-start | bytes 1769476
  302.3 40.8 %copy-start.9 = (s32[1,4096]{1,0:T(1,128)S(1)}, s32[1,4096]{1,0:T(1,128)}, u32[]{:S(2)}) copy-start(s32[1,4096]{1,0:T(1,128)} %copy-done.8) | copy-start | bytes 49156
  302.3 40.8 %copy-start.11 = (s32[2]{0:T(128)S(1)}, s32[2]{0:T(128)}, u32[]{:S(2)}) copy-start(s32[2]{0:T(128)} %copy-done.10) | copy-start | bytes 28
  343.1 89.2 %copy-start.37 = (bf16[2,1152]{1,0:T(2,128)(2,1)S(1)}, bf16[2,1152]{1,0:T(2,128)(2,1)}, u32[]{:S(2)}) copy-start(bf16[2,1152]{1,0:T(2,128)(2,1)} %param.15) | copy-start | bytes 13828
  343.1 89.3 %copy-start.34 = (f32[2,1152]{1,0:T(2,128)S(1)}, f32[2,1152]{1,0:T(2,128)}, u32[]{:S(2)}) copy-start(f32[2,1152]{1,0:T(2,128)} %copy-done.33) | copy-start | bytes 27652
  431.3 2.0 copy-start.16
  545.1 3.4 copy-start.22
  545.1 3.4 copy-start.23
  545.1 3.4 copy-start.24
  550.0 2.0 copy-start.31
  554.9 1.7 copy-start.19
  555.0 1.6 copy-start.5
  555.0 1.8 copy-start.32
  558.5 1.9 copy-start.20
  558.5 1.9 copy-start.21
  560.6 2.9 copy-start.3
  564.7 1.6 copy-start.1
  (16 other events, 17.0 us)
